TPU v7x, 32 devices: a whole 2x2x4 slice. The times are simulated.
32 devices in a mesh: grp: 4 (over y, x), seq: 8 (over z, core).
Axes of the slice: x: 2, y: 2, z: 4, core: 2. Of those that a mesh axis runs over, the one named last changes fastest.
Arguments:
- events: bfloat16 [8192, 1024], P(('grp', 'seq')), may hold values from -6 to 6
- lengths: int32 [32, 8], P(('grp', 'seq')), may hold values from 1 to 48, as said below
- destinations: int32 [32, 8], P(('grp', 'seq')), may hold values from 0 to 7, as said below
- history: int32 [8192], P(('grp', 'seq')), may hold values from 0 to 4095, as said below
- negatives: int32 [8192, 3], P(('grp', 'seq')), may hold values from 0 to 4095, as said below
- in_weight: bfloat16 [1024, 2048], replicated, may hold values from -0.1875 to 0.1875
- out_weight: bfloat16 [1024, 512], replicated, may hold values from -0.25 to 0.25
- item_table: bfloat16 [4096, 1024], P('seq'), may hold values from -0.1875 to 0.1875
Outputs:
- layer_out: bfloat16 [8192, 1024], P(('grp', 'seq'))
- in_grad: float32 [1024, 2048], P('seq')
- out_grad: float32 [1024, 512], P('seq')
- table_grad: float32 [4096, 1024], P('seq')
Inputs may be any that keep to these rules, and one draw needn't show every extreme that they name: Each loader device holds 8 users whose lengths sum to 256; the longest history is 48. `destinations`: the 8 users of a loader device go to the 8 different devices of its group, one to each, and every device of a group receives users with 256 rows in all. `history`: item i lies in row i % 512 of owner i // 512. The 4 candidates of an event lie on 4 different owners, and after the relayout every device holds exactly 128 candidates of each owner. `negatives`: numbered as history; see there.
All inputs are finite; a program needn't handle non-finite values.
Results may differ from a plain program's by a relative error of at most 0.02.
Values may be sent and summed in bfloat16 or wider, within the bound.
No kernel may reach another device: no remote copies, remote signals or barrier semaphores. Data moves between devices by JAX's collectives and lax.ppermute only.
A program may use at most 128 MiB of HBM per device.

v0:
```python
import jax
import jax.numpy as jnp
from jax import lax
from jax.sharding import PartitionSpec as P

D = 1024
HEADS = 4
HEAD_DIM = 128
NCAND = 4
VOCAB_DEV = 512


epsilon = 1e-05
softmax_warmth = 0.05


def center_scale(values):
    average = jnp.mean(values, -1, keepdims=True)
    centered = values - average
    inverse = lax.rsqrt(jnp.mean(centered * centered, -1, keepdims=True) + epsilon)
    return (centered * inverse, inverse)


def silu_slope(values):
    sigmoid = jax.nn.sigmoid(values)
    return sigmoid * (1.0 + values * (1.0 - sigmoid))


def batch_stacked(pattern, first_operand, second_operand):
    return jnp.einsum(pattern, first_operand, second_operand, preferred_element_type=jnp.float32)


def layer_forward(tokens, attend_mask, in_weight, out_weight, batch_count):
    hidden_width = out_weight.shape[1]
    scoring_scale = HEAD_DIM ** (-0.5)
    features = tokens.astype(jnp.float32)
    normed_in = center_scale(features)[0].astype(jnp.bfloat16)
    preact = jnp.dot(normed_in, in_weight, preferred_element_type=jnp.float32)
    projected = jax.nn.silu(preact).astype(jnp.bfloat16)
    gate_part = projected[:, :hidden_width]
    value_portion = projected[:, hidden_width : 2 * hidden_width].reshape(
        batch_count, -1, hidden_width
    )
    query_portion = projected[:, 2 * hidden_width : 3 * hidden_width].reshape(
        batch_count, -1, hidden_width
    )
    key_portion = projected[:, 3 * hidden_width :].reshape(batch_count, -1, hidden_width)
    score_list, weight_pieces, output_pieces = ([], [], [])
    for current_head in range(HEADS):
        column_begin = current_head * HEAD_DIM
        column_end = column_begin + HEAD_DIM
        attention_scores = (
            batch_stacked(
                "ptx,pux->ptu",
                query_portion[..., column_begin:column_end],
                key_portion[..., column_begin:column_end],
            )
            * scoring_scale
        )
        attention_weight = (jax.nn.silu(attention_scores) * attend_mask).astype(jnp.bfloat16)
        output_pieces.append(
            batch_stacked(
                "fjz,fzy->fjy", attention_weight, value_portion[..., column_begin:column_end]
            )
        )
        score_list.append(attention_scores)
        weight_pieces.append(attention_weight)
    attended = jnp.concatenate(output_pieces, -1).reshape(-1, hidden_width)
    normed, inverse = center_scale(attended)
    gated_rows = (normed * gate_part.astype(jnp.float32)).astype(jnp.bfloat16)
    result = features + lax.dot_general(
        gated_rows, out_weight, (((1,), (1,)), ((), ())), preferred_element_type=jnp.float32
    )
    saved_state = (
        normed_in,
        preact,
        gate_part,
        value_portion,
        query_portion,
        key_portion,
        score_list,
        weight_pieces,
        normed,
        inverse,
        gated_rows,
    )
    return (result, saved_state)


def layer_backward(upstream, saved_state, attend_mask, out_weight, batch_count):
    (
        normed_in,
        preact,
        gate_part,
        value_portion,
        query_portion,
        key_portion,
        score_list,
        weight_pieces,
        normed,
        inverse,
        gated_rows,
    ) = saved_state
    hidden_width = out_weight.shape[1]
    scoring_scale = HEAD_DIM ** (-0.5)
    upstream_b = upstream.astype(jnp.bfloat16)
    grad_gated = jnp.dot(upstream_b, out_weight, preferred_element_type=jnp.float32)
    grad_gate = grad_gated * normed
    grad_normed = grad_gated * gate_part.astype(jnp.float32)
    grad_attended = inverse * (
        grad_normed
        - jnp.mean(grad_normed, -1, keepdims=True)
        - normed * jnp.mean(grad_normed * normed, -1, keepdims=True)
    )
    grad_attended = grad_attended.astype(jnp.bfloat16).reshape(batch_count, -1, hidden_width)
    value_gradient, query_gradient, key_gradient = ([], [], [])
    for current_head in range(HEADS):
        column_begin = current_head * HEAD_DIM
        column_end = column_begin + HEAD_DIM
        gradient_portion = grad_attended[..., column_begin:column_end]
        weight_gradient = batch_stacked(
            "ptx,pux->ptu", gradient_portion, value_portion[..., column_begin:column_end]
        )
        value_gradient.append(
            batch_stacked("hyo,hyx->hox", weight_pieces[current_head], gradient_portion)
        )
        score_gradient = (
            weight_gradient * attend_mask * silu_slope(score_list[current_head]) * scoring_scale
        ).astype(jnp.bfloat16)
        query_gradient.append(
            batch_stacked("fjz,fzy->fjy", score_gradient, key_portion[..., column_begin:column_end])
        )
        key_gradient.append(
            batch_stacked(
                "hyo,hyx->hox", score_gradient, query_portion[..., column_begin:column_end]
            )
        )
    grad_project = jnp.concatenate(
        [
            grad_gate,
            jnp.concatenate(value_gradient, -1).reshape(-1, hidden_width),
            jnp.concatenate(query_gradient, -1).reshape(-1, hidden_width),
            jnp.concatenate(key_gradient, -1).reshape(-1, hidden_width),
        ],
        -1,
    )
    grad_preact = (grad_project * silu_slope(preact)).astype(jnp.bfloat16)
    return (normed_in, grad_preact, upstream_b, gated_rows)


def item_scores(result, cand_rows):
    length_out = jnp.sqrt(jnp.sum(result * result, -1, keepdims=True) + epsilon)
    single_output = result / length_out
    row_float = cand_rows.astype(jnp.float32)
    row_length = jnp.sqrt(jnp.sum(row_float * row_float, -1, keepdims=True) + epsilon)
    single_row = row_float / row_length
    logit_values = jnp.sum(single_output[:, None, :] * single_row, -1) / softmax_warmth
    exponent = jnp.exp(logit_values)
    softmax_weights = exponent / jnp.sum(exponent, -1, keepdims=True)
    logit_gradient = softmax_weights - (jnp.arange(NCAND) == 0).astype(jnp.float32)[None, :]
    gathered_rows = jnp.sum(logit_gradient[..., None] * single_row, 1) / softmax_warmth
    upstream = (
        gathered_rows - single_output * jnp.sum(single_output * gathered_rows, -1, keepdims=True)
    ) / length_out
    scattered_rows = logit_gradient[..., None] * single_output[:, None, :] / softmax_warmth
    grad_rows = (
        (scattered_rows - single_row * jnp.sum(single_row * scattered_rows, -1, keepdims=True))
        / row_length
    ).astype(jnp.bfloat16)
    return (upstream, grad_rows)


def body(events, lengths, destinations, history, negatives, in_weight, out_weight, item_table):
    owners = lax.axis_size("seq")
    hidden_width = out_weight.shape[1]
    tok_rows = events.shape[0]
    slot_rows = 3 * tok_rows // (2 * owners)
    user_lengths = lengths[0]
    user_dests = destinations[0]
    starts = jnp.cumsum(user_lengths) - user_lengths
    candidates = jnp.concatenate([history[:, None], negatives], 1)
    chosen_user = (user_dests[None, :] == jnp.arange(owners)[:, None]).astype(jnp.int32)
    send_length = jnp.sum(chosen_user * user_lengths[None, :], 1)
    send_start = jnp.sum(chosen_user * starts[None, :], 1)
    slot_index = jnp.arange(slot_rows)
    filled = slot_index[None, :] < send_length[:, None]
    sources = jnp.clip(send_start[:, None] + slot_index[None, :], 0, tok_rows - 1)
    send_tokens = jnp.where(filled[..., None], events[sources], jnp.zeros((), jnp.bfloat16))
    send_items = jnp.where(filled[..., None], candidates[sources], 0)
    got_tokens, got_items, got_length = (
        lax.all_to_all(send_tokens, "seq", split_axis=0, concat_axis=0, tiled=True),
        lax.all_to_all(send_items, "seq", split_axis=0, concat_axis=0, tiled=True),
        lax.all_to_all(send_length[:, None], "seq", split_axis=0, concat_axis=0, tiled=True),
    )
    counts = got_length[:, 0]
    block_ends = jnp.cumsum(counts)
    offsets = block_ends - counts
    positions = jnp.arange(tok_rows)
    anchor = jnp.minimum(
        jnp.sum((block_ends[None, :] <= positions[:, None]).astype(jnp.int32), 1), owners - 1
    )
    placed = anchor * slot_rows + positions - offsets[anchor]
    slot_tokens = got_tokens.reshape(owners * slot_rows, D)
    relayed_items = got_items.reshape(owners * slot_rows, NCAND)[placed]
    attend_mask = (
        (anchor[:, None] == anchor[None, :]) & (positions[None, :] <= positions[:, None])
    ).astype(jnp.float32)[None]
    batch_count = 1
    result_rows, saved_state = layer_forward(
        slot_tokens[placed], attend_mask, in_weight, out_weight, batch_count
    )
    per_owner = tok_rows * NCAND // owners
    flat_items = relayed_items.reshape(-1)
    owner_order = jnp.argsort(flat_items // VOCAB_DEV, stable=True)
    asked_rows = (flat_items % VOCAB_DEV)[owner_order].reshape(owners, per_owner)
    requested = lax.all_to_all(asked_rows, "seq", split_axis=0, concat_axis=0, tiled=True)
    found_rows = item_table[requested]
    fetched, requested = (
        lax.all_to_all(found_rows, "seq", split_axis=0, concat_axis=0, tiled=True),
        requested,
    )
    cand_rows = (
        jnp.zeros((tok_rows * NCAND, D), jnp.bfloat16)
        .at[owner_order]
        .set(fetched.reshape(-1, D))
        .reshape(tok_rows, NCAND, D)
    )
    upstream, grad_rows = item_scores(result_rows, cand_rows)
    outgoing = grad_rows.reshape(-1, D)[owner_order].reshape(owners, per_owner, D)
    returned = lax.all_to_all(outgoing, "seq", split_axis=0, concat_axis=0, tiled=True)
    table_part = jax.ops.segment_sum(
        returned.reshape(-1, D).astype(jnp.float32), requested.reshape(-1), num_segments=VOCAB_DEV
    )
    normed_in, grad_preact, upstream_b, gated_rows = layer_backward(
        upstream, saved_state, attend_mask, out_weight, batch_count
    )
    first_term = lax.dot_general(
        lax.slice_in_dim(normed_in, 0, lax.axis_size("seq") * (D // owners), axis=1),
        grad_preact,
        (((0,), (0,)), ((), ())),
        preferred_element_type=jnp.float32,
    )
    second_term = lax.dot_general(
        lax.slice_in_dim(upstream_b, 0, lax.axis_size("seq") * (D // owners), axis=1),
        gated_rows,
        (((0,), (0,)), ((), ())),
        preferred_element_type=jnp.float32,
    )
    weight_shard = lax.psum_scatter(
        jnp.concatenate([first_term, second_term], 1).astype(jnp.bfloat16),
        "seq",
        scatter_dimension=0,
        tiled=True,
    ).astype(jnp.float32)
    table_grad, weight_shard = (
        lax.psum(table_part.astype(jnp.bfloat16), "grp").astype(jnp.float32),
        lax.psum(weight_shard.astype(jnp.bfloat16), "grp").astype(jnp.float32),
    )
    layer_out = result_rows.astype(jnp.bfloat16)
    return (
        layer_out,
        weight_shard[:, : 4 * hidden_width],
        weight_shard[:, 4 * hidden_width :],
        table_grad,
    )


def solution(mesh):
    return jax.shard_map(
        body,
        mesh=mesh,
        in_specs=(
            P(("grp", "seq"), None),
            P(("grp", "seq"), None),
            P(("grp", "seq"), None),
            P(("grp", "seq")),
            P(("grp", "seq"), None),
            P(),
            P(),
            P("seq", None),
        ),
        out_specs=(P(("grp", "seq"), None), P("seq", None), P("seq", None), P("seq", None)),
        check_vma=False,
    )
```

profile of v0, /device:TPU:0, one launch (start us, length us, event | category | flops | bytes accessed | tf_op | source)
XLA Modules:
  0.0 357.4 jit_solution(6090691244825131999)
XLA Ops:
  10.3 6.3 %all-to-all-start.1 = ((s32[8,1,1]{2,1,0:T(1,128)}), s32[8,1,1]{2,1,0:T(1,128)S(1)}, u32[]{:S(2)}, u32[]{:S(2)}) async-start(s32[8,1,1]{2,1,0:T(1,128)} %copy.91), calls=%async_computation.1 | async-start | bytes 8192 | tf_op jit(solution)/shard_map/all_to_all | solution.py:193
  17.7 3.9 %gather_fusion = bf16[384,1024]{1,0:T(8,128)(2,1)S(1)} fusion(bf16[256,1024]{1,0:T(8,128)(2,1)} %param.8, s32[1024]{0:T(1024)S(1)} %pad_clamp_fusion.1), kind=kCustom, calls=%fused_computation | custom fusion | bytes 1574400 | tf_op jit(solution)/shard_map/gather | solution.py:188
  23.5 5.1 %all-to-all-start.2 = ((s32[8,1,192]{2,1,0:T(1,128)}), s32[8,1,192]{2,1,0:T(1,128)S(1)}, u32[]{:S(2)}, u32[]{:S(2)}) async-start(s32[8,1,192]{2,1,0:T(1,128)} %reshape.709), calls=%async_computation.2 | async-start | bytes 16384 | tf_op jit(solution)/shard_map/all_to_all | solution.py:192
  29.9 4.4 %compare_select_fusion.5 = s32[256,1]{0,1:T(1,128)S(1)} fusion(s32[]{:T(128)} %bitcast.9, s32[]{:T(128)} %bitcast.10, s32[]{:T(128)} %bitcast.11, s32[]{:T(128)} %bitcast.12, s32[]{:T(128)} %bitcast.13, s32[]{:T(128)} %bitcast.15, s32[]{:T(128)} %bitcast.14, s32[256,1]{0,1:T(1,128)S(1)} %bitcast.232), kind=kLoop, calls=%fused_computation.149 | loop fusion | flops 3840 | bytes 2076 | tf_op jit(solution)/shard_map/gather | solution.py:202
  37.3 4.4 %sort.17 = (s32[1024]{0:T(1024)}, s32[1024]{0:T(1024)S(1)}) sort(s32[1024]{0:T(1024)S(1)} %get-tuple-element.22, s32[1024]{0:T(1024)S(1)} %iota.37), dimensions={0}, to_apply=%region_13.14 | sort | flops 10240 | bytes 16384 | tf_op jit(solution)/shard_map/jit(argsort)/sort | solution.py:214
  41.7 8.8 %gather_fusion.4 = s32[1024]{0:T(1024)} fusion(s32[1024]{0:T(1024)S(1)} %get-tuple-element.21, s32[1024]{0:T(1024)S(1)} %get-tuple-element.19), kind=kCustom, calls=%fused_computation.4 | custom fusion | bytes 12288 | tf_op jit(solution)/shard_map/gather | solution.py:215
  50.5 5.1 %all-to-all-start.3 = ((s32[8,1,128]{2,1,0:T(1,128)}), s32[8,1,128]{2,1,0:T(1,128)S(1)}, u32[]{:S(2)}, u32[]{:S(2)}) async-start(s32[8,1,128]{2,1,0:T(1,128)} %bitcast.42), calls=%async_computation.3 | async-start | bytes 8192 | tf_op jit(solution)/shard_map/all_to_all | solution.py:216
  56.6 4.5 %all-to-all-done.3 = s32[8,1,128]{2,1,0:T(1,128)S(1)} async-done(((s32[8,1,128]{2,1,0:T(1,128)}), s32[8,1,128]{2,1,0:T(1,128)S(1)}, u32[]{:S(2)}, u32[]{:S(2)}) %all-to-all-start.3) | async-done | bytes 4128 | tf_op jit(solution)/shard_map/all_to_all | solution.py:216
  61.1 3.5 all-to-all-start
  65.2 5.4 %gather_fusion.5 = bf16[1024,1024]{1,0:T(8,128)(2,1)} fusion(bf16[512,1024]{1,0:T(8,128)(2,1)S(1)} %copy-done, s32[1024]{0:T(1024)S(1)} %fusion.34), kind=kCustom, calls=%fused_computation.5 | custom fusion | bytes 4198400 | tf_op jit(solution)/shard_map/gather | solution.py:217
  70.5 15.0 %all-to-all-done = bf16[8,48,1024]{2,1,0:T(8,128)(2,1)S(1)} async-done(((bf16[8,48,1024]{2,1,0:T(8,128)(2,1)}), bf16[8,48,1024]{2,1,0:T(8,128)(2,1)S(1)}, u32[]{:S(2)}, u32[]{:S(2)}) %all-to-all-start) | async-done | bytes 786464 | tf_op jit(solution)/shard_map/all_to_all | solution.py:191
  85.5 4.4 %all-to-all-start.4 = ((bf16[8,128,1024]{2,1,0:T(8,128)(2,1)}), bf16[8,128,1024]{2,1,0:T(8,128)(2,1)}, u32[]{:S(2)}, u32[]{:S(2)}) async-start(bf16[8,128,1024]{2,1,0:T(8,128)(2,1)} %bitcast.202), calls=%async_computation.4 | async-start | bytes 4194304 | tf_op jit(solution)/shard_map/all_to_all | solution.py:219
  91.8 4.9 %multiply_convert_fusion = (bf16[256,2048]{1,0:T(8,128)(2,1)S(1)}, f32[256,2048]{1,0:T(8,128)}) fusion(bf16[1024,2048]{1,0:T(8,128)(2,1)} %param.13, bf16[256,1024]{1,0:T(8,128)(2,1)S(1)} %gather_fusion.1, f32[256]{0:T(256)S(1)} %add_rsqrt_fusion.1, f32[256]{0:T(256)S(1)} %broadcast_multiply_fusion.2), kind=kOutput, calls=%fused_computation.22 | convolution fusion | flops 1077411840 | bytes 7866368 | tf_op jit(solution)/shard_map/dot_general | solution.py:38
  100.0 1.8 multiply_reduce_fusion.5
  102.8 3.1 mul.315
  106.0 5.4 %mul.316 = f32[1024,1024]{1,0:T(8,128)} reshape(f32[256,4,1024]{2,1,0:T(4,128)} %mul.315) | data formatting | bytes 8388608 | tf_op jit(solution)/shard_map/mul | solution.py:157
  111.3 27.6 %all-to-all-done.4 = bf16[8,128,1024]{2,1,0:T(8,128)(2,1)} async-done(((bf16[8,128,1024]{2,1,0:T(8,128)(2,1)}), bf16[8,128,1024]{2,1,0:T(8,128)(2,1)}, u32[]{:S(2)}, u32[]{:S(2)}) %all-to-all-start.4) | async-done | bytes 2097184 | tf_op jit(solution)/shard_map/all_to_all | solution.py:219
  138.9 6.8 %scatter_custom_fusion = bf16[1024,1024]{1,0:T(8,128)(2,1)S(1)} fusion(s32[1024]{0:T(1024)S(1)} %get-tuple-element.20, bf16[1024,1024]{1,0:T(8,128)(2,1)} %bitcast.46, bf16[]{:T(256)} %constant.83.clone.1), kind=kCustom, calls=%fused_computation.67 | custom fusion | bytes 2097664 | tf_op jit(solution)/shard_map/scatter | solution.py:225
  146.2 3.0 reshape.577
  150.1 2.9 multiply_reduce_fusion.2
  155.8 4.6 %multiply_reduce_fusion.1 = f32[256,1024]{1,0:T(8,128)S(1)} fusion(f32[256,4,1024]{2,1,0:T(4,128)} %reshape.577, f32[256,4]{1,0:T(8,128)} %sqrt.22, f32[256,4]{1,0:T(8,128)S(1)} %divide_subtract_fusion), kind=kLoop, calls=%fused_computation.15 | loop fusion | flops 2883584 | bytes 5251072 | tf_op jit(solution)/shard_map/reduce_sum | solution.py:161
  169.9 1.6 convolution_convert_fusion
  171.5 2.7 pad_maximum_fusion
  175.2 3.3 multiply_reduce_fusion
  178.6 2.7 divide_convert_fusion
  181.4 5.3 %gather_fusion.6 = bf16[1024,1024]{1,0:T(8,128)(2,1)} fusion(bf16[1024,1024]{1,0:T(8,128)(2,1)S(1)} %divide_convert_fusion, s32[1024]{0:T(1024)S(1)} %get-tuple-element.19), kind=kCustom, calls=%fused_computation.6 | custom fusion | bytes 4198400 | tf_op jit(solution)/shard_map/gather | solution.py:229
  186.7 82.8 %all_to_all.41 = bf16[8,128,1024]{2,1,0:T(8,128)(2,1)S(1)} all-to-all(bf16[8,128,1024]{2,1,0:T(8,128)(2,1)} %bitcast.203), channel_id=1, replica_groups=mesh['grp'=4,'seq'=8] {'seq'}, dimensions={0} | all-to-all | bytes 4194304 | tf_op jit(solution)/shard_map/all_to_all | solution.py:230
  269.5 10.5 %scatter_custom_fusion.1 = f32[512,1024]{1,0:T(8,128)} fusion(s32[1024]{0:T(1024)} %bitcast.230, bf16[1024,1024]{1,0:T(8,128)(2,1)S(1)} %bitcast.204, f32[]{:T(128)} %constant.88.clone.1), kind=kCustom, calls=%fused_computation.10 | custom fusion | flops 2097152 | bytes 4194816 | tf_op jit(solution)/shard_map/scatter-add | solution.py:231
  280.1 2.7 convert_element_type.134
  282.8 62.3 %all-reduce.3.cloned.1.call-done = (bf16[128,2560]{1,0:T(8,128)(2,1)}, bf16[512,1024]{1,0:T(8,128)(2,1)}) async-done(((bf16[128,2560]{1,0:T(8,128)(2,1)}, bf16[512,1024]{1,0:T(8,128)(2,1)}), (bf16[128,2560]{1,0:T(8,128)(2,1)}, bf16[512,1024]{1,0:T(8,128)(2,1)})) %all-reduce.3.cloned.1.call-update) | async-done | bytes 1703952 | tf_op jit(solution)/shard_map/psum | solution.py:257
  345.1 2.3 slice.143
  347.3 1.6 slice.144
  (204 shorter events, 33.6 us)
Async XLA Ops:
  7.2 58.0 %copy-start = (bf16[512,1024]{1,0:T(8,128)(2,1)S(1)}, bf16[512,1024]{1,0:T(8,128)(2,1)}, u32[]{:S(2)}) copy-start(bf16[512,1024]{1,0:T(8,128)(2,1)} %param.15) | copy-start | bytes 3145732
  10.3 13.3 %all-to-all-start.1 = ((s32[8,1,1]{2,1,0:T(1,128)}), s32[8,1,1]{2,1,0:T(1,128)S(1)}, u32[]{:S(2)}, u32[]{:S(2)}) async-start(s32[8,1,1]{2,1,0:T(1,128)} %copy.91), calls=%async_computation.1 | async-start | bytes 8192 | tf_op jit(solution)/shard_map/all_to_all | solution.py:193
  23.5 11.4 %all-to-all-start.2 = ((s32[8,1,192]{2,1,0:T(1,128)}), s32[8,1,192]{2,1,0:T(1,128)S(1)}, u32[]{:S(2)}, u32[]{:S(2)}) async-start(s32[8,1,192]{2,1,0:T(1,128)} %reshape.709), calls=%async_computation.2 | async-start | bytes 16384 | tf_op jit(solution)/shard_map/all_to_all | solution.py:192
  29.8 67.5 %copy-start.38 = (s32[256]{0:T(256)}, s32[256]{0:T(256)S(1)}, u32[]{:S(2)}) copy-start(s32[256]{0:T(256)S(1)} %broadcast_minimum_fusion) | copy-start | bytes 3076
  50.5 10.6 %all-to-all-start.3 = ((s32[8,1,128]{2,1,0:T(1,128)}), s32[8,1,128]{2,1,0:T(1,128)S(1)}, u32[]{:S(2)}, u32[]{:S(2)}) async-start(s32[8,1,128]{2,1,0:T(1,128)} %bitcast.42), calls=%async_computation.3 | async-start | bytes 8192 | tf_op jit(solution)/shard_map/all_to_all | solution.py:216
  61.1 9.5 %copy-start.33 = (s32[8,1,128]{2,1,0:T(1,128)}, s32[8,1,128]{2,1,0:T(1,128)S(1)}, u32[]{:S(2)}) copy-start(s32[8,1,128]{2,1,0:T(1,128)S(1)} %all-to-all-done.3) | copy-start | bytes 12292
  61.1 24.5 %all-to-all-start = ((bf16[8,48,1024]{2,1,0:T(8,128)(2,1)}), bf16[8,48,1024]{2,1,0:T(8,128)(2,1)S(1)}, u32[]{:S(2)}, u32[]{:S(2)}) async-start(bf16[8,48,1024]{2,1,0:T(8,128)(2,1)} %broadcast_select_fusion), calls=%async_computation | async-start | bytes 1572864 | tf_op jit(solution)/shard_map/all_to_all | solution.py:191
  85.5 53.4 %all-to-all-start.4 = ((bf16[8,128,1024]{2,1,0:T(8,128)(2,1)}), bf16[8,128,1024]{2,1,0:T(8,128)(2,1)}, u32[]{:S(2)}, u32[]{:S(2)}) async-start(bf16[8,128,1024]{2,1,0:T(8,128)(2,1)} %bitcast.202), calls=%async_computation.4 | async-start | bytes 4194304 | tf_op jit(solution)/shard_map/all_to_all | solution.py:219
  89.9 192.9 %reduce-scatter.2.cloned.1.call-start = ((), (), s32[]{:S(2)}) async-start(), calls=%async_computation.7 | async-start | bytes 5898240 | tf_op jit(solution)/shard_map/reduce_scatter | solution.py:249
  91.3 8.7 %copy-start.4 = (bf16[256,1024]{1,0:T(8,128)(2,1)}, bf16[256,1024]{1,0:T(8,128)(2,1)S(1)}, u32[]{:S(2)}) copy-start(bf16[256,1024]{1,0:T(8,128)(2,1)S(1)} %gather_fusion.1) | copy-start | bytes 1572868
  91.4 5.2 %copy-start.40 = (f32[256]{0:T(256)}, f32[256]{0:T(256)S(1)}, u32[]{:S(2)}) copy-start(f32[256]{0:T(256)S(1)} %broadcast_multiply_fusion.2) | copy-start | bytes 3076
  91.7 4.9 %copy-start.45 = (f32[256]{0:T(256)}, f32[256]{0:T(256)S(1)}, u32[]{:S(2)}) copy-start(f32[256]{0:T(256)S(1)} %add_rsqrt_fusion.1) | copy-start | bytes 3076
  96.7 3.4 copy-start.17
  96.7 1.6 copy-start.6
  96.7 2.7 copy-start.15
  98.4 3.5 copy-start.19
  98.4 3.5 copy-start.21
  98.4 3.5 copy-start.23
  98.4 3.5 copy-start.25
  99.1 2.8 copy-start.8
  99.4 2.5 copy-start.10
  99.8 2.1 copy-start.12
  99.8 2.1 copy-start.34
  100.0 2.8 copy-start.42
  101.9 4.0 %copy-start.36 = (f32[256]{0:T(256)}, f32[256]{0:T(256)S(1)}, u32[]{:S(2)}) copy-start(f32[256]{0:T(256)S(1)} %add_sqrt_fusion.1) | copy-start | bytes 3076
  145.7 29.4 %copy-start.2 = (bf16[1024,1024]{1,0:T(8,128)(2,1)}, bf16[1024,1024]{1,0:T(8,128)(2,1)S(1)}, u32[]{:S(2)}) copy-start(bf16[1024,1024]{1,0:T(8,128)(2,1)S(1)} %scatter_custom_fusion) | copy-start | bytes 6291460
  160.5 1.7 copy-start.47
  168.1 1.8 copy-start.49
  174.2 170.9 %all-reduce.3.cloned.1.call-start = ((), (), s32[]{:S(2)}) async-start(), calls=%async_computation.8 | async-start | bytes 3407872 | tf_op jit(solution)/shard_map/psum | solution.py:257
  175.2 3.5 copy-start.3
  345.1 3.9 %copy-start.14 = (bf16[512,1024]{1,0:T(8,128)(2,1)S(1)}, bf16[512,1024]{1,0:T(8,128)(2,1)}, u32[]{:S(2)}) copy-start(bf16[512,1024]{1,0:T(8,128)(2,1)} %get-tuple-element.11) | copy-start | bytes 3145732
  345.1 5.5 %copy-start.1 = (bf16[512,1024]{1,0:T(8,128)(2,1)S(1)}, bf16[512,1024]{1,0:T(8,128)(2,1)}, u32[]{:S(2)}) copy-start(bf16[512,1024]{1,0:T(8,128)(2,1)} %param.15) | copy-start | bytes 3145732
  (25 other events, 29.1 us)
Sparse Core Ops, SparseCore 0:
  174.3 89.8 reduce-scatter.1
  282.9 62.0 all-reduce.2
where the time goes:
time: 359 us; the launch traced here: 357 us
  waiting for transfers between devices  109 us (30%)
  blocking collectives  82.8 us (23%)
  local copies, waits for them, and re-layouts  58.8 us (16%)
  other arithmetic  51.4 us (14%)
  starting transfers between devices  24.7 us (7%)
  matrix products  15.2 us (4%)
  between operations  15.1 us (4%)
    all_to_all x1, blocking collectives, body(): lax.all_to_all(outgoing, 'seq', split_axis=0, concat_axis=0, tiled=True)  82.8 us
    psum x1, waiting for transfers between devices, body(): lax.psum(weight_shard.astype(jnp.bfloat16), 'grp').astype(jnp.float32)  62.3 us
    all_to_all x1, waiting for transfers between devices, body(): lax.all_to_all(found_rows, 'seq', split_axis=0, concat_axis=0, tiled=True)  27.6 us
    all_to_all x1, waiting for transfers between devices, body(): lax.all_to_all(send_tokens, 'seq', split_axis=0, concat_axis=0, tiled=True)  15 us
    scatter-add x1, other arithmetic, body(): jax.ops.segment_sum(returned.reshape(-1, D).astype(jnp.float32), requeste...  10.5 us
    gather x1, local copies, waits for them, and re-layouts, body(): (flat_items % VOCAB_DEV)[owner_order].reshape(owners, per_owner)  8.83 us
    mul x2, local copies, waits for them, and re-layouts, item_scores(): single_output[:, None, :] * single_row  8.51 us
  transfers between devices with their start and end apart: 7, of which 4 were waited for; matrix products, arithmetic and copies ran while one was open for 18% of the time, Pallas kernels for 0%

commit v1 on v0

v1 whole, which is shorter than its diff:
```python
import jax
import jax.numpy as jnp
from jax import lax
from jax.sharding import PartitionSpec as P

HEADS = 4
HEAD_DIM = 128
NCAND = 4

epsilon = 1e-05
softmax_warmth = 0.05


def center_scale(values):
    average = jnp.mean(values, -1, keepdims=True)
    centered = values - average
    inverse = lax.rsqrt(jnp.mean(centered * centered, -1, keepdims=True) + epsilon)
    return (centered * inverse, inverse)


def silu_slope(values):
    sigmoid = jax.nn.sigmoid(values)
    return sigmoid * (1.0 + values * (1.0 - sigmoid))


def dot(a, b, dims):
    return lax.dot_general(a, b, (dims, ((), ())), preferred_element_type=jnp.float32)


NN = ((1,), (0,))
NT = ((1,), (1,))
TN = ((0,), (0,))


def layer_forward(tokens, mask, in_weight, out_weight):
    hidden = out_weight.shape[1]
    scale = HEAD_DIM ** (-0.5)
    features = tokens.astype(jnp.float32)
    normed_in = center_scale(features)[0].astype(jnp.bfloat16)
    preact = dot(normed_in, in_weight, NN)
    projected = jax.nn.silu(preact).astype(jnp.bfloat16)
    u, v, q, k = [projected[:, i * hidden : (i + 1) * hidden] for i in range(4)]
    scores, weights, outputs = ([], [], [])
    for head in range(HEADS):
        cols = slice(head * HEAD_DIM, (head + 1) * HEAD_DIM)
        score = dot(q[:, cols], k[:, cols], NT) * scale
        weight = jnp.where(mask, jax.nn.silu(score), 0.0).astype(jnp.bfloat16)
        outputs.append(dot(weight, v[:, cols], NN))
        scores.append(score)
        weights.append(weight)
    attended = jnp.concatenate(outputs, -1)
    normed, inverse = center_scale(attended)
    gated = (normed * u.astype(jnp.float32)).astype(jnp.bfloat16)
    result = features + dot(gated, out_weight, NT)
    return (result, (normed_in, preact, u, v, q, k, scores, weights, normed, inverse, gated))


def layer_backward(upstream_b, saved, mask, out_weight):
    normed_in, preact, u, v, q, k, scores, weights, normed, inverse, gated = saved
    scale = HEAD_DIM ** (-0.5)
    grad_gated = dot(upstream_b, out_weight, NN)
    grad_u = grad_gated * normed
    grad_normed = grad_gated * u.astype(jnp.float32)
    grad_attended = inverse * (
        grad_normed
        - jnp.mean(grad_normed, -1, keepdims=True)
        - normed * jnp.mean(grad_normed * normed, -1, keepdims=True)
    )
    grad_attended = grad_attended.astype(jnp.bfloat16)
    grad_v, grad_q, grad_k = ([], [], [])
    for head in range(HEADS):
        cols = slice(head * HEAD_DIM, (head + 1) * HEAD_DIM)
        part = grad_attended[:, cols]
        grad_attn = dot(part, v[:, cols], NT)
        grad_v.append(dot(weights[head], part, TN))
        grad_score = jnp.where(mask, grad_attn * silu_slope(scores[head]) * scale, 0.0)
        grad_score = grad_score.astype(jnp.bfloat16)
        grad_q.append(dot(grad_score, k[:, cols], NN))
        grad_k.append(dot(grad_score, q[:, cols], TN))
    grad_project = jnp.concatenate([grad_u] + grad_v + grad_q + grad_k, -1)
    return (grad_project * silu_slope(preact)).astype(jnp.bfloat16)


def body(events, lengths, destinations, history, negatives, in_weight, out_weight, item_table):
    groups = lax.axis_size("grp")
    owners = lax.axis_size("seq")
    chips = owners // 2
    grp = lax.axis_index("grp")
    seq = lax.axis_index("seq")
    chip, core = seq // 2, seq % 2
    tok = events.shape[0]
    vocab_dev, width = item_table.shape
    hidden = out_weight.shape[1]
    share = vocab_dev // groups
    slot = 3 * tok // (2 * owners)
    f32, b16 = jnp.float32, jnp.bfloat16

    def to_chip(x, d):
        pairs = [(2 * a + b, 2 * ((a + d) % chips) + b) for a in range(chips) for b in range(2)]
        return lax.ppermute(x, "seq", pairs)

    def to_group(x, k):
        return lax.ppermute(x, "grp", [(a, a ^ k) for a in range(groups)])

    def to_core(x):
        return lax.ppermute(x, "seq", [(a, a ^ 1) for a in range(owners)])

    table = item_table.astype(f32)
    table_inv = lax.rsqrt(jnp.sum(table * table, -1, keepdims=True) + epsilon)
    own = (table * table_inv).astype(b16)
    quarter = lax.dynamic_slice_in_dim(own, grp * share, share, 0)
    quarter_inv = lax.dynamic_slice_in_dim(table_inv, grp * share, share, 0)
    others = jnp.concatenate([to_chip(quarter, d) for d in range(1, chips)], 0)
    pieces = [own, others] + [to_group(others, k) for k in range(1, groups)]
    blocks = []
    row = jnp.arange(vocab_dev)
    far = jnp.arange((chips - 1) * share)
    for away in range(2):
        side = core ^ away
        for n, piece in enumerate(pieces):
            if n == 0:
                ids = (2 * chip + side) * vocab_dev + row
            else:
                at = (chip - 1 - far // share + chips) % chips
                ids = (2 * at + side) * vocab_dev + (grp ^ (n - 1)) * share + far % share
            blocks.append((to_core(piece) if away else piece, ids))

    user_lengths, user_dests = lengths[0], destinations[0]
    ends = jnp.cumsum(user_lengths)
    starts = ends - user_lengths
    position = jnp.arange(tok)
    inside = (starts[None, :] <= position[:, None]) & (position[:, None] < ends[None, :])
    user = jnp.sum(jnp.where(inside, jnp.arange(owners)[None, :], 0), 1)
    dest = jnp.sum(jnp.where(inside, user_dests[None, :], 0), 1)
    within = position - jnp.sum(jnp.where(inside, starts[None, :], 0), 1)
    mask = (user[:, None] == user[None, :]) & (position[None, :] <= position[:, None])
    send_length = jnp.sum(
        jnp.where(user_dests[None, :] == jnp.arange(owners)[:, None], user_lengths[None, :], 0), 1
    )
    counts = lax.all_to_all(send_length[:, None], "seq", 0, 0, tiled=True)[:, 0]

    result, saved = layer_forward(events, mask, in_weight, out_weight)
    normed_in, gated = saved[0], saved[-1]

    slot_id = jnp.arange(owners * slot)
    place = (dest * slot + within)[None, :] == slot_id[:, None]
    outgoing = dot(place.astype(b16), result.astype(b16), NN).astype(b16)
    arrived = lax.all_to_all(
        outgoing.reshape(owners, slot, width), "seq", 0, 0, tiled=True
    ).reshape(owners * slot, width)
    first = jnp.cumsum(counts) - counts
    slot_row = slot_id % slot
    target = jnp.where(slot_row < jnp.repeat(counts, slot), jnp.repeat(first, slot) + slot_row, -1)
    layer_out = dot((position[:, None] == target[None, :]).astype(b16), arrived, NN).astype(b16)

    length_out = jnp.sqrt(jnp.sum(result * result, -1, keepdims=True) + epsilon)
    unit = result / length_out
    unit_b = unit.astype(b16)
    candidates = jnp.concatenate([history[:, None], negatives], 1)
    logits = [0.0] * NCAND
    for block, ids in blocks:
        product = dot(unit_b, block, NT)
        for c in range(NCAND):
            hit = candidates[:, c : c + 1] == ids[None, :]
            logits[c] += jnp.sum(jnp.where(hit, product, 0.0), -1, keepdims=True)
    exponent = jnp.exp(jnp.concatenate(logits, 1) / softmax_warmth)
    softmax = exponent / jnp.sum(exponent, -1, keepdims=True)
    coef = (softmax - (jnp.arange(NCAND) == 0).astype(f32)[None, :]) / softmax_warmth
    pulled = 0.0
    for block, ids in blocks:
        spread = 0.0
        for c in range(NCAND):
            hit = candidates[:, c : c + 1] == ids[None, :]
            spread += jnp.where(hit, coef[:, c : c + 1], 0.0)
        pulled += dot(spread.astype(b16), block, NN)
    upstream = (pulled - unit * jnp.sum(unit * pulled, -1, keepdims=True)) / length_out
    upstream_b = upstream.astype(b16)

    units = jnp.stack([unit_b] + [to_group(unit_b, k) for k in range(1, groups)])
    tags = jnp.concatenate([coef.T, candidates.T.astype(f32)], 0)
    tags = jnp.stack([tags] + [to_group(tags, k) for k in range(1, groups)])
    units = jnp.concatenate([units, to_core(units)], 0).reshape(-1, width)
    tags = jnp.concatenate([tags, to_core(tags)], 0).transpose(1, 0, 2).reshape(2 * NCAND, -1)
    mine = jnp.arange(chips * share)
    mine_ids = (2 * ((chip - mine // share + chips) % chips) + core) * vocab_dev + grp * share + mine % share
    spread = 0.0
    for c in range(NCAND):
        hit = tags[NCAND + c][None, :] == mine_ids.astype(f32)[:, None]
        spread += jnp.where(hit, tags[c][None, :], 0.0)
    summed = dot(spread.astype(b16), units, NN)
    near = jnp.concatenate([quarter, others], 0).astype(f32)
    summed = summed - near * jnp.sum(near * summed, -1, keepdims=True)
    summed = summed.astype(b16).reshape(chips, share, width)
    total = summed[0].astype(f32)
    for d in range(1, chips):
        total += to_chip(summed[d], -d).astype(f32)
    total = (total * quarter_inv).astype(b16)
    table_grad = jnp.zeros((vocab_dev, width), f32)
    for k in range(groups):
        part = to_group(total, k) if k else total
        table_grad = lax.dynamic_update_slice_in_dim(table_grad, part.astype(f32), (grp ^ k) * share, 0)

    grad_preact = layer_backward(upstream_b, saved, mask, out_weight)
    rows = width // owners

    def both_cores(x):
        x = x.reshape(tok, chips, 2, rows)
        even, odd = x[:, :, 0].reshape(tok, -1), x[:, :, 1].reshape(tok, -1)
        keep = jnp.where(core == 0, even, odd)
        give = jnp.where(core == 0, odd, even)
        return jnp.concatenate([keep, to_core(give)], 0)

    def doubled(x):
        return jnp.concatenate([x, to_core(x)], 0)

    in_part = dot(both_cores(normed_in), doubled(grad_preact), TN)
    out_part = dot(both_cores(upstream_b), doubled(gated), TN)
    weight = jnp.concatenate([in_part, out_part], 1).astype(b16)
    fine = rows // groups
    weight = weight.reshape(chips, groups, fine, 5 * hidden)
    sums = lax.dynamic_index_in_dim(weight, grp, 1, False).astype(f32)
    for k in range(1, groups):
        sums += to_group(lax.dynamic_index_in_dim(weight, grp ^ k, 1, False), k).astype(f32)
    sums = sums.astype(b16)
    line = lax.dynamic_index_in_dim(sums, chip, 0, False).astype(f32)
    for d in range(1, chips):
        line += to_chip(lax.dynamic_index_in_dim(sums, (chip + d) % chips, 0, False), d).astype(f32)
    line = line.astype(b16)
    shard = jnp.zeros((rows, 5 * hidden), f32)
    for k in range(groups):
        part = to_group(line, k) if k else line
        shard = lax.dynamic_update_slice_in_dim(shard, part.astype(f32), (grp ^ k) * fine, 0)
    return (layer_out, shard[:, : 4 * hidden], shard[:, 4 * hidden :], table_grad)


def solution(mesh):
    return jax.shard_map(
        body,
        mesh=mesh,
        in_specs=(
            P(("grp", "seq"), None),
            P(("grp", "seq"), None),
            P(("grp", "seq"), None),
            P(("grp", "seq")),
            P(("grp", "seq"), None),
            P(),
            P(),
            P("seq", None),
        ),
        out_specs=(P(("grp", "seq"), None), P("seq", None), P("seq", None), P("seq", None)),
        check_vma=False,
    )
```

time: 359 us -> 285 us (0.79)
  blocking collectives: 82.8 us -> 0 us
  matrix products: 15.2 us -> 53 us
  starting transfers between devices: 24.7 us -> 50.9 us
  local copies, waits for them, and re-layouts: 58.8 us -> 36.8 us
  other arithmetic: 51.4 us -> 34.3 us
  between operations: 15.1 us -> 1.97 us
    ppermute x0 -> x38, waiting for transfers between devices: none -> 107 us  [the longest x18 83.2 us: to_group(): return lax.ppermute(x, 'grp', [(a, a ^ k) for a in range(groups)])]
    all_to_all x1 -> x0, blocking collectives: 82.8 us -> none  [body(): lax.all_to_all(outgoing, 'seq', split_axis=0, concat_axis=0, tiled=True)]
    psum x1 -> x0, waiting for transfers between devices: 62.3 us -> none  [body(): lax.psum(weight_shard.astype(jnp.bfloat16), 'grp').astype(jnp.float32)]
    all_to_all x5 -> x2, waiting for transfers between devices: 47.1 us -> 0.01 us  [the longest x1 0.01 us: body(): lax.all_to_all(outgoing.reshape(owners, slot, width), 'seq', 0, 0, tiled=...]
    ppermute x0 -> x38, starting transfers between devices: none -> 43 us  [the longest x18 21 us: to_group(): return lax.ppermute(x, 'grp', [(a, a ^ k) for a in range(groups)])]
    dot_general x29 -> x52, matrix products: 15.2 us -> 53 us  [dot(): lax.dot_general(a, b, (dims, ((), ())), preferred_element_type=jnp.float32)]
    gather x9 -> x0, local copies, waits for them, and re-layouts: 27.2 us -> none  [the longest x1 8.83 us: body(): (flat_items % VOCAB_DEV)[owner_order].reshape(owners, per_owner)]
    all_to_all x5 -> x2, starting transfers between devices: 24.4 us -> 7.96 us  [the longest x1 4.68 us: body(): lax.all_to_all(outgoing.reshape(owners, slot, width), 'seq', 0, 0, tiled=...]
  transfers between devices with their start and end apart: 7 -> 40, of which waited for: 4 -> 15; matrix products, arithmetic and copies ran while one was open for 18% -> 40% of each run, Pallas kernels for 0% -> 0%
where the time goes in v1:
time: 285 us; the launch traced here: 284 us
  waiting for transfers between devices  107 us (38%)
  matrix products  53 us (19%)
  starting transfers between devices  50.9 us (18%)
  local copies, waits for them, and re-layouts  36.8 us (13%)
  other arithmetic  34.3 us (12%)
    ppermute x18, waiting for transfers between devices, to_group(): return lax.ppermute(x, 'grp', [(a, a ^ k) for a in range(groups)])  83.2 us
    dot_general x52, matrix products, dot(): lax.dot_general(a, b, (dims, ((), ())), preferred_element_type=jnp.float32)  53 us
    ppermute x9, waiting for transfers between devices, to_chip(): return lax.ppermute(x, 'seq', pairs)  22.2 us
    ppermute x18, starting transfers between devices, to_group(): return lax.ppermute(x, 'grp', [(a, a ^ k) for a in range(groups)])  21 us
    ppermute x9, starting transfers between devices, to_chip(): return lax.ppermute(x, 'seq', pairs)  19.5 us
    unnamed x158, local copies, waits for them, and re-layouts  14.8 us
  transfers between devices with their start and end apart: 40, of which 15 were waited for; matrix products, arithmetic and copies ran while one was open for 40% of the time, Pallas kernels for 0%

profile of v1, /device:TPU:0, one launch (start us, length us, event | category | flops | bytes accessed | tf_op | source)
XLA Modules:
  0.0 283.9 jit_solution(16467595978691857114)
XLA Ops:
  2.9 2.5 fusion.2
  7.1 3.0 %collective-permute-start.1 = (bf16[128,1024]{1,0:T(8,128)(2,1)}, bf16[128,1024]{1,0:T(8,128)(2,1)}, u32[]{:S(2)}, u32[]{:S(2)}) collective-permute-start(bf16[128,1024]{1,0:T(8,128)(2,1)} %constant_dynamic-slice_fusion), channel_id=1, source_target_pairs={{0,2},{1,3},{2,4},{3,5},{4,6},{5,7},{6,0},{7,1},{8,10},{9,11},{10,... | collective-permute-start | bytes 786440 | tf_op jit(solution)/shard_map/ppermute | solution.py:100
  10.1 2.6 collective-permute-start.2
  14.8 3.3 %all-to-all-start = ((s32[8,1,1]{2,1,0:T(1,128)}), s32[8,1,1]{2,1,0:T(1,128)S(1)}, u32[]{:S(2)}, u32[]{:S(2)}) async-start(s32[8,1,1]{2,1,0:T(1,128)} %copy.98), calls=%async_computation | async-start | bytes 8192 | tf_op jit(solution)/shard_map/all_to_all | solution.py:140
  18.9 5.0 %multiply_convert_fusion.1 = (bf16[256,2048]{1,0:T(8,128)(2,1)S(1)}, f32[256,2048]{1,0:T(8,128)}) fusion(bf16[256,1024]{1,0:T(8,128)(2,1)S(1)} %fusion.43, bf16[1024,2048]{1,0:T(8,128)(2,1)} %param.13), kind=kOutput, calls=%fused_computation.34 | convolution fusion | flops 1076363264 | bytes 7864320 | tf_op jit(solution)/shard_map/dot_general | solution.py:27
  46.3 2.5 fusion.366
  56.9 4.7 %all-to-all-start.1 = ((bf16[8,48,1024]{2,1,0:T(8,128)(2,1)}), bf16[8,48,1024]{2,1,0:T(8,128)(2,1)S(1)}, u32[]{:S(2)}, u32[]{:S(2)}) async-start(bf16[8,48,1024]{2,1,0:T(8,128)(2,1)} %bitcast.8), calls=%async_computation.1 | async-start | bytes 1572864 | tf_op jit(solution)/shard_map/all_to_all | solution.py:148
  70.7 7.7 %collective-permute-done.28 = bf16[256,1024]{1,0:T(8,128)(2,1)S(1)} collective-permute-done((bf16[256,1024]{1,0:T(8,128)(2,1)S(1)}, bf16[256,1024]{1,0:T(8,128)(2,1)S(1)}, u32[]{:S(2)}, u32[]{:S(2)}) %collective-permute-start.28) | collective-permute-done | bytes 524320 | tf_op jit(solution)/shard_map/ppermute | solution.py:103
  80.7 10.8 %collective-permute-done.29 = bf16[256,1024]{1,0:T(8,128)(2,1)S(1)} collective-permute-done((bf16[256,1024]{1,0:T(8,128)(2,1)S(1)}, bf16[256,1024]{1,0:T(8,128)(2,1)S(1)}, u32[]{:S(2)}, u32[]{:S(2)}) %collective-permute-start.29) | collective-permute-done | bytes 524320 | tf_op jit(solution)/shard_map/ppermute | solution.py:103
  96.7 9.8 %collective-permute-done.4 = bf16[384,1024]{1,0:T(8,128)(2,1)S(1)} collective-permute-done((bf16[384,1024]{1,0:T(8,128)(2,1)S(1)}, bf16[384,1024]{1,0:T(8,128)(2,1)S(1)}, u32[]{:S(2)}, u32[]{:S(2)}) %collective-permute-start.4) | collective-permute-done | bytes 786464 | tf_op jit(solution)/shard_map/ppermute | solution.py:103
  107.0 20.2 %collective-permute-done.5 = bf16[384,1024]{1,0:T(8,128)(2,1)S(1)} collective-permute-done((bf16[384,1024]{1,0:T(8,128)(2,1)S(1)}, bf16[384,1024]{1,0:T(8,128)(2,1)S(1)}, u32[]{:S(2)}, u32[]{:S(2)}) %collective-permute-start.5) | collective-permute-done | bytes 786464 | tf_op jit(solution)/shard_map/ppermute | solution.py:103
  129.9 2.1 fusion.58
  134.8 2.0 fusion.114
  137.7 1.9 fusion.148
  142.4 1.9 fusion.146
  169.2 3.4 %multiply_convert_fusion = bf16[256,2048]{1,0:T(8,128)(2,1)} fusion(f32[256,2048]{1,0:T(8,128)S(1)} %convolution_dynamic-update-slice_fusion, f32[256,2048]{1,0:T(8,128)} %get-tuple-element.120), kind=kLoop, calls=%fused_computation.33 | loop fusion | flops 4718592 | bytes 5242880 | tf_op jit(solution)/shard_map/convert_element_type | solution.py:81
  178.1 5.2 %fusion.3 = (f32[512]{0:T(512)S(1)}, f32[512,1024]{1,0:T(8,128)S(1)}) fusion(bf16[128,1024]{1,0:T(8,128)(2,1)} %collective-permute-done.3, bf16[128,1024]{1,0:T(8,128)(2,1)} %collective-permute-done.2, bf16[128,1024]{1,0:T(8,128)(2,1)} %collective-permute-done.1, bf16[128,1024]{1,0:T(8,128)(2,1)} %constant_dynamic-slice_fusion, ...), kind=kOutput, calls=%fused_computation.17 | convolution fusion | flops 2165308928 | bytes 7409664 | tf_op jit(solution)/shard_map/dot_general | solution.py:27
  186.8 2.4 collective-permute-start.33
  193.3 3.7 %collective-permute-done.34 = bf16[128,1024]{1,0:T(8,128)(2,1)S(1)} collective-permute-done((bf16[128,1024]{1,0:T(8,128)(2,1)}, bf16[128,1024]{1,0:T(8,128)(2,1)S(1)}, u32[]{:S(2)}, u32[]{:S(2)}) %collective-permute-start.34) | collective-permute-done | bytes 262176 | tf_op jit(solution)/shard_map/ppermute | solution.py:100
  197.1 10.8 %collective-permute-done.33 = bf16[128,1024]{1,0:T(8,128)(2,1)S(1)} collective-permute-done((bf16[128,1024]{1,0:T(8,128)(2,1)}, bf16[128,1024]{1,0:T(8,128)(2,1)S(1)}, u32[]{:S(2)}, u32[]{:S(2)}) %collective-permute-start.33) | collective-permute-done | bytes 262176 | tf_op jit(solution)/shard_map/ppermute | solution.py:100
  210.8 2.8 convolution_convert_fusion
  214.9 2.6 collective-permute-start.17
  222.8 1.8 convert_dynamic-update-slice_fusion.2
  224.6 10.3 %collective-permute-done.17 = bf16[4,32,2560]{2,1,0:T(8,128)(2,1)} collective-permute-done((bf16[4,32,2560]{2,1,0:T(8,128)(2,1)}, bf16[4,32,2560]{2,1,0:T(8,128)(2,1)}, u32[]{:S(2)}, u32[]{:S(2)}) %collective-permute-start.17) | collective-permute-done | bytes 655392 | tf_op jit(solution)/shard_map/ppermute | solution.py:103
  234.9 18.8 %collective-permute-done.16 = bf16[4,32,2560]{2,1,0:T(8,128)(2,1)} collective-permute-done((bf16[4,32,2560]{2,1,0:T(8,128)(2,1)}, bf16[4,32,2560]{2,1,0:T(8,128)(2,1)}, u32[]{:S(2)}, u32[]{:S(2)}) %collective-permute-start.16) | collective-permute-done | bytes 655392 | tf_op jit(solution)/shard_map/ppermute | solution.py:103
  253.7 1.8 fusion.27
  255.6 6.5 %collective-permute-start.20 = (bf16[32,2560]{1,0:T(8,128)(2,1)S(1)}, bf16[32,2560]{1,0:T(8,128)(2,1)S(1)}, u32[]{:S(2)}, u32[]{:S(2)}) collective-permute-start(bf16[32,2560]{1,0:T(8,128)(2,1)S(1)} %get-tuple-element.92), channel_id=1, source_target_pairs={{0,6},{1,7},{2,0},{3,1},{4,2},{5,3},{6,4},{7,5},{8,14},{9,15},{10,... | collective-permute-start | bytes 491528 | tf_op jit(solution)/shard_map/ppermute | solution.py:100
  264.1 1.8 collective-permute-done.20
  265.9 5.9 %collective-permute-done.19 = bf16[32,2560]{1,0:T(8,128)(2,1)S(1)} collective-permute-done((bf16[32,2560]{1,0:T(8,128)(2,1)S(1)}, bf16[32,2560]{1,0:T(8,128)(2,1)S(1)}, u32[]{:S(2)}, u32[]{:S(2)}) %collective-permute-start.19) | collective-permute-done | bytes 163872 | tf_op jit(solution)/shard_map/ppermute | solution.py:100
  274.2 2.3 collective-permute-start.23
  276.5 2.6 collective-permute-done.21
  279.1 3.0 %collective-permute-done.22 = bf16[32,2560]{1,0:T(8,128)(2,1)S(1)} collective-permute-done((bf16[32,2560]{1,0:T(8,128)(2,1)S(1)}, bf16[32,2560]{1,0:T(8,128)(2,1)S(1)}, u32[]{:S(2)}, u32[]{:S(2)}) %collective-permute-start.22) | collective-permute-done | bytes 163872 | tf_op jit(solution)/shard_map/ppermute | solution.py:103
  (346 shorter events, 116.1 us)
Async XLA Ops:
  7.1 56.6 %collective-permute-start.1 = (bf16[128,1024]{1,0:T(8,128)(2,1)}, bf16[128,1024]{1,0:T(8,128)(2,1)}, u32[]{:S(2)}, u32[]{:S(2)}) collective-permute-start(bf16[128,1024]{1,0:T(8,128)(2,1)} %constant_dynamic-slice_fusion), channel_id=1, source_target_pairs={{0,2},{1,3},{2,4},{3,5},{4,6},{5,7},{6,0},{7,1},{8,10},{9,11},{10,... | collective-permute-start | bytes 786440 | tf_op jit(solution)/shard_map/ppermute | solution.py:100
  10.1 56.0 %collective-permute-start.2 = (bf16[128,1024]{1,0:T(8,128)(2,1)}, bf16[128,1024]{1,0:T(8,128)(2,1)}, u32[]{:S(2)}, u32[]{:S(2)}) collective-permute-start(bf16[128,1024]{1,0:T(8,128)(2,1)} %constant_dynamic-slice_fusion), channel_id=1, source_target_pairs={{0,4},{1,5},{2,6},{3,7},{4,0},{5,1},{6,2},{7,3},{8,12},{9,13},{10,... | collective-permute-start | bytes 786440 | tf_op jit(solution)/shard_map/ppermute | solution.py:100
  12.7 56.0 %collective-permute-start.3 = (bf16[128,1024]{1,0:T(8,128)(2,1)}, bf16[128,1024]{1,0:T(8,128)(2,1)}, u32[]{:S(2)}, u32[]{:S(2)}) collective-permute-start(bf16[128,1024]{1,0:T(8,128)(2,1)} %constant_dynamic-slice_fusion), channel_id=1, source_target_pairs={{0,6},{1,7},{2,0},{3,1},{4,2},{5,3},{6,4},{7,5},{8,14},{9,15},{10,... | collective-permute-start | bytes 786440 | tf_op jit(solution)/shard_map/ppermute | solution.py:100
  14.0 115.3 %collective-permute-start.7 = (bf16[512,1024]{1,0:T(8,128)(2,1)}, bf16[512,1024]{1,0:T(8,128)(2,1)}, u32[]{:S(2)}, u32[]{:S(2)}) collective-permute-start(bf16[512,1024]{1,0:T(8,128)(2,1)} %fusion.2), channel_id=1, source_target_pairs={{0,1},{1,0},{2,3},{3,2},{4,5},{5,4},{6,7},{7,6},{8,9},{9,8},{10,11... | collective-permute-start | bytes 3145736 | tf_op jit(solution)/shard_map/ppermute | solution.py:106
  14.8 42.1 %all-to-all-start = ((s32[8,1,1]{2,1,0:T(1,128)}), s32[8,1,1]{2,1,0:T(1,128)S(1)}, u32[]{:S(2)}, u32[]{:S(2)}) async-start(s32[8,1,1]{2,1,0:T(1,128)} %copy.98), calls=%async_computation | async-start | bytes 8192 | tf_op jit(solution)/shard_map/all_to_all | solution.py:140
  37.0 152.2 %collective-permute-start.14 = (bf16[256,512]{1,0:T(8,128)(2,1)}, bf16[256,512]{1,0:T(8,128)(2,1)}, u32[]{:S(2)}, u32[]{:S(2)}) collective-permute-start(bf16[256,512]{1,0:T(8,128)(2,1)} %fusion.52), channel_id=1, source_target_pairs={{0,1},{1,0},{2,3},{3,2},{4,5},{5,4},{6,7},{7,6},{8,9},{9,8},{10,11... | collective-permute-start | bytes 786440 | tf_op jit(solution)/shard_map/ppermute | solution.py:106
  56.9 161.5 %all-to-all-start.1 = ((bf16[8,48,1024]{2,1,0:T(8,128)(2,1)}), bf16[8,48,1024]{2,1,0:T(8,128)(2,1)S(1)}, u32[]{:S(2)}, u32[]{:S(2)}) async-start(bf16[8,48,1024]{2,1,0:T(8,128)(2,1)} %bitcast.8), calls=%async_computation.1 | async-start | bytes 1572864 | tf_op jit(solution)/shard_map/all_to_all | solution.py:148
  63.7 14.7 %collective-permute-start.28 = (bf16[256,1024]{1,0:T(8,128)(2,1)S(1)}, bf16[256,1024]{1,0:T(8,128)(2,1)S(1)}, u32[]{:S(2)}, u32[]{:S(2)}) collective-permute-start(bf16[256,1024]{1,0:T(8,128)(2,1)S(1)} %get-tuple-element.80), channel_id=1, source_target_pairs={{0,8},{8,0},{16,24},{24,16},{1,9},{9,1},{17,25},{25,17},{2,10},{10... | collective-permute-start | bytes 1572872 | tf_op jit(solution)/shard_map/ppermute | solution.py:103
  66.1 25.4 %collective-permute-start.29 = (bf16[256,1024]{1,0:T(8,128)(2,1)S(1)}, bf16[256,1024]{1,0:T(8,128)(2,1)S(1)}, u32[]{:S(2)}, u32[]{:S(2)}) collective-permute-start(bf16[256,1024]{1,0:T(8,128)(2,1)S(1)} %get-tuple-element.80), channel_id=1, source_target_pairs={{0,16},{8,24},{16,0},{24,8},{1,17},{9,25},{17,1},{25,9},{2,18},{10... | collective-permute-start | bytes 1572872 | tf_op jit(solution)/shard_map/ppermute | solution.py:103
  68.7 25.2 %collective-permute-start.30 = (bf16[256,1024]{1,0:T(8,128)(2,1)S(1)}, bf16[256,1024]{1,0:T(8,128)(2,1)S(1)}, u32[]{:S(2)}, u32[]{:S(2)}) collective-permute-start(bf16[256,1024]{1,0:T(8,128)(2,1)S(1)} %get-tuple-element.80), channel_id=1, source_target_pairs={{0,24},{8,16},{16,8},{24,0},{1,25},{9,17},{17,9},{25,1},{2,26},{10... | collective-permute-start | bytes 1572872 | tf_op jit(solution)/shard_map/ppermute | solution.py:103
  78.4 28.1 %collective-permute-start.4 = (bf16[384,1024]{1,0:T(8,128)(2,1)S(1)}, bf16[384,1024]{1,0:T(8,128)(2,1)S(1)}, u32[]{:S(2)}, u32[]{:S(2)}) collective-permute-start(bf16[384,1024]{1,0:T(8,128)(2,1)S(1)} %constant_dynamic-update-slice_fusion), channel_id=1, source_target_pairs={{0,8},{8,0},{16,24},{24,16},{1,9},{9,1},{17,25},{25,17},{2,10},{10... | collective-permute-start | bytes 2359304 | tf_op jit(solution)/shard_map/ppermute | solution.py:103
  91.5 35.7 %collective-permute-start.5 = (bf16[384,1024]{1,0:T(8,128)(2,1)S(1)}, bf16[384,1024]{1,0:T(8,128)(2,1)S(1)}, u32[]{:S(2)}, u32[]{:S(2)}) collective-permute-start(bf16[384,1024]{1,0:T(8,128)(2,1)S(1)} %constant_dynamic-update-slice_fusion), channel_id=1, source_target_pairs={{0,16},{8,24},{16,0},{24,8},{1,17},{9,25},{17,1},{25,9},{2,18},{10... | collective-permute-start | bytes 2359304 | tf_op jit(solution)/shard_map/ppermute | solution.py:103
  93.9 33.8 %collective-permute-start.6 = (bf16[384,1024]{1,0:T(8,128)(2,1)S(1)}, bf16[384,1024]{1,0:T(8,128)(2,1)S(1)}, u32[]{:S(2)}, u32[]{:S(2)}) collective-permute-start(bf16[384,1024]{1,0:T(8,128)(2,1)S(1)} %constant_dynamic-update-slice_fusion), channel_id=1, source_target_pairs={{0,24},{8,16},{16,8},{24,0},{1,25},{9,17},{17,9},{25,1},{2,26},{10... | collective-permute-start | bytes 2359304 | tf_op jit(solution)/shard_map/ppermute | solution.py:103
  106.5 22.2 %collective-permute-start.8 = (bf16[384,1024]{1,0:T(8,128)(2,1)S(1)}, bf16[384,1024]{1,0:T(8,128)(2,1)S(1)}, u32[]{:S(2)}, u32[]{:S(2)}) collective-permute-start(bf16[384,1024]{1,0:T(8,128)(2,1)S(1)} %constant_dynamic-update-slice_fusion), channel_id=1, source_target_pairs={{0,1},{1,0},{2,3},{3,2},{4,5},{5,4},{6,7},{7,6},{8,9},{9,8},{10,11... | collective-permute-start | bytes 2359304 | tf_op jit(solution)/shard_map/ppermute | solution.py:106
  127.2 49.1 %collective-permute-start.31 = (bf16[4,256,1024]{2,1,0:T(8,128)(2,1)}, bf16[4,256,1024]{2,1,0:T(8,128)(2,1)}, u32[]{:S(2)}, u32[]{:S(2)}) collective-permute-start(bf16[4,256,1024]{2,1,0:T(8,128)(2,1)} %pad_maximum_fusion), channel_id=1, source_target_pairs={{0,1},{1,0},{2,3},{3,2},{4,5},{5,4},{6,7},{7,6},{8,9},{9,8},{10,11... | collective-permute-start | bytes 6291464 | tf_op jit(solution)/shard_map/ppermute | solution.py:106
  155.6 17.1 %collective-permute-start.24 = (f32[8,256]{1,0:T(8,128)}, f32[8,256]{1,0:T(8,128)}, u32[]{:S(2)}, u32[]{:S(2)}) collective-permute-start(f32[8,256]{1,0:T(8,128)} %get-tuple-element.111), channel_id=1, source_target_pairs={{0,8},{8,0},{16,24},{24,16},{1,9},{9,1},{17,25},{25,17},{2,10},{10... | collective-permute-start | bytes 24584 | tf_op jit(solution)/shard_map/ppermute | solution.py:103
  155.9 16.8 %collective-permute-start.25 = (f32[8,256]{1,0:T(8,128)}, f32[8,256]{1,0:T(8,128)}, u32[]{:S(2)}, u32[]{:S(2)}) collective-permute-start(f32[8,256]{1,0:T(8,128)} %get-tuple-element.111), channel_id=1, source_target_pairs={{0,16},{8,24},{16,0},{24,8},{1,17},{9,25},{17,1},{25,9},{2,18},{10... | collective-permute-start | bytes 24584 | tf_op jit(solution)/shard_map/ppermute | solution.py:103
  157.7 15.6 %collective-permute-start.26 = (f32[8,256]{1,0:T(8,128)}, f32[8,256]{1,0:T(8,128)}, u32[]{:S(2)}, u32[]{:S(2)}) collective-permute-start(f32[8,256]{1,0:T(8,128)} %get-tuple-element.111), channel_id=1, source_target_pairs={{0,24},{8,16},{16,8},{24,0},{1,25},{9,17},{17,9},{25,1},{2,26},{10... | collective-permute-start | bytes 24584 | tf_op jit(solution)/shard_map/ppermute | solution.py:103
  172.7 38.0 %collective-permute-start.12 = (bf16[256,2048]{1,0:T(8,128)(2,1)}, bf16[256,2048]{1,0:T(8,128)(2,1)}, u32[]{:S(2)}, u32[]{:S(2)}) collective-permute-start(bf16[256,2048]{1,0:T(8,128)(2,1)} %multiply_convert_fusion), channel_id=1, source_target_pairs={{0,1},{1,0},{2,3},{3,2},{4,5},{5,4},{6,7},{7,6},{8,9},{9,8},{10,11... | collective-permute-start | bytes 3145736 | tf_op jit(solution)/shard_map/ppermute | solution.py:106
  172.8 18.2 %collective-permute-start.13 = (bf16[256,512]{0,1:T(8,128)(2,1)}, bf16[256,512]{0,1:T(8,128)(2,1)S(1)}, u32[]{:S(2)}, u32[]{:S(2)}) collective-permute-start(bf16[256,512]{0,1:T(8,128)(2,1)} %bitcast.25), channel_id=1, source_target_pairs={{0,1},{1,0},{2,3},{3,2},{4,5},{5,4},{6,7},{7,6},{8,9},{9,8},{10,11... | collective-permute-start | bytes 786440 | tf_op jit(solution)/shard_map/ppermute | solution.py:106
  185.8 11.3 %collective-permute-start.34 = (bf16[128,1024]{1,0:T(8,128)(2,1)}, bf16[128,1024]{1,0:T(8,128)(2,1)S(1)}, u32[]{:S(2)}, u32[]{:S(2)}) collective-permute-start(bf16[128,1024]{1,0:T(8,128)(2,1)} %get-tuple-element.89), channel_id=1, source_target_pairs={{0,2},{1,3},{2,4},{3,5},{4,6},{5,7},{6,0},{7,1},{8,10},{9,11},{10,... | collective-permute-start | bytes 786440 | tf_op jit(solution)/shard_map/ppermute | solution.py:100
  186.8 21.0 %collective-permute-start.33 = (bf16[128,1024]{1,0:T(8,128)(2,1)}, bf16[128,1024]{1,0:T(8,128)(2,1)S(1)}, u32[]{:S(2)}, u32[]{:S(2)}) collective-permute-start(bf16[128,1024]{1,0:T(8,128)(2,1)} %get-tuple-element.90), channel_id=1, source_target_pairs={{0,4},{1,5},{2,6},{3,7},{4,0},{5,1},{6,2},{7,3},{8,12},{9,13},{10,... | collective-permute-start | bytes 786440 | tf_op jit(solution)/shard_map/ppermute | solution.py:100
  189.2 18.6 %collective-permute-start.32 = (bf16[128,1024]{1,0:T(8,128)(2,1)}, bf16[128,1024]{1,0:T(8,128)(2,1)S(1)}, u32[]{:S(2)}, u32[]{:S(2)}) collective-permute-start(bf16[128,1024]{1,0:T(8,128)(2,1)} %get-tuple-element.88), channel_id=1, source_target_pairs={{0,6},{1,7},{2,0},{3,1},{4,2},{5,3},{6,4},{7,5},{8,14},{9,15},{10,... | collective-permute-start | bytes 786440 | tf_op jit(solution)/shard_map/ppermute | solution.py:100
  191.0 19.7 %collective-permute-start = (bf16[256,512]{0,1:T(8,128)(2,1)S(1)}, bf16[256,512]{0,1:T(8,128)(2,1)S(1)}, u32[]{:S(2)}, u32[]{:S(2)}) collective-permute-start(bf16[256,512]{0,1:T(8,128)(2,1)S(1)} %bitcast.150), channel_id=1, source_target_pairs={{0,1},{1,0},{2,3},{3,2},{4,5},{5,4},{6,7},{7,6},{8,9},{9,8},{10,11... | collective-permute-start | bytes 786440 | tf_op jit(solution)/shard_map/ppermute | solution.py:106
  210.4 10.9 %collective-permute-start.35 = (bf16[128,1024]{1,0:T(8,128)(2,1)}, bf16[128,1024]{1,0:T(8,128)(2,1)}, u32[]{:S(2)}, u32[]{:S(2)}) collective-permute-start(bf16[128,1024]{1,0:T(8,128)(2,1)} %get-tuple-element.78), channel_id=1, source_target_pairs={{0,8},{8,0},{16,24},{24,16},{1,9},{9,1},{17,25},{25,17},{2,10},{10... | collective-permute-start | bytes 786440 | tf_op jit(solution)/shard_map/ppermute | solution.py:103
  214.9 20.0 %collective-permute-start.17 = (bf16[4,32,2560]{2,1,0:T(8,128)(2,1)}, bf16[4,32,2560]{2,1,0:T(8,128)(2,1)}, u32[]{:S(2)}, u32[]{:S(2)}) collective-permute-start(bf16[4,32,2560]{2,1,0:T(8,128)(2,1)} %get-tuple-element.85), channel_id=1, source_target_pairs={{0,24},{8,16},{16,8},{24,0},{1,25},{9,17},{17,9},{25,1},{2,26},{10... | collective-permute-start | bytes 1966088 | tf_op jit(solution)/shard_map/ppermute | solution.py:103
  217.6 36.2 %collective-permute-start.16 = (bf16[4,32,2560]{2,1,0:T(8,128)(2,1)}, bf16[4,32,2560]{2,1,0:T(8,128)(2,1)}, u32[]{:S(2)}, u32[]{:S(2)}) collective-permute-start(bf16[4,32,2560]{2,1,0:T(8,128)(2,1)} %get-tuple-element.84), channel_id=1, source_target_pairs={{0,16},{8,24},{16,0},{24,8},{1,17},{9,25},{17,1},{25,9},{2,18},{10... | collective-permute-start | bytes 1966088 | tf_op jit(solution)/shard_map/ppermute | solution.py:103
  218.1 35.6 %collective-permute-start.15 = (bf16[4,32,2560]{2,1,0:T(8,128)(2,1)}, bf16[4,32,2560]{2,1,0:T(8,128)(2,1)}, u32[]{:S(2)}, u32[]{:S(2)}) collective-permute-start(bf16[4,32,2560]{2,1,0:T(8,128)(2,1)} %get-tuple-element.83), channel_id=1, source_target_pairs={{0,8},{8,0},{16,24},{24,16},{1,9},{9,1},{17,25},{25,17},{2,10},{10... | collective-permute-start | bytes 1966088 | tf_op jit(solution)/shard_map/ppermute | solution.py:103
  219.7 43.6 %collective-permute-start.36 = (bf16[128,1024]{1,0:T(8,128)(2,1)}, bf16[128,1024]{1,0:T(8,128)(2,1)S(1)}, u32[]{:S(2)}, u32[]{:S(2)}) collective-permute-start(bf16[128,1024]{1,0:T(8,128)(2,1)} %get-tuple-element.78), channel_id=1, source_target_pairs={{0,16},{8,24},{16,0},{24,8},{1,17},{9,25},{17,1},{25,9},{2,18},{10... | collective-permute-start | bytes 786440 | tf_op jit(solution)/shard_map/ppermute | solution.py:103
  221.4 51.8 %collective-permute-start.37 = (bf16[128,1024]{1,0:T(8,128)(2,1)}, bf16[128,1024]{1,0:T(8,128)(2,1)S(1)}, u32[]{:S(2)}, u32[]{:S(2)}) collective-permute-start(bf16[128,1024]{1,0:T(8,128)(2,1)} %get-tuple-element.78), channel_id=1, source_target_pairs={{0,24},{8,16},{16,8},{24,0},{1,25},{9,17},{17,9},{25,1},{2,26},{10... | collective-permute-start | bytes 786440 | tf_op jit(solution)/shard_map/ppermute | solution.py:103
  255.6 10.3 %collective-permute-start.20 = (bf16[32,2560]{1,0:T(8,128)(2,1)S(1)}, bf16[32,2560]{1,0:T(8,128)(2,1)S(1)}, u32[]{:S(2)}, u32[]{:S(2)}) collective-permute-start(bf16[32,2560]{1,0:T(8,128)(2,1)S(1)} %get-tuple-element.92), channel_id=1, source_target_pairs={{0,6},{1,7},{2,0},{3,1},{4,2},{5,3},{6,4},{7,5},{8,14},{9,15},{10,... | collective-permute-start | bytes 491528 | tf_op jit(solution)/shard_map/ppermute | solution.py:100
  262.1 9.8 %collective-permute-start.19 = (bf16[32,2560]{1,0:T(8,128)(2,1)S(1)}, bf16[32,2560]{1,0:T(8,128)(2,1)S(1)}, u32[]{:S(2)}, u32[]{:S(2)}) collective-permute-start(bf16[32,2560]{1,0:T(8,128)(2,1)S(1)} %get-tuple-element.93), channel_id=1, source_target_pairs={{0,4},{1,5},{2,6},{3,7},{4,0},{5,1},{6,2},{7,3},{8,12},{9,13},{10,... | collective-permute-start | bytes 491528 | tf_op jit(solution)/shard_map/ppermute | solution.py:100
  (81 other events, 491.0 us)

commit v2 on v1

v2 whole, which is shorter than its diff:
```python
import jax
import jax.numpy as jnp
from jax import lax
from jax.experimental import pallas as pl
from jax.experimental.pallas import tpu as pltpu
from jax.sharding import PartitionSpec as P

HEADS = 4
HEAD_DIM = 128
NCAND = 4

epsilon = 1e-05
softmax_warmth = 0.05

f32, b16, i32 = jnp.float32, jnp.bfloat16, jnp.int32
NN = ((1,), (0,))
NT = ((1,), (1,))
TN = ((0,), (0,))
VMEM = pl.BlockSpec(memory_space=pltpu.VMEM)
SMEM = pl.BlockSpec(memory_space=pltpu.SMEM)
ANY = pl.BlockSpec(memory_space=pl.ANY)


def dot(a, b, dims):
    return lax.dot_general(a, b, (dims, ((), ())), preferred_element_type=f32)


def iota(shape, axis):
    return lax.broadcasted_iota(i32, shape, axis)


def center_scale(values):
    average = jnp.mean(values, -1, keepdims=True)
    centered = values - average
    inverse = lax.rsqrt(jnp.mean(centered * centered, -1, keepdims=True) + epsilon)
    return (centered * inverse, inverse)


def sigmoid(values):
    return 1.0 / (1.0 + jnp.exp(-values))


def split_columns(x, owners, core):
    rows = x.shape[1] // owners
    blocks = [x[:, i * rows : (i + 1) * rows] for i in range(owners)]
    even, odd = jnp.concatenate(blocks[0::2], 1), jnp.concatenate(blocks[1::2], 1)
    first = jnp.broadcast_to(core, even.shape) == 0
    return jnp.where(first, even, odd), jnp.where(first, odd, even)


def call(kernel, out, specs, args, scratch=(), flops=0, nbytes=0):
    return pl.pallas_call(
        kernel,
        out_shape=[jax.ShapeDtypeStruct(s, t) for s, t in out],
        in_specs=specs,
        out_specs=[VMEM] * len(out),
        scratch_shapes=list(scratch),
        cost_estimate=pl.CostEstimate(flops=flops, bytes_accessed=nbytes, transcendentals=0),
        compiler_params=pltpu.CompilerParams(vmem_limit_bytes=48 * 2**20),
    )(*args)


def forward_kernel(
    owners, slot, lengths, dests, events, in_weight, out_weight,
    keep, give, proj, slope, attn, attn_slope, normed_out, inv_out, gated_out, unit, unit_b, inv_len, outgoing,
):
    tok = events.shape[0]
    hidden = out_weight.shape[1]
    scale = HEAD_DIM ** (-0.5)
    core = lax.axis_index("seq") % 2
    x = events[...].astype(f32)
    normed_in = center_scale(x)[0]
    mine, other = split_columns(normed_in, owners, core)
    keep[...] = mine.astype(b16)
    give[...] = other.astype(b16)
    normed_in = normed_in.astype(b16)
    for i in range(4):
        cols = slice(i * hidden, (i + 1) * hidden)
        p = dot(normed_in, in_weight[:, cols], NN)
        sig = sigmoid(p)
        proj[:, cols] = (p * sig).astype(b16)
        slope[:, cols] = (sig * (1.0 + p * (1.0 - sig))).astype(b16)

    pos_c, pos_r = iota((tok, 1), 0), iota((1, tok), 1)
    user_c, user_r = jnp.zeros((tok, 1), i32), jnp.zeros((1, tok), i32)
    target = jnp.zeros((1, tok), i32)
    start = jnp.int32(0)
    for j in range(lengths.shape[1]):
        end = start + lengths[0, j]
        user_c += (pos_c >= end).astype(i32)
        user_r += (pos_r >= end).astype(i32)
        here = (pos_r >= start) & (pos_r < end)
        target = jnp.where(here, dests[0, j] * slot + pos_r - start, target)
        start = end
    mask = (user_c == user_r) & (pos_r <= pos_c)

    outputs = []
    for h in range(HEADS):
        v = proj[:, hidden + h * HEAD_DIM : hidden + (h + 1) * HEAD_DIM]
        q = proj[:, 2 * hidden + h * HEAD_DIM : 2 * hidden + (h + 1) * HEAD_DIM]
        k = proj[:, 3 * hidden + h * HEAD_DIM : 3 * hidden + (h + 1) * HEAD_DIM]
        s = dot(q, k, NT) * scale
        sig = sigmoid(s)
        weight = jnp.where(mask, s * sig, 0.0).astype(b16)
        attn[h] = weight
        attn_slope[h] = jnp.where(mask, sig * (1.0 + s * (1.0 - sig)) * scale, 0.0).astype(b16)
        outputs.append(dot(weight, v, NN))
    normed, inverse = center_scale(jnp.concatenate(outputs, 1))
    normed_out[...] = normed
    inv_out[...] = inverse
    gated = (normed * proj[:, :hidden].astype(f32)).astype(b16)
    gated_out[...] = gated
    result = x + dot(gated, out_weight[...], NT)
    inverse = lax.rsqrt(jnp.sum(result * result, -1, keepdims=True) + epsilon)
    inv_len[...] = inverse
    yn = result * inverse
    unit[...] = yn
    unit_b[...] = yn.astype(b16)
    place = (iota((outgoing.shape[0], 1), 0) == target).astype(b16)
    outgoing[...] = dot(place, result.astype(b16), NN).astype(b16)


def score_kernel(groups, owners, share, count, cand, unit_b, unit, inv_len, *refs):
    pieces, (tags, up, up_keep, up_give, table, sems) = refs[:count], refs[count:]
    chips = owners // 2
    vocab_dev = share * groups
    grp, seq = lax.axis_index("grp"), lax.axis_index("seq")
    chip, core = seq // 2, seq % 2
    tok = unit_b.shape[0]
    runs, copies, at = [], [], 0
    owner_of = {}
    for side in range(2):
        for d in range(chips):
            owner_of[side, d] = 2 * ((chip + chips - d) % chips) + (core ^ side)
    for n in range(count):
        side, index = n // (groups + 1), n % (groups + 1)
        rows = pieces[n].shape[0]
        copies.append(pltpu.make_async_copy(pieces[n], table.at[pl.ds(at, rows)], sems.at[n]))
        copies[-1].start()
        if index == 0:
            here = [((side, 0), 0, vocab_dev, owner_of[side, 0] * vocab_dev)]
        else:
            first = (grp ^ (index - 1)) * share
            here = [
                ((side, d), (d - 1) * share, share, owner_of[side, d] * vocab_dev + first)
                for d in range(1, chips)
            ]
        runs.append((at, rows, here))
        at += rows
    candidates = cand[...]
    sel = {}
    for key, owner in owner_of.items():
        chosen = jnp.full((tok, 1), -1, i32)
        for c in range(NCAND):
            one = candidates[:, c : c + 1]
            chosen = jnp.where(one // vocab_dev == owner, one, chosen)
        sel[key] = chosen
    yb = unit_b[...]
    logits = [jnp.zeros((tok, 1), f32) for _ in range(NCAND)]
    value = {key: jnp.zeros((tok, 1), f32) for key in owner_of}
    for n, (at, rows, here) in enumerate(runs):
        copies[n].wait()
        product = dot(yb, table[at : at + rows], NT)
        for key, off, wide, base in here:
            hit = sel[key] == base + iota((1, wide), 1)
            value[key] += jnp.sum(jnp.where(hit, product[:, off : off + wide], 0.0), -1, keepdims=True)
    total = jnp.zeros((tok, 1), f32)
    for c in range(NCAND):
        owner = candidates[:, c : c + 1] // vocab_dev
        for key in owner_of:
            logits[c] += jnp.where(owner == owner_of[key], value[key], 0.0)
        logits[c] = jnp.exp(logits[c] / softmax_warmth)
        total += logits[c]
    coef = [(logits[c] / total - (1.0 if c == 0 else 0.0)) / softmax_warmth for c in range(NCAND)]
    lane = iota((tok, 128), 1)
    packed = jnp.zeros((tok, 128), f32)
    for c in range(NCAND):
        packed = jnp.where(lane == c, coef[c], packed)
        packed = jnp.where(lane == NCAND + c, candidates[:, c : c + 1].astype(f32), packed)
    tags[...] = packed.T[: 2 * NCAND]
    amount = {}
    for key in owner_of:
        amount[key] = jnp.zeros((tok, 1), f32)
        for c in range(NCAND):
            owner = candidates[:, c : c + 1] // vocab_dev
            amount[key] += jnp.where(owner == owner_of[key], coef[c], 0.0)
    pulled = jnp.zeros(unit.shape, f32)
    for at, rows, here in runs:
        parts = []
        for key, off, wide, base in here:
            hit = sel[key] == base + iota((1, wide), 1)
            parts.append(jnp.where(hit, amount[key], 0.0).astype(b16))
        spread = jnp.concatenate(parts, 1) if len(parts) > 1 else parts[0]
        pulled += dot(spread, table[at : at + rows], NN)
    yn = unit[...]
    upstream = (pulled - yn * jnp.sum(yn * pulled, -1, keepdims=True)) * inv_len[...]
    up[...] = upstream.astype(b16)
    mine, other = split_columns(upstream, owners, core)
    up_keep[...] = mine.astype(b16)
    up_give[...] = other.astype(b16)


def backward_kernel(up, out_weight, proj, slope, attn, attn_slope, normed_ref, inverse, grad):
    hidden = out_weight.shape[1]
    normed = normed_ref[...]
    grad_gated = dot(up[...], out_weight[...], NN)
    grad[:, :hidden] = (grad_gated * normed * slope[:, :hidden].astype(f32)).astype(b16)
    grad_normed = grad_gated * proj[:, :hidden].astype(f32)
    grad_attended = inverse[...] * (
        grad_normed
        - jnp.mean(grad_normed, -1, keepdims=True)
        - normed * jnp.mean(grad_normed * normed, -1, keepdims=True)
    )
    grad_attended = grad_attended.astype(b16)
    for h in range(HEADS):
        cv, cq, ck = [slice(i * hidden + h * HEAD_DIM, i * hidden + (h + 1) * HEAD_DIM) for i in (1, 2, 3)]
        part = grad_attended[:, h * HEAD_DIM : (h + 1) * HEAD_DIM]
        grad_attn = dot(part, proj[:, cv], NT)
        grad_score = (grad_attn * attn_slope[h].astype(f32)).astype(b16)
        grad[:, cv] = (dot(attn[h], part, TN) * slope[:, cv].astype(f32)).astype(b16)
        grad[:, cq] = (dot(grad_score, proj[:, ck], NN) * slope[:, cq].astype(f32)).astype(b16)
        grad[:, ck] = (dot(grad_score, proj[:, cq], TN) * slope[:, ck].astype(f32)).astype(b16)


def item_kernel(groups, owners, share, count, *refs):
    units, tags, (quarter, others, out) = refs[:count], refs[count : 2 * count], refs[2 * count :]
    chips = owners // 2
    vocab_dev = share * groups
    grp, seq = lax.axis_index("grp"), lax.axis_index("seq")
    chip, core = seq // 2, seq % 2
    bases = [(2 * ((chip + chips - d) % chips) + core) * vocab_dev for d in range(chips)]
    summed = jnp.zeros((chips * share, quarter.shape[1]), f32)
    for n in range(count):
        row = tags[n][...]
        items = row[NCAND:].astype(i32)
        parts = []
        for d in range(chips):
            chosen = jnp.full((1, row.shape[1]), -1, i32)
            amount = jnp.zeros((1, row.shape[1]), f32)
            for c in range(NCAND):
                one = items[c : c + 1]
                here = (one >= bases[d]) & (one < bases[d] + vocab_dev)
                chosen = jnp.where(here, one, chosen)
                amount = jnp.where(here, row[c : c + 1], amount)
            hit = bases[d] + grp * share + iota((share, 1), 0) == chosen
            parts.append(jnp.where(hit, amount, 0.0).astype(b16))
        summed += dot(jnp.concatenate(parts, 0), units[n][...], NN)
    near = jnp.concatenate([quarter[...], others[...]], 0).astype(f32)
    out[...] = (summed - near * jnp.sum(near * summed, -1, keepdims=True)).astype(b16)


def relay_kernel(slot, counts, arrived, out):
    tok = out.shape[0]
    lane = iota((1, arrived.shape[0]), 1)
    target = jnp.full(lane.shape, -1, i32)
    first = jnp.int32(0)
    for j in range(counts.shape[0]):
        within = lane - j * slot
        here = (within >= 0) & (within < counts[j, 0])
        target = jnp.where(here, within + first, target)
        first += counts[j, 0]
    place = (iota((tok, 1), 0) == target).astype(b16)
    out[...] = dot(place, arrived[...], NN).astype(b16)


def body(events, lengths, destinations, history, negatives, in_weight, out_weight, item_table):
    groups = lax.axis_size("grp")
    owners = lax.axis_size("seq")
    chips = owners // 2
    grp = lax.axis_index("grp")
    seq = lax.axis_index("seq")
    chip, core = seq // 2, seq % 2
    tok = events.shape[0]
    vocab_dev, width = item_table.shape
    hidden = out_weight.shape[1]
    share = vocab_dev // groups
    slot = 3 * tok // (2 * owners)
    rows = width // owners
    fine = rows // groups

    def to_chip(x, d):
        pairs = [(2 * a + b, 2 * ((a + d) % chips) + b) for a in range(chips) for b in range(2)]
        return lax.ppermute(x, "seq", pairs)

    def to_group(x, k):
        return lax.ppermute(x, "grp", [(a, a ^ k) for a in range(groups)])

    def to_core(x):
        return lax.ppermute(x, "seq", [(a, a ^ 1) for a in range(owners)])

    table = item_table.astype(f32)
    table_inv = lax.rsqrt(jnp.sum(table * table, -1, keepdims=True) + epsilon)
    own = (table * table_inv).astype(b16)
    quarter = lax.dynamic_slice_in_dim(own, grp * share, share, 0)
    quarter_inv = lax.dynamic_slice_in_dim(table_inv, grp * share, share, 0)
    others = jnp.concatenate([to_chip(quarter, d) for d in range(1, chips)], 0)
    pieces = [own, others] + [to_group(others, k) for k in range(1, groups)]
    pieces = pieces + [to_core(piece) for piece in pieces]

    send_length = jnp.sum(
        jnp.where(destinations == jnp.arange(owners)[:, None], lengths, 0), 1, keepdims=True
    )
    counts = lax.all_to_all(send_length, "seq", 0, 0, tiled=True)

    outs = [
        ((tok, width // 2), b16), ((tok, width // 2), b16), ((tok, 4 * hidden), b16), ((tok, 4 * hidden), b16),
        ((HEADS, tok, tok), b16), ((HEADS, tok, tok), b16), ((tok, hidden), f32), ((tok, 1), f32),
        ((tok, hidden), b16), ((tok, width), f32), ((tok, width), b16), ((tok, 1), f32),
        ((owners * slot, width), b16),
    ]
    (keep, give, proj, slope, attn, attn_slope, normed, inverse, gated, unit, unit_b, inv_len, outgoing) = call(
        lambda *refs: forward_kernel(owners, slot, *refs), outs, [SMEM, SMEM, VMEM, VMEM, VMEM],
        [lengths, destinations, events, in_weight, out_weight],
        flops=2 * tok * width * 6 * hidden, nbytes=24 * tok * width + 10 * width * hidden,
    )

    arrived = lax.all_to_all(
        outgoing.reshape(owners, slot, width), "seq", 0, 0, tiled=True
    ).reshape(owners * slot, width)
    layer_out, = call(
        lambda *refs: relay_kernel(slot, *refs), [((tok, width), b16)], [SMEM, VMEM], [counts, arrived],
        flops=3 * tok * tok * width, nbytes=6 * tok * width,
    )

    candidates = jnp.concatenate([history[:, None], negatives], 1)
    outs = [((2 * NCAND, tok), f32), ((tok, width), b16), ((tok, width // 2), b16), ((tok, width // 2), b16)]
    vocab = vocab_dev * owners
    tags, up, up_keep, up_give = call(
        lambda *refs: score_kernel(groups, owners, share, len(pieces), *refs),
        outs, [VMEM] * 4 + [ANY] * len(pieces), [candidates, unit_b, unit, inv_len] + pieces,
        [pltpu.VMEM((vocab, width), b16), pltpu.SemaphoreType.DMA((len(pieces),))],
        flops=4 * tok * width * vocab, nbytes=2 * vocab * width + 12 * tok * width,
    )

    units = [unit_b] + [to_group(unit_b, k) for k in range(1, groups)]
    units = units + [to_core(x) for x in units]
    tags = [tags] + [to_group(tags, k) for k in range(1, groups)]
    tags = tags + [to_core(x) for x in tags]
    summed, = call(
        lambda *refs: item_kernel(groups, owners, share, len(units), *refs),
        [((chips * share, width), b16)], [VMEM] * (2 * len(units) + 2), units + tags + [quarter, others],
        flops=4 * groups * tok * width * chips * share, nbytes=4 * tok * groups * width,
    )
    summed = summed.reshape(chips, share, width)
    total = summed[0].astype(f32)
    for d in range(1, chips):
        total += to_chip(summed[d], -d).astype(f32)
    total = (total * quarter_inv).astype(b16)
    table_grad = jnp.zeros((vocab_dev, width), f32)
    for k in range(groups):
        part = to_group(total, k) if k else total
        table_grad = lax.dynamic_update_slice_in_dim(table_grad, part.astype(f32), (grp ^ k) * share, 0)

    grad, = call(
        backward_kernel, [((tok, 4 * hidden), b16)], [VMEM] * 8,
        [up, out_weight, proj, slope, attn, attn_slope, normed, inverse],
        flops=2 * tok * width * hidden, nbytes=20 * tok * width,
    )

    def both(x, y):
        return jnp.concatenate([x, to_core(y)], 0)

    in_part = dot(both(keep, give), both(grad, grad), TN)
    out_part = dot(both(up_keep, up_give), both(gated, gated), TN)
    weight = jnp.concatenate([in_part, out_part], 1).astype(b16)
    weight = weight.reshape(chips, groups, fine, 5 * hidden)
    sums = lax.dynamic_index_in_dim(weight, grp, 1, False).astype(f32)
    for k in range(1, groups):
        sums += to_group(lax.dynamic_index_in_dim(weight, grp ^ k, 1, False), k).astype(f32)
    sums = sums.astype(b16)
    line = lax.dynamic_index_in_dim(sums, chip, 0, False).astype(f32)
    for d in range(1, chips):
        line += to_chip(lax.dynamic_index_in_dim(sums, (chip + d) % chips, 0, False), d).astype(f32)
    line = line.astype(b16)
    shard = jnp.zeros((rows, 5 * hidden), f32)
    for k in range(groups):
        part = to_group(line, k) if k else line
        shard = lax.dynamic_update_slice_in_dim(shard, part.astype(f32), (grp ^ k) * fine, 0)
    return (layer_out, shard[:, : 4 * hidden], shard[:, 4 * hidden :], table_grad)


def solution(mesh):
    return jax.shard_map(
        body,
        mesh=mesh,
        in_specs=(
            P(("grp", "seq"), None),
            P(("grp", "seq"), None),
            P(("grp", "seq"), None),
            P(("grp", "seq")),
            P(("grp", "seq"), None),
            P(),
            P(),
            P("seq", None),
        ),
        out_specs=(P(("grp", "seq"), None), P("seq", None), P("seq", None), P("seq", None)),
        check_vma=False,
    )
```

time: 285 us -> 231 us (0.81)
  matrix products: 53 us -> 4.1 us
  Pallas kernels: 0 us -> 30.5 us
  other arithmetic: 34.3 us -> 13.2 us
  local copies, waits for them, and re-layouts: 36.8 us -> 21.7 us
  starting transfers between devices: 50.9 us -> 58.1 us
  waiting for transfers between devices: 107 us -> 100 us
    dot_general x52 -> x2, matrix products: 53 us -> 4.1 us  [dot(): return lax.dot_general(a, b, (dims, ((), ())), preferred_element_type=f32)]
    pallas_call x0 -> x5, Pallas kernels: none -> 30.5 us  [call(): pl.pallas_call(kernel, out_shape=[jax.ShapeDtypeStruct(s, t) for s, t in...]
    ppermute x18, waiting for transfers between devices: 83.2 us -> 56.8 us  [to_group(): return lax.ppermute(x, 'grp', [(a, a ^ k) for a in range(groups)])]
    ppermute x9, waiting for transfers between devices: 22.2 us -> 38.3 us  [to_chip(): return lax.ppermute(x, 'seq', pairs)]
    convert_element_type x9 -> x0, other arithmetic: 7.81 us -> none  [the longest x1 3.45 us: layer_backward(): return (grad_project * silu_slope(preact)).astype(jnp.bfloat16)]
    another operation x5 -> x0, other arithmetic: 4.45 us -> none  [the longest x1 1.59 us: body(): jnp.stack([unit_b] + [to_group(unit_b, k) for k in range(1, groups)])]
    dot_general x4 -> x0, local copies, waits for them, and re-layouts: 4.06 us -> none  [dot(): lax.dot_general(a, b, (dims, ((), ())), preferred_element_type=jnp.float32)]
    slice x5 -> x0, local copies, waits for them, and re-layouts: 4.05 us -> none  [the longest x2 3.39 us: both_cores(): even, odd = (x[:, :, 0].reshape(tok, -1), x[:, :, 1].reshape(tok, -1))]
  transfers between devices with their start and end apart: 40 -> 46, of which waited for: 15 -> 17; matrix products, arithmetic and copies ran while one was open for 40% -> 8% of each run, Pallas kernels for 0% -> 13%
where the time goes in v2:
time: 231 us; the launch traced here: 229 us
  waiting for transfers between devices  100 us (43%)
  starting transfers between devices  58.1 us (25%)
  Pallas kernels  30.5 us (13%)
  local copies, waits for them, and re-layouts  21.7 us (9%)
  other arithmetic  13.2 us (6%)
  matrix products  4.1 us (2%)
    ppermute x18, waiting for transfers between devices, to_group(): return lax.ppermute(x, 'grp', [(a, a ^ k) for a in range(groups)])  56.8 us
    ppermute x9, waiting for transfers between devices, to_chip(): return lax.ppermute(x, 'seq', pairs)  38.3 us
    pallas_call x5, Pallas kernels, call(): pl.pallas_call(kernel, out_shape=[jax.ShapeDtypeStruct(s, t) for s, t in...  30.5 us
    ppermute x18, starting transfers between devices, to_group(): return lax.ppermute(x, 'grp', [(a, a ^ k) for a in range(groups)])  23.2 us
    ppermute x9, starting transfers between devices, to_chip(): return lax.ppermute(x, 'seq', pairs)  19.8 us
    unnamed x74, local copies, waits for them, and re-layouts  14.9 us
    all_to_all x1, starting transfers between devices, body(): counts = lax.all_to_all(send_length, 'seq', 0, 0, tiled=True)  6.81 us
    dynamic_update_slice x4, other arithmetic, body(): lax.dynamic_update_slice_in_dim(table_grad, part.astype(f32), (grp ^ k) *...  5.61 us
  transfers between devices with their start and end apart: 46, of which 17 were waited for; matrix products, arithmetic and copies ran while one was open for 8% of the time, Pallas kernels for 13%

profile of v2, /device:TPU:0, one launch (start us, length us, event | category | flops | bytes accessed | tf_op | source)
XLA Modules:
  0.0 228.8 jit_solution(5730246024177195278)
XLA Ops:
  2.2 2.4 %fusion.1.refs_4_ = bf16[512,1024]{1,0:T(8,128)(2,1)} fusion(bf16[512,1024]{1,0:T(8,128)(2,1)} %param.15, f32[512]{0:T(512)S(1)} %add_rsqrt_fusion), kind=kLoop, calls=%fused_computation.12 | loop fusion | flops 1572864 | bytes 2099200 | tf_op jit(solution)/shard_map/convert_element_type | solution.py:293
  5.7 3.1 %collective-permute-start.1 = (bf16[128,1024]{1,0:T(8,128)(2,1)S(1)}, bf16[128,1024]{1,0:T(8,128)(2,1)S(1)}, u32[]{:S(2)}, u32[]{:S(2)}) collective-permute-start(bf16[128,1024]{1,0:T(8,128)(2,1)S(1)} %constant_dynamic-slice_fusion.refs_16_), channel_id=1, source_target_pairs={{0,2},{1,3},{2,4},{3,5},{4,6},{5,7},{6,0},{7,1},{8,10},{9,11},{10,... | collective-permute-start | bytes 786440 | tf_op jit(solution)/shard_map/ppermute | solution.py:283
  8.8 2.6 %collective-permute-start.2 = (bf16[128,1024]{1,0:T(8,128)(2,1)S(1)}, bf16[128,1024]{1,0:T(8,128)(2,1)S(1)}, u32[]{:S(2)}, u32[]{:S(2)}) collective-permute-start(bf16[128,1024]{1,0:T(8,128)(2,1)S(1)} %constant_dynamic-slice_fusion.refs_16_), channel_id=1, source_target_pairs={{0,4},{1,5},{2,6},{3,7},{4,0},{5,1},{6,2},{7,3},{8,12},{9,13},{10,... | collective-permute-start | bytes 786440 | tf_op jit(solution)/shard_map/ppermute | solution.py:283
  12.7 7.4 %shard_map.111 = (bf16[256,512]{1,0:T(8,128)(2,1)S(1)}, bf16[256,512]{1,0:T(8,128)(2,1)S(1)}, bf16[256,2048]{1,0:T(8,128)(2,1)S(1)}, bf16[256,2048]{1,0:T(8,128)...) custom-call(s32[1,8]{1,0:T(1,128)S(1)} %copy-done.21, ...), custom_call_target="tpu_custom_call" | custom-call | flops 1610612736 | bytes 11534336 | tf_op jit(solution)/shard_map/pallas_call | solution.py:52
  21.5 1.6 collective-permute-start.24
  25.3 3.1 %collective-permute-done.2 = bf16[128,1024]{1,0:T(8,128)(2,1)S(1)} collective-permute-done((bf16[128,1024]{1,0:T(8,128)(2,1)S(1)}, bf16[128,1024]{1,0:T(8,128)(2,1)S(1)}, u32[]{:S(2)}, u32[]{:S(2)}) %collective-permute-start.2) | collective-permute-done | bytes 262176 | tf_op jit(solution)/shard_map/ppermute | solution.py:283
  33.4 1.7 collective-permute-done.24.refs_1_
  35.1 2.4 %collective-permute-start.26 = (bf16[256,1024]{1,0:T(8,128)(2,1)S(1)}, bf16[256,1024]{1,0:T(8,128)(2,1)}, u32[]{:S(2)}, u32[]{:S(2)}) collective-permute-start(bf16[256,1024]{1,0:T(8,128)(2,1)S(1)} %get-tuple-element.24.refs_1_.refs_0_), channel_id=1, source_target_pairs={{0,24},{8,16},{16,8},{24,0},{1,25},{9,17},{17,9},{25,1},{2,26},{10... | collective-permute-start | bytes 1572872 | tf_op jit(solution)/shard_map/ppermute | solution.py:286
  37.5 17.4 %collective-permute-done.25.refs_2_ = bf16[256,1024]{1,0:T(8,128)(2,1)} collective-permute-done((bf16[256,1024]{1,0:T(8,128)(2,1)S(1)}, bf16[256,1024]{1,0:T(8,128)(2,1)}, u32[]{:S(2)}, u32[]{:S(2)}) %collective-permute-start.25) | collective-permute-done | bytes 524320 | tf_op jit(solution)/shard_map/ppermute | solution.py:286
  54.9 25.7 %collective-permute-done.26.refs_3_ = bf16[256,1024]{1,0:T(8,128)(2,1)} collective-permute-done((bf16[256,1024]{1,0:T(8,128)(2,1)S(1)}, bf16[256,1024]{1,0:T(8,128)(2,1)}, u32[]{:S(2)}, u32[]{:S(2)}) %collective-permute-start.26) | collective-permute-done | bytes 524320 | tf_op jit(solution)/shard_map/ppermute | solution.py:286
  85.6 2.1 collective-permute-done.9.refs_11_
  89.7 13.2 %shard_map.113 = (f32[8,256]{1,0:T(8,128)S(1)}, bf16[256,1024]{1,0:T(8,128)(2,1)S(1)}, bf16[256,512]{1,0:T(8,128)(2,1)S(1)}, bf16[256,512]{1,0:T(8,128)(2,1)S(1)}) custom-call(s32[256,4]{1,0:T(8,128)S(1)} %copy.33.refs_0_, bf16[256,1024]{1,0:T(8,128)(2,1)S(1)} %copy-done.7, f32[256,1024]{1,0:T(8,128)} %get-tuple-element.25.refs_2_, f32[256,1]{1,0:T(8,128)S(1)} %copy-done.27, ...), custom_call_target="tpu_custom_call" | custom-call | flops 4294967296 | bytes 11534336 | tf_op jit(solution)/shard_map/pallas_call | solution.py:52
  104.1 2.9 %shard_map.114 = bf16[256,2048]{1,0:T(8,128)(2,1)S(1)} custom-call(bf16[256,1024]{1,0:T(8,128)(2,1)S(1)} %get-tuple-element.27.up, bf16[1024,512]{1,0:T(8,128)(2,1)S(1)} %copy-done, bf16[256,2048]{1,0:T(8,128)(2,1)S(1)} %get-tuple-element.28.proj, bf16[256,2048]{1,0:T(8,128)(2,1)} %get-tuple-element.29.slope, ...), custom_call_target="tpu_custom_call" | custom-call | flops 268435456 | bytes 5242880 | tf_op jit(solution)/shard_map/pallas_call | solution.py:52
  114.5 1.7 collective-permute-done.33.refs_11_
  116.9 6.8 %all-to-all-start = ((s32[8,1,1]{2,1,0:T(1,128)}), s32[8,1,1]{2,1,0:T(1,128)S(1)}, u32[]{:S(2)}, u32[]{:S(2)}) async-start(s32[8,1,1]{2,1,0:T(1,128)} %copy.31), calls=%async_computation | async-start | bytes 8192 | tf_op jit(solution)/shard_map/all_to_all | solution.py:303
  130.7 5.1 %shard_map.115 = bf16[512,1024]{1,0:T(8,128)(2,1)} custom-call(bf16[256,1024]{1,0:T(8,128)(2,1)S(1)} %copy-done.8, bf16[256,1024]{1,0:T(8,128)(2,1)} %collective-permute-done.24.refs_1_, bf16[256,1024]{1,0:T(8,128)(2,1)} %collective-permute-done.25.refs_2_, bf16[256,1024]{1,0:T(8,128)(2,1)} %collective-permute-done.26.refs_3_, ...), custom_call_target="tpu_custom_call" | custom-call | flops 2147483648 | bytes 4194304 | tf_op jit(solution)/shard_map/pallas_call | solution.py:52
  135.9 4.9 %all-to-all-start.1 = ((bf16[8,48,1024]{2,1,0:T(8,128)(2,1)}), bf16[8,48,1024]{2,1,0:T(8,128)(2,1)S(1)}, u32[]{:S(2)}, u32[]{:S(2)}) async-start(bf16[8,48,1024]{2,1,0:T(8,128)(2,1)} %bitcast.4), calls=%async_computation.1 | async-start | bytes 1572864 | tf_op jit(solution)/shard_map/all_to_all | solution.py:317
  140.9 3.9 %collective-permute-start.38 = (bf16[128,1024]{1,0:T(8,128)(2,1)S(1)}, bf16[128,1024]{1,0:T(8,128)(2,1)S(1)}, u32[]{:S(2)}, u32[]{:S(2)}) collective-permute-start(bf16[128,1024]{1,0:T(8,128)(2,1)S(1)} %get-tuple-element.45), channel_id=1, source_target_pairs={{0,6},{1,7},{2,0},{3,1},{4,2},{5,3},{6,4},{7,5},{8,14},{9,15},{10,... | collective-permute-start | bytes 786440 | tf_op jit(solution)/shard_map/ppermute | solution.py:283
  147.4 2.6 %convolution_convert_fusion = bf16[512,2048]{1,0:T(8,128)(2,1)S(1)} fusion(bf16[256,2048]{1,0:T(8,128)(2,1)} %collective-permute-done.12, bf16[256,2048]{1,0:T(8,128)(2,1)S(1)} %shard_map.114, bf16[256,512]{1,0:T(8,128)(2,1)} %collective-permute-done, bf16[256,512]{1,0:T(8,128)(2,1)S(1)} %copy-done.25), kind=kOutput, calls=%fused_computation.4 | convolution fusion | flops 1080033280 | bytes 4718592 | tf_op jit(solution)/shard_map/dot_general | solution.py:25
  154.0 8.3 %collective-permute-done.38 = bf16[128,1024]{1,0:T(8,128)(2,1)S(1)} collective-permute-done((bf16[128,1024]{1,0:T(8,128)(2,1)S(1)}, bf16[128,1024]{1,0:T(8,128)(2,1)S(1)}, u32[]{:S(2)}, u32[]{:S(2)}) %collective-permute-start.38) | collective-permute-done | bytes 262176 | tf_op jit(solution)/shard_map/ppermute | solution.py:283
  163.7 20.5 %collective-permute-done.39 = bf16[128,1024]{1,0:T(8,128)(2,1)S(1)} collective-permute-done((bf16[128,1024]{1,0:T(8,128)(2,1)S(1)}, bf16[128,1024]{1,0:T(8,128)(2,1)S(1)}, u32[]{:S(2)}, u32[]{:S(2)}) %collective-permute-start.39) | collective-permute-done | bytes 262176 | tf_op jit(solution)/shard_map/ppermute | solution.py:283
  184.3 1.6 broadcast_in_dim.31
  185.9 2.1 convert_dynamic-update-slice_fusion.3
  188.5 1.8 shard_map.112
  191.9 4.3 %collective-permute-done.41 = bf16[128,1024]{1,0:T(8,128)(2,1)} collective-permute-done((bf16[128,1024]{1,0:T(8,128)(2,1)}, bf16[128,1024]{1,0:T(8,128)(2,1)}, u32[]{:S(2)}, u32[]{:S(2)}) %collective-permute-start.41) | collective-permute-done | bytes 262176 | tf_op jit(solution)/shard_map/ppermute | solution.py:286
  197.7 1.8 convert_dynamic-update-slice_fusion.2
  199.5 1.9 fusion.7
  201.4 5.3 %collective-permute-start.18 = (bf16[32,2560]{1,0:T(8,128)(2,1)S(1)}, bf16[32,2560]{1,0:T(8,128)(2,1)S(1)}, u32[]{:S(2)}, u32[]{:S(2)}) collective-permute-start(bf16[32,2560]{1,0:T(8,128)(2,1)S(1)} %get-tuple-element.48), channel_id=1, source_target_pairs={{0,2},{1,3},{2,4},{3,5},{4,6},{5,7},{6,0},{7,1},{8,10},{9,11},{10,... | collective-permute-start | bytes 491528 | tf_op jit(solution)/shard_map/ppermute | solution.py:283
  206.7 2.4 %collective-permute-start.20 = (bf16[32,2560]{1,0:T(8,128)(2,1)S(1)}, bf16[32,2560]{1,0:T(8,128)(2,1)S(1)}, u32[]{:S(2)}, u32[]{:S(2)}) collective-permute-start(bf16[32,2560]{1,0:T(8,128)(2,1)S(1)} %get-tuple-element.49), channel_id=1, source_target_pairs={{0,6},{1,7},{2,0},{3,1},{4,2},{5,3},{6,4},{7,5},{8,14},{9,15},{10,... | collective-permute-start | bytes 491528 | tf_op jit(solution)/shard_map/ppermute | solution.py:283
  211.4 4.9 %collective-permute-done.19 = bf16[32,2560]{1,0:T(8,128)(2,1)S(1)} collective-permute-done((bf16[32,2560]{1,0:T(8,128)(2,1)S(1)}, bf16[32,2560]{1,0:T(8,128)(2,1)S(1)}, u32[]{:S(2)}, u32[]{:S(2)}) %collective-permute-start.19) | collective-permute-done | bytes 163872 | tf_op jit(solution)/shard_map/ppermute | solution.py:283
  220.9 1.8 collective-permute-done.21
  222.7 4.3 %collective-permute-done.22 = bf16[32,2560]{1,0:T(8,128)(2,1)S(1)} collective-permute-done((bf16[32,2560]{1,0:T(8,128)(2,1)S(1)}, bf16[32,2560]{1,0:T(8,128)(2,1)S(1)}, u32[]{:S(2)}, u32[]{:S(2)}) %collective-permute-start.22) | collective-permute-done | bytes 163872 | tf_op jit(solution)/shard_map/ppermute | solution.py:286
  (167 shorter events, 56.2 us)
Async XLA Ops:
  5.7 18.9 %collective-permute-start.1 = (bf16[128,1024]{1,0:T(8,128)(2,1)S(1)}, bf16[128,1024]{1,0:T(8,128)(2,1)S(1)}, u32[]{:S(2)}, u32[]{:S(2)}) collective-permute-start(bf16[128,1024]{1,0:T(8,128)(2,1)S(1)} %constant_dynamic-slice_fusion.refs_16_), channel_id=1, source_target_pairs={{0,2},{1,3},{2,4},{3,5},{4,6},{5,7},{6,0},{7,1},{8,10},{9,11},{10,... | collective-permute-start | bytes 786440 | tf_op jit(solution)/shard_map/ppermute | solution.py:283
  8.8 19.7 %collective-permute-start.2 = (bf16[128,1024]{1,0:T(8,128)(2,1)S(1)}, bf16[128,1024]{1,0:T(8,128)(2,1)S(1)}, u32[]{:S(2)}, u32[]{:S(2)}) collective-permute-start(bf16[128,1024]{1,0:T(8,128)(2,1)S(1)} %constant_dynamic-slice_fusion.refs_16_), channel_id=1, source_target_pairs={{0,4},{1,5},{2,6},{3,7},{4,0},{5,1},{6,2},{7,3},{8,12},{9,13},{10,... | collective-permute-start | bytes 786440 | tf_op jit(solution)/shard_map/ppermute | solution.py:283
  11.4 17.8 %collective-permute-start.3 = (bf16[128,1024]{1,0:T(8,128)(2,1)S(1)}, bf16[128,1024]{1,0:T(8,128)(2,1)S(1)}, u32[]{:S(2)}, u32[]{:S(2)}) collective-permute-start(bf16[128,1024]{1,0:T(8,128)(2,1)S(1)} %constant_dynamic-slice_fusion.refs_16_), channel_id=1, source_target_pairs={{0,6},{1,7},{2,0},{3,1},{4,2},{5,3},{6,4},{7,5},{8,14},{9,15},{10,... | collective-permute-start | bytes 786440 | tf_op jit(solution)/shard_map/ppermute | solution.py:283
  21.5 13.5 %collective-permute-start.24 = (bf16[256,1024]{1,0:T(8,128)(2,1)S(1)}, bf16[256,1024]{1,0:T(8,128)(2,1)}, u32[]{:S(2)}, u32[]{:S(2)}) collective-permute-start(bf16[256,1024]{1,0:T(8,128)(2,1)S(1)} %get-tuple-element.24.refs_1_.refs_0_), channel_id=1, source_target_pairs={{0,8},{8,0},{16,24},{24,16},{1,9},{9,1},{17,25},{25,17},{2,10},{10... | collective-permute-start | bytes 1572872 | tf_op jit(solution)/shard_map/ppermute | solution.py:286
  23.1 31.8 %collective-permute-start.25 = (bf16[256,1024]{1,0:T(8,128)(2,1)S(1)}, bf16[256,1024]{1,0:T(8,128)(2,1)}, u32[]{:S(2)}, u32[]{:S(2)}) collective-permute-start(bf16[256,1024]{1,0:T(8,128)(2,1)S(1)} %get-tuple-element.24.refs_1_.refs_0_), channel_id=1, source_target_pairs={{0,16},{8,24},{16,0},{24,8},{1,17},{9,25},{17,1},{25,9},{2,18},{10... | collective-permute-start | bytes 1572872 | tf_op jit(solution)/shard_map/ppermute | solution.py:286
  29.9 50.8 %collective-permute-start.5 = (bf16[384,1024]{1,0:T(8,128)(2,1)}, bf16[384,1024]{1,0:T(8,128)(2,1)}, u32[]{:S(2)}, u32[]{:S(2)}) collective-permute-start(bf16[384,1024]{1,0:T(8,128)(2,1)} %constant_dynamic-update-slice_fusion.refs_5_.refs_17_), channel_id=1, source_target_pairs={{0,16},{8,24},{16,0},{24,8},{1,17},{9,25},{17,1},{25,9},{2,18},{10... | collective-permute-start | bytes 2359304 | tf_op jit(solution)/shard_map/ppermute | solution.py:286
  31.4 49.7 %collective-permute-start.6 = (bf16[384,1024]{1,0:T(8,128)(2,1)}, bf16[384,1024]{1,0:T(8,128)(2,1)}, u32[]{:S(2)}, u32[]{:S(2)}) collective-permute-start(bf16[384,1024]{1,0:T(8,128)(2,1)} %constant_dynamic-update-slice_fusion.refs_5_.refs_17_), channel_id=1, source_target_pairs={{0,24},{8,16},{16,8},{24,0},{1,25},{9,17},{17,9},{25,1},{2,26},{10... | collective-permute-start | bytes 2359304 | tf_op jit(solution)/shard_map/ppermute | solution.py:286
  32.8 48.4 %collective-permute-start.4 = (bf16[384,1024]{1,0:T(8,128)(2,1)}, bf16[384,1024]{1,0:T(8,128)(2,1)}, u32[]{:S(2)}, u32[]{:S(2)}) collective-permute-start(bf16[384,1024]{1,0:T(8,128)(2,1)} %constant_dynamic-update-slice_fusion.refs_5_.refs_17_), channel_id=1, source_target_pairs={{0,8},{8,0},{16,24},{24,16},{1,9},{9,1},{17,25},{25,17},{2,10},{10... | collective-permute-start | bytes 2359304 | tf_op jit(solution)/shard_map/ppermute | solution.py:286
  35.1 45.5 %collective-permute-start.26 = (bf16[256,1024]{1,0:T(8,128)(2,1)S(1)}, bf16[256,1024]{1,0:T(8,128)(2,1)}, u32[]{:S(2)}, u32[]{:S(2)}) collective-permute-start(bf16[256,1024]{1,0:T(8,128)(2,1)S(1)} %get-tuple-element.24.refs_1_.refs_0_), channel_id=1, source_target_pairs={{0,24},{8,16},{16,8},{24,0},{1,25},{9,17},{17,9},{25,1},{2,26},{10... | collective-permute-start | bytes 1572872 | tf_op jit(solution)/shard_map/ppermute | solution.py:286
  54.9 28.4 %collective-permute-start.7 = (bf16[512,1024]{1,0:T(8,128)(2,1)}, bf16[512,1024]{1,0:T(8,128)(2,1)}, u32[]{:S(2)}, u32[]{:S(2)}) collective-permute-start(bf16[512,1024]{1,0:T(8,128)(2,1)} %fusion.1.refs_4_), channel_id=1, source_target_pairs={{0,1},{1,0},{2,3},{3,2},{4,5},{5,4},{6,7},{7,6},{8,9},{9,8},{10,11... | collective-permute-start | bytes 3145736 | tf_op jit(solution)/shard_map/ppermute | solution.py:289
  83.2 24.0 %collective-permute-start.27 = (bf16[256,1024]{1,0:T(8,128)(2,1)}, bf16[256,1024]{1,0:T(8,128)(2,1)S(1)}, u32[]{:S(2)}, u32[]{:S(2)}) collective-permute-start(bf16[256,1024]{1,0:T(8,128)(2,1)} %copy-done.6), channel_id=1, source_target_pairs={{0,1},{1,0},{2,3},{3,2},{4,5},{5,4},{6,7},{7,6},{8,9},{9,8},{10,11... | collective-permute-start | bytes 1572872 | tf_op jit(solution)/shard_map/ppermute | solution.py:289
  83.4 26.0 %collective-permute-start.28 = (bf16[256,1024]{1,0:T(8,128)(2,1)}, bf16[256,1024]{1,0:T(8,128)(2,1)S(1)}, u32[]{:S(2)}, u32[]{:S(2)}) collective-permute-start(bf16[256,1024]{1,0:T(8,128)(2,1)} %collective-permute-done.24.refs_1_), channel_id=1, source_target_pairs={{0,1},{1,0},{2,3},{3,2},{4,5},{5,4},{6,7},{7,6},{8,9},{9,8},{10,11... | collective-permute-start | bytes 1572872 | tf_op jit(solution)/shard_map/ppermute | solution.py:289
  84.3 26.5 %collective-permute-start.29 = (bf16[256,1024]{1,0:T(8,128)(2,1)}, bf16[256,1024]{1,0:T(8,128)(2,1)S(1)}, u32[]{:S(2)}, u32[]{:S(2)}) collective-permute-start(bf16[256,1024]{1,0:T(8,128)(2,1)} %collective-permute-done.25.refs_2_), channel_id=1, source_target_pairs={{0,1},{1,0},{2,3},{3,2},{4,5},{5,4},{6,7},{7,6},{8,9},{9,8},{10,11... | collective-permute-start | bytes 1572872 | tf_op jit(solution)/shard_map/ppermute | solution.py:289
  85.5 27.6 %collective-permute-start.30 = (bf16[256,1024]{1,0:T(8,128)(2,1)}, bf16[256,1024]{1,0:T(8,128)(2,1)S(1)}, u32[]{:S(2)}, u32[]{:S(2)}) collective-permute-start(bf16[256,1024]{1,0:T(8,128)(2,1)} %collective-permute-done.26.refs_3_), channel_id=1, source_target_pairs={{0,1},{1,0},{2,3},{3,2},{4,5},{5,4},{6,7},{7,6},{8,9},{9,8},{10,11... | collective-permute-start | bytes 1572872 | tf_op jit(solution)/shard_map/ppermute | solution.py:289
  107.0 40.4 %collective-permute-start.12 = (bf16[256,2048]{1,0:T(8,128)(2,1)S(1)}, bf16[256,2048]{1,0:T(8,128)(2,1)}, u32[]{:S(2)}, u32[]{:S(2)}) collective-permute-start(bf16[256,2048]{1,0:T(8,128)(2,1)S(1)} %shard_map.114), channel_id=1, source_target_pairs={{0,1},{1,0},{2,3},{3,2},{4,5},{5,4},{6,7},{7,6},{8,9},{9,8},{10,11... | collective-permute-start | bytes 3145736 | tf_op jit(solution)/shard_map/ppermute | solution.py:289
  113.9 10.6 %collective-permute-start.34 = (f32[8,256]{1,0:T(8,128)S(1)}, f32[8,256]{1,0:T(8,128)S(1)}, u32[]{:S(2)}, u32[]{:S(2)}) collective-permute-start(f32[8,256]{1,0:T(8,128)S(1)} %get-tuple-element.37.refs_8_), channel_id=1, source_target_pairs={{0,1},{1,0},{2,3},{3,2},{4,5},{5,4},{6,7},{7,6},{8,9},{9,8},{10,11... | collective-permute-start | bytes 24584 | tf_op jit(solution)/shard_map/ppermute | solution.py:289
  113.9 11.1 %collective-permute-start.35 = (f32[8,256]{1,0:T(8,128)S(1)}, f32[8,256]{1,0:T(8,128)S(1)}, u32[]{:S(2)}, u32[]{:S(2)}) collective-permute-start(f32[8,256]{1,0:T(8,128)S(1)} %collective-permute-done.31.refs_9_), channel_id=1, source_target_pairs={{0,1},{1,0},{2,3},{3,2},{4,5},{5,4},{6,7},{7,6},{8,9},{9,8},{10,11... | collective-permute-start | bytes 24584 | tf_op jit(solution)/shard_map/ppermute | solution.py:289
  114.4 10.7 %collective-permute-start.36 = (f32[8,256]{1,0:T(8,128)S(1)}, f32[8,256]{1,0:T(8,128)S(1)}, u32[]{:S(2)}, u32[]{:S(2)}) collective-permute-start(f32[8,256]{1,0:T(8,128)S(1)} %collective-permute-done.32.refs_10_), channel_id=1, source_target_pairs={{0,1},{1,0},{2,3},{3,2},{4,5},{5,4},{6,7},{7,6},{8,9},{9,8},{10,11... | collective-permute-start | bytes 24584 | tf_op jit(solution)/shard_map/ppermute | solution.py:289
  116.9 18.9 %all-to-all-start = ((s32[8,1,1]{2,1,0:T(1,128)}), s32[8,1,1]{2,1,0:T(1,128)S(1)}, u32[]{:S(2)}, u32[]{:S(2)}) async-start(s32[8,1,1]{2,1,0:T(1,128)} %copy.31), calls=%async_computation | async-start | bytes 8192 | tf_op jit(solution)/shard_map/all_to_all | solution.py:303
  124.5 20.2 %collective-permute-start.14 = (bf16[256,512]{1,0:T(8,128)(2,1)}, bf16[256,512]{1,0:T(8,128)(2,1)}, u32[]{:S(2)}, u32[]{:S(2)}) collective-permute-start(bf16[256,512]{1,0:T(8,128)(2,1)} %copy-done.18), channel_id=1, source_target_pairs={{0,1},{1,0},{2,3},{3,2},{4,5},{5,4},{6,7},{7,6},{8,9},{9,8},{10,11... | collective-permute-start | bytes 786440 | tf_op jit(solution)/shard_map/ppermute | solution.py:289
  125.0 22.4 %collective-permute-start = (bf16[256,512]{1,0:T(8,128)(2,1)}, bf16[256,512]{1,0:T(8,128)(2,1)}, u32[]{:S(2)}, u32[]{:S(2)}) collective-permute-start(bf16[256,512]{1,0:T(8,128)(2,1)} %copy-done.17), channel_id=1, source_target_pairs={{0,1},{1,0},{2,3},{3,2},{4,5},{5,4},{6,7},{7,6},{8,9},{9,8},{10,11... | collective-permute-start | bytes 786440 | tf_op jit(solution)/shard_map/ppermute | solution.py:289
  125.1 19.7 %collective-permute-start.13 = (bf16[256,512]{1,0:T(8,128)(2,1)}, bf16[256,512]{1,0:T(8,128)(2,1)}, u32[]{:S(2)}, u32[]{:S(2)}) collective-permute-start(bf16[256,512]{1,0:T(8,128)(2,1)} %copy-done.20), channel_id=1, source_target_pairs={{0,1},{1,0},{2,3},{3,2},{4,5},{5,4},{6,7},{7,6},{8,9},{9,8},{10,11... | collective-permute-start | bytes 786440 | tf_op jit(solution)/shard_map/ppermute | solution.py:289
  135.9 52.7 %all-to-all-start.1 = ((bf16[8,48,1024]{2,1,0:T(8,128)(2,1)}), bf16[8,48,1024]{2,1,0:T(8,128)(2,1)S(1)}, u32[]{:S(2)}, u32[]{:S(2)}) async-start(bf16[8,48,1024]{2,1,0:T(8,128)(2,1)} %bitcast.4), calls=%async_computation.1 | async-start | bytes 1572864 | tf_op jit(solution)/shard_map/all_to_all | solution.py:317
  140.9 21.4 %collective-permute-start.38 = (bf16[128,1024]{1,0:T(8,128)(2,1)S(1)}, bf16[128,1024]{1,0:T(8,128)(2,1)S(1)}, u32[]{:S(2)}, u32[]{:S(2)}) collective-permute-start(bf16[128,1024]{1,0:T(8,128)(2,1)S(1)} %get-tuple-element.45), channel_id=1, source_target_pairs={{0,6},{1,7},{2,0},{3,1},{4,2},{5,3},{6,4},{7,5},{8,14},{9,15},{10,... | collective-permute-start | bytes 786440 | tf_op jit(solution)/shard_map/ppermute | solution.py:283
  144.7 39.6 %collective-permute-start.39 = (bf16[128,1024]{1,0:T(8,128)(2,1)S(1)}, bf16[128,1024]{1,0:T(8,128)(2,1)S(1)}, u32[]{:S(2)}, u32[]{:S(2)}) collective-permute-start(bf16[128,1024]{1,0:T(8,128)(2,1)S(1)} %get-tuple-element.47), channel_id=1, source_target_pairs={{0,4},{1,5},{2,6},{3,7},{4,0},{5,1},{6,2},{7,3},{8,12},{9,13},{10,... | collective-permute-start | bytes 786440 | tf_op jit(solution)/shard_map/ppermute | solution.py:283
  144.7 39.5 %collective-permute-start.40 = (bf16[128,1024]{1,0:T(8,128)(2,1)S(1)}, bf16[128,1024]{1,0:T(8,128)(2,1)S(1)}, u32[]{:S(2)}, u32[]{:S(2)}) collective-permute-start(bf16[128,1024]{1,0:T(8,128)(2,1)S(1)} %get-tuple-element.46), channel_id=1, source_target_pairs={{0,2},{1,3},{2,4},{3,5},{4,6},{5,7},{6,0},{7,1},{8,10},{9,11},{10,... | collective-permute-start | bytes 786440 | tf_op jit(solution)/shard_map/ppermute | solution.py:283
  151.9 47.5 %collective-permute-start.15 = (bf16[4,32,2560]{2,1,0:T(8,128)(2,1)}, bf16[4,32,2560]{2,1,0:T(8,128)(2,1)}, u32[]{:S(2)}, u32[]{:S(2)}) collective-permute-start(bf16[4,32,2560]{2,1,0:T(8,128)(2,1)} %get-tuple-element.42), channel_id=1, source_target_pairs={{0,8},{8,0},{16,24},{24,16},{1,9},{9,1},{17,25},{25,17},{2,10},{10... | collective-permute-start | bytes 1966088 | tf_op jit(solution)/shard_map/ppermute | solution.py:286
  152.5 47.0 %collective-permute-start.16 = (bf16[4,32,2560]{2,1,0:T(8,128)(2,1)}, bf16[4,32,2560]{2,1,0:T(8,128)(2,1)}, u32[]{:S(2)}, u32[]{:S(2)}) collective-permute-start(bf16[4,32,2560]{2,1,0:T(8,128)(2,1)} %get-tuple-element.43), channel_id=1, source_target_pairs={{0,16},{8,24},{16,0},{24,8},{1,17},{9,25},{17,1},{25,9},{2,18},{10... | collective-permute-start | bytes 1966088 | tf_op jit(solution)/shard_map/ppermute | solution.py:286
  162.2 37.2 %collective-permute-start.17 = (bf16[4,32,2560]{2,1,0:T(8,128)(2,1)}, bf16[4,32,2560]{2,1,0:T(8,128)(2,1)}, u32[]{:S(2)}, u32[]{:S(2)}) collective-permute-start(bf16[4,32,2560]{2,1,0:T(8,128)(2,1)} %get-tuple-element.44), channel_id=1, source_target_pairs={{0,24},{8,16},{16,8},{24,0},{1,25},{9,17},{17,9},{25,1},{2,26},{10... | collective-permute-start | bytes 1966088 | tf_op jit(solution)/shard_map/ppermute | solution.py:286
  190.4 18.8 %collective-permute-start.42 = (bf16[128,1024]{1,0:T(8,128)(2,1)}, bf16[128,1024]{1,0:T(8,128)(2,1)S(1)}, u32[]{:S(2)}, u32[]{:S(2)}) collective-permute-start(bf16[128,1024]{1,0:T(8,128)(2,1)} %get-tuple-element.39), channel_id=1, source_target_pairs={{0,16},{8,24},{16,0},{24,8},{1,17},{9,25},{17,1},{25,9},{2,18},{10... | collective-permute-start | bytes 786440 | tf_op jit(solution)/shard_map/ppermute | solution.py:286
  196.2 21.9 %collective-permute-start.43 = (bf16[128,1024]{1,0:T(8,128)(2,1)}, bf16[128,1024]{1,0:T(8,128)(2,1)S(1)}, u32[]{:S(2)}, u32[]{:S(2)}) collective-permute-start(bf16[128,1024]{1,0:T(8,128)(2,1)} %get-tuple-element.39), channel_id=1, source_target_pairs={{0,24},{8,16},{16,8},{24,0},{1,25},{9,17},{17,9},{25,1},{2,26},{10... | collective-permute-start | bytes 786440 | tf_op jit(solution)/shard_map/ppermute | solution.py:286
  201.4 10.0 %collective-permute-start.18 = (bf16[32,2560]{1,0:T(8,128)(2,1)S(1)}, bf16[32,2560]{1,0:T(8,128)(2,1)S(1)}, u32[]{:S(2)}, u32[]{:S(2)}) collective-permute-start(bf16[32,2560]{1,0:T(8,128)(2,1)S(1)} %get-tuple-element.48), channel_id=1, source_target_pairs={{0,2},{1,3},{2,4},{3,5},{4,6},{5,7},{6,0},{7,1},{8,10},{9,11},{10,... | collective-permute-start | bytes 491528 | tf_op jit(solution)/shard_map/ppermute | solution.py:283
  (50 other events, 670.8 us)

commit v3 on v2

v3 whole, which is shorter than its diff:
```python
import jax
import jax.numpy as jnp
from jax import lax
from jax.experimental import pallas as pl
from jax.experimental.pallas import tpu as pltpu
from jax.sharding import PartitionSpec as P

HEADS = 4
HEAD_DIM = 128
NCAND = 4

epsilon = 1e-05
softmax_warmth = 0.05
EMPTY = 2.0**100

f32, b16, i32 = jnp.float32, jnp.bfloat16, jnp.int32
NN = ((1,), (0,))
NT = ((1,), (1,))
TN = ((0,), (0,))
VMEM = pl.BlockSpec(memory_space=pltpu.VMEM)
SMEM = pl.BlockSpec(memory_space=pltpu.SMEM)
ANY = pl.BlockSpec(memory_space=pl.ANY)


def dot(a, b, dims):
    return lax.dot_general(a, b, (dims, ((), ())), preferred_element_type=f32)


def iota(shape, axis):
    return lax.broadcasted_iota(i32, shape, axis)


def center_scale(values):
    average = jnp.mean(values, -1, keepdims=True)
    centered = values - average
    inverse = lax.rsqrt(jnp.mean(centered * centered, -1, keepdims=True) + epsilon)
    return (centered * inverse, inverse)


def sigmoid(values):
    return 1.0 / (1.0 + jnp.exp(-values))


def split_columns(x, owners, core):
    rows = x.shape[1] // owners
    blocks = [x[:, i * rows : (i + 1) * rows] for i in range(owners)]
    even, odd = jnp.concatenate(blocks[0::2], 1), jnp.concatenate(blocks[1::2], 1)
    first = jnp.broadcast_to(core, even.shape) == 0
    return jnp.where(first, even, odd), jnp.where(first, odd, even)


def call(kernel, out, specs, args, scratch=(), flops=0, nbytes=0, room=32):
    return pl.pallas_call(
        kernel,
        out_shape=[jax.ShapeDtypeStruct(s, t) for s, t in out],
        in_specs=specs,
        out_specs=[VMEM] * len(out),
        scratch_shapes=list(scratch),
        cost_estimate=pl.CostEstimate(flops=flops, bytes_accessed=nbytes, transcendentals=0),
        compiler_params=pltpu.CompilerParams(vmem_limit_bytes=room * 2**20),
    )(*args)


def forward_kernel(
    owners, slot, lengths, dests, events, in_weight, out_weight,
    keep, give, proj, slope, attn, attn_slope, normed_out, inv_out, gated_out, unit, unit_b, inv_len, outgoing,
):
    tok = events.shape[0]
    hidden = out_weight.shape[1]
    scale = HEAD_DIM ** (-0.5)
    core = lax.axis_index("seq") % 2
    x = events[...].astype(f32)
    normed_in = center_scale(x)[0]
    mine, other = split_columns(normed_in, owners, core)
    keep[...] = mine.astype(b16)
    give[...] = other.astype(b16)
    normed_in = normed_in.astype(b16)
    for i in range(4):
        cols = slice(i * hidden, (i + 1) * hidden)
        p = dot(normed_in, in_weight[:, cols], NN)
        sig = sigmoid(p)
        proj[:, cols] = (p * sig).astype(b16)
        slope[:, cols] = (sig * (1.0 + p * (1.0 - sig))).astype(b16)

    pos_c, pos_r = iota((tok, 1), 0), iota((1, tok), 1)
    user_c, user_r = jnp.zeros((tok, 1), i32), jnp.zeros((1, tok), i32)
    target = jnp.zeros((1, tok), i32)
    start = jnp.int32(0)
    for j in range(lengths.shape[1]):
        end = start + lengths[0, j]
        user_c += (pos_c >= end).astype(i32)
        user_r += (pos_r >= end).astype(i32)
        here = (pos_r >= start) & (pos_r < end)
        target = jnp.where(here, dests[0, j] * slot + pos_r - start, target)
        start = end
    mask = (user_c == user_r) & (pos_r <= pos_c)

    outputs = []
    for h in range(HEADS):
        v = proj[:, hidden + h * HEAD_DIM : hidden + (h + 1) * HEAD_DIM]
        q = proj[:, 2 * hidden + h * HEAD_DIM : 2 * hidden + (h + 1) * HEAD_DIM]
        k = proj[:, 3 * hidden + h * HEAD_DIM : 3 * hidden + (h + 1) * HEAD_DIM]
        s = dot(q, k, NT) * scale
        sig = sigmoid(s)
        weight = jnp.where(mask, s * sig, 0.0).astype(b16)
        attn[h] = weight
        attn_slope[h] = jnp.where(mask, sig * (1.0 + s * (1.0 - sig)) * scale, 0.0).astype(b16)
        outputs.append(dot(weight, v, NN))
    normed, inverse = center_scale(jnp.concatenate(outputs, 1))
    normed_out[...] = normed
    inv_out[...] = inverse
    gated = (normed * proj[:, :hidden].astype(f32)).astype(b16)
    gated_out[...] = gated
    result = x + dot(gated, out_weight[...], NT)
    inverse = lax.rsqrt(jnp.sum(result * result, -1, keepdims=True) + epsilon)
    inv_len[...] = inverse
    yn = result * inverse
    unit[...] = yn
    unit_b[...] = yn.astype(b16)
    row = iota((outgoing.shape[0], 1), 0)
    filled = jnp.zeros(row.shape, i32)
    for j in range(lengths.shape[1]):
        at = dests[0, j] * slot
        filled = jnp.where((row >= at) & (row < at + lengths[0, j]), 1, filled)
    placed = dot((row == target).astype(b16), result.astype(b16), NN)
    outgoing[...] = jnp.where(filled == 1, placed, EMPTY).astype(b16)


def owner_ids(owners):
    seq = lax.axis_index("seq")
    chip, core = seq // 2, seq % 2
    chips = owners // 2
    return [2 * ((chip + chips - d) % chips) + (core ^ side) for side in range(2) for d in range(chips)]


def normalise_kernel(share, item_table, own, quarter, quarter_inv):
    grp = lax.axis_index("grp")
    x = item_table[...].astype(f32)
    own[...] = (x * lax.rsqrt(jnp.sum(x * x, -1, keepdims=True) + epsilon)).astype(b16)
    x = item_table[pl.ds(pl.multiple_of(grp * share, share), share)].astype(f32)
    inverse = lax.rsqrt(jnp.sum(x * x, -1, keepdims=True) + epsilon)
    quarter[...] = (x * inverse).astype(b16)
    quarter_inv[...] = inverse


def score_kernel(groups, owners, share, places, cand, unit_b, unit, inv_len, *refs):
    count = len(places)
    pieces, (tags, up, up_keep, up_give, table, spread, sems) = refs[:count], refs[count:]
    chips = owners // 2
    vocab_dev = share * groups
    grp, core = lax.axis_index("grp"), lax.axis_index("seq") % 2
    tok, width = unit_b.shape
    block = vocab_dev + groups * (chips - 1) * share
    copies = {}
    for n, (side, k, left, wide) in enumerate(places):
        rows = pieces[n].shape[0]
        at = side * block + (0 if k < 0 else vocab_dev + k * rows)
        copy = pltpu.make_async_copy(pieces[n], table.at[pl.ds(at, rows), pl.ds(left, wide)], sems.at[n])
        copy.start()
        copies.setdefault((side, k), []).append(copy)
    ids = owner_ids(owners)
    lane = iota((1, 128), 1)
    owner = jnp.full((1, 128), -1, i32)
    for j in range(owners):
        owner = jnp.where(lane == j, ids[j], owner)
    candidates = cand[...]
    chosen = jnp.full((tok, 128), -1, i32)
    first = jnp.zeros((tok, 128), f32)
    for c in range(NCAND):
        here = candidates[:, c : c + 1] // vocab_dev == owner
        chosen = jnp.where(here, candidates[:, c : c + 1], chosen)
        if c == 0:
            first = here.astype(f32)
    wanted = [jnp.broadcast_to(chosen[:, j : j + 1], (tok, 128)) for j in range(owners)]

    def runs(key):
        side, k = key
        at = side * block + (0 if k < 0 else vocab_dev + k * (chips - 1) * share)
        if k < 0:
            return at, vocab_dev, [(side * chips, 0, vocab_dev, ids[side * chips] * vocab_dev)]
        begin = (grp ^ k) * share
        return at, (chips - 1) * share, [
            (side * chips + d, (d - 1) * share, share, ids[side * chips + d] * vocab_dev + begin)
            for d in range(1, chips)
        ]

    def tiles(key):
        at, rows, here = runs(key)
        for j, off, wide, base in here:
            step = min(wide, 128)
            for o in range(0, wide, step):
                hit = wanted[j][:, :step] == base + o + iota((1, step), 1)
                yield j, off + o, step, hit

    yb = unit_b[...]
    value = [[] for _ in range(owners)]
    for key in copies:
        for copy in copies[key]:
            copy.wait()
        at, rows, _ = runs(key)
        product = dot(yb, table[at : at + rows], NT)
        for j, off, step, hit in tiles(key):
            value[j].append(jnp.where(hit, product[:, off : off + step], 0.0))
    logits = jnp.zeros((tok, 128), f32)
    for j in range(owners):
        total = value[j][0]
        for part in value[j][1:]:
            total = total + part
        logits = jnp.where(lane == j, jnp.sum(total, -1, keepdims=True), logits)
    exponent = jnp.where(chosen >= 0, jnp.exp(logits / softmax_warmth), 0.0)
    coef = (exponent / jnp.sum(exponent, -1, keepdims=True) - first) / softmax_warmth
    tags[:owners] = coef.T[:owners]
    tags[owners:] = chosen.astype(f32).T[:owners]
    amount = [jnp.broadcast_to(coef[:, j : j + 1], (tok, 128)) for j in range(owners)]
    for key in copies:
        at = runs(key)[0]
        for j, off, step, hit in tiles(key):
            spread[:, at + off : at + off + step] = jnp.where(hit, amount[j][:, :step], 0.0).astype(b16)
    pulled = dot(spread[...], table[...], NN)
    yn = unit[...]
    upstream = (pulled - yn * jnp.sum(yn * pulled, -1, keepdims=True)) * inv_len[...]
    up[...] = upstream.astype(b16)
    mine, other = split_columns(upstream, owners, core)
    up_keep[...] = mine.astype(b16)
    up_give[...] = other.astype(b16)


def backward_kernel(up, out_weight, proj, slope, attn, attn_slope, normed_ref, inverse, grad):
    hidden = out_weight.shape[1]
    normed = normed_ref[...]
    grad_gated = dot(up[...], out_weight[...], NN)
    grad[:, :hidden] = (grad_gated * normed * slope[:, :hidden].astype(f32)).astype(b16)
    grad_normed = grad_gated * proj[:, :hidden].astype(f32)
    grad_attended = inverse[...] * (
        grad_normed
        - jnp.mean(grad_normed, -1, keepdims=True)
        - normed * jnp.mean(grad_normed * normed, -1, keepdims=True)
    )
    grad_attended = grad_attended.astype(b16)
    for h in range(HEADS):
        cv, cq, ck = [slice(i * hidden + h * HEAD_DIM, i * hidden + (h + 1) * HEAD_DIM) for i in (1, 2, 3)]
        part = grad_attended[:, h * HEAD_DIM : (h + 1) * HEAD_DIM]
        grad_attn = dot(part, proj[:, cv], NT)
        grad_score = (grad_attn * attn_slope[h].astype(f32)).astype(b16)
        grad[:, cv] = (dot(attn[h], part, TN) * slope[:, cv].astype(f32)).astype(b16)
        grad[:, cq] = (dot(grad_score, proj[:, ck], NN) * slope[:, cq].astype(f32)).astype(b16)
        grad[:, ck] = (dot(grad_score, proj[:, cq], TN) * slope[:, ck].astype(f32)).astype(b16)


def item_kernel(groups, owners, share, places, *refs):
    count = len(places)
    units, tags = refs[:count], refs[count : count + groups]
    own, others, far_own, far_others, keep, give, gathered, near, sems = refs[count + groups :]
    chips = owners // 2
    vocab_dev = share * groups
    grp = lax.axis_index("grp")
    tok = tags[0].shape[1]
    copies = []
    for n, (k, left, wide) in enumerate(places):
        copies.append(pltpu.make_async_copy(units[n], gathered.at[pl.ds(k * tok, tok), pl.ds(left, wide)], sems.at[n]))
    begin = pl.multiple_of(grp * share, share)
    for side, (full, part) in enumerate(((own, others), (far_own, far_others))):
        at, n = side * chips * share, count + 2 * side
        copies.append(pltpu.make_async_copy(full.at[pl.ds(begin, share)], near.at[pl.ds(at, share)], sems.at[n]))
        copies.append(
            pltpu.make_async_copy(part, near.at[pl.ds(at + share, (chips - 1) * share)], sems.at[n + 1])
        )
    for copy in copies:
        copy.start()
    ids = owner_ids(owners)
    amounts = jnp.concatenate([t[:owners] for t in tags], 1)
    chosen = jnp.concatenate([t[owners:] for t in tags], 1).astype(i32)
    for copy in copies:
        copy.wait()
    for side, out in ((0, keep), (1, give)):
        parts = []
        for d in range(chips):
            j = side * chips + d
            hit = ids[j] * vocab_dev + grp * share + iota((share, 1), 0) == chosen[j : j + 1]
            parts.append(jnp.where(hit, amounts[j : j + 1], 0.0).astype(b16))
        summed = dot(jnp.concatenate(parts, 0), gathered[...], NN)
        row = near[side * chips * share : (side + 1) * chips * share].astype(f32)
        out[...] = (summed - row * jnp.sum(row * summed, -1, keepdims=True)).astype(b16)


def weight_kernel(groups, owners, keep, give, up_keep, up_give, grad, far_grad, gated, far_gated, *refs):
    outs, whole = refs[:-1], refs[-1]
    chips = owners // 2
    grp = lax.axis_index("grp")
    wide = grad.shape[1]
    step = gated.shape[1]
    for i in range(0, wide, step):
        cols = slice(i, i + step)
        part = dot(keep[...], grad[:, cols], TN) + dot(give[...], far_grad[:, cols], TN)
        whole[:, cols] = part.astype(b16)
    part = dot(up_keep[...], gated[...], TN) + dot(up_give[...], far_gated[...], TN)
    whole[:, wide:] = part.astype(b16)
    rows = whole.shape[0] // chips
    fine = rows // groups
    half = whole.shape[1] // 2
    for z in range(chips):
        for k in range(groups):
            piece = whole[pl.ds(pl.multiple_of(z * rows + (grp ^ k) * fine, fine), fine)]
            if k == 3:
                outs[3][z] = piece[:, :half]
                outs[4][z] = piece[:, half:]
            else:
                outs[k][z] = piece


def assemble_kernel(groups, columns, *refs):
    parts, outs = refs[:groups], refs[groups:]
    grp = lax.axis_index("grp")
    fine = parts[0].shape[0]
    for k in range(groups):
        at = pl.ds(pl.multiple_of((grp ^ k) * fine, fine), fine)
        left = 0
        for out, wide in zip(outs, columns):
            out[at] = parts[k][:, left : left + wide].astype(f32)
            left += wide


def relay_kernel(arrived, out):
    tok, slots = out.shape[0], arrived.shape[0]
    filled = (arrived[:, :128].astype(f32) < EMPTY / 2).astype(b16)
    before = (iota((slots, 1), 0) > iota((1, slots), 1)).astype(b16)
    rank = dot(before, filled, NN)[:, :1].astype(i32)
    rank = jnp.where(filled[:, :1].astype(f32) > 0, rank, -1)
    place = (rank == iota((1, tok), 1)).astype(b16)
    out[...] = dot(place, arrived[...], TN).astype(b16)


def body(events, lengths, destinations, history, negatives, in_weight, out_weight, item_table):
    groups = lax.axis_size("grp")
    owners = lax.axis_size("seq")
    chips = owners // 2
    grp = lax.axis_index("grp")
    seq = lax.axis_index("seq")
    chip, core = seq // 2, seq % 2
    tok = events.shape[0]
    vocab_dev, width = item_table.shape
    hidden = out_weight.shape[1]
    share = vocab_dev // groups
    slot = 3 * tok // (2 * owners)
    rows = width // owners
    fine = rows // groups

    def to_chip(x, d):
        pairs = [(2 * a + b, 2 * ((a + d) % chips) + b) for a in range(chips) for b in range(2)]
        return lax.ppermute(x, "seq", pairs)

    def to_group(x, k):
        return lax.ppermute(x, "grp", [(a, a ^ k) for a in range(groups)])

    def to_core(x):
        return lax.ppermute(x, "seq", [(a, a ^ 1) for a in range(owners)])

    def gather_groups(x):
        wide = x.shape[1]
        if groups != 4:
            return [(k, 0, wide, to_group(x, k) if k else x) for k in range(groups)]
        one, two = to_group(x, 1), to_group(x, 2)
        half = wide // 2
        left, right = to_group(one[:, :half], 2), to_group(two[:, half:], 1)
        return [(0, 0, wide, x), (1, 0, wide, one), (2, 0, wide, two), (3, 0, half, left), (3, half, half, right)]

    own, quarter, quarter_inv = call(
        lambda *refs: normalise_kernel(share, *refs),
        [((vocab_dev, width), b16), ((share, width), b16), ((share, 1), f32)],
        [VMEM], [item_table], flops=8 * vocab_dev * width, nbytes=5 * vocab_dev * width, room=24,
    )
    others = jnp.concatenate([to_chip(quarter, d) for d in range(1, chips)], 0)
    pieces = [(0, -1, 0, width, own)] + [(0,) + p for p in gather_groups(others)]
    pieces = pieces + [(1,) + p[1:4] + (to_core(p[4]),) for p in pieces]
    far_own, far_others = [p[4] for p in pieces if p[0] == 1 and p[1] <= 0]

    outs = [
        ((tok, width // 2), b16), ((tok, width // 2), b16), ((tok, 4 * hidden), b16), ((tok, 4 * hidden), b16),
        ((HEADS, tok, tok), b16), ((HEADS, tok, tok), b16), ((tok, hidden), f32), ((tok, 1), f32),
        ((tok, hidden), b16), ((tok, width), f32), ((tok, width), b16), ((tok, 1), f32),
        ((owners * slot, width), b16),
    ]
    (keep, give, proj, slope, attn, attn_slope, normed, inverse, gated, unit, unit_b, inv_len, outgoing) = call(
        lambda *refs: forward_kernel(owners, slot, *refs), outs, [SMEM, SMEM, VMEM, VMEM, VMEM],
        [lengths, destinations, events, in_weight, out_weight],
        flops=2 * tok * width * 6 * hidden, nbytes=24 * tok * width + 10 * width * hidden,
    )

    arrived = lax.all_to_all(
        outgoing.reshape(owners, slot, width), "seq", 0, 0, tiled=True
    ).reshape(owners * slot, width)
    layer_out, = call(
        relay_kernel, [((tok, width), b16)], [VMEM], [arrived],
        flops=3 * tok * tok * width, nbytes=6 * tok * width, room=16,
    )

    candidates = jnp.concatenate([history[:, None], negatives], 1)
    vocab = vocab_dev * owners
    layer_out, score_unit = lax.optimization_barrier((layer_out, unit))
    tags, up, up_keep, up_give = call(
        lambda *refs: score_kernel(groups, owners, share, [p[:4] for p in pieces], *refs),
        [((2 * owners, tok), f32), ((tok, width), b16), ((tok, width // 2), b16), ((tok, width // 2), b16)],
        [VMEM] * 4 + [ANY] * len(pieces), [candidates, unit_b, score_unit, inv_len] + [p[4] for p in pieces],
        [pltpu.VMEM((vocab, width), b16), pltpu.VMEM((tok, vocab), b16), pltpu.SemaphoreType.DMA((len(pieces),))],
        flops=4 * tok * width * vocab, nbytes=2 * vocab * width + 12 * tok * width, room=24 + vocab // 256,
    )

    grad, = call(
        backward_kernel, [((tok, 4 * hidden), b16)], [VMEM] * 8,
        [up, out_weight, proj, slope, attn, attn_slope, normed, inverse],
        flops=2 * tok * width * hidden, nbytes=20 * tok * width,
    )

    far = [to_core(x) for x in (give, up_give, grad, gated)]
    half = 5 * hidden // 2
    if groups == 4:
        block = (chips, fine, 5 * hidden)
        split = (chips, fine, half)
        parts = call(
            lambda *refs: weight_kernel(groups, owners, *refs),
            [(block, b16)] * 3 + [(split, b16)] * 2, [VMEM] * 8,
            [keep, far[0], up_keep, far[1], grad, far[2], gated, far[3]],
            [pltpu.VMEM((width // 2, 5 * hidden), b16)],
            flops=2 * tok * width * 5 * hidden, nbytes=20 * tok * width, room=24,
        )
        after = parts[0]
        left, right = to_group(parts[3], 1).astype(f32), to_group(parts[4], 2).astype(f32)
        one, two = parts[1].astype(f32), parts[2].astype(f32)
        one = jnp.concatenate([one[..., :half], one[..., half:] + right], 2).astype(b16)
        two = jnp.concatenate([two[..., :half] + left, two[..., half:]], 2).astype(b16)
        sums = parts[0].astype(f32) + to_group(one, 1).astype(f32) + to_group(two, 2).astype(f32)
    else:
        def both(x, y):
            return jnp.concatenate([x, y], 0)

        in_part = dot(both(keep, far[0]), both(grad, far[2]), TN)
        out_part = dot(both(up_keep, far[1]), both(gated, far[3]), TN)
        weight = jnp.concatenate([in_part, out_part], 1).astype(b16)
        weight = weight.reshape(chips, groups, fine, 5 * hidden)
        after = weight
        sums = lax.dynamic_index_in_dim(weight, grp, 1, False).astype(f32)
        for k in range(1, groups):
            sums += to_group(lax.dynamic_index_in_dim(weight, grp ^ k, 1, False), k).astype(f32)
    sums = sums.astype(b16)

    units = gather_groups(unit_b)
    all_tags = [to_group(tags, k) if k else tags for k in range(groups)]
    first_unit, after = lax.optimization_barrier((units[0][3], after))
    mine, other = call(
        lambda *refs: item_kernel(groups, owners, share, [p[:3] for p in units], *refs),
        [((chips * share, width), b16)] * 2, [ANY] * len(units) + [VMEM] * groups + [ANY] * 4,
        [first_unit] + [p[3] for p in units[1:]] + all_tags + [own, others, far_own, far_others],
        [pltpu.VMEM((groups * tok, width), b16), pltpu.VMEM((2 * chips * share, width), b16),
         pltpu.SemaphoreType.DMA((len(units) + 4,))],
        flops=4 * groups * tok * width * chips * share, nbytes=4 * tok * groups * width, room=32 if groups == 4 else 48,
    )
    summed = (mine.astype(f32) + to_core(other).astype(f32)).astype(b16).reshape(chips, share, width)
    total = summed[0].astype(f32)
    for d in range(1, chips):
        total += to_chip(summed[d], -d).astype(f32)
    total = (total * quarter_inv).astype(b16)
    table_grad, = call(
        lambda *refs: assemble_kernel(groups, [width], *refs), [((vocab_dev, width), f32)], [VMEM] * groups,
        [to_group(total, k) if k else total for k in range(groups)],
        flops=vocab_dev * width, nbytes=6 * vocab_dev * width, room=16,
    )

    line = lax.dynamic_index_in_dim(sums, chip, 0, False).astype(f32)
    for d in range(1, chips):
        line += to_chip(lax.dynamic_index_in_dim(sums, (chip + d) % chips, 0, False), d).astype(f32)
    line = line.astype(b16)
    lines = [to_group(line, k) if k else line for k in range(groups)]
    if fine % 16 == 0:
        in_grad, out_grad = call(
            lambda *refs: assemble_kernel(groups, [4 * hidden, hidden], *refs),
            [((rows, 4 * hidden), f32), ((rows, hidden), f32)], [VMEM] * groups, lines,
            flops=rows * hidden, nbytes=30 * rows * hidden, room=16,
        )
    else:
        shard = jnp.zeros((rows, 5 * hidden), f32)
        for k in range(groups):
            shard = lax.dynamic_update_slice_in_dim(shard, lines[k].astype(f32), (grp ^ k) * fine, 0)
        in_grad, out_grad = shard[:, : 4 * hidden], shard[:, 4 * hidden :]
    return (layer_out, in_grad, out_grad, table_grad)


def solution(mesh):
    return jax.shard_map(
        body,
        mesh=mesh,
        in_specs=(
            P(("grp", "seq"), None),
            P(("grp", "seq"), None),
            P(("grp", "seq"), None),
            P(("grp", "seq")),
            P(("grp", "seq"), None),
            P(),
            P(),
            P("seq", None),
        ),
        out_specs=(P(("grp", "seq"), None), P("seq", None), P("seq", None), P("seq", None)),
        check_vma=False,
    )
```

time: 231 us -> 213 us (0.922)
  other arithmetic: 13.2 us -> 4.2 us
  waiting for transfers between devices: 100 us -> 109 us
  starting transfers between devices: 58.1 us -> 50 us
  Pallas kernels: 30.5 us -> 26.2 us
  matrix products: 4.1 us -> 0 us
    all_to_all x1 -> x0, starting transfers between devices: 6.81 us -> none  [body(): counts = lax.all_to_all(send_length, 'seq', 0, 0, tiled=True)]
    all_to_all x1, waiting for transfers between devices: 0.01 us -> 6.07 us  [body(): lax.all_to_all(outgoing.reshape(owners, slot, width), 'seq', 0, 0, tiled=...]
    ppermute x9, waiting for transfers between devices: 38.3 us -> 44.2 us  [to_chip(): return lax.ppermute(x, 'seq', pairs)]
    dynamic_update_slice x8 -> x0, other arithmetic: 5.8 us -> none  [the longest x4 5.61 us: body(): lax.dynamic_update_slice_in_dim(table_grad, part.astype(f32), (grp ^ k) *...]
    ppermute x9, starting transfers between devices: 19.8 us -> 14.2 us  [to_chip(): return lax.ppermute(x, 'seq', pairs)]
    pallas_call x5 -> x9, Pallas kernels: 30.5 us -> 26.2 us  [call(): pl.pallas_call(kernel, out_shape=[jax.ShapeDtypeStruct(s, t) for s, t in...]
    dot_general x2 -> x0, matrix products: 4.1 us -> none  [dot(): return lax.dot_general(a, b, (dims, ((), ())), preferred_element_type=f32)]
    unnamed x74 -> x78, local copies, waits for them, and re-layouts: 14.9 us -> 18.7 us
  transfers between devices with their start and end apart: 46 -> 42, of which waited for: 17 -> 20; matrix products, arithmetic and copies ran while one was open for 8% -> 4% of each run, Pallas kernels for 13% -> 6%
where the time goes in v3:
time: 213 us
  waiting for transfers between devices  109 us (51%)
  starting transfers between devices  50 us (23%)
  Pallas kernels  26.2 us (12%)
  local copies, waits for them, and re-layouts  22.4 us (11%)
  other arithmetic  4.2 us (2%)
    ppermute x21, waiting for transfers between devices, to_group(): return lax.ppermute(x, 'grp', [(a, a ^ k) for a in range(groups)])  55.6 us
    ppermute x9, waiting for transfers between devices, to_chip(): return lax.ppermute(x, 'seq', pairs)  44.2 us
    pallas_call x9, Pallas kernels, call(): pl.pallas_call(kernel, out_shape=[jax.ShapeDtypeStruct(s, t) for s, t in...  26.2 us
    ppermute x21, starting transfers between devices, to_group(): return lax.ppermute(x, 'grp', [(a, a ^ k) for a in range(groups)])  25 us
    unnamed x78, local copies, waits for them, and re-layouts  18.7 us
    ppermute x9, starting transfers between devices, to_chip(): return lax.ppermute(x, 'seq', pairs)  14.2 us
    all_to_all x1, starting transfers between devices, body(): lax.all_to_all(outgoing.reshape(owners, slot, width), 'seq', 0, 0, tiled=...  8.6 us
    all_to_all x1, waiting for transfers between devices, body(): lax.all_to_all(outgoing.reshape(owners, slot, width), 'seq', 0, 0, tiled=...  6.07 us
  transfers between devices with their start and end apart: 42, of which 20 were waited for; matrix products, arithmetic and copies ran while one was open for 4% of the time, Pallas kernels for 6%

profile of v3, /device:TPU:0, one launch (start us, length us, event | category | flops | bytes accessed | tf_op | source)
XLA Modules:
  0.0 212.6 jit_solution(6144463318665616522)
XLA Ops:
  2.4 3.1 %collective-permute-start.1 = (bf16[128,1024]{1,0:T(8,128)(2,1)S(1)}, bf16[128,1024]{1,0:T(8,128)(2,1)S(1)}, u32[]{:S(2)}, u32[]{:S(2)}) collective-permute-start(bf16[128,1024]{1,0:T(8,128)(2,1)S(1)} %get-tuple-element.45), channel_id=1, source_target_pairs={{0,2},{1,3},{2,4},{3,5},{4,6},{5,7},{6,0},{7,1},{8,10},{9,11},{10,... | collective-permute-start | bytes 786440 | tf_op jit(solution)/shard_map/ppermute | solution.py:350
  5.5 2.6 %collective-permute-start.2 = (bf16[128,1024]{1,0:T(8,128)(2,1)S(1)}, bf16[128,1024]{1,0:T(8,128)(2,1)S(1)}, u32[]{:S(2)}, u32[]{:S(2)}) collective-permute-start(bf16[128,1024]{1,0:T(8,128)(2,1)S(1)} %get-tuple-element.45), channel_id=1, source_target_pairs={{0,4},{1,5},{2,6},{3,7},{4,0},{5,1},{6,2},{7,3},{8,12},{9,13},{10,... | collective-permute-start | bytes 786440 | tf_op jit(solution)/shard_map/ppermute | solution.py:350
  9.4 5.4 %collective-permute-done.1 = bf16[128,1024]{1,0:T(8,128)(2,1)S(1)} collective-permute-done((bf16[128,1024]{1,0:T(8,128)(2,1)S(1)}, bf16[128,1024]{1,0:T(8,128)(2,1)S(1)}, u32[]{:S(2)}, u32[]{:S(2)}) %collective-permute-start.1) | collective-permute-done | bytes 262176 | tf_op jit(solution)/shard_map/ppermute | solution.py:350
  15.5 9.6 %collective-permute-done.2 = bf16[128,1024]{1,0:T(8,128)(2,1)S(1)} collective-permute-done((bf16[128,1024]{1,0:T(8,128)(2,1)S(1)}, bf16[128,1024]{1,0:T(8,128)(2,1)S(1)}, u32[]{:S(2)}, u32[]{:S(2)}) %collective-permute-start.2) | collective-permute-done | bytes 262176 | tf_op jit(solution)/shard_map/ppermute | solution.py:350
  26.6 1.5 collective-permute-start.5
  29.7 2.2 %copy-done.12 = bf16[1024,2048]{1,0:T(8,128)(2,1)S(1)} copy-done((bf16[1024,2048]{1,0:T(8,128)(2,1)S(1)}, bf16[1024,2048]{1,0:T(8,128)(2,1)}, u32[]{:S(2)}) %copy-start.12) | copy-done | bytes 4194328
  31.9 4.6 %shard_map.111 = (bf16[256,512]{1,0:T(8,128)(2,1)S(1)}, bf16[256,512]{1,0:T(8,128)(2,1)S(1)}, bf16[256,2048]{1,0:T(8,128)(2,1)S(1)}, bf16[256,2048]{1,0:T(8,128)...) custom-call(s32[1,8]{1,0:T(1,128)S(1)} %copy-done.28, ...), custom_call_target="tpu_custom_call" | custom-call | flops 1610612736 | bytes 11534336 | tf_op jit(solution)/shard_map/pallas_call | solution.py:53
  44.5 8.6 %all-to-all-start = ((bf16[8,48,1024]{2,1,0:T(8,128)(2,1)}), bf16[8,48,1024]{2,1,0:T(8,128)(2,1)S(1)}, u32[]{:S(2)}, u32[]{:S(2)}) async-start(bf16[8,48,1024]{2,1,0:T(8,128)(2,1)} %bitcast.13), calls=%async_computation | async-start | bytes 1572864 | tf_op jit(solution)/shard_map/all_to_all | solution.py:389
  57.4 8.5 %collective-permute-done.7.refs_9_ = bf16[384,512]{1,0:T(8,128)(2,1)} collective-permute-done((bf16[384,512]{1,0:T(8,128)(2,1)S(1)}, bf16[384,512]{1,0:T(8,128)(2,1)}, u32[]{:S(2)}, u32[]{:S(2)}) %collective-permute-start.7) | collective-permute-done | bytes 393248 | tf_op jit(solution)/shard_map/ppermute | solution.py:353
  68.0 6.1 %all-to-all-done = bf16[8,48,1024]{2,1,0:T(8,128)(2,1)S(1)} async-done(((bf16[8,48,1024]{2,1,0:T(8,128)(2,1)}), bf16[8,48,1024]{2,1,0:T(8,128)(2,1)S(1)}, u32[]{:S(2)}, u32[]{:S(2)}) %all-to-all-start) | async-done | bytes 786464 | tf_op jit(solution)/shard_map/all_to_all | solution.py:389
  74.1 1.6 shard_map.112
  78.1 9.1 %shard_map.114 = (f32[16,256]{1,0:T(8,128)S(1)}, bf16[256,1024]{1,0:T(8,128)(2,1)S(1)}, bf16[256,512]{1,0:T(8,128)(2,1)S(1)}, bf16[256,512]{1,0:T(8,128)(2,1)S(1)}) custom-call(s32[256,4]{1,0:T(8,128)S(1)} %copy-done.9, bf16[256,1024]{1,0:T(8,128)(2,1)S(1)} %copy-done.18, f32[256,1024]{1,0:T(8,128)S(1)} %copy-done.31, f32[256,1]{1,0:T(8,128)S(1)} %copy-done.35, ...), custom_call_target="tpu_custom_call" | custom-call | flops 4294967296 | bytes 11534336 | tf_op jit(solution)/shard_map/pallas_call | solution.py:53
  87.2 1.6 shard_map.115.refs_4_
  89.9 2.0 collective-permute-done.refs_1_
  92.6 1.7 shard_map.116
  97.0 1.6 collective-permute-start.17
  98.6 6.4 %collective-permute-done.19 = bf16[4,32,1280]{2,1,0:T(8,128)(2,1)S(1)} collective-permute-done((bf16[4,32,1280]{2,1,0:T(8,128)(2,1)S(1)}, bf16[4,32,1280]{2,1,0:T(8,128)(2,1)S(1)}, u32[]{:S(2)}, u32[]{:S(2)}) %collective-permute-start.19) | collective-permute-done | bytes 327712 | tf_op jit(solution)/shard_map/ppermute | solution.py:353
  106.4 10.3 %collective-permute-done.17 = bf16[4,32,1280]{2,1,0:T(8,128)(2,1)S(1)} collective-permute-done((bf16[4,32,1280]{2,1,0:T(8,128)(2,1)S(1)}, bf16[4,32,1280]{2,1,0:T(8,128)(2,1)S(1)}, u32[]{:S(2)}, u32[]{:S(2)}) %collective-permute-start.17) | collective-permute-done | bytes 327712 | tf_op jit(solution)/shard_map/ppermute | solution.py:353
  120.5 2.4 %collective-permute-start.33 = (f32[16,256]{1,0:T(8,128)S(1)}, f32[16,256]{1,0:T(8,128)S(1)}, u32[]{:S(2)}, u32[]{:S(2)}) collective-permute-start(f32[16,256]{1,0:T(8,128)S(1)} %get-tuple-element.64.refs_5_), channel_id=1, source_target_pairs={{0,24},{8,16},{16,8},{24,0},{1,25},{9,17},{17,9},{25,1},{2,26},{10... | collective-permute-start | bytes 49160 | tf_op jit(solution)/shard_map/ppermute | solution.py:353
  122.9 15.4 %collective-permute-done.30.refs_4_ = bf16[256,512]{1,0:T(8,128)(2,1)S(1)} collective-permute-done((bf16[256,512]{1,0:T(8,128)(2,1)S(1)}, bf16[256,512]{1,0:T(8,128)(2,1)S(1)}, u32[]{:S(2)}, u32[]{:S(2)}) %collective-permute-start.30) | collective-permute-done | bytes 262176 | tf_op jit(solution)/shard_map/ppermute | solution.py:353
  145.8 4.7 %shard_map.118 = (bf16[512,1024]{1,0:T(8,128)(2,1)S(1)}, bf16[512,1024]{1,0:T(8,128)(2,1)S(1)}) custom-call(bf16[256,1024]{1,0:T(8,128)(2,1)S(1)} %copy-done.19, bf16[256,1024]{1,0:T(8,128)(2,1)S(1)} %collective-permute-done.27.refs_1_, bf16[256,1024]{1,0:T(8,128)(2,1)S(1)} %collective-permute-done.28.refs_2_, bf16[256,512]{1,0:T(8,128)(2,1)S(1)} %copy-done.23, ...), custom_call_target="tpu_custom_call" | custom-call | flops 2147483648 | bytes 4194304 | tf_op jit(solution)/shard_map/pallas_call | solution.py:53
  150.6 1.5 add_convert_fusion.1
  152.2 3.8 %collective-permute-start.23 = (bf16[32,2560]{1,0:T(8,128)(2,1)S(1)}, bf16[32,2560]{1,0:T(8,128)(2,1)S(1)}, u32[]{:S(2)}, u32[]{:S(2)}) collective-permute-start(bf16[32,2560]{1,0:T(8,128)(2,1)S(1)} %get-tuple-element.72), channel_id=1, source_target_pairs={{0,6},{1,7},{2,0},{3,1},{4,2},{5,3},{6,4},{7,5},{8,14},{9,15},{10,... | collective-permute-start | bytes 491528 | tf_op jit(solution)/shard_map/ppermute | solution.py:350
  158.6 2.5 %collective-permute-done.21 = bf16[32,2560]{1,0:T(8,128)(2,1)S(1)} collective-permute-done((bf16[32,2560]{1,0:T(8,128)(2,1)S(1)}, bf16[32,2560]{1,0:T(8,128)(2,1)S(1)}, u32[]{:S(2)}, u32[]{:S(2)}) %collective-permute-start.21) | collective-permute-done | bytes 163872 | tf_op jit(solution)/shard_map/ppermute | solution.py:350
  162.3 2.6 %collective-permute-done.23 = bf16[32,2560]{1,0:T(8,128)(2,1)S(1)} collective-permute-done((bf16[32,2560]{1,0:T(8,128)(2,1)S(1)}, bf16[32,2560]{1,0:T(8,128)(2,1)S(1)}, u32[]{:S(2)}, u32[]{:S(2)}) %collective-permute-start.23) | collective-permute-done | bytes 163872 | tf_op jit(solution)/shard_map/ppermute | solution.py:350
  164.9 4.7 %collective-permute-done.22 = bf16[32,2560]{1,0:T(8,128)(2,1)S(1)} collective-permute-done((bf16[32,2560]{1,0:T(8,128)(2,1)S(1)}, bf16[32,2560]{1,0:T(8,128)(2,1)S(1)}, u32[]{:S(2)}, u32[]{:S(2)}) %collective-permute-start.22) | collective-permute-done | bytes 163872 | tf_op jit(solution)/shard_map/ppermute | solution.py:350
  169.7 2.5 %collective-permute-start.26 = (bf16[32,2560]{1,0:T(8,128)(2,1)S(1)}, bf16[32,2560]{1,0:T(8,128)(2,1)S(1)}, u32[]{:S(2)}, u32[]{:S(2)}) collective-permute-start(bf16[32,2560]{1,0:T(8,128)(2,1)S(1)} %fusion.2.refs_0_), channel_id=1, source_target_pairs={{0,24},{8,16},{16,8},{24,0},{1,25},{9,17},{17,9},{25,1},{2,26},{10... | collective-permute-start | bytes 491528 | tf_op jit(solution)/shard_map/ppermute | solution.py:353
  172.2 7.3 %collective-permute-done.37 = bf16[128,1024]{1,0:T(8,128)(2,1)S(1)} collective-permute-done((bf16[128,1024]{1,0:T(8,128)(2,1)S(1)}, bf16[128,1024]{1,0:T(8,128)(2,1)S(1)}, u32[]{:S(2)}, u32[]{:S(2)}) %collective-permute-start.37) | collective-permute-done | bytes 262176 | tf_op jit(solution)/shard_map/ppermute | solution.py:350
  179.5 12.2 %collective-permute-done.36 = bf16[128,1024]{1,0:T(8,128)(2,1)S(1)} collective-permute-done((bf16[128,1024]{1,0:T(8,128)(2,1)S(1)}, bf16[128,1024]{1,0:T(8,128)(2,1)S(1)}, u32[]{:S(2)}, u32[]{:S(2)}) %collective-permute-start.36) | collective-permute-done | bytes 262176 | tf_op jit(solution)/shard_map/ppermute | solution.py:350
  191.8 2.5 %collective-permute-start.40 = (bf16[128,1024]{1,0:T(8,128)(2,1)S(1)}, bf16[128,1024]{1,0:T(8,128)(2,1)S(1)}, u32[]{:S(2)}, u32[]{:S(2)}) collective-permute-start(bf16[128,1024]{1,0:T(8,128)(2,1)S(1)} %multiply_convert_fusion.refs_0_), channel_id=1, source_target_pairs={{0,24},{8,16},{16,8},{24,0},{1,25},{9,17},{17,9},{25,1},{2,26},{10... | collective-permute-start | bytes 786440 | tf_op jit(solution)/shard_map/ppermute | solution.py:353
  195.4 1.5 collective-permute-start.25
  198.4 11.4 %collective-permute-done.25.refs_2_ = bf16[32,2560]{1,0:T(8,128)(2,1)S(1)} collective-permute-done((bf16[32,2560]{1,0:T(8,128)(2,1)S(1)}, bf16[32,2560]{1,0:T(8,128)(2,1)S(1)}, u32[]{:S(2)}, u32[]{:S(2)}) %collective-permute-start.25) | collective-permute-done | bytes 163872 | tf_op jit(solution)/shard_map/ppermute | solution.py:353
  (159 shorter events, 50.1 us)
Async XLA Ops:
  2.4 12.4 %collective-permute-start.1 = (bf16[128,1024]{1,0:T(8,128)(2,1)S(1)}, bf16[128,1024]{1,0:T(8,128)(2,1)S(1)}, u32[]{:S(2)}, u32[]{:S(2)}) collective-permute-start(bf16[128,1024]{1,0:T(8,128)(2,1)S(1)} %get-tuple-element.45), channel_id=1, source_target_pairs={{0,2},{1,3},{2,4},{3,5},{4,6},{5,7},{6,0},{7,1},{8,10},{9,11},{10,... | collective-permute-start | bytes 786440 | tf_op jit(solution)/shard_map/ppermute | solution.py:350
  5.5 19.7 %collective-permute-start.2 = (bf16[128,1024]{1,0:T(8,128)(2,1)S(1)}, bf16[128,1024]{1,0:T(8,128)(2,1)S(1)}, u32[]{:S(2)}, u32[]{:S(2)}) collective-permute-start(bf16[128,1024]{1,0:T(8,128)(2,1)S(1)} %get-tuple-element.45), channel_id=1, source_target_pairs={{0,4},{1,5},{2,6},{3,7},{4,0},{5,1},{6,2},{7,3},{8,12},{9,13},{10,... | collective-permute-start | bytes 786440 | tf_op jit(solution)/shard_map/ppermute | solution.py:350
  8.1 17.9 %collective-permute-start.3 = (bf16[128,1024]{1,0:T(8,128)(2,1)S(1)}, bf16[128,1024]{1,0:T(8,128)(2,1)S(1)}, u32[]{:S(2)}, u32[]{:S(2)}) collective-permute-start(bf16[128,1024]{1,0:T(8,128)(2,1)S(1)} %get-tuple-element.45), channel_id=1, source_target_pairs={{0,6},{1,7},{2,0},{3,1},{4,2},{5,3},{6,4},{7,5},{8,14},{9,15},{10,... | collective-permute-start | bytes 786440 | tf_op jit(solution)/shard_map/ppermute | solution.py:350
  26.6 27.0 %collective-permute-start.5 = (bf16[384,1024]{1,0:T(8,128)(2,1)}, bf16[384,1024]{1,0:T(8,128)(2,1)}, u32[]{:S(2)}, u32[]{:S(2)}) collective-permute-start(bf16[384,1024]{1,0:T(8,128)(2,1)} %constant_dynamic-update-slice_fusion.refs_5_.refs_10_), channel_id=1, source_target_pairs={{0,16},{8,24},{16,0},{24,8},{1,17},{9,25},{17,1},{25,9},{2,18},{10... | collective-permute-start | bytes 2359304 | tf_op jit(solution)/shard_map/ppermute | solution.py:353
  28.2 27.1 %collective-permute-start.4 = (bf16[384,1024]{1,0:T(8,128)(2,1)}, bf16[384,1024]{1,0:T(8,128)(2,1)}, u32[]{:S(2)}, u32[]{:S(2)}) collective-permute-start(bf16[384,1024]{1,0:T(8,128)(2,1)} %constant_dynamic-update-slice_fusion.refs_5_.refs_10_), channel_id=1, source_target_pairs={{0,8},{8,0},{16,24},{24,16},{1,9},{9,1},{17,25},{25,17},{2,10},{10... | collective-permute-start | bytes 2359304 | tf_op jit(solution)/shard_map/ppermute | solution.py:353
  29.7 27.2 %collective-permute-start.9 = (bf16[384,1024]{1,0:T(8,128)(2,1)}, bf16[384,1024]{1,0:T(8,128)(2,1)}, u32[]{:S(2)}, u32[]{:S(2)}) collective-permute-start(bf16[384,1024]{1,0:T(8,128)(2,1)} %constant_dynamic-update-slice_fusion.refs_5_.refs_10_), channel_id=1, source_target_pairs={{0,1},{1,0},{2,3},{3,2},{4,5},{5,4},{6,7},{7,6},{8,9},{9,8},{10,11... | collective-permute-start | bytes 2359304 | tf_op jit(solution)/shard_map/ppermute | solution.py:356
  44.5 29.6 %all-to-all-start = ((bf16[8,48,1024]{2,1,0:T(8,128)(2,1)}), bf16[8,48,1024]{2,1,0:T(8,128)(2,1)S(1)}, u32[]{:S(2)}, u32[]{:S(2)}) async-start(bf16[8,48,1024]{2,1,0:T(8,128)(2,1)} %bitcast.13), calls=%async_computation | async-start | bytes 1572864 | tf_op jit(solution)/shard_map/all_to_all | solution.py:389
  53.1 22.6 %collective-permute-start.8 = (bf16[512,1024]{1,0:T(8,128)(2,1)}, bf16[512,1024]{1,0:T(8,128)(2,1)}, u32[]{:S(2)}, u32[]{:S(2)}) collective-permute-start(bf16[512,1024]{1,0:T(8,128)(2,1)} %copy-done.13), channel_id=1, source_target_pairs={{0,1},{1,0},{2,3},{3,2},{4,5},{5,4},{6,7},{7,6},{8,9},{9,8},{10,11... | collective-permute-start | bytes 3145736 | tf_op jit(solution)/shard_map/ppermute | solution.py:356
  54.7 11.2 %collective-permute-start.7 = (bf16[384,512]{1,0:T(8,128)(2,1)S(1)}, bf16[384,512]{1,0:T(8,128)(2,1)}, u32[]{:S(2)}, u32[]{:S(2)}) collective-permute-start(bf16[384,512]{1,0:T(8,128)(2,1)S(1)} %slice.63), channel_id=1, source_target_pairs={{0,8},{8,0},{16,24},{24,16},{1,9},{9,1},{17,25},{25,17},{2,10},{10... | collective-permute-start | bytes 1179656 | tf_op jit(solution)/shard_map/ppermute | solution.py:353
  56.3 10.9 %collective-permute-start.6 = (bf16[384,512]{1,0:T(8,128)(2,1)S(1)}, bf16[384,512]{1,0:T(8,128)(2,1)}, u32[]{:S(2)}, u32[]{:S(2)}) collective-permute-start(bf16[384,512]{1,0:T(8,128)(2,1)S(1)} %slice.62), channel_id=1, source_target_pairs={{0,16},{8,24},{16,0},{24,8},{1,17},{9,25},{17,1},{25,9},{2,18},{10... | collective-permute-start | bytes 1179656 | tf_op jit(solution)/shard_map/ppermute | solution.py:353
  56.9 18.9 %collective-permute-start.11 = (bf16[384,1024]{1,0:T(8,128)(2,1)}, bf16[384,1024]{1,0:T(8,128)(2,1)}, u32[]{:S(2)}, u32[]{:S(2)}) collective-permute-start(bf16[384,1024]{1,0:T(8,128)(2,1)} %collective-permute-done.5.refs_7_), channel_id=1, source_target_pairs={{0,1},{1,0},{2,3},{3,2},{4,5},{5,4},{6,7},{7,6},{8,9},{9,8},{10,11... | collective-permute-start | bytes 2359304 | tf_op jit(solution)/shard_map/ppermute | solution.py:356
  56.9 18.9 %collective-permute-start.10 = (bf16[384,1024]{1,0:T(8,128)(2,1)}, bf16[384,1024]{1,0:T(8,128)(2,1)}, u32[]{:S(2)}, u32[]{:S(2)}) collective-permute-start(bf16[384,1024]{1,0:T(8,128)(2,1)} %collective-permute-done.4.refs_6_), channel_id=1, source_target_pairs={{0,1},{1,0},{2,3},{3,2},{4,5},{5,4},{6,7},{7,6},{8,9},{9,8},{10,11... | collective-permute-start | bytes 2359304 | tf_op jit(solution)/shard_map/ppermute | solution.py:356
  94.3 10.6 %collective-permute-start.19 = (bf16[4,32,1280]{2,1,0:T(8,128)(2,1)S(1)}, bf16[4,32,1280]{2,1,0:T(8,128)(2,1)S(1)}, u32[]{:S(2)}, u32[]{:S(2)}) collective-permute-start(bf16[4,32,1280]{2,1,0:T(8,128)(2,1)S(1)} %get-tuple-element.60), channel_id=1, source_target_pairs={{0,8},{8,0},{16,24},{24,16},{1,9},{9,1},{17,25},{25,17},{2,10},{10... | collective-permute-start | bytes 983048 | tf_op jit(solution)/shard_map/ppermute | solution.py:353
  94.9 24.3 %collective-permute-start.28 = (bf16[256,1024]{1,0:T(8,128)(2,1)S(1)}, bf16[256,1024]{1,0:T(8,128)(2,1)S(1)}, u32[]{:S(2)}, u32[]{:S(2)}) collective-permute-start(bf16[256,1024]{1,0:T(8,128)(2,1)S(1)} %copy-done.18), channel_id=1, source_target_pairs={{0,16},{8,24},{16,0},{24,8},{1,17},{9,25},{17,1},{25,9},{2,18},{10... | collective-permute-start | bytes 1572872 | tf_op jit(solution)/shard_map/ppermute | solution.py:353
  95.4 24.4 %collective-permute-start.27 = (bf16[256,1024]{1,0:T(8,128)(2,1)S(1)}, bf16[256,1024]{1,0:T(8,128)(2,1)S(1)}, u32[]{:S(2)}, u32[]{:S(2)}) collective-permute-start(bf16[256,1024]{1,0:T(8,128)(2,1)S(1)} %copy-done.18), channel_id=1, source_target_pairs={{0,8},{8,0},{16,24},{24,16},{1,9},{9,1},{17,25},{25,17},{2,10},{10... | collective-permute-start | bytes 1572872 | tf_op jit(solution)/shard_map/ppermute | solution.py:353
  97.0 19.8 %collective-permute-start.17 = (bf16[4,32,1280]{2,1,0:T(8,128)(2,1)S(1)}, bf16[4,32,1280]{2,1,0:T(8,128)(2,1)S(1)}, u32[]{:S(2)}, u32[]{:S(2)}) collective-permute-start(bf16[4,32,1280]{2,1,0:T(8,128)(2,1)S(1)} %get-tuple-element.58), channel_id=1, source_target_pairs={{0,16},{8,24},{16,0},{24,8},{1,17},{9,25},{17,1},{25,9},{2,18},{10... | collective-permute-start | bytes 983048 | tf_op jit(solution)/shard_map/ppermute | solution.py:353
  105.9 44.7 %collective-permute-start.20 = (bf16[4,32,2560]{2,1,0:T(8,128)(2,1)}, bf16[4,32,2560]{2,1,0:T(8,128)(2,1)}, u32[]{:S(2)}, u32[]{:S(2)}) collective-permute-start(bf16[4,32,2560]{2,1,0:T(8,128)(2,1)} %pad_maximum_fusion.1), channel_id=1, source_target_pairs={{0,16},{8,24},{16,0},{24,8},{1,17},{9,25},{17,1},{25,9},{2,18},{10... | collective-permute-start | bytes 1966088 | tf_op jit(solution)/shard_map/ppermute | solution.py:353
  117.8 32.8 %collective-permute-start.18 = (bf16[4,32,2560]{2,1,0:T(8,128)(2,1)}, bf16[4,32,2560]{2,1,0:T(8,128)(2,1)}, u32[]{:S(2)}, u32[]{:S(2)}) collective-permute-start(bf16[4,32,2560]{2,1,0:T(8,128)(2,1)} %pad_maximum_fusion), channel_id=1, source_target_pairs={{0,8},{8,0},{16,24},{24,16},{1,9},{9,1},{17,25},{25,17},{2,10},{10... | collective-permute-start | bytes 1966088 | tf_op jit(solution)/shard_map/ppermute | solution.py:353
  119.3 19.0 %collective-permute-start.30 = (bf16[256,512]{1,0:T(8,128)(2,1)S(1)}, bf16[256,512]{1,0:T(8,128)(2,1)S(1)}, u32[]{:S(2)}, u32[]{:S(2)}) collective-permute-start(bf16[256,512]{1,0:T(8,128)(2,1)S(1)} %slice.65), channel_id=1, source_target_pairs={{0,8},{8,0},{16,24},{24,16},{1,9},{9,1},{17,25},{25,17},{2,10},{10... | collective-permute-start | bytes 786440 | tf_op jit(solution)/shard_map/ppermute | solution.py:353
  119.9 19.6 %collective-permute-start.29 = (bf16[256,512]{1,0:T(8,128)(2,1)S(1)}, bf16[256,512]{1,0:T(8,128)(2,1)S(1)}, u32[]{:S(2)}, u32[]{:S(2)}) collective-permute-start(bf16[256,512]{1,0:T(8,128)(2,1)S(1)} %slice.64), channel_id=1, source_target_pairs={{0,16},{8,24},{16,0},{24,8},{1,17},{9,25},{17,1},{25,9},{2,18},{10... | collective-permute-start | bytes 786440 | tf_op jit(solution)/shard_map/ppermute | solution.py:353
  120.5 21.3 %collective-permute-start.33 = (f32[16,256]{1,0:T(8,128)S(1)}, f32[16,256]{1,0:T(8,128)S(1)}, u32[]{:S(2)}, u32[]{:S(2)}) collective-permute-start(f32[16,256]{1,0:T(8,128)S(1)} %get-tuple-element.64.refs_5_), channel_id=1, source_target_pairs={{0,24},{8,16},{16,8},{24,0},{1,25},{9,17},{17,9},{25,1},{2,26},{10... | collective-permute-start | bytes 49160 | tf_op jit(solution)/shard_map/ppermute | solution.py:353
  152.2 12.7 %collective-permute-start.23 = (bf16[32,2560]{1,0:T(8,128)(2,1)S(1)}, bf16[32,2560]{1,0:T(8,128)(2,1)S(1)}, u32[]{:S(2)}, u32[]{:S(2)}) collective-permute-start(bf16[32,2560]{1,0:T(8,128)(2,1)S(1)} %get-tuple-element.72), channel_id=1, source_target_pairs={{0,6},{1,7},{2,0},{3,1},{4,2},{5,3},{6,4},{7,5},{8,14},{9,15},{10,... | collective-permute-start | bytes 491528 | tf_op jit(solution)/shard_map/ppermute | solution.py:350
  156.1 13.5 %collective-permute-start.22 = (bf16[32,2560]{1,0:T(8,128)(2,1)S(1)}, bf16[32,2560]{1,0:T(8,128)(2,1)S(1)}, u32[]{:S(2)}, u32[]{:S(2)}) collective-permute-start(bf16[32,2560]{1,0:T(8,128)(2,1)S(1)} %get-tuple-element.73), channel_id=1, source_target_pairs={{0,4},{1,5},{2,6},{3,7},{4,0},{5,1},{6,2},{7,3},{8,12},{9,13},{10,... | collective-permute-start | bytes 491528 | tf_op jit(solution)/shard_map/ppermute | solution.py:350
  156.5 15.7 %collective-permute-start.35 = (bf16[128,1024]{1,0:T(8,128)(2,1)S(1)}, bf16[128,1024]{1,0:T(8,128)(2,1)S(1)}, u32[]{:S(2)}, u32[]{:S(2)}) collective-permute-start(bf16[128,1024]{1,0:T(8,128)(2,1)S(1)} %get-tuple-element.68), channel_id=1, source_target_pairs={{0,6},{1,7},{2,0},{3,1},{4,2},{5,3},{6,4},{7,5},{8,14},{9,15},{10,... | collective-permute-start | bytes 786440 | tf_op jit(solution)/shard_map/ppermute | solution.py:350
  157.2 22.3 %collective-permute-start.37 = (bf16[128,1024]{1,0:T(8,128)(2,1)S(1)}, bf16[128,1024]{1,0:T(8,128)(2,1)S(1)}, u32[]{:S(2)}, u32[]{:S(2)}) collective-permute-start(bf16[128,1024]{1,0:T(8,128)(2,1)S(1)} %get-tuple-element.69), channel_id=1, source_target_pairs={{0,2},{1,3},{2,4},{3,5},{4,6},{5,7},{6,0},{7,1},{8,10},{9,11},{10,... | collective-permute-start | bytes 786440 | tf_op jit(solution)/shard_map/ppermute | solution.py:350
  161.1 30.6 %collective-permute-start.36 = (bf16[128,1024]{1,0:T(8,128)(2,1)S(1)}, bf16[128,1024]{1,0:T(8,128)(2,1)S(1)}, u32[]{:S(2)}, u32[]{:S(2)}) collective-permute-start(bf16[128,1024]{1,0:T(8,128)(2,1)S(1)} %get-tuple-element.70), channel_id=1, source_target_pairs={{0,4},{1,5},{2,6},{3,7},{4,0},{5,1},{6,2},{7,3},{8,12},{9,13},{10,... | collective-permute-start | bytes 786440 | tf_op jit(solution)/shard_map/ppermute | solution.py:350
  169.7 27.2 %collective-permute-start.26 = (bf16[32,2560]{1,0:T(8,128)(2,1)S(1)}, bf16[32,2560]{1,0:T(8,128)(2,1)S(1)}, u32[]{:S(2)}, u32[]{:S(2)}) collective-permute-start(bf16[32,2560]{1,0:T(8,128)(2,1)S(1)} %fusion.2.refs_0_), channel_id=1, source_target_pairs={{0,24},{8,16},{16,8},{24,0},{1,25},{9,17},{17,9},{25,1},{2,26},{10... | collective-permute-start | bytes 491528 | tf_op jit(solution)/shard_map/ppermute | solution.py:353
  191.8 19.3 %collective-permute-start.40 = (bf16[128,1024]{1,0:T(8,128)(2,1)S(1)}, bf16[128,1024]{1,0:T(8,128)(2,1)S(1)}, u32[]{:S(2)}, u32[]{:S(2)}) collective-permute-start(bf16[128,1024]{1,0:T(8,128)(2,1)S(1)} %multiply_convert_fusion.refs_0_), channel_id=1, source_target_pairs={{0,24},{8,16},{16,8},{24,0},{1,25},{9,17},{17,9},{25,1},{2,26},{10... | collective-permute-start | bytes 786440 | tf_op jit(solution)/shard_map/ppermute | solution.py:353
  194.3 16.7 %collective-permute-start.39 = (bf16[128,1024]{1,0:T(8,128)(2,1)S(1)}, bf16[128,1024]{1,0:T(8,128)(2,1)S(1)}, u32[]{:S(2)}, u32[]{:S(2)}) collective-permute-start(bf16[128,1024]{1,0:T(8,128)(2,1)S(1)} %multiply_convert_fusion.refs_0_), channel_id=1, source_target_pairs={{0,16},{8,24},{16,0},{24,8},{1,17},{9,25},{17,1},{25,9},{2,18},{10... | collective-permute-start | bytes 786440 | tf_op jit(solution)/shard_map/ppermute | solution.py:353
  194.8 16.2 %collective-permute-start.38 = (bf16[128,1024]{1,0:T(8,128)(2,1)S(1)}, bf16[128,1024]{1,0:T(8,128)(2,1)S(1)}, u32[]{:S(2)}, u32[]{:S(2)}) collective-permute-start(bf16[128,1024]{1,0:T(8,128)(2,1)S(1)} %multiply_convert_fusion.refs_0_), channel_id=1, source_target_pairs={{0,8},{8,0},{16,24},{24,16},{1,9},{9,1},{17,25},{25,17},{2,10},{10... | collective-permute-start | bytes 786440 | tf_op jit(solution)/shard_map/ppermute | solution.py:353
  195.4 14.4 %collective-permute-start.25 = (bf16[32,2560]{1,0:T(8,128)(2,1)S(1)}, bf16[32,2560]{1,0:T(8,128)(2,1)S(1)}, u32[]{:S(2)}, u32[]{:S(2)}) collective-permute-start(bf16[32,2560]{1,0:T(8,128)(2,1)S(1)} %fusion.2.refs_0_), channel_id=1, source_target_pairs={{0,16},{8,24},{16,0},{24,8},{1,17},{9,25},{17,1},{25,9},{2,18},{10... | collective-permute-start | bytes 491528 | tf_op jit(solution)/shard_map/ppermute | solution.py:353
  196.9 13.0 %collective-permute-start.24 = (bf16[32,2560]{1,0:T(8,128)(2,1)S(1)}, bf16[32,2560]{1,0:T(8,128)(2,1)S(1)}, u32[]{:S(2)}, u32[]{:S(2)}) collective-permute-start(bf16[32,2560]{1,0:T(8,128)(2,1)S(1)} %fusion.2.refs_0_), channel_id=1, source_target_pairs={{0,8},{8,0},{16,24},{24,16},{1,9},{9,1},{17,25},{25,17},{2,10},{10... | collective-permute-start | bytes 491528 | tf_op jit(solution)/shard_map/ppermute | solution.py:353
  (48 other events, 403.1 us)

commit v4 on v3

--- a/solution.py
+++ b/solution.py
@@ -49,7 +49,7 @@
     return jnp.where(first, even, odd), jnp.where(first, odd, even)
 
 
-def call(kernel, out, specs, args, scratch=(), flops=0, nbytes=0, room=32):
+def call(kernel, out, specs, args, scratch=(), flops=0, nbytes=0, room=14):
     return pl.pallas_call(
         kernel,
         out_shape=[jax.ShapeDtypeStruct(s, t) for s, t in out],
@@ -367,12 +367,10 @@
     own, quarter, quarter_inv = call(
         lambda *refs: normalise_kernel(share, *refs),
         [((vocab_dev, width), b16), ((share, width), b16), ((share, 1), f32)],
-        [VMEM], [item_table], flops=8 * vocab_dev * width, nbytes=5 * vocab_dev * width, room=24,
-    )
-    others = jnp.concatenate([to_chip(quarter, d) for d in range(1, chips)], 0)
-    pieces = [(0, -1, 0, width, own)] + [(0,) + p for p in gather_groups(others)]
-    pieces = pieces + [(1,) + p[1:4] + (to_core(p[4]),) for p in pieces]
-    far_own, far_others = [p[4] for p in pieces if p[0] == 1 and p[1] <= 0]
+        [VMEM], [item_table], flops=8 * vocab_dev * width, nbytes=5 * vocab_dev * width, room=8,
+    )
+    got = [to_chip(quarter, d) for d in range(1, chips)]
+    far_own = to_core(own)
 
     outs = [
         ((tok, width // 2), b16), ((tok, width // 2), b16), ((tok, 4 * hidden), b16), ((tok, 4 * hidden), b16),
@@ -383,27 +381,50 @@
     (keep, give, proj, slope, attn, attn_slope, normed, inverse, gated, unit, unit_b, inv_len, outgoing) = call(
         lambda *refs: forward_kernel(owners, slot, *refs), outs, [SMEM, SMEM, VMEM, VMEM, VMEM],
         [lengths, destinations, events, in_weight, out_weight],
-        flops=2 * tok * width * 6 * hidden, nbytes=24 * tok * width + 10 * width * hidden,
-    )
+        flops=2 * tok * width * 6 * hidden, nbytes=24 * tok * width + 10 * width * hidden, room=28,
+    )
+
+    got, far_own, unit_b = lax.optimization_barrier((got, far_own, unit_b))
+    others = jnp.concatenate(got, 0)
+    pieces = [(0, -1, 0, width, own)] + [(0,) + p for p in gather_groups(others)]
+    pieces = pieces + [(1, -1, 0, width, far_own)] + [(1,) + p[1:4] + (to_core(p[4]),) for p in pieces[1:]]
+    far_others = [p[4] for p in pieces if p[0] == 1 and p[1] == 0][0]
+    sent_unit, _ = lax.optimization_barrier((unit_b, [p[4] for p in pieces if p[0] == 0]))
+    unit_sent = gather_groups(sent_unit)
+    outgoing, others = lax.optimization_barrier((outgoing, others))
 
     arrived = lax.all_to_all(
         outgoing.reshape(owners, slot, width), "seq", 0, 0, tiled=True
     ).reshape(owners * slot, width)
     layer_out, = call(
         relay_kernel, [((tok, width), b16)], [VMEM], [arrived],
-        flops=3 * tok * tok * width, nbytes=6 * tok * width, room=16,
+        flops=3 * tok * tok * width, nbytes=6 * tok * width, room=8,
     )
 
     candidates = jnp.concatenate([history[:, None], negatives], 1)
     vocab = vocab_dev * owners
     layer_out, score_unit = lax.optimization_barrier((layer_out, unit))
+    units = [p[3] for p in unit_sent]
     tags, up, up_keep, up_give = call(
         lambda *refs: score_kernel(groups, owners, share, [p[:4] for p in pieces], *refs),
         [((2 * owners, tok), f32), ((tok, width), b16), ((tok, width // 2), b16), ((tok, width // 2), b16)],
         [VMEM] * 4 + [ANY] * len(pieces), [candidates, unit_b, score_unit, inv_len] + [p[4] for p in pieces],
         [pltpu.VMEM((vocab, width), b16), pltpu.VMEM((tok, vocab), b16), pltpu.SemaphoreType.DMA((len(pieces),))],
-        flops=4 * tok * width * vocab, nbytes=2 * vocab * width + 12 * tok * width, room=24 + vocab // 256,
-    )
+        flops=4 * tok * width * vocab, nbytes=2 * vocab * width + 12 * tok * width, room=24 if groups == 4 else 58,
+    )
+
+    all_tags = [to_group(tags, k) if k else tags for k in range(groups)]
+    mine, other = call(
+        lambda *refs: item_kernel(groups, owners, share, [p[:3] for p in unit_sent], *refs),
+        [((chips * share, width), b16)] * 2, [ANY] * len(units) + [VMEM] * groups + [ANY] * 4,
+        units + all_tags + [own, others, far_own, far_others],
+        [pltpu.VMEM((groups * tok, width), b16), pltpu.VMEM((2 * chips * share, width), b16),
+         pltpu.SemaphoreType.DMA((len(units) + 4,))],
+        flops=4 * groups * tok * width * chips * share, nbytes=4 * tok * groups * width, room=16 if groups == 4 else 48,
+    )
+    far_mine = to_core(other)
+
+    up, _ = lax.optimization_barrier((up, [p[3] for p in unit_sent[1:3]]))
 
     grad, = call(
         backward_kernel, [((tok, 4 * hidden), b16)], [VMEM] * 8,
@@ -412,6 +433,7 @@
     )
 
     far = [to_core(x) for x in (give, up_give, grad, gated)]
+    far, mine = lax.optimization_barrier((far, mine))
     half = 5 * hidden // 2
     if groups == 4:
         block = (chips, fine, 5 * hidden)
@@ -421,9 +443,8 @@
             [(block, b16)] * 3 + [(split, b16)] * 2, [VMEM] * 8,
             [keep, far[0], up_keep, far[1], grad, far[2], gated, far[3]],
             [pltpu.VMEM((width // 2, 5 * hidden), b16)],
-            flops=2 * tok * width * 5 * hidden, nbytes=20 * tok * width, room=24,
+            flops=2 * tok * width * 5 * hidden, nbytes=20 * tok * width, room=14,
         )
-        after = parts[0]
         left, right = to_group(parts[3], 1).astype(f32), to_group(parts[4], 2).astype(f32)
         one, two = parts[1].astype(f32), parts[2].astype(f32)
         one = jnp.concatenate([one[..., :half], one[..., half:] + right], 2).astype(b16)
@@ -437,24 +458,12 @@
         out_part = dot(both(up_keep, far[1]), both(gated, far[3]), TN)
         weight = jnp.concatenate([in_part, out_part], 1).astype(b16)
         weight = weight.reshape(chips, groups, fine, 5 * hidden)
-        after = weight
         sums = lax.dynamic_index_in_dim(weight, grp, 1, False).astype(f32)
         for k in range(1, groups):
             sums += to_group(lax.dynamic_index_in_dim(weight, grp ^ k, 1, False), k).astype(f32)
     sums = sums.astype(b16)
 
-    units = gather_groups(unit_b)
-    all_tags = [to_group(tags, k) if k else tags for k in range(groups)]
-    first_unit, after = lax.optimization_barrier((units[0][3], after))
-    mine, other = call(
-        lambda *refs: item_kernel(groups, owners, share, [p[:3] for p in units], *refs),
-        [((chips * share, width), b16)] * 2, [ANY] * len(units) + [VMEM] * groups + [ANY] * 4,
-        [first_unit] + [p[3] for p in units[1:]] + all_tags + [own, others, far_own, far_others],
-        [pltpu.VMEM((groups * tok, width), b16), pltpu.VMEM((2 * chips * share, width), b16),
-         pltpu.SemaphoreType.DMA((len(units) + 4,))],
-        flops=4 * groups * tok * width * chips * share, nbytes=4 * tok * groups * width, room=32 if groups == 4 else 48,
-    )
-    summed = (mine.astype(f32) + to_core(other).astype(f32)).astype(b16).reshape(chips, share, width)
+    summed = (mine.astype(f32) + far_mine.astype(f32)).astype(b16).reshape(chips, share, width)
     total = summed[0].astype(f32)
     for d in range(1, chips):
         total += to_chip(summed[d], -d).astype(f32)
@@ -462,7 +471,7 @@
     table_grad, = call(
         lambda *refs: assemble_kernel(groups, [width], *refs), [((vocab_dev, width), f32)], [VMEM] * groups,
         [to_group(total, k) if k else total for k in range(groups)],
-        flops=vocab_dev * width, nbytes=6 * vocab_dev * width, room=16,
+        flops=vocab_dev * width, nbytes=6 * vocab_dev * width, room=8,
     )
 
     line = lax.dynamic_index_in_dim(sums, chip, 0, False).astype(f32)
@@ -474,7 +483,7 @@
         in_grad, out_grad = call(
             lambda *refs: assemble_kernel(groups, [4 * hidden, hidden], *refs),
             [((rows, 4 * hidden), f32), ((rows, hidden), f32)], [VMEM] * groups, lines,
-            flops=rows * hidden, nbytes=30 * rows * hidden, room=16,
+            flops=rows * hidden, nbytes=30 * rows * hidden, room=8,
         )
     else:
         shard = jnp.zeros((rows, 5 * hidden), f32)

time: 213 us -> 184 us (0.86); the launches traced: 213 us -> 181 us
  waiting for transfers between devices: 109 us -> 59.8 us
  starting transfers between devices: 50 us -> 60.8 us
  local copies, waits for them, and re-layouts: 22.4 us -> 26.7 us
    ppermute x9, waiting for transfers between devices: 44.2 us -> 13.7 us  [to_chip(): return lax.ppermute(x, 'seq', pairs)]
    ppermute x21, waiting for transfers between devices: 55.6 us -> 46.1 us  [to_group(): return lax.ppermute(x, 'grp', [(a, a ^ k) for a in range(groups)])]
    ppermute x9, starting transfers between devices: 14.2 us -> 22.9 us  [to_chip(): return lax.ppermute(x, 'seq', pairs)]
    all_to_all x1, waiting for transfers between devices: 6.07 us -> 0.01 us  [body(): lax.all_to_all(outgoing.reshape(owners, slot, width), 'seq', 0, 0, tiled=...]
    ppermute x11, waiting for transfers between devices: 2.78 us -> 0.03 us  [to_core(): return lax.ppermute(x, 'seq', [(a, a ^ 1) for a in range(owners)])]
    ppermute x21, starting transfers between devices: 25 us -> 27.5 us  [to_group(): return lax.ppermute(x, 'grp', [(a, a ^ k) for a in range(groups)])]
    unnamed x78 -> x72, local copies, waits for them, and re-layouts: 18.7 us -> 21.1 us
  transfers between devices with their start and end apart: 42 -> 42, of which waited for: 20 -> 13; matrix products, arithmetic and copies ran while one was open for 4% -> 6% of each run, Pallas kernels for 6% -> 13%
where the time goes in v4:
time: 184 us; the launch traced here: 181 us
  starting transfers between devices  60.8 us (33%)
  waiting for transfers between devices  59.8 us (32%)
  Pallas kernels  27.4 us (15%)
  local copies, waits for them, and re-layouts  26.7 us (15%)
  other arithmetic  5.21 us (3%)
    ppermute x21, waiting for transfers between devices, to_group(): return lax.ppermute(x, 'grp', [(a, a ^ k) for a in range(groups)])  46.1 us
    ppermute x21, starting transfers between devices, to_group(): return lax.ppermute(x, 'grp', [(a, a ^ k) for a in range(groups)])  27.5 us
    pallas_call x9, Pallas kernels, call(): pl.pallas_call(kernel, out_shape=[jax.ShapeDtypeStruct(s, t) for s, t in...  27.4 us
    ppermute x9, starting transfers between devices, to_chip(): return lax.ppermute(x, 'seq', pairs)  22.9 us
    unnamed x72, local copies, waits for them, and re-layouts  21.1 us
    ppermute x9, waiting for transfers between devices, to_chip(): return lax.ppermute(x, 'seq', pairs)  13.7 us
    all_to_all x1, starting transfers between devices, body(): lax.all_to_all(outgoing.reshape(owners, slot, width), 'seq', 0, 0, tiled=...  8.56 us
    slice x4, local copies, waits for them, and re-layouts, gather_groups(): left, right = (to_group(one[:, :half], 2), to_group(two[:, half:], 1))  3.98 us
  transfers between devices with their start and end apart: 42, of which 13 were waited for; matrix products, arithmetic and copies ran while one was open for 6% of the time, Pallas kernels for 13%

profile of v4, /device:TPU:0, one launch (start us, length us, event | category | flops | bytes accessed | tf_op | source)
XLA Modules:
  0.0 181.0 jit_solution(16652289380310956862)
XLA Ops:
  3.3 2.6 %collective-permute-start = (bf16[128,1024]{1,0:T(8,128)(2,1)S(1)}, bf16[128,1024]{1,0:T(8,128)(2,1)S(1)}, u32[]{:S(2)}, u32[]{:S(2)}) collective-permute-start(bf16[128,1024]{1,0:T(8,128)(2,1)S(1)} %get-tuple-element.50), channel_id=1, source_target_pairs={{0,2},{1,3},{2,4},{3,5},{4,6},{5,7},{6,0},{7,1},{8,10},{9,11},{10,... | collective-permute-start | bytes 786440 | tf_op jit(solution)/shard_map/ppermute | solution.py:350
  5.9 2.6 %collective-permute-start.1 = (bf16[128,1024]{1,0:T(8,128)(2,1)S(1)}, bf16[128,1024]{1,0:T(8,128)(2,1)S(1)}, u32[]{:S(2)}, u32[]{:S(2)}) collective-permute-start(bf16[128,1024]{1,0:T(8,128)(2,1)S(1)} %get-tuple-element.50), channel_id=1, source_target_pairs={{0,4},{1,5},{2,6},{3,7},{4,0},{5,1},{6,2},{7,3},{8,12},{9,13},{10,... | collective-permute-start | bytes 786440 | tf_op jit(solution)/shard_map/ppermute | solution.py:350
  11.1 2.2 %copy-done.11 = bf16[1024,2048]{1,0:T(8,128)(2,1)S(1)} copy-done((bf16[1024,2048]{1,0:T(8,128)(2,1)S(1)}, bf16[1024,2048]{1,0:T(8,128)(2,1)}, u32[]{:S(2)}) %copy-start.11) | copy-done | bytes 4194328
  15.6 5.2 %shard_map.111 = (bf16[256,512]{1,0:T(8,128)(2,1)S(1)}, bf16[256,512]{1,0:T(8,128)(2,1)S(1)}, bf16[256,2048]{1,0:T(8,128)(2,1)S(1)}, bf16[256,2048]{1,0:T(8,128)...) custom-call(s32[1,8]{1,0:T(1,128)S(1)} %copy-done.25, ...), custom_call_target="tpu_custom_call" | custom-call | flops 1610612736 | bytes 11534336 | tf_op jit(solution)/shard_map/pallas_call | solution.py:53
  29.4 1.5 collective-permute-start.5
  30.9 1.5 collective-permute-start.6
  32.4 8.6 %all-to-all-start = ((bf16[8,48,1024]{2,1,0:T(8,128)(2,1)}), bf16[8,48,1024]{2,1,0:T(8,128)(2,1)S(1)}, u32[]{:S(2)}, u32[]{:S(2)}) async-start(bf16[8,48,1024]{2,1,0:T(8,128)(2,1)} %bitcast.13), calls=%async_computation | async-start | bytes 1572864 | tf_op jit(solution)/shard_map/all_to_all | solution.py:396
  41.5 7.7 %collective-permute-done.5.refs_6_ = bf16[384,1024]{1,0:T(8,128)(2,1)} collective-permute-done((bf16[384,1024]{1,0:T(8,128)(2,1)}, bf16[384,1024]{1,0:T(8,128)(2,1)}, u32[]{:S(2)}, u32[]{:S(2)}) %collective-permute-start.5) | collective-permute-done | bytes 786464 | tf_op jit(solution)/shard_map/ppermute | solution.py:353
  50.2 1.6 collective-permute-start.7
  53.1 1.5 collective-permute-start.8
  54.6 7.3 %collective-permute-done.7.refs_8_ = bf16[384,512]{1,0:T(8,128)(2,1)} collective-permute-done((bf16[384,512]{1,0:T(8,128)(2,1)S(1)}, bf16[384,512]{1,0:T(8,128)(2,1)}, u32[]{:S(2)}, u32[]{:S(2)}) %collective-permute-start.7) | collective-permute-done | bytes 393248 | tf_op jit(solution)/shard_map/ppermute | solution.py:353
  61.9 2.6 %collective-permute-done.8.refs_9_ = bf16[384,512]{1,0:T(8,128)(2,1)} collective-permute-done((bf16[384,512]{1,0:T(8,128)(2,1)S(1)}, bf16[384,512]{1,0:T(8,128)(2,1)}, u32[]{:S(2)}, u32[]{:S(2)}) %collective-permute-start.8) | collective-permute-done | bytes 393248 | tf_op jit(solution)/shard_map/ppermute | solution.py:353
  69.1 1.6 shard_map.113
  75.5 10.0 %shard_map.114 = (f32[16,256]{1,0:T(8,128)S(1)}, bf16[256,1024]{1,0:T(8,128)(2,1)S(1)}, bf16[256,512]{1,0:T(8,128)(2,1)S(1)}, bf16[256,512]{1,0:T(8,128)(2,1)S(1)}) custom-call(s32[256,4]{1,0:T(8,128)S(1)} %copy-done.8, bf16[256,1024]{1,0:T(8,128)(2,1)} %get-tuple-element.67.refs_1_.refs_0_, f32[256,1024]{1,0:T(8,128)S(1)} %copy-done.28, ...), custom_call_target="tpu_custom_call" | custom-call | flops 4294967296 | bytes 11534336 | tf_op jit(solution)/shard_map/pallas_call | solution.py:53
  85.5 1.6 shard_map.115.refs_4_
  88.1 1.6 collective-permute-start.19
  93.3 6.2 %collective-permute-done.21.refs_6_ = f32[16,256]{1,0:T(8,128)S(1)} collective-permute-done((f32[16,256]{1,0:T(8,128)S(1)}, f32[16,256]{1,0:T(8,128)S(1)}, u32[]{:S(2)}, u32[]{:S(2)}) %collective-permute-start.21) | collective-permute-done | bytes 16416 | tf_op jit(solution)/shard_map/ppermute | solution.py:353
  100.0 4.1 %collective-permute-done.23.refs_8_ = f32[16,256]{1,0:T(8,128)S(1)} collective-permute-done((f32[16,256]{1,0:T(8,128)S(1)}, f32[16,256]{1,0:T(8,128)S(1)}, u32[]{:S(2)}, u32[]{:S(2)}) %collective-permute-start.23) | collective-permute-done | bytes 16416 | tf_op jit(solution)/shard_map/ppermute | solution.py:353
  104.7 4.5 %shard_map.116 = (bf16[512,1024]{1,0:T(8,128)(2,1)S(1)}, bf16[512,1024]{1,0:T(8,128)(2,1)S(1)}) custom-call(bf16[256,1024]{1,0:T(8,128)(2,1)} %get-tuple-element.67.refs_1_.refs_0_, bf16[256,1024]{1,0:T(8,128)(2,1)} %collective-permute-done.15.refs_1_, bf16[256,1024]{1,0:T(8,128)(2,1)} %collective-permute-done.16.refs_2_, ...), custom_call_target="tpu_custom_call" | custom-call | flops 2147483648 | bytes 4194304 | tf_op jit(solution)/shard_map/pallas_call | solution.py:53
  109.2 1.7 shard_map.117
  112.1 8.5 %collective-permute-done.26 = bf16[4,32,1280]{2,1,0:T(8,128)(2,1)S(1)} collective-permute-done((bf16[4,32,1280]{2,1,0:T(8,128)(2,1)S(1)}, bf16[4,32,1280]{2,1,0:T(8,128)(2,1)S(1)}, u32[]{:S(2)}, u32[]{:S(2)}) %collective-permute-start.26) | collective-permute-done | bytes 327712 | tf_op jit(solution)/shard_map/ppermute | solution.py:353
  124.3 1.6 add_convert_fusion
  126.0 6.2 %collective-permute-start.37 = (bf16[128,1024]{1,0:T(8,128)(2,1)S(1)}, bf16[128,1024]{1,0:T(8,128)(2,1)S(1)}, u32[]{:S(2)}, u32[]{:S(2)}) collective-permute-start(bf16[128,1024]{1,0:T(8,128)(2,1)S(1)} %get-tuple-element.95), channel_id=1, source_target_pairs={{0,2},{1,3},{2,4},{3,5},{4,6},{5,7},{6,0},{7,1},{8,10},{9,11},{10,... | collective-permute-start | bytes 786440 | tf_op jit(solution)/shard_map/ppermute | solution.py:350
  134.6 3.1 %collective-permute-done.27 = bf16[4,32,2560]{2,1,0:T(8,128)(2,1)S(1)} collective-permute-done((bf16[4,32,2560]{2,1,0:T(8,128)(2,1)}, bf16[4,32,2560]{2,1,0:T(8,128)(2,1)S(1)}, u32[]{:S(2)}, u32[]{:S(2)}) %collective-permute-start.27) | collective-permute-done | bytes 655392 | tf_op jit(solution)/shard_map/ppermute | solution.py:353
  137.7 1.6 collective-permute-done.25
  140.7 6.9 %collective-permute-start.30 = (bf16[32,2560]{1,0:T(8,128)(2,1)S(1)}, bf16[32,2560]{1,0:T(8,128)(2,1)S(1)}, u32[]{:S(2)}, u32[]{:S(2)}) collective-permute-start(bf16[32,2560]{1,0:T(8,128)(2,1)S(1)} %get-tuple-element.98), channel_id=1, source_target_pairs={{0,6},{1,7},{2,0},{3,1},{4,2},{5,3},{6,4},{7,5},{8,14},{9,15},{10,... | collective-permute-start | bytes 491528 | tf_op jit(solution)/shard_map/ppermute | solution.py:350
  148.4 1.8 %collective-permute-done.36 = bf16[128,1024]{1,0:T(8,128)(2,1)S(1)} collective-permute-done((bf16[128,1024]{1,0:T(8,128)(2,1)S(1)}, bf16[128,1024]{1,0:T(8,128)(2,1)S(1)}, u32[]{:S(2)}, u32[]{:S(2)}) %collective-permute-start.36) | collective-permute-done | bytes 262176 | tf_op jit(solution)/shard_map/ppermute | solution.py:350
  150.4 6.9 %collective-permute-start.38 = (bf16[128,1024]{1,0:T(8,128)(2,1)S(1)}, bf16[128,1024]{1,0:T(8,128)(2,1)S(1)}, u32[]{:S(2)}, u32[]{:S(2)}) collective-permute-start(bf16[128,1024]{1,0:T(8,128)(2,1)S(1)} %multiply_convert_fusion.refs_0_), channel_id=1, source_target_pairs={{0,8},{8,0},{16,24},{24,16},{1,9},{9,1},{17,25},{25,17},{2,10},{10... | collective-permute-start | bytes 786440 | tf_op jit(solution)/shard_map/ppermute | solution.py:353
  158.9 10.9 %collective-permute-done.29 = bf16[32,2560]{1,0:T(8,128)(2,1)S(1)} collective-permute-done((bf16[32,2560]{1,0:T(8,128)(2,1)S(1)}, bf16[32,2560]{1,0:T(8,128)(2,1)S(1)}, u32[]{:S(2)}, u32[]{:S(2)}) %collective-permute-start.29) | collective-permute-done | bytes 163872 | tf_op jit(solution)/shard_map/ppermute | solution.py:350
  171.7 1.8 collective-permute-start.33
  174.9 2.1 %collective-permute-done.31.refs_1_ = bf16[32,2560]{1,0:T(8,128)(2,1)S(1)} collective-permute-done((bf16[32,2560]{1,0:T(8,128)(2,1)S(1)}, bf16[32,2560]{1,0:T(8,128)(2,1)S(1)}, u32[]{:S(2)}, u32[]{:S(2)}) %collective-permute-start.31) | collective-permute-done | bytes 163872 | tf_op jit(solution)/shard_map/ppermute | solution.py:353
  177.0 2.8 %collective-permute-done.32.refs_2_ = bf16[32,2560]{1,0:T(8,128)(2,1)S(1)} collective-permute-done((bf16[32,2560]{1,0:T(8,128)(2,1)S(1)}, bf16[32,2560]{1,0:T(8,128)(2,1)S(1)}, u32[]{:S(2)}, u32[]{:S(2)}) %collective-permute-start.32) | collective-permute-done | bytes 163872 | tf_op jit(solution)/shard_map/ppermute | solution.py:353
  (153 shorter events, 49.7 us)
Async XLA Ops:
  2.9 23.4 %collective-permute-start.3 = (bf16[512,1024]{1,0:T(8,128)(2,1)S(1)}, bf16[512,1024]{1,0:T(8,128)(2,1)S(1)}, u32[]{:S(2)}, u32[]{:S(2)}) collective-permute-start(bf16[512,1024]{1,0:T(8,128)(2,1)S(1)} %get-tuple-element.51.refs_4_.refs_9_), channel_id=1, source_target_pairs={{0,1},{1,0},{2,3},{3,2},{4,5},{5,4},{6,7},{7,6},{8,9},{9,8},{10,11... | collective-permute-start | bytes 3145736 | tf_op jit(solution)/shard_map/ppermute | solution.py:356
  3.3 22.0 %collective-permute-start = (bf16[128,1024]{1,0:T(8,128)(2,1)S(1)}, bf16[128,1024]{1,0:T(8,128)(2,1)S(1)}, u32[]{:S(2)}, u32[]{:S(2)}) collective-permute-start(bf16[128,1024]{1,0:T(8,128)(2,1)S(1)} %get-tuple-element.50), channel_id=1, source_target_pairs={{0,2},{1,3},{2,4},{3,5},{4,6},{5,7},{6,0},{7,1},{8,10},{9,11},{10,... | collective-permute-start | bytes 786440 | tf_op jit(solution)/shard_map/ppermute | solution.py:350
  5.9 20.3 %collective-permute-start.1 = (bf16[128,1024]{1,0:T(8,128)(2,1)S(1)}, bf16[128,1024]{1,0:T(8,128)(2,1)S(1)}, u32[]{:S(2)}, u32[]{:S(2)}) collective-permute-start(bf16[128,1024]{1,0:T(8,128)(2,1)S(1)} %get-tuple-element.50), channel_id=1, source_target_pairs={{0,4},{1,5},{2,6},{3,7},{4,0},{5,1},{6,2},{7,3},{8,12},{9,13},{10,... | collective-permute-start | bytes 786440 | tf_op jit(solution)/shard_map/ppermute | solution.py:350
  8.5 17.8 %collective-permute-start.2 = (bf16[128,1024]{1,0:T(8,128)(2,1)S(1)}, bf16[128,1024]{1,0:T(8,128)(2,1)S(1)}, u32[]{:S(2)}, u32[]{:S(2)}) collective-permute-start(bf16[128,1024]{1,0:T(8,128)(2,1)S(1)} %get-tuple-element.50), channel_id=1, source_target_pairs={{0,6},{1,7},{2,0},{3,1},{4,2},{5,3},{6,4},{7,5},{8,14},{9,15},{10,... | collective-permute-start | bytes 786440 | tf_op jit(solution)/shard_map/ppermute | solution.py:350
  29.4 19.7 %collective-permute-start.5 = (bf16[384,1024]{1,0:T(8,128)(2,1)}, bf16[384,1024]{1,0:T(8,128)(2,1)}, u32[]{:S(2)}, u32[]{:S(2)}) collective-permute-start(bf16[384,1024]{1,0:T(8,128)(2,1)} %constant_dynamic-update-slice_fusion.refs_5_.refs_10_), channel_id=1, source_target_pairs={{0,8},{8,0},{16,24},{24,16},{1,9},{9,1},{17,25},{25,17},{2,10},{10... | collective-permute-start | bytes 2359304 | tf_op jit(solution)/shard_map/ppermute | solution.py:353
  30.9 20.9 %collective-permute-start.6 = (bf16[384,1024]{1,0:T(8,128)(2,1)}, bf16[384,1024]{1,0:T(8,128)(2,1)}, u32[]{:S(2)}, u32[]{:S(2)}) collective-permute-start(bf16[384,1024]{1,0:T(8,128)(2,1)} %constant_dynamic-update-slice_fusion.refs_5_.refs_10_), channel_id=1, source_target_pairs={{0,16},{8,24},{16,0},{24,8},{1,17},{9,25},{17,1},{25,9},{2,18},{10... | collective-permute-start | bytes 2359304 | tf_op jit(solution)/shard_map/ppermute | solution.py:353
  32.4 36.7 %all-to-all-start = ((bf16[8,48,1024]{2,1,0:T(8,128)(2,1)}), bf16[8,48,1024]{2,1,0:T(8,128)(2,1)S(1)}, u32[]{:S(2)}, u32[]{:S(2)}) async-start(bf16[8,48,1024]{2,1,0:T(8,128)(2,1)} %bitcast.13), calls=%async_computation | async-start | bytes 1572864 | tf_op jit(solution)/shard_map/all_to_all | solution.py:396
  41.0 23.5 %collective-permute-start.9 = (bf16[384,1024]{1,0:T(8,128)(2,1)}, bf16[384,1024]{1,0:T(8,128)(2,1)S(1)}, u32[]{:S(2)}, u32[]{:S(2)}) collective-permute-start(bf16[384,1024]{1,0:T(8,128)(2,1)} %constant_dynamic-update-slice_fusion.refs_5_.refs_10_), channel_id=1, source_target_pairs={{0,1},{1,0},{2,3},{3,2},{4,5},{5,4},{6,7},{7,6},{8,9},{9,8},{10,11... | collective-permute-start | bytes 2359304 | tf_op jit(solution)/shard_map/ppermute | solution.py:356
  49.1 17.7 %collective-permute-start.10 = (bf16[384,1024]{1,0:T(8,128)(2,1)}, bf16[384,1024]{1,0:T(8,128)(2,1)S(1)}, u32[]{:S(2)}, u32[]{:S(2)}) collective-permute-start(bf16[384,1024]{1,0:T(8,128)(2,1)} %collective-permute-done.5.refs_6_), channel_id=1, source_target_pairs={{0,1},{1,0},{2,3},{3,2},{4,5},{5,4},{6,7},{7,6},{8,9},{9,8},{10,11... | collective-permute-start | bytes 2359304 | tf_op jit(solution)/shard_map/ppermute | solution.py:356
  50.2 11.7 %collective-permute-start.7 = (bf16[384,512]{1,0:T(8,128)(2,1)S(1)}, bf16[384,512]{1,0:T(8,128)(2,1)}, u32[]{:S(2)}, u32[]{:S(2)}) collective-permute-start(bf16[384,512]{1,0:T(8,128)(2,1)S(1)} %slice.62), channel_id=1, source_target_pairs={{0,16},{8,24},{16,0},{24,8},{1,17},{9,25},{17,1},{25,9},{2,18},{10... | collective-permute-start | bytes 1179656 | tf_op jit(solution)/shard_map/ppermute | solution.py:353
  52.8 17.9 %collective-permute-start.11 = (bf16[384,1024]{1,0:T(8,128)(2,1)}, bf16[384,1024]{1,0:T(8,128)(2,1)}, u32[]{:S(2)}, u32[]{:S(2)}) collective-permute-start(bf16[384,1024]{1,0:T(8,128)(2,1)} %collective-permute-done.6.refs_7_), channel_id=1, source_target_pairs={{0,1},{1,0},{2,3},{3,2},{4,5},{5,4},{6,7},{7,6},{8,9},{9,8},{10,11... | collective-permute-start | bytes 2359304 | tf_op jit(solution)/shard_map/ppermute | solution.py:356
  53.1 11.4 %collective-permute-start.8 = (bf16[384,512]{1,0:T(8,128)(2,1)S(1)}, bf16[384,512]{1,0:T(8,128)(2,1)}, u32[]{:S(2)}, u32[]{:S(2)}) collective-permute-start(bf16[384,512]{1,0:T(8,128)(2,1)S(1)} %slice.63), channel_id=1, source_target_pairs={{0,8},{8,0},{16,24},{24,16},{1,9},{9,1},{17,25},{25,17},{2,10},{10... | collective-permute-start | bytes 1179656 | tf_op jit(solution)/shard_map/ppermute | solution.py:353
  65.4 20.1 %collective-permute-start.15 = (bf16[256,1024]{1,0:T(8,128)(2,1)}, bf16[256,1024]{1,0:T(8,128)(2,1)}, u32[]{:S(2)}, u32[]{:S(2)}) collective-permute-start(bf16[256,1024]{1,0:T(8,128)(2,1)} %get-tuple-element.67.refs_1_.refs_0_), channel_id=1, source_target_pairs={{0,8},{8,0},{16,24},{24,16},{1,9},{9,1},{17,25},{25,17},{2,10},{10... | collective-permute-start | bytes 1572872 | tf_op jit(solution)/shard_map/ppermute | solution.py:353
  67.8 17.7 %collective-permute-start.16 = (bf16[256,1024]{1,0:T(8,128)(2,1)}, bf16[256,1024]{1,0:T(8,128)(2,1)}, u32[]{:S(2)}, u32[]{:S(2)}) collective-permute-start(bf16[256,1024]{1,0:T(8,128)(2,1)} %get-tuple-element.67.refs_1_.refs_0_), channel_id=1, source_target_pairs={{0,16},{8,24},{16,0},{24,8},{1,17},{9,25},{17,1},{25,9},{2,18},{10... | collective-permute-start | bytes 1572872 | tf_op jit(solution)/shard_map/ppermute | solution.py:353
  87.1 22.1 %collective-permute-start.17 = (bf16[256,2048]{1,0:T(8,128)(2,1)S(1)}, bf16[256,2048]{1,0:T(8,128)(2,1)S(1)}, u32[]{:S(2)}, u32[]{:S(2)}) collective-permute-start(bf16[256,2048]{1,0:T(8,128)(2,1)S(1)} %shard_map.115.refs_4_), channel_id=1, source_target_pairs={{0,1},{1,0},{2,3},{3,2},{4,5},{5,4},{6,7},{7,6},{8,9},{9,8},{10,11... | collective-permute-start | bytes 3145736 | tf_op jit(solution)/shard_map/ppermute | solution.py:356
  88.1 16.0 %collective-permute-start.19 = (bf16[256,512]{1,0:T(8,128)(2,1)S(1)}, bf16[256,512]{1,0:T(8,128)(2,1)S(1)}, u32[]{:S(2)}, u32[]{:S(2)}) collective-permute-start(bf16[256,512]{1,0:T(8,128)(2,1)S(1)} %slice.64), channel_id=1, source_target_pairs={{0,16},{8,24},{16,0},{24,8},{1,17},{9,25},{17,1},{25,9},{2,18},{10... | collective-permute-start | bytes 786440 | tf_op jit(solution)/shard_map/ppermute | solution.py:353
  90.7 14.0 %collective-permute-start.20 = (bf16[256,512]{1,0:T(8,128)(2,1)S(1)}, bf16[256,512]{1,0:T(8,128)(2,1)S(1)}, u32[]{:S(2)}, u32[]{:S(2)}) collective-permute-start(bf16[256,512]{1,0:T(8,128)(2,1)S(1)} %slice.65), channel_id=1, source_target_pairs={{0,8},{8,0},{16,24},{24,16},{1,9},{9,1},{17,25},{25,17},{2,10},{10... | collective-permute-start | bytes 786440 | tf_op jit(solution)/shard_map/ppermute | solution.py:353
  110.9 9.8 %collective-permute-start.26 = (bf16[4,32,1280]{2,1,0:T(8,128)(2,1)S(1)}, bf16[4,32,1280]{2,1,0:T(8,128)(2,1)S(1)}, u32[]{:S(2)}, u32[]{:S(2)}) collective-permute-start(bf16[4,32,1280]{2,1,0:T(8,128)(2,1)S(1)} %get-tuple-element.88), channel_id=1, source_target_pairs={{0,8},{8,0},{16,24},{24,16},{1,9},{9,1},{17,25},{25,17},{2,10},{10... | collective-permute-start | bytes 983048 | tf_op jit(solution)/shard_map/ppermute | solution.py:353
  111.5 12.8 %collective-permute-start.34 = (bf16[512,1024]{1,0:T(8,128)(2,1)S(1)}, bf16[512,1024]{1,0:T(8,128)(2,1)}, u32[]{:S(2)}, u32[]{:S(2)}) collective-permute-start(bf16[512,1024]{1,0:T(8,128)(2,1)S(1)} %get-tuple-element.92), channel_id=1, source_target_pairs={{0,1},{1,0},{2,3},{3,2},{4,5},{5,4},{6,7},{7,6},{8,9},{9,8},{10,11... | collective-permute-start | bytes 3145736 | tf_op jit(solution)/shard_map/ppermute | solution.py:356
  111.5 10.6 %collective-permute-start.24 = (bf16[4,32,1280]{2,1,0:T(8,128)(2,1)S(1)}, bf16[4,32,1280]{2,1,0:T(8,128)(2,1)S(1)}, u32[]{:S(2)}, u32[]{:S(2)}) collective-permute-start(bf16[4,32,1280]{2,1,0:T(8,128)(2,1)S(1)} %get-tuple-element.86), channel_id=1, source_target_pairs={{0,16},{8,24},{16,0},{24,8},{1,17},{9,25},{17,1},{25,9},{2,18},{10... | collective-permute-start | bytes 983048 | tf_op jit(solution)/shard_map/ppermute | solution.py:353
  121.6 16.1 %collective-permute-start.27 = (bf16[4,32,2560]{2,1,0:T(8,128)(2,1)}, bf16[4,32,2560]{2,1,0:T(8,128)(2,1)S(1)}, u32[]{:S(2)}, u32[]{:S(2)}) collective-permute-start(bf16[4,32,2560]{2,1,0:T(8,128)(2,1)} %pad_maximum_fusion.1), channel_id=1, source_target_pairs={{0,16},{8,24},{16,0},{24,8},{1,17},{9,25},{17,1},{25,9},{2,18},{10... | collective-permute-start | bytes 1966088 | tf_op jit(solution)/shard_map/ppermute | solution.py:353
  123.1 16.3 %collective-permute-start.25 = (bf16[4,32,2560]{2,1,0:T(8,128)(2,1)}, bf16[4,32,2560]{2,1,0:T(8,128)(2,1)}, u32[]{:S(2)}, u32[]{:S(2)}) collective-permute-start(bf16[4,32,2560]{2,1,0:T(8,128)(2,1)} %pad_maximum_fusion), channel_id=1, source_target_pairs={{0,8},{8,0},{16,24},{24,16},{1,9},{9,1},{17,25},{25,17},{2,10},{10... | collective-permute-start | bytes 1966088 | tf_op jit(solution)/shard_map/ppermute | solution.py:353
  126.0 22.5 %collective-permute-start.37 = (bf16[128,1024]{1,0:T(8,128)(2,1)S(1)}, bf16[128,1024]{1,0:T(8,128)(2,1)S(1)}, u32[]{:S(2)}, u32[]{:S(2)}) collective-permute-start(bf16[128,1024]{1,0:T(8,128)(2,1)S(1)} %get-tuple-element.95), channel_id=1, source_target_pairs={{0,2},{1,3},{2,4},{3,5},{4,6},{5,7},{6,0},{7,1},{8,10},{9,11},{10,... | collective-permute-start | bytes 786440 | tf_op jit(solution)/shard_map/ppermute | solution.py:350
  132.2 18.0 %collective-permute-start.36 = (bf16[128,1024]{1,0:T(8,128)(2,1)S(1)}, bf16[128,1024]{1,0:T(8,128)(2,1)S(1)}, u32[]{:S(2)}, u32[]{:S(2)}) collective-permute-start(bf16[128,1024]{1,0:T(8,128)(2,1)S(1)} %get-tuple-element.96), channel_id=1, source_target_pairs={{0,4},{1,5},{2,6},{3,7},{4,0},{5,1},{6,2},{7,3},{8,12},{9,13},{10,... | collective-permute-start | bytes 786440 | tf_op jit(solution)/shard_map/ppermute | solution.py:350
  133.5 16.8 %collective-permute-start.35 = (bf16[128,1024]{1,0:T(8,128)(2,1)S(1)}, bf16[128,1024]{1,0:T(8,128)(2,1)S(1)}, u32[]{:S(2)}, u32[]{:S(2)}) collective-permute-start(bf16[128,1024]{1,0:T(8,128)(2,1)S(1)} %get-tuple-element.94), channel_id=1, source_target_pairs={{0,6},{1,7},{2,0},{3,1},{4,2},{5,3},{6,4},{7,5},{8,14},{9,15},{10,... | collective-permute-start | bytes 786440 | tf_op jit(solution)/shard_map/ppermute | solution.py:350
  140.7 17.4 %collective-permute-start.30 = (bf16[32,2560]{1,0:T(8,128)(2,1)S(1)}, bf16[32,2560]{1,0:T(8,128)(2,1)S(1)}, u32[]{:S(2)}, u32[]{:S(2)}) collective-permute-start(bf16[32,2560]{1,0:T(8,128)(2,1)S(1)} %get-tuple-element.98), channel_id=1, source_target_pairs={{0,6},{1,7},{2,0},{3,1},{4,2},{5,3},{6,4},{7,5},{8,14},{9,15},{10,... | collective-permute-start | bytes 491528 | tf_op jit(solution)/shard_map/ppermute | solution.py:350
  147.7 22.1 %collective-permute-start.29 = (bf16[32,2560]{1,0:T(8,128)(2,1)S(1)}, bf16[32,2560]{1,0:T(8,128)(2,1)S(1)}, u32[]{:S(2)}, u32[]{:S(2)}) collective-permute-start(bf16[32,2560]{1,0:T(8,128)(2,1)S(1)} %get-tuple-element.99), channel_id=1, source_target_pairs={{0,4},{1,5},{2,6},{3,7},{4,0},{5,1},{6,2},{7,3},{8,12},{9,13},{10,... | collective-permute-start | bytes 491528 | tf_op jit(solution)/shard_map/ppermute | solution.py:350
  148.4 21.4 %collective-permute-start.28 = (bf16[32,2560]{1,0:T(8,128)(2,1)S(1)}, bf16[32,2560]{1,0:T(8,128)(2,1)S(1)}, u32[]{:S(2)}, u32[]{:S(2)}) collective-permute-start(bf16[32,2560]{1,0:T(8,128)(2,1)S(1)} %get-tuple-element.97), channel_id=1, source_target_pairs={{0,2},{1,3},{2,4},{3,5},{4,6},{5,7},{6,0},{7,1},{8,10},{9,11},{10,... | collective-permute-start | bytes 491528 | tf_op jit(solution)/shard_map/ppermute | solution.py:350
  150.4 21.2 %collective-permute-start.38 = (bf16[128,1024]{1,0:T(8,128)(2,1)S(1)}, bf16[128,1024]{1,0:T(8,128)(2,1)S(1)}, u32[]{:S(2)}, u32[]{:S(2)}) collective-permute-start(bf16[128,1024]{1,0:T(8,128)(2,1)S(1)} %multiply_convert_fusion.refs_0_), channel_id=1, source_target_pairs={{0,8},{8,0},{16,24},{24,16},{1,9},{9,1},{17,25},{25,17},{2,10},{10... | collective-permute-start | bytes 786440 | tf_op jit(solution)/shard_map/ppermute | solution.py:353
  157.4 16.1 %collective-permute-start.39 = (bf16[128,1024]{1,0:T(8,128)(2,1)S(1)}, bf16[128,1024]{1,0:T(8,128)(2,1)S(1)}, u32[]{:S(2)}, u32[]{:S(2)}) collective-permute-start(bf16[128,1024]{1,0:T(8,128)(2,1)S(1)} %multiply_convert_fusion.refs_0_), channel_id=1, source_target_pairs={{0,16},{8,24},{16,0},{24,8},{1,17},{9,25},{17,1},{25,9},{2,18},{10... | collective-permute-start | bytes 786440 | tf_op jit(solution)/shard_map/ppermute | solution.py:353
  158.1 15.3 %collective-permute-start.40 = (bf16[128,1024]{1,0:T(8,128)(2,1)S(1)}, bf16[128,1024]{1,0:T(8,128)(2,1)S(1)}, u32[]{:S(2)}, u32[]{:S(2)}) collective-permute-start(bf16[128,1024]{1,0:T(8,128)(2,1)S(1)} %multiply_convert_fusion.refs_0_), channel_id=1, source_target_pairs={{0,24},{8,16},{16,8},{24,0},{1,25},{9,17},{17,9},{25,1},{2,26},{10... | collective-permute-start | bytes 786440 | tf_op jit(solution)/shard_map/ppermute | solution.py:353
  170.5 9.4 %collective-permute-start.32 = (bf16[32,2560]{1,0:T(8,128)(2,1)S(1)}, bf16[32,2560]{1,0:T(8,128)(2,1)S(1)}, u32[]{:S(2)}, u32[]{:S(2)}) collective-permute-start(bf16[32,2560]{1,0:T(8,128)(2,1)S(1)} %fusion.2.refs_0_), channel_id=1, source_target_pairs={{0,16},{8,24},{16,0},{24,8},{1,17},{9,25},{17,1},{25,9},{2,18},{10... | collective-permute-start | bytes 491528 | tf_op jit(solution)/shard_map/ppermute | solution.py:353
  (45 other events, 268.7 us)

commit v5 on v4

--- a/solution.py
+++ b/solution.py
@@ -143,21 +143,38 @@
     quarter_inv[...] = inverse
 
 
-def score_kernel(groups, owners, share, places, cand, unit_b, unit, inv_len, *refs):
+def score_kernel(groups, owners, share, chunks, places, final, cand, unit_hbm, *refs):
     count = len(places)
-    pieces, (tags, up, up_keep, up_give, table, spread, sems) = refs[:count], refs[count:]
+    if final:
+        inv_len, partial, yn_hbm, *refs = refs
+        pieces, (tags, up, up_keep, up_give, table, unit_b, sems, spread, unit) = refs[:count], refs[count:]
+    else:
+        pieces, (partial_out, table, unit_b, sems) = refs[:count], refs[count:]
     chips = owners // 2
     vocab_dev = share * groups
     grp, core = lax.axis_index("grp"), lax.axis_index("seq") % 2
-    tok, width = unit_b.shape
+    tok = unit_b.shape[0]
     block = vocab_dev + groups * (chips - 1) * share
+
+    def place(key):
+        side, chunk, k = key
+        if chunk < 0:
+            return side * block, vocab_dev
+        before = sum(len(ds) for ds in chunks[:chunk]) * groups * share
+        rows = len(chunks[chunk]) * share
+        return side * block + vocab_dev + before + k * rows, rows
+
+    load_unit = pltpu.make_async_copy(unit_hbm, unit_b, sems.at[count])
+    load_unit.start()
     copies = {}
-    for n, (side, k, left, wide) in enumerate(places):
-        rows = pieces[n].shape[0]
-        at = side * block + (0 if k < 0 else vocab_dev + k * rows)
+    for n, (*key, left, wide) in enumerate(places):
+        at, rows = place(key)
         copy = pltpu.make_async_copy(pieces[n], table.at[pl.ds(at, rows), pl.ds(left, wide)], sems.at[n])
         copy.start()
-        copies.setdefault((side, k), []).append(copy)
+        copies.setdefault(tuple(key), []).append(copy)
+    if final:
+        load_yn = pltpu.make_async_copy(yn_hbm, unit, sems.at[count + 1])
+        load_yn.start()
     ids = owner_ids(owners)
     lane = iota((1, 128), 1)
     owner = jnp.full((1, 128), -1, i32)
@@ -174,14 +191,14 @@
     wanted = [jnp.broadcast_to(chosen[:, j : j + 1], (tok, 128)) for j in range(owners)]
 
     def runs(key):
-        side, k = key
-        at = side * block + (0 if k < 0 else vocab_dev + k * (chips - 1) * share)
-        if k < 0:
-            return at, vocab_dev, [(side * chips, 0, vocab_dev, ids[side * chips] * vocab_dev)]
+        side, chunk, k = key
+        at, rows = place(key)
+        if chunk < 0:
+            return at, rows, [(side * chips, 0, vocab_dev, ids[side * chips] * vocab_dev)]
         begin = (grp ^ k) * share
-        return at, (chips - 1) * share, [
-            (side * chips + d, (d - 1) * share, share, ids[side * chips + d] * vocab_dev + begin)
-            for d in range(1, chips)
+        return at, rows, [
+            (side * chips + d, i * share, share, ids[side * chips + d] * vocab_dev + begin)
+            for i, d in enumerate(chunks[chunk])
         ]
 
     def tiles(key):
@@ -192,21 +209,29 @@
                 hit = wanted[j][:, :step] == base + o + iota((1, step), 1)
                 yield j, off + o, step, hit
 
+    load_unit.wait()
     yb = unit_b[...]
     value = [[] for _ in range(owners)]
     for key in copies:
         for copy in copies[key]:
             copy.wait()
+        if key[0] != int(final):
+            continue
         at, rows, _ = runs(key)
         product = dot(yb, table[at : at + rows], NT)
         for j, off, step, hit in tiles(key):
             value[j].append(jnp.where(hit, product[:, off : off + step], 0.0))
-    logits = jnp.zeros((tok, 128), f32)
+    logits = partial[...] if final else jnp.zeros((tok, 128), f32)
     for j in range(owners):
+        if not value[j]:
+            continue
         total = value[j][0]
         for part in value[j][1:]:
             total = total + part
         logits = jnp.where(lane == j, jnp.sum(total, -1, keepdims=True), logits)
+    if not final:
+        partial_out[...] = logits
+        return
     exponent = jnp.where(chosen >= 0, jnp.exp(logits / softmax_warmth), 0.0)
     coef = (exponent / jnp.sum(exponent, -1, keepdims=True) - first) / softmax_warmth
     tags[:owners] = coef.T[:owners]
@@ -217,6 +242,7 @@
         for j, off, step, hit in tiles(key):
             spread[:, at + off : at + off + step] = jnp.where(hit, amount[j][:, :step], 0.0).astype(b16)
     pulled = dot(spread[...], table[...], NN)
+    load_yn.wait()
     yn = unit[...]
     upstream = (pulled - yn * jnp.sum(yn * pulled, -1, keepdims=True)) * inv_len[...]
     up[...] = upstream.astype(b16)
@@ -247,10 +273,10 @@
         grad[:, ck] = (dot(grad_score, proj[:, cq], TN) * slope[:, ck].astype(f32)).astype(b16)
 
 
-def item_kernel(groups, owners, share, places, *refs):
+def item_kernel(groups, owners, share, chunks, places, *refs):
     count = len(places)
     units, tags = refs[:count], refs[count : count + groups]
-    own, others, far_own, far_others, keep, give, gathered, near, sems = refs[count + groups :]
+    parts, (keep, give, gathered, near, sems) = refs[count + groups : -5], refs[-5:]
     chips = owners // 2
     vocab_dev = share * groups
     grp = lax.axis_index("grp")
@@ -259,12 +285,12 @@
     for n, (k, left, wide) in enumerate(places):
         copies.append(pltpu.make_async_copy(units[n], gathered.at[pl.ds(k * tok, tok), pl.ds(left, wide)], sems.at[n]))
     begin = pl.multiple_of(grp * share, share)
-    for side, (full, part) in enumerate(((own, others), (far_own, far_others))):
-        at, n = side * chips * share, count + 2 * side
-        copies.append(pltpu.make_async_copy(full.at[pl.ds(begin, share)], near.at[pl.ds(at, share)], sems.at[n]))
-        copies.append(
-            pltpu.make_async_copy(part, near.at[pl.ds(at + share, (chips - 1) * share)], sems.at[n + 1])
-        )
+    for n, part in enumerate(parts):
+        side, chunk = n // (len(chunks) + 1), n % (len(chunks) + 1) - 1
+        for i, d in enumerate([0] if chunk < 0 else chunks[chunk]):
+            rows = pl.ds(begin if chunk < 0 else i * share, share)
+            at = pl.ds((side * chips + d) * share, share)
+            copies.append(pltpu.make_async_copy(part.at[rows], near.at[at], sems.at[len(copies)]))
     for copy in copies:
         copy.start()
     ids = owner_ids(owners)
@@ -301,11 +327,33 @@
     for z in range(chips):
         for k in range(groups):
             piece = whole[pl.ds(pl.multiple_of(z * rows + (grp ^ k) * fine, fine), fine)]
-            if k == 3:
-                outs[3][z] = piece[:, :half]
-                outs[4][z] = piece[:, half:]
+            if k == 0:
+                outs[0][z] = piece
             else:
-                outs[k][z] = piece
+                outs[2 * k - 1][z] = piece[:, :half]
+                outs[2 * k][z] = piece[:, half:]
+
+
+def sum_kernel(halves, base, *refs):
+    parts, outs = refs[: 2 * halves], refs[2 * halves :]
+    chips = len(outs)
+    chip = lax.axis_index("seq") // 2
+    half = base.shape[2] // 2
+    for d in range(chips):
+        z = lax.rem(chip + d, chips)
+        for i in range(2):
+            cols = slice(i * half, (i + 1) * half)
+            total = base[z][:, cols].astype(f32)
+            for n in range(halves):
+                total += parts[2 * n + i][z].astype(f32)
+            outs[d][:, cols] = total.astype(b16)
+
+
+def pair_kernel(x, y, *outs):
+    rows = outs[0].shape[0]
+    for d, out in enumerate(outs):
+        at = slice(d * rows, (d + 1) * rows)
+        out[...] = (x[at].astype(f32) + y[at].astype(f32)).astype(b16)
 
 
 def assemble_kernel(groups, columns, *refs):
@@ -355,11 +403,11 @@
     def to_core(x):
         return lax.ppermute(x, "seq", [(a, a ^ 1) for a in range(owners)])
 
-    def gather_groups(x):
+    def gather_groups(x, near=None):
         wide = x.shape[1]
         if groups != 4:
             return [(k, 0, wide, to_group(x, k) if k else x) for k in range(groups)]
-        one, two = to_group(x, 1), to_group(x, 2)
+        one, two = near or [to_group(x, k) for k in (1, 2)]
         half = wide // 2
         left, right = to_group(one[:, :half], 2), to_group(two[:, half:], 1)
         return [(0, 0, wide, x), (1, 0, wide, one), (2, 0, wide, two), (3, 0, half, left), (3, half, half, right)]
@@ -369,9 +417,11 @@
         [((vocab_dev, width), b16), ((share, width), b16), ((share, 1), f32)],
         [VMEM], [item_table], flops=8 * vocab_dev * width, nbytes=5 * vocab_dev * width, room=8,
     )
-    got = [to_chip(quarter, d) for d in range(1, chips)]
+    chunks = [[d for d in range(1, chips) if d % 2 == 0], [d for d in range(1, chips) if d % 2]]
+    even = [to_chip(quarter, d) for d in chunks[0]]
+    even, later = lax.optimization_barrier((even, quarter))
+    odd = [to_chip(later, d) for d in chunks[1]]
     far_own = to_core(own)
-
     outs = [
         ((tok, width // 2), b16), ((tok, width // 2), b16), ((tok, 4 * hidden), b16), ((tok, 4 * hidden), b16),
         ((HEADS, tok, tok), b16), ((HEADS, tok, tok), b16), ((tok, hidden), f32), ((tok, 1), f32),
@@ -384,14 +434,16 @@
         flops=2 * tok * width * 6 * hidden, nbytes=24 * tok * width + 10 * width * hidden, room=28,
     )
 
-    got, far_own, unit_b = lax.optimization_barrier((got, far_own, unit_b))
-    others = jnp.concatenate(got, 0)
-    pieces = [(0, -1, 0, width, own)] + [(0,) + p for p in gather_groups(others)]
-    pieces = pieces + [(1, -1, 0, width, far_own)] + [(1,) + p[1:4] + (to_core(p[4]),) for p in pieces[1:]]
-    far_others = [p[4] for p in pieces if p[0] == 1 and p[1] == 0][0]
-    sent_unit, _ = lax.optimization_barrier((unit_b, [p[4] for p in pieces if p[0] == 0]))
-    unit_sent = gather_groups(sent_unit)
-    outgoing, others = lax.optimization_barrier((outgoing, others))
+    even = jnp.concatenate(even, 0) if len(even) > 1 else even[0]
+    near = [to_group(even, k) for k in (1, 2)]
+    odd, far_own, unit_b, near = lax.optimization_barrier((odd, far_own, unit_b, near))
+    others = [even, jnp.concatenate(odd, 0)]
+    pieces = [(0, -1, 0, 0, width, own)]
+    for j, x in enumerate(others):
+        pieces += [(0, j) + p for p in gather_groups(x, None if j else near)]
+    pieces = pieces + [(1,) + p[1:5] + (to_core(p[5]) if p[1] >= 0 else far_own,) for p in pieces]
+    near = [p[5] for p in pieces if p[2] == 0]
+    outgoing, _ = lax.optimization_barrier((outgoing, others))
 
     arrived = lax.all_to_all(
         outgoing.reshape(owners, slot, width), "seq", 0, 0, tiled=True
@@ -403,26 +455,29 @@
 
     candidates = jnp.concatenate([history[:, None], negatives], 1)
     vocab = vocab_dev * owners
-    layer_out, score_unit = lax.optimization_barrier((layer_out, unit))
+    far_give, far_gated = to_core(give), to_core(gated)
+    mine = [p for p in pieces if p[0] == 0]
+    partial, = call(
+        lambda *refs: score_kernel(groups, owners, share, chunks, [p[:5] for p in mine], False, *refs),
+        [((tok, 128), f32)], [VMEM] + [ANY] * (len(mine) + 1), [candidates, unit_b] + [p[5] for p in mine],
+        [pltpu.VMEM((vocab // 2, width), b16), pltpu.VMEM((tok, width), b16),
+         pltpu.SemaphoreType.DMA((len(mine) + 1,))],
+        flops=tok * width * vocab, nbytes=vocab * width + 2 * tok * width, room=14 if groups == 4 else 40,
+    )
+    sent_unit, _ = lax.optimization_barrier((unit_b, partial))
+    unit_sent = gather_groups(sent_unit)
+    layer_out, partial, far_give, far_gated = lax.optimization_barrier((layer_out, partial, far_give, far_gated))
+    order = [p for p in pieces if p[0] == 1] + mine
+    tags, up, up_keep, up_give = call(
+        lambda *refs: score_kernel(groups, owners, share, chunks, [p[:5] for p in order], True, *refs),
+        [((2 * owners, tok), f32), ((tok, width), b16), ((tok, width // 2), b16), ((tok, width // 2), b16)],
+        [VMEM, ANY, VMEM, VMEM] + [ANY] * (len(order) + 1),
+        [candidates, unit_b, inv_len, partial, unit] + [p[5] for p in order],
+        [pltpu.VMEM((vocab, width), b16), pltpu.VMEM((tok, width), b16), pltpu.SemaphoreType.DMA((len(order) + 2,)),
+         pltpu.VMEM((tok, vocab), b16), pltpu.VMEM((tok, width), f32)],
+        flops=3 * tok * width * vocab, nbytes=2 * vocab * width + 12 * tok * width, room=24 if groups == 4 else 58,
+    )
     units = [p[3] for p in unit_sent]
-    tags, up, up_keep, up_give = call(
-        lambda *refs: score_kernel(groups, owners, share, [p[:4] for p in pieces], *refs),
-        [((2 * owners, tok), f32), ((tok, width), b16), ((tok, width // 2), b16), ((tok, width // 2), b16)],
-        [VMEM] * 4 + [ANY] * len(pieces), [candidates, unit_b, score_unit, inv_len] + [p[4] for p in pieces],
-        [pltpu.VMEM((vocab, width), b16), pltpu.VMEM((tok, vocab), b16), pltpu.SemaphoreType.DMA((len(pieces),))],
-        flops=4 * tok * width * vocab, nbytes=2 * vocab * width + 12 * tok * width, room=24 if groups == 4 else 58,
-    )
-
-    all_tags = [to_group(tags, k) if k else tags for k in range(groups)]
-    mine, other = call(
-        lambda *refs: item_kernel(groups, owners, share, [p[:3] for p in unit_sent], *refs),
-        [((chips * share, width), b16)] * 2, [ANY] * len(units) + [VMEM] * groups + [ANY] * 4,
-        units + all_tags + [own, others, far_own, far_others],
-        [pltpu.VMEM((groups * tok, width), b16), pltpu.VMEM((2 * chips * share, width), b16),
-         pltpu.SemaphoreType.DMA((len(units) + 4,))],
-        flops=4 * groups * tok * width * chips * share, nbytes=4 * tok * groups * width, room=16 if groups == 4 else 48,
-    )
-    far_mine = to_core(other)
 
     up, _ = lax.optimization_barrier((up, [p[3] for p in unit_sent[1:3]]))
 
@@ -432,7 +487,17 @@
         flops=2 * tok * width * hidden, nbytes=20 * tok * width,
     )
 
-    far = [to_core(x) for x in (give, up_give, grad, gated)]
+    all_tags = [to_group(tags, k) if k else tags for k in range(groups)]
+    far = [far_give, to_core(up_give), to_core(grad), far_gated]
+    mine, other = call(
+        lambda *refs: item_kernel(groups, owners, share, chunks, [p[:3] for p in unit_sent], *refs),
+        [((chips * share, width), b16)] * 2, [ANY] * len(units) + [VMEM] * groups + [ANY] * len(near),
+        units + all_tags + near,
+        [pltpu.VMEM((groups * tok, width), b16), pltpu.VMEM((2 * chips * share, width), b16),
+         pltpu.SemaphoreType.DMA((len(units) + 2 * chips,))],
+        flops=4 * groups * tok * width * chips * share, nbytes=4 * tok * groups * width, room=16 if groups == 4 else 48,
+    )
+    far_mine = to_core(other)
     far, mine = lax.optimization_barrier((far, mine))
     half = 5 * hidden // 2
     if groups == 4:
@@ -440,16 +505,16 @@
         split = (chips, fine, half)
         parts = call(
             lambda *refs: weight_kernel(groups, owners, *refs),
-            [(block, b16)] * 3 + [(split, b16)] * 2, [VMEM] * 8,
+            [(block, b16)] + [(split, b16)] * 6, [VMEM] * 8,
             [keep, far[0], up_keep, far[1], grad, far[2], gated, far[3]],
             [pltpu.VMEM((width // 2, 5 * hidden), b16)],
             flops=2 * tok * width * 5 * hidden, nbytes=20 * tok * width, room=14,
         )
-        left, right = to_group(parts[3], 1).astype(f32), to_group(parts[4], 2).astype(f32)
-        one, two = parts[1].astype(f32), parts[2].astype(f32)
-        one = jnp.concatenate([one[..., :half], one[..., half:] + right], 2).astype(b16)
-        two = jnp.concatenate([two[..., :half] + left, two[..., half:]], 2).astype(b16)
-        sums = parts[0].astype(f32) + to_group(one, 1).astype(f32) + to_group(two, 2).astype(f32)
+        left, right = to_group(parts[5], 1), to_group(parts[6], 2)
+        one_left, two_right = to_group(parts[1], 1), to_group(parts[4], 2)
+        one_right = (parts[2].astype(f32) + right.astype(f32)).astype(b16)
+        two_left = (parts[3].astype(f32) + left.astype(f32)).astype(b16)
+        arrived = [one_left, to_group(one_right, 1), to_group(two_left, 2), two_right]
     else:
         def both(x, y):
             return jnp.concatenate([x, y], 0)
@@ -461,12 +526,16 @@
         sums = lax.dynamic_index_in_dim(weight, grp, 1, False).astype(f32)
         for k in range(1, groups):
             sums += to_group(lax.dynamic_index_in_dim(weight, grp ^ k, 1, False), k).astype(f32)
-    sums = sums.astype(b16)
-
-    summed = (mine.astype(f32) + far_mine.astype(f32)).astype(b16).reshape(chips, share, width)
+
+
+    summed = call(
+        pair_kernel, [((share, width), b16)] * chips, [VMEM] * 2, [mine, far_mine],
+        flops=chips * share * width, nbytes=6 * chips * share * width, room=8,
+    )
+    come = [to_chip(summed[d], -d) for d in range(1, chips)]
     total = summed[0].astype(f32)
-    for d in range(1, chips):
-        total += to_chip(summed[d], -d).astype(f32)
+    for x in come:
+        total += x.astype(f32)
     total = (total * quarter_inv).astype(b16)
     table_grad, = call(
         lambda *refs: assemble_kernel(groups, [width], *refs), [((vocab_dev, width), f32)], [VMEM] * groups,
@@ -474,9 +543,19 @@
         flops=vocab_dev * width, nbytes=6 * vocab_dev * width, room=8,
     )
 
-    line = lax.dynamic_index_in_dim(sums, chip, 0, False).astype(f32)
+    if groups == 4:
+        base, _ = lax.optimization_barrier((parts[0], come[0]))
+        sums = call(
+            lambda *refs: sum_kernel(2, *refs), [((fine, 5 * hidden), b16)] * chips, [VMEM] * 5, [base] + arrived,
+            flops=chips * fine * 5 * hidden, nbytes=40 * chips * fine * hidden, room=10,
+        )
+    else:
+        sums = [
+            lax.dynamic_index_in_dim(sums, (chip + d) % chips, 0, False).astype(b16) for d in range(chips)
+        ]
+    line = sums[0].astype(f32)
     for d in range(1, chips):
-        line += to_chip(lax.dynamic_index_in_dim(sums, (chip + d) % chips, 0, False), d).astype(f32)
+        line += to_chip(sums[d], d).astype(f32)
     line = line.astype(b16)
     lines = [to_group(line, k) if k else line for k in range(groups)]
     if fine % 16 == 0:

time: 184 us -> 216 us (1.17); the launches traced: 181 us -> 215 us
  waiting for transfers between devices: 59.8 us -> 84.7 us
  local copies, waits for them, and re-layouts: 26.7 us -> 46.9 us
  starting transfers between devices: 60.8 us -> 48 us
  Pallas kernels: 27.4 us -> 32.3 us
  other arithmetic: 5.21 us -> 2.33 us
    unnamed x72 -> x137, local copies, waits for them, and re-layouts: 21.1 us -> 42 us
    ppermute x9, waiting for transfers between devices: 13.7 us -> 31 us  [to_chip(): return lax.ppermute(x, 'seq', pairs)]
    ppermute x9, starting transfers between devices: 22.9 us -> 11 us  [to_chip(): return lax.ppermute(x, 'seq', pairs)]
    all_to_all x1, starting transfers between devices: 8.56 us -> 3.55 us  [body(): lax.all_to_all(outgoing.reshape(owners, slot, width), 'seq', 0, 0, tiled=...]
    pallas_call x9 -> x12, Pallas kernels: 27.4 us -> 32.3 us  [call(): pl.pallas_call(kernel, out_shape=[jax.ShapeDtypeStruct(s, t) for s, t in...]
    ppermute x21 -> x27, waiting for transfers between devices: 46.1 us -> 50.1 us  [to_group(): return lax.ppermute(x, 'grp', [(a, a ^ k) for a in range(groups)])]
    ppermute x11 -> x16, waiting for transfers between devices: 0.03 us -> 3.55 us  [to_core(): return lax.ppermute(x, 'seq', [(a, a ^ 1) for a in range(owners)])]
    ppermute x21 -> x27, starting transfers between devices: 27.5 us -> 30.4 us  [to_group(): return lax.ppermute(x, 'grp', [(a, a ^ k) for a in range(groups)])]
  transfers between devices with their start and end apart: 42 -> 53, of which waited for: 13 -> 22; matrix products, arithmetic and copies ran while one was open for 6% -> 3% of each run, Pallas kernels for 13% -> 14%
where the time goes in v5:
time: 216 us; the launch traced here: 215 us
  waiting for transfers between devices  84.7 us (39%)
  starting transfers between devices  48 us (22%)
  local copies, waits for them, and re-layouts  46.9 us (22%)
  Pallas kernels  32.3 us (15%)
  other arithmetic  2.33 us (1%)
    ppermute x27, waiting for transfers between devices, to_group(): return lax.ppermute(x, 'grp', [(a, a ^ k) for a in range(groups)])  50.1 us
    unnamed x137, local copies, waits for them, and re-layouts  42 us
    pallas_call x12, Pallas kernels, call(): pl.pallas_call(kernel, out_shape=[jax.ShapeDtypeStruct(s, t) for s, t in...  32.3 us
    ppermute x9, waiting for transfers between devices, to_chip(): return lax.ppermute(x, 'seq', pairs)  31 us
    ppermute x27, starting transfers between devices, to_group(): return lax.ppermute(x, 'grp', [(a, a ^ k) for a in range(groups)])  30.4 us
    ppermute x9, starting transfers between devices, to_chip(): return lax.ppermute(x, 'seq', pairs)  11 us
    slice x6, local copies, waits for them, and re-layouts, gather_groups(): left, right = (to_group(one[:, :half], 2), to_group(two[:, half:], 1))  4.72 us
  transfers between devices with their start and end apart: 53, of which 22 were waited for; matrix products, arithmetic and copies ran while one was open for 3% of the time, Pallas kernels for 14%

profile of v5, /device:TPU:0, one launch (start us, length us, event | category | flops | bytes accessed | tf_op | source)
XLA Modules:
  0.0 215.3 jit_solution(18248709086350989011)
XLA Ops:
  3.3 3.6 %collective-permute-start = (bf16[128,1024]{1,0:T(8,128)(2,1)S(1)}, bf16[128,1024]{1,0:T(8,128)(2,1)S(1)}, u32[]{:S(2)}, u32[]{:S(2)}) collective-permute-start(bf16[128,1024]{1,0:T(8,128)(2,1)S(1)} %get-tuple-element.67), channel_id=1, source_target_pairs={{0,4},{1,5},{2,6},{3,7},{4,0},{5,1},{6,2},{7,3},{8,12},{9,13},{10,... | collective-permute-start | bytes 786440 | tf_op jit(solution)/shard_map/ppermute | solution.py:398
  6.9 12.6 %collective-permute-done.refs_3_.refs_17_.refs_10_ = bf16[128,1024]{1,0:T(8,128)(2,1)S(1)} collective-permute-done((bf16[128,1024]{1,0:T(8,128)(2,1)S(1)}, bf16[128,1024]{1,0:T(8,128)(2,1)S(1)}, u32[]{:S(2)}, u32[]{:S(2)}) %collective-permute-start) | collective-permute-done | bytes 262176 | tf_op jit(solution)/shard_map/ppermute | solution.py:398
  20.3 3.1 %collective-permute-start.2 = (bf16[128,1024]{1,0:T(8,128)(2,1)S(1)}, bf16[128,1024]{1,0:T(8,128)(2,1)S(1)}, u32[]{:S(2)}, u32[]{:S(2)}) collective-permute-start(bf16[128,1024]{1,0:T(8,128)(2,1)S(1)} %get-tuple-element.67), channel_id=1, source_target_pairs={{0,6},{1,7},{2,0},{3,1},{4,2},{5,3},{6,4},{7,5},{8,14},{9,15},{10,... | collective-permute-start | bytes 786440 | tf_op jit(solution)/shard_map/ppermute | solution.py:398
  23.3 1.5 collective-permute-start.4
  27.6 2.2 %copy-done.42 = bf16[1024,2048]{1,0:T(8,128)(2,1)S(1)} copy-done((bf16[1024,2048]{1,0:T(8,128)(2,1)S(1)}, bf16[1024,2048]{1,0:T(8,128)(2,1)}, u32[]{:S(2)}) %copy-start.42) | copy-done | bytes 4194328
  32.2 4.6 %shard_map.111 = (bf16[256,512]{1,0:T(8,128)(2,1)S(1)}, bf16[256,512]{1,0:T(8,128)(2,1)S(1)}, bf16[256,2048]{1,0:T(8,128)(2,1)S(1)}, bf16[256,2048]{1,0:T(8,128)...) custom-call(s32[1,8]{1,0:T(1,128)S(1)} %copy-done.57, ...), custom_call_target="tpu_custom_call" | custom-call | flops 1610612736 | bytes 11534336 | tf_op jit(solution)/shard_map/pallas_call | solution.py:53
  48.6 3.5 %all-to-all-start = ((bf16[8,48,1024]{2,1,0:T(8,128)(2,1)}), bf16[8,48,1024]{2,1,0:T(8,128)(2,1)S(1)}, u32[]{:S(2)}, u32[]{:S(2)}) async-start(bf16[8,48,1024]{2,1,0:T(8,128)(2,1)} %bitcast.4), calls=%async_computation | async-start | bytes 1572864 | tf_op jit(solution)/shard_map/all_to_all | solution.py:448
  53.1 1.6 collective-permute-start.6
  55.7 1.6 collective-permute-start.7
  57.2 4.5 %collective-permute-done.8.refs_9_.refs_23_ = bf16[256,1024]{1,0:T(8,128)(2,1)S(1)} collective-permute-done((bf16[256,1024]{1,0:T(8,128)(2,1)S(1)}, bf16[256,1024]{1,0:T(8,128)(2,1)S(1)}, u32[]{:S(2)}, u32[]{:S(2)}) %collective-permute-start.8) | collective-permute-done | bytes 524320 | tf_op jit(solution)/shard_map/ppermute | solution.py:401
  66.7 2.5 %collective-permute-done.10.refs_11_.refs_25_ = bf16[256,512]{1,0:T(8,128)(2,1)} collective-permute-done((bf16[256,512]{1,0:T(8,128)(2,1)}, bf16[256,512]{1,0:T(8,128)(2,1)}, u32[]{:S(2)}, u32[]{:S(2)}) %collective-permute-start.10) | collective-permute-done | bytes 262176 | tf_op jit(solution)/shard_map/ppermute | solution.py:401
  76.1 5.1 %shard_map.114.refs_3_ = f32[256,128]{1,0:T(8,128)S(1)} custom-call(s32[256,4]{1,0:T(8,128)S(1)} %copy.15.refs_0_, bf16[256,1024]{1,0:T(8,128)(2,1)S(1)} %copy-done.15, bf16[512,1024]{1,0:T(8,128)(2,1)S(1)} %get-tuple-element.68.refs_2_.refs_16_.refs_9_, bf16[128,1024]{1,0:T(8,128)(2,1)S(1)} %copy-done.24, bf16[128,1024]{1,0:T(8,128)(2,1)S(1)} %copy-done.9, ...), custom_call_target="tpu_custom_call" | custom-call | flops 1073741824 | bytes 4718592 | tf_op jit(solution)/shard_map/pallas_call | solution.py:53
  81.2 1.6 collective-permute-start.25
  87.7 7.9 %collective-permute-done.25.refs_1_ = bf16[256,1024]{1,0:T(8,128)(2,1)S(1)} collective-permute-done((bf16[256,1024]{1,0:T(8,128)(2,1)S(1)}, bf16[256,1024]{1,0:T(8,128)(2,1)S(1)}, u32[]{:S(2)}, u32[]{:S(2)}) %collective-permute-start.25) | collective-permute-done | bytes 524320 | tf_op jit(solution)/shard_map/ppermute | solution.py:401
  100.0 1.6 shard_map.113
  117.3 9.0 %shard_map.115 = (f32[16,256]{1,0:T(8,128)S(1)}, bf16[256,1024]{1,0:T(8,128)(2,1)S(1)}, bf16[256,512]{1,0:T(8,128)(2,1)S(1)}, bf16[256,512]{1,0:T(8,128)(2,1)S(1)}) custom-call(s32[256,4]{1,0:T(8,128)S(1)} %copy.15.refs_0_, bf16[256,1024]{1,0:T(8,128)(2,1)S(1)} %copy-done.16, f32[256,1]{1,0:T(8,128)S(1)} %copy-done.64, f32[256,128]{1,0:T(8,128)S(1)} %copy-done.35, ...), custom_call_target="tpu_custom_call" | custom-call | flops 3221225472 | bytes 11534336 | tf_op jit(solution)/shard_map/pallas_call | solution.py:53
  126.4 1.6 shard_map.116.refs_4_
  130.2 1.7 collective-permute-done.30.refs_6_
  133.4 3.2 %collective-permute-done.32.refs_8_ = f32[16,256]{1,0:T(8,128)S(1)} collective-permute-done((f32[16,256]{1,0:T(8,128)S(1)}, f32[16,256]{1,0:T(8,128)S(1)}, u32[]{:S(2)}, u32[]{:S(2)}) %collective-permute-start.32) | collective-permute-done | bytes 16416 | tf_op jit(solution)/shard_map/ppermute | solution.py:401
  136.6 4.2 %shard_map.117 = (bf16[512,1024]{1,0:T(8,128)(2,1)S(1)}, bf16[512,1024]{1,0:T(8,128)(2,1)S(1)}) custom-call(bf16[256,1024]{1,0:T(8,128)(2,1)S(1)} %copy-done.16, bf16[256,1024]{1,0:T(8,128)(2,1)S(1)} %copy-done.37, bf16[256,1024]{1,0:T(8,128)(2,1)S(1)} %copy-done.39, bf16[256,512]{1,0:T(8,128)(2,1)S(1)} %collective-permute-done.28.refs_3_, ...), custom_call_target="tpu_custom_call" | custom-call | flops 2147483648 | bytes 4194304 | tf_op jit(solution)/shard_map/pallas_call | solution.py:53
  141.4 2.5 %collective-permute-done.24.refs_3_ = bf16[256,512]{1,0:T(8,128)(2,1)S(1)} collective-permute-done((bf16[256,512]{1,0:T(8,128)(2,1)S(1)}, bf16[256,512]{1,0:T(8,128)(2,1)S(1)}, u32[]{:S(2)}, u32[]{:S(2)}) %collective-permute-start.24) | collective-permute-done | bytes 262176 | tf_op jit(solution)/shard_map/ppermute | solution.py:404
  143.9 2.7 %shard_map.118 = (bf16[4,32,2560]{2,1,0:T(8,128)(2,1)S(1)}, bf16[4,32,1280]{2,1,0:T(8,128)(2,1)S(1)}, bf16[4,32,1280]{2,1,0:T(8,128)(2,1)S(1)}, bf16[4,32,1280]{...) custom-call(bf16[256,512]{1,0:T(8,128)(2,1)S(1)} %copy-done.62, ...), custom_call_target="tpu_custom_call" | custom-call | flops 1342177280 | bytes 5242880 | tf_op jit(solution)/shard_map/pallas_call | solution.py:53
  151.5 5.8 %collective-permute-done.36 = bf16[4,32,1280]{2,1,0:T(8,128)(2,1)S(1)} collective-permute-done((bf16[4,32,1280]{2,1,0:T(8,128)(2,1)S(1)}, bf16[4,32,1280]{2,1,0:T(8,128)(2,1)S(1)}, u32[]{:S(2)}, u32[]{:S(2)}) %collective-permute-start.36) | collective-permute-done | bytes 327712 | tf_op jit(solution)/shard_map/ppermute | solution.py:401
  158.2 6.9 %collective-permute-done.38 = bf16[4,32,1280]{2,1,0:T(8,128)(2,1)S(1)} collective-permute-done((bf16[4,32,1280]{2,1,0:T(8,128)(2,1)S(1)}, bf16[4,32,1280]{2,1,0:T(8,128)(2,1)S(1)}, u32[]{:S(2)}, u32[]{:S(2)}) %collective-permute-start.38) | collective-permute-done | bytes 327712 | tf_op jit(solution)/shard_map/ppermute | solution.py:401
  168.3 2.7 %collective-permute-done.37.refs_2_ = bf16[4,32,1280]{2,1,0:T(8,128)(2,1)S(1)} collective-permute-done((bf16[4,32,1280]{2,1,0:T(8,128)(2,1)S(1)}, bf16[4,32,1280]{2,1,0:T(8,128)(2,1)S(1)}, u32[]{:S(2)}, u32[]{:S(2)}) %collective-permute-start.37) | collective-permute-done | bytes 327712 | tf_op jit(solution)/shard_map/ppermute | solution.py:401
  171.1 2.6 %collective-permute-done.39.refs_3_ = bf16[4,32,1280]{2,1,0:T(8,128)(2,1)S(1)} collective-permute-done((bf16[4,32,1280]{2,1,0:T(8,128)(2,1)}, bf16[4,32,1280]{2,1,0:T(8,128)(2,1)S(1)}, u32[]{:S(2)}, u32[]{:S(2)}) %collective-permute-start.39) | collective-permute-done | bytes 327712 | tf_op jit(solution)/shard_map/ppermute | solution.py:401
  176.0 2.5 %collective-permute-done.48 = bf16[128,1024]{1,0:T(8,128)(2,1)} collective-permute-done((bf16[128,1024]{1,0:T(8,128)(2,1)S(1)}, bf16[128,1024]{1,0:T(8,128)(2,1)}, u32[]{:S(2)}, u32[]{:S(2)}) %collective-permute-start.48) | collective-permute-done | bytes 262176 | tf_op jit(solution)/shard_map/ppermute | solution.py:398
  178.4 14.8 %collective-permute-done.47 = bf16[128,1024]{1,0:T(8,128)(2,1)} collective-permute-done((bf16[128,1024]{1,0:T(8,128)(2,1)S(1)}, bf16[128,1024]{1,0:T(8,128)(2,1)}, u32[]{:S(2)}, u32[]{:S(2)}) %collective-permute-start.47) | collective-permute-done | bytes 262176 | tf_op jit(solution)/shard_map/ppermute | solution.py:398
  201.5 2.4 %collective-permute-done.49.refs_1_ = bf16[128,1024]{1,0:T(8,128)(2,1)S(1)} collective-permute-done((bf16[128,1024]{1,0:T(8,128)(2,1)S(1)}, bf16[128,1024]{1,0:T(8,128)(2,1)S(1)}, u32[]{:S(2)}, u32[]{:S(2)}) %collective-permute-start.49) | collective-permute-done | bytes 262176 | tf_op jit(solution)/shard_map/ppermute | solution.py:401
  205.4 2.0 collective-permute-done.50.refs_2_
  207.4 2.4 %collective-permute-done.51.refs_3_ = bf16[128,1024]{1,0:T(8,128)(2,1)S(1)} collective-permute-done((bf16[128,1024]{1,0:T(8,128)(2,1)S(1)}, bf16[128,1024]{1,0:T(8,128)(2,1)S(1)}, u32[]{:S(2)}, u32[]{:S(2)}) %collective-permute-start.51) | collective-permute-done | bytes 262176 | tf_op jit(solution)/shard_map/ppermute | solution.py:401
  211.9 2.3 %collective-permute-done.45.refs_2_ = bf16[32,2560]{1,0:T(8,128)(2,1)S(1)} collective-permute-done((bf16[32,2560]{1,0:T(8,128)(2,1)S(1)}, bf16[32,2560]{1,0:T(8,128)(2,1)S(1)}, u32[]{:S(2)}, u32[]{:S(2)}) %collective-permute-start.45) | collective-permute-done | bytes 163872 | tf_op jit(solution)/shard_map/ppermute | solution.py:401
  (237 shorter events, 87.2 us)
Async XLA Ops:
  2.9 43.5 %collective-permute-start.3 = (bf16[512,1024]{1,0:T(8,128)(2,1)S(1)}, bf16[512,1024]{1,0:T(8,128)(2,1)S(1)}, u32[]{:S(2)}, u32[]{:S(2)}) collective-permute-start(bf16[512,1024]{1,0:T(8,128)(2,1)S(1)} %get-tuple-element.68.refs_2_.refs_16_.refs_9_), channel_id=1, source_target_pairs={{0,1},{1,0},{2,3},{3,2},{4,5},{5,4},{6,7},{7,6},{8,9},{9,8},{10,11... | collective-permute-start | bytes 3145736 | tf_op jit(solution)/shard_map/ppermute | solution.py:404
  3.3 16.2 %collective-permute-start = (bf16[128,1024]{1,0:T(8,128)(2,1)S(1)}, bf16[128,1024]{1,0:T(8,128)(2,1)S(1)}, u32[]{:S(2)}, u32[]{:S(2)}) collective-permute-start(bf16[128,1024]{1,0:T(8,128)(2,1)S(1)} %get-tuple-element.67), channel_id=1, source_target_pairs={{0,4},{1,5},{2,6},{3,7},{4,0},{5,1},{6,2},{7,3},{8,12},{9,13},{10,... | collective-permute-start | bytes 786440 | tf_op jit(solution)/shard_map/ppermute | solution.py:398
  19.5 26.8 %collective-permute-start.1 = (bf16[128,1024]{1,0:T(8,128)(2,1)S(1)}, bf16[128,1024]{1,0:T(8,128)(2,1)S(1)}, u32[]{:S(2)}, u32[]{:S(2)}) collective-permute-start(bf16[128,1024]{1,0:T(8,128)(2,1)S(1)} %get-tuple-element.67), channel_id=1, source_target_pairs={{0,2},{1,3},{2,4},{3,5},{4,6},{5,7},{6,0},{7,1},{8,10},{9,11},{10,... | collective-permute-start | bytes 786440 | tf_op jit(solution)/shard_map/ppermute | solution.py:398
  20.3 26.0 %collective-permute-start.2 = (bf16[128,1024]{1,0:T(8,128)(2,1)S(1)}, bf16[128,1024]{1,0:T(8,128)(2,1)S(1)}, u32[]{:S(2)}, u32[]{:S(2)}) collective-permute-start(bf16[128,1024]{1,0:T(8,128)(2,1)S(1)} %get-tuple-element.67), channel_id=1, source_target_pairs={{0,6},{1,7},{2,0},{3,1},{4,2},{5,3},{6,4},{7,5},{8,14},{9,15},{10,... | collective-permute-start | bytes 786440 | tf_op jit(solution)/shard_map/ppermute | solution.py:398
  23.3 23.0 %collective-permute-start.4 = (bf16[128,1024]{1,0:T(8,128)(2,1)S(1)}, bf16[128,1024]{1,0:T(8,128)(2,1)S(1)}, u32[]{:S(2)}, u32[]{:S(2)}) collective-permute-start(bf16[128,1024]{1,0:T(8,128)(2,1)S(1)} %collective-permute-done.refs_3_.refs_17_.refs_10_), channel_id=1, source_target_pairs={{0,8},{8,0},{16,24},{24,16},{1,9},{9,1},{17,25},{25,17},{2,10},{10... | collective-permute-start | bytes 786440 | tf_op jit(solution)/shard_map/ppermute | solution.py:401
  24.9 21.5 %collective-permute-start.5 = (bf16[128,1024]{1,0:T(8,128)(2,1)S(1)}, bf16[128,1024]{1,0:T(8,128)(2,1)S(1)}, u32[]{:S(2)}, u32[]{:S(2)}) collective-permute-start(bf16[128,1024]{1,0:T(8,128)(2,1)S(1)} %collective-permute-done.refs_3_.refs_17_.refs_10_), channel_id=1, source_target_pairs={{0,16},{8,24},{16,0},{24,8},{1,17},{9,25},{17,1},{25,9},{2,18},{10... | collective-permute-start | bytes 786440 | tf_op jit(solution)/shard_map/ppermute | solution.py:401
  47.7 14.1 %collective-permute-start.8 = (bf16[256,1024]{1,0:T(8,128)(2,1)S(1)}, bf16[256,1024]{1,0:T(8,128)(2,1)S(1)}, u32[]{:S(2)}, u32[]{:S(2)}) collective-permute-start(bf16[256,1024]{1,0:T(8,128)(2,1)S(1)} %constant_dynamic-update-slice_fusion.refs_8_.refs_22_.refs_11_), channel_id=1, source_target_pairs={{0,8},{8,0},{16,24},{24,16},{1,9},{9,1},{17,25},{25,17},{2,10},{10... | collective-permute-start | bytes 1572872 | tf_op jit(solution)/shard_map/ppermute | solution.py:401
  48.2 14.8 %collective-permute-start.9 = (bf16[256,1024]{1,0:T(8,128)(2,1)S(1)}, bf16[256,1024]{1,0:T(8,128)(2,1)S(1)}, u32[]{:S(2)}, u32[]{:S(2)}) collective-permute-start(bf16[256,1024]{1,0:T(8,128)(2,1)S(1)} %constant_dynamic-update-slice_fusion.refs_8_.refs_22_.refs_11_), channel_id=1, source_target_pairs={{0,16},{8,24},{16,0},{24,8},{1,17},{9,25},{17,1},{25,9},{2,18},{10... | collective-permute-start | bytes 1572872 | tf_op jit(solution)/shard_map/ppermute | solution.py:401
  48.6 51.3 %all-to-all-start = ((bf16[8,48,1024]{2,1,0:T(8,128)(2,1)}), bf16[8,48,1024]{2,1,0:T(8,128)(2,1)S(1)}, u32[]{:S(2)}, u32[]{:S(2)}) async-start(bf16[8,48,1024]{2,1,0:T(8,128)(2,1)} %bitcast.4), calls=%async_computation | async-start | bytes 1572864 | tf_op jit(solution)/shard_map/all_to_all | solution.py:448
  65.3 16.0 %collective-permute-start.12 = (bf16[256,512]{1,0:T(8,128)(2,1)}, bf16[256,512]{1,0:T(8,128)(2,1)}, u32[]{:S(2)}, u32[]{:S(2)}) collective-permute-start(bf16[256,512]{1,0:T(8,128)(2,1)} %copy-done.50), channel_id=1, source_target_pairs={{0,1},{1,0},{2,3},{3,2},{4,5},{5,4},{6,7},{7,6},{8,9},{9,8},{10,11... | collective-permute-start | bytes 786440 | tf_op jit(solution)/shard_map/ppermute | solution.py:404
  65.3 17.6 %collective-permute-start.13 = (bf16[256,512]{1,0:T(8,128)(2,1)}, bf16[256,512]{1,0:T(8,128)(2,1)}, u32[]{:S(2)}, u32[]{:S(2)}) collective-permute-start(bf16[256,512]{1,0:T(8,128)(2,1)} %copy-done.46), channel_id=1, source_target_pairs={{0,1},{1,0},{2,3},{3,2},{4,5},{5,4},{6,7},{7,6},{8,9},{9,8},{10,11... | collective-permute-start | bytes 786440 | tf_op jit(solution)/shard_map/ppermute | solution.py:404
  66.4 16.9 %collective-permute-start.14 = (bf16[128,1024]{1,0:T(8,128)(2,1)}, bf16[128,1024]{1,0:T(8,128)(2,1)}, u32[]{:S(2)}, u32[]{:S(2)}) collective-permute-start(bf16[128,1024]{1,0:T(8,128)(2,1)} %copy-done.23), channel_id=1, source_target_pairs={{0,1},{1,0},{2,3},{3,2},{4,5},{5,4},{6,7},{7,6},{8,9},{9,8},{10,11... | collective-permute-start | bytes 786440 | tf_op jit(solution)/shard_map/ppermute | solution.py:404
  69.2 17.3 %collective-permute-start.15 = (bf16[128,1024]{1,0:T(8,128)(2,1)}, bf16[128,1024]{1,0:T(8,128)(2,1)S(1)}, u32[]{:S(2)}, u32[]{:S(2)}) collective-permute-start(bf16[128,1024]{1,0:T(8,128)(2,1)} %copy-done.8), channel_id=1, source_target_pairs={{0,1},{1,0},{2,3},{3,2},{4,5},{5,4},{6,7},{7,6},{8,9},{9,8},{10,11... | collective-permute-start | bytes 786440 | tf_op jit(solution)/shard_map/ppermute | solution.py:404
  81.2 14.4 %collective-permute-start.25 = (bf16[256,1024]{1,0:T(8,128)(2,1)S(1)}, bf16[256,1024]{1,0:T(8,128)(2,1)S(1)}, u32[]{:S(2)}, u32[]{:S(2)}) collective-permute-start(bf16[256,1024]{1,0:T(8,128)(2,1)S(1)} %copy-done.15), channel_id=1, source_target_pairs={{0,8},{8,0},{16,24},{24,16},{1,9},{9,1},{17,25},{25,17},{2,10},{10... | collective-permute-start | bytes 1572872 | tf_op jit(solution)/shard_map/ppermute | solution.py:401
  82.8 14.1 %collective-permute-start.26 = (bf16[256,1024]{1,0:T(8,128)(2,1)S(1)}, bf16[256,1024]{1,0:T(8,128)(2,1)S(1)}, u32[]{:S(2)}, u32[]{:S(2)}) collective-permute-start(bf16[256,1024]{1,0:T(8,128)(2,1)S(1)} %copy-done.15), channel_id=1, source_target_pairs={{0,16},{8,24},{16,0},{24,8},{1,17},{9,25},{17,1},{25,9},{2,18},{10... | collective-permute-start | bytes 1572872 | tf_op jit(solution)/shard_map/ppermute | solution.py:401
  86.1 15.5 %collective-permute-start.19 = (bf16[256,1024]{1,0:T(8,128)(2,1)S(1)}, bf16[256,1024]{1,0:T(8,128)(2,1)}, u32[]{:S(2)}, u32[]{:S(2)}) collective-permute-start(bf16[256,1024]{1,0:T(8,128)(2,1)S(1)} %constant_dynamic-update-slice_fusion.refs_8_.refs_22_.refs_11_), channel_id=1, source_target_pairs={{0,1},{1,0},{2,3},{3,2},{4,5},{5,4},{6,7},{7,6},{8,9},{9,8},{10,11... | collective-permute-start | bytes 1572872 | tf_op jit(solution)/shard_map/ppermute | solution.py:404
  86.5 17.1 %collective-permute-start.20 = (bf16[256,1024]{1,0:T(8,128)(2,1)S(1)}, bf16[256,1024]{1,0:T(8,128)(2,1)}, u32[]{:S(2)}, u32[]{:S(2)}) collective-permute-start(bf16[256,1024]{1,0:T(8,128)(2,1)S(1)} %collective-permute-done.8.refs_9_.refs_23_), channel_id=1, source_target_pairs={{0,1},{1,0},{2,3},{3,2},{4,5},{5,4},{6,7},{7,6},{8,9},{9,8},{10,11... | collective-permute-start | bytes 1572872 | tf_op jit(solution)/shard_map/ppermute | solution.py:404
  87.4 16.3 %collective-permute-start.21 = (bf16[256,1024]{1,0:T(8,128)(2,1)S(1)}, bf16[256,1024]{1,0:T(8,128)(2,1)}, u32[]{:S(2)}, u32[]{:S(2)}) collective-permute-start(bf16[256,1024]{1,0:T(8,128)(2,1)S(1)} %collective-permute-done.9.refs_10_.refs_24_), channel_id=1, source_target_pairs={{0,1},{1,0},{2,3},{3,2},{4,5},{5,4},{6,7},{7,6},{8,9},{9,8},{10,11... | collective-permute-start | bytes 1572872 | tf_op jit(solution)/shard_map/ppermute | solution.py:404
  101.6 35.0 %collective-permute-start.28 = (bf16[256,512]{1,0:T(8,128)(2,1)}, bf16[256,512]{1,0:T(8,128)(2,1)S(1)}, u32[]{:S(2)}, u32[]{:S(2)}) collective-permute-start(bf16[256,512]{1,0:T(8,128)(2,1)} %slice.26), channel_id=1, source_target_pairs={{0,16},{8,24},{16,0},{24,8},{1,17},{9,25},{17,1},{25,9},{2,18},{10... | collective-permute-start | bytes 786440 | tf_op jit(solution)/shard_map/ppermute | solution.py:401
  102.4 34.2 %collective-permute-start.29 = (bf16[256,512]{1,0:T(8,128)(2,1)}, bf16[256,512]{1,0:T(8,128)(2,1)S(1)}, u32[]{:S(2)}, u32[]{:S(2)}) collective-permute-start(bf16[256,512]{1,0:T(8,128)(2,1)} %slice.27), channel_id=1, source_target_pairs={{0,8},{8,0},{16,24},{24,16},{1,9},{9,1},{17,25},{25,17},{2,10},{10... | collective-permute-start | bytes 786440 | tf_op jit(solution)/shard_map/ppermute | solution.py:401
  128.0 15.9 %collective-permute-start.27 = (bf16[256,2048]{1,0:T(8,128)(2,1)S(1)}, bf16[256,2048]{1,0:T(8,128)(2,1)S(1)}, u32[]{:S(2)}, u32[]{:S(2)}) collective-permute-start(bf16[256,2048]{1,0:T(8,128)(2,1)S(1)} %shard_map.116.refs_4_), channel_id=1, source_target_pairs={{0,1},{1,0},{2,3},{3,2},{4,5},{5,4},{6,7},{7,6},{8,9},{9,8},{10,11... | collective-permute-start | bytes 3145736 | tf_op jit(solution)/shard_map/ppermute | solution.py:404
  147.6 19.7 %collective-permute-start.35 = (bf16[4,32,1280]{2,1,0:T(8,128)(2,1)S(1)}, bf16[4,32,1280]{2,1,0:T(8,128)(2,1)S(1)}, u32[]{:S(2)}, u32[]{:S(2)}) collective-permute-start(bf16[4,32,1280]{2,1,0:T(8,128)(2,1)S(1)} %get-tuple-element.108), channel_id=1, source_target_pairs={{0,8},{8,0},{16,24},{24,16},{1,9},{9,1},{17,25},{25,17},{2,10},{10... | collective-permute-start | bytes 983048 | tf_op jit(solution)/shard_map/ppermute | solution.py:401
  148.8 16.4 %collective-permute-start.38 = (bf16[4,32,1280]{2,1,0:T(8,128)(2,1)S(1)}, bf16[4,32,1280]{2,1,0:T(8,128)(2,1)S(1)}, u32[]{:S(2)}, u32[]{:S(2)}) collective-permute-start(bf16[4,32,1280]{2,1,0:T(8,128)(2,1)S(1)} %get-tuple-element.112), channel_id=1, source_target_pairs={{0,8},{8,0},{16,24},{24,16},{1,9},{9,1},{17,25},{25,17},{2,10},{10... | collective-permute-start | bytes 983048 | tf_op jit(solution)/shard_map/ppermute | solution.py:401
  149.6 18.7 %collective-permute-start.40 = (bf16[4,32,1280]{2,1,0:T(8,128)(2,1)S(1)}, bf16[4,32,1280]{2,1,0:T(8,128)(2,1)S(1)}, u32[]{:S(2)}, u32[]{:S(2)}) collective-permute-start(bf16[4,32,1280]{2,1,0:T(8,128)(2,1)S(1)} %get-tuple-element.113), channel_id=1, source_target_pairs={{0,16},{8,24},{16,0},{24,8},{1,17},{9,25},{17,1},{25,9},{2,18},{10... | collective-permute-start | bytes 983048 | tf_op jit(solution)/shard_map/ppermute | solution.py:401
  151.1 16.2 %collective-permute-start.34 = (bf16[128,1024]{1,0:T(8,128)(2,1)S(1)}, bf16[128,1024]{1,0:T(8,128)(2,1)S(1)}, u32[]{:S(2)}, u32[]{:S(2)}) collective-permute-start(bf16[128,1024]{1,0:T(8,128)(2,1)S(1)} %get-tuple-element.106), channel_id=1, source_target_pairs={{0,6},{1,7},{2,0},{3,1},{4,2},{5,3},{6,4},{7,5},{8,14},{9,15},{10,... | collective-permute-start | bytes 786440 | tf_op jit(solution)/shard_map/ppermute | solution.py:398
  157.4 13.7 %collective-permute-start.37 = (bf16[4,32,1280]{2,1,0:T(8,128)(2,1)S(1)}, bf16[4,32,1280]{2,1,0:T(8,128)(2,1)S(1)}, u32[]{:S(2)}, u32[]{:S(2)}) collective-permute-start(bf16[4,32,1280]{2,1,0:T(8,128)(2,1)S(1)} %add_convert_fusion.1), channel_id=1, source_target_pairs={{0,8},{8,0},{16,24},{24,16},{1,9},{9,1},{17,25},{25,17},{2,10},{10... | collective-permute-start | bytes 983048 | tf_op jit(solution)/shard_map/ppermute | solution.py:401
  167.2 26.1 %collective-permute-start.47 = (bf16[128,1024]{1,0:T(8,128)(2,1)S(1)}, bf16[128,1024]{1,0:T(8,128)(2,1)}, u32[]{:S(2)}, u32[]{:S(2)}) collective-permute-start(bf16[128,1024]{1,0:T(8,128)(2,1)S(1)} %get-tuple-element.121), channel_id=1, source_target_pairs={{0,4},{1,5},{2,6},{3,7},{4,0},{5,1},{6,2},{7,3},{8,12},{9,13},{10,... | collective-permute-start | bytes 786440 | tf_op jit(solution)/shard_map/ppermute | solution.py:398
  173.9 22.8 %collective-permute-start.43 = (bf16[32,2560]{1,0:T(8,128)(2,1)S(1)}, bf16[32,2560]{1,0:T(8,128)(2,1)S(1)}, u32[]{:S(2)}, u32[]{:S(2)}) collective-permute-start(bf16[32,2560]{1,0:T(8,128)(2,1)S(1)} %get-tuple-element.117), channel_id=1, source_target_pairs={{0,6},{1,7},{2,0},{3,1},{4,2},{5,3},{6,4},{7,5},{8,14},{9,15},{10,... | collective-permute-start | bytes 491528 | tf_op jit(solution)/shard_map/ppermute | solution.py:398
  175.2 24.0 %collective-permute-start.42 = (bf16[32,2560]{1,0:T(8,128)(2,1)S(1)}, bf16[32,2560]{1,0:T(8,128)(2,1)S(1)}, u32[]{:S(2)}, u32[]{:S(2)}) collective-permute-start(bf16[32,2560]{1,0:T(8,128)(2,1)S(1)} %get-tuple-element.116), channel_id=1, source_target_pairs={{0,4},{1,5},{2,6},{3,7},{4,0},{5,1},{6,2},{7,3},{8,12},{9,13},{10,... | collective-permute-start | bytes 491528 | tf_op jit(solution)/shard_map/ppermute | solution.py:398
  175.3 24.0 %collective-permute-start.41 = (bf16[32,2560]{1,0:T(8,128)(2,1)S(1)}, bf16[32,2560]{1,0:T(8,128)(2,1)S(1)}, u32[]{:S(2)}, u32[]{:S(2)}) collective-permute-start(bf16[32,2560]{1,0:T(8,128)(2,1)S(1)} %get-tuple-element.115), channel_id=1, source_target_pairs={{0,2},{1,3},{2,4},{3,5},{4,6},{5,7},{6,0},{7,1},{8,10},{9,11},{10,... | collective-permute-start | bytes 491528 | tf_op jit(solution)/shard_map/ppermute | solution.py:398
  196.7 13.1 %collective-permute-start.51 = (bf16[128,1024]{1,0:T(8,128)(2,1)S(1)}, bf16[128,1024]{1,0:T(8,128)(2,1)S(1)}, u32[]{:S(2)}, u32[]{:S(2)}) collective-permute-start(bf16[128,1024]{1,0:T(8,128)(2,1)S(1)} %multiply_convert_fusion.refs_0_), channel_id=1, source_target_pairs={{0,24},{8,16},{16,8},{24,0},{1,25},{9,17},{17,9},{25,1},{2,26},{10... | collective-permute-start | bytes 786440 | tf_op jit(solution)/shard_map/ppermute | solution.py:401
  200.2 14.0 %collective-permute-start.45 = (bf16[32,2560]{1,0:T(8,128)(2,1)S(1)}, bf16[32,2560]{1,0:T(8,128)(2,1)S(1)}, u32[]{:S(2)}, u32[]{:S(2)}) collective-permute-start(bf16[32,2560]{1,0:T(8,128)(2,1)S(1)} %add_convert_fusion.2.refs_0_), channel_id=1, source_target_pairs={{0,16},{8,24},{16,0},{24,8},{1,17},{9,25},{17,1},{25,9},{2,18},{10... | collective-permute-start | bytes 491528 | tf_op jit(solution)/shard_map/ppermute | solution.py:401
  (89 other events, 540.7 us)

commit v6 on v5

--- a/solution.py
+++ b/solution.py
@@ -143,13 +143,9 @@
     quarter_inv[...] = inverse
 
 
-def score_kernel(groups, owners, share, chunks, places, final, cand, unit_hbm, *refs):
+def score_kernel(groups, owners, share, chunks, places, cand, inv_len, unit_hbm, yn_hbm, *refs):
     count = len(places)
-    if final:
-        inv_len, partial, yn_hbm, *refs = refs
-        pieces, (tags, up, up_keep, up_give, table, unit_b, sems, spread, unit) = refs[:count], refs[count:]
-    else:
-        pieces, (partial_out, table, unit_b, sems) = refs[:count], refs[count:]
+    pieces, (tags, up, up_keep, up_give, table, spread, unit_b, unit, sems) = refs[:count], refs[count:]
     chips = owners // 2
     vocab_dev = share * groups
     grp, core = lax.axis_index("grp"), lax.axis_index("seq") % 2
@@ -172,9 +168,8 @@
         copy = pltpu.make_async_copy(pieces[n], table.at[pl.ds(at, rows), pl.ds(left, wide)], sems.at[n])
         copy.start()
         copies.setdefault(tuple(key), []).append(copy)
-    if final:
-        load_yn = pltpu.make_async_copy(yn_hbm, unit, sems.at[count + 1])
-        load_yn.start()
+    load_yn = pltpu.make_async_copy(yn_hbm, unit, sems.at[count + 1])
+    load_yn.start()
     ids = owner_ids(owners)
     lane = iota((1, 128), 1)
     owner = jnp.full((1, 128), -1, i32)
@@ -215,23 +210,16 @@
     for key in copies:
         for copy in copies[key]:
             copy.wait()
-        if key[0] != int(final):
-            continue
         at, rows, _ = runs(key)
         product = dot(yb, table[at : at + rows], NT)
         for j, off, step, hit in tiles(key):
             value[j].append(jnp.where(hit, product[:, off : off + step], 0.0))
-    logits = partial[...] if final else jnp.zeros((tok, 128), f32)
+    logits = jnp.zeros((tok, 128), f32)
     for j in range(owners):
-        if not value[j]:
-            continue
         total = value[j][0]
         for part in value[j][1:]:
             total = total + part
         logits = jnp.where(lane == j, jnp.sum(total, -1, keepdims=True), logits)
-    if not final:
-        partial_out[...] = logits
-        return
     exponent = jnp.where(chosen >= 0, jnp.exp(logits / softmax_warmth), 0.0)
     coef = (exponent / jnp.sum(exponent, -1, keepdims=True) - first) / softmax_warmth
     tags[:owners] = coef.T[:owners]
@@ -324,29 +312,26 @@
     rows = whole.shape[0] // chips
     fine = rows // groups
     half = whole.shape[1] // 2
+    base, by_one, by_two, one_right, two_left = outs
     for z in range(chips):
-        for k in range(groups):
-            piece = whole[pl.ds(pl.multiple_of(z * rows + (grp ^ k) * fine, fine), fine)]
-            if k == 0:
-                outs[0][z] = piece
-            else:
-                outs[2 * k - 1][z] = piece[:, :half]
-                outs[2 * k][z] = piece[:, half:]
-
-
-def sum_kernel(halves, base, *refs):
-    parts, outs = refs[: 2 * halves], refs[2 * halves :]
+        piece = [whole[pl.ds(pl.multiple_of(z * rows + (grp ^ k) * fine, fine), fine)] for k in range(groups)]
+        base[z] = piece[0]
+        by_one[0, z], by_one[1, z] = piece[3][:, :half], piece[1][:, :half]
+        by_two[0, z], by_two[1, z] = piece[3][:, half:], piece[2][:, half:]
+        one_right[z], two_left[z] = piece[1][:, half:], piece[2][:, :half]
+
+
+def sum_kernel(base, by_one, by_two, one_right, two_left, *outs):
     chips = len(outs)
     chip = lax.axis_index("seq") // 2
     half = base.shape[2] // 2
     for d in range(chips):
         z = lax.rem(chip + d, chips)
-        for i in range(2):
-            cols = slice(i * half, (i + 1) * half)
-            total = base[z][:, cols].astype(f32)
-            for n in range(halves):
-                total += parts[2 * n + i][z].astype(f32)
-            outs[d][:, cols] = total.astype(b16)
+        own = base[z].astype(f32)
+        left = own[:, :half] + by_one[1, z].astype(f32) + two_left[z].astype(f32)
+        right = own[:, half:] + by_two[1, z].astype(f32) + one_right[z].astype(f32)
+        outs[d][:, :half] = left.astype(b16)
+        outs[d][:, half:] = right.astype(b16)
 
 
 def pair_kernel(x, y, *outs):
@@ -403,11 +388,11 @@
     def to_core(x):
         return lax.ppermute(x, "seq", [(a, a ^ 1) for a in range(owners)])
 
-    def gather_groups(x, near=None):
+    def gather_groups(x):
         wide = x.shape[1]
         if groups != 4:
             return [(k, 0, wide, to_group(x, k) if k else x) for k in range(groups)]
-        one, two = near or [to_group(x, k) for k in (1, 2)]
+        one, two = to_group(x, 1), to_group(x, 2)
         half = wide // 2
         left, right = to_group(one[:, :half], 2), to_group(two[:, half:], 1)
         return [(0, 0, wide, x), (1, 0, wide, one), (2, 0, wide, two), (3, 0, half, left), (3, half, half, right)]
@@ -417,10 +402,8 @@
         [((vocab_dev, width), b16), ((share, width), b16), ((share, 1), f32)],
         [VMEM], [item_table], flops=8 * vocab_dev * width, nbytes=5 * vocab_dev * width, room=8,
     )
-    chunks = [[d for d in range(1, chips) if d % 2 == 0], [d for d in range(1, chips) if d % 2]]
-    even = [to_chip(quarter, d) for d in chunks[0]]
-    even, later = lax.optimization_barrier((even, quarter))
-    odd = [to_chip(later, d) for d in chunks[1]]
+    chunks = [list(range(1, chips))]
+    got = [to_chip(quarter, d) for d in chunks[0]]
     far_own = to_core(own)
     outs = [
         ((tok, width // 2), b16), ((tok, width // 2), b16), ((tok, 4 * hidden), b16), ((tok, 4 * hidden), b16),
@@ -434,15 +417,15 @@
         flops=2 * tok * width * 6 * hidden, nbytes=24 * tok * width + 10 * width * hidden, room=28,
     )
 
-    even = jnp.concatenate(even, 0) if len(even) > 1 else even[0]
-    near = [to_group(even, k) for k in (1, 2)]
-    odd, far_own, unit_b, near = lax.optimization_barrier((odd, far_own, unit_b, near))
-    others = [even, jnp.concatenate(odd, 0)]
+    got, far_own, unit_b = lax.optimization_barrier((got, far_own, unit_b))
+    others = [jnp.concatenate(got, 0)]
     pieces = [(0, -1, 0, 0, width, own)]
     for j, x in enumerate(others):
-        pieces += [(0, j) + p for p in gather_groups(x, None if j else near)]
+        pieces += [(0, j) + p for p in gather_groups(x)]
     pieces = pieces + [(1,) + p[1:5] + (to_core(p[5]) if p[1] >= 0 else far_own,) for p in pieces]
     near = [p[5] for p in pieces if p[2] == 0]
+    sent_unit, _ = lax.optimization_barrier((unit_b, [p[5] for p in pieces if p[0] == 0]))
+    unit_sent = gather_groups(sent_unit)
     outgoing, _ = lax.optimization_barrier((outgoing, others))
 
     arrived = lax.all_to_all(
@@ -456,26 +439,14 @@
     candidates = jnp.concatenate([history[:, None], negatives], 1)
     vocab = vocab_dev * owners
     far_give, far_gated = to_core(give), to_core(gated)
-    mine = [p for p in pieces if p[0] == 0]
-    partial, = call(
-        lambda *refs: score_kernel(groups, owners, share, chunks, [p[:5] for p in mine], False, *refs),
-        [((tok, 128), f32)], [VMEM] + [ANY] * (len(mine) + 1), [candidates, unit_b] + [p[5] for p in mine],
-        [pltpu.VMEM((vocab // 2, width), b16), pltpu.VMEM((tok, width), b16),
-         pltpu.SemaphoreType.DMA((len(mine) + 1,))],
-        flops=tok * width * vocab, nbytes=vocab * width + 2 * tok * width, room=14 if groups == 4 else 40,
-    )
-    sent_unit, _ = lax.optimization_barrier((unit_b, partial))
-    unit_sent = gather_groups(sent_unit)
-    layer_out, partial, far_give, far_gated = lax.optimization_barrier((layer_out, partial, far_give, far_gated))
-    order = [p for p in pieces if p[0] == 1] + mine
+    layer_out, score_unit, far_give, far_gated = lax.optimization_barrier((layer_out, unit, far_give, far_gated))
     tags, up, up_keep, up_give = call(
-        lambda *refs: score_kernel(groups, owners, share, chunks, [p[:5] for p in order], True, *refs),
+        lambda *refs: score_kernel(groups, owners, share, chunks, [p[:5] for p in pieces], *refs),
         [((2 * owners, tok), f32), ((tok, width), b16), ((tok, width // 2), b16), ((tok, width // 2), b16)],
-        [VMEM, ANY, VMEM, VMEM] + [ANY] * (len(order) + 1),
-        [candidates, unit_b, inv_len, partial, unit] + [p[5] for p in order],
-        [pltpu.VMEM((vocab, width), b16), pltpu.VMEM((tok, width), b16), pltpu.SemaphoreType.DMA((len(order) + 2,)),
-         pltpu.VMEM((tok, vocab), b16), pltpu.VMEM((tok, width), f32)],
-        flops=3 * tok * width * vocab, nbytes=2 * vocab * width + 12 * tok * width, room=24 if groups == 4 else 58,
+        [VMEM] * 2 + [ANY] * (len(pieces) + 2), [candidates, inv_len, unit_b, score_unit] + [p[5] for p in pieces],
+        [pltpu.VMEM((vocab, width), b16), pltpu.VMEM((tok, vocab), b16), pltpu.VMEM((tok, width), b16),
+         pltpu.VMEM((tok, width), f32), pltpu.SemaphoreType.DMA((len(pieces) + 2,))],
+        flops=4 * tok * width * vocab, nbytes=2 * vocab * width + 12 * tok * width, room=24 if groups == 4 else 58,
     )
     units = [p[3] for p in unit_sent]
 
@@ -505,16 +476,15 @@
         split = (chips, fine, half)
         parts = call(
             lambda *refs: weight_kernel(groups, owners, *refs),
-            [(block, b16)] + [(split, b16)] * 6, [VMEM] * 8,
+            [(block, b16)] + [((2,) + split, b16)] * 2 + [(split, b16)] * 2, [VMEM] * 8,
             [keep, far[0], up_keep, far[1], grad, far[2], gated, far[3]],
             [pltpu.VMEM((width // 2, 5 * hidden), b16)],
             flops=2 * tok * width * 5 * hidden, nbytes=20 * tok * width, room=14,
         )
-        left, right = to_group(parts[5], 1), to_group(parts[6], 2)
-        one_left, two_right = to_group(parts[1], 1), to_group(parts[4], 2)
-        one_right = (parts[2].astype(f32) + right.astype(f32)).astype(b16)
-        two_left = (parts[3].astype(f32) + left.astype(f32)).astype(b16)
-        arrived = [one_left, to_group(one_right, 1), to_group(two_left, 2), two_right]
+        by_one, by_two = to_group(parts[1], 1), to_group(parts[2], 2)
+        one_right = (parts[3].astype(f32) + by_two[0].astype(f32)).astype(b16)
+        two_left = (parts[4].astype(f32) + by_one[0].astype(f32)).astype(b16)
+        arrived = [by_one, by_two, to_group(one_right, 1), to_group(two_left, 2)]
     else:
         def both(x, y):
             return jnp.concatenate([x, y], 0)
@@ -546,7 +516,7 @@
     if groups == 4:
         base, _ = lax.optimization_barrier((parts[0], come[0]))
         sums = call(
-            lambda *refs: sum_kernel(2, *refs), [((fine, 5 * hidden), b16)] * chips, [VMEM] * 5, [base] + arrived,
+            sum_kernel, [((fine, 5 * hidden), b16)] * chips, [VMEM] * 5, [base] + arrived,
             flops=chips * fine * 5 * hidden, nbytes=40 * chips * fine * hidden, room=10,
         )
     else:

time: 216 us -> 192 us (0.89)
  waiting for transfers between devices: 84.7 us -> 63.3 us
  starting transfers between devices: 48 us -> 63.8 us
  local copies, waits for them, and re-layouts: 46.9 us -> 32.9 us
  Pallas kernels: 32.3 us -> 27 us
    ppermute x9, waiting for transfers between devices: 31 us -> 12.8 us  [to_chip(): return lax.ppermute(x, 'seq', pairs)]
    ppermute x9, starting transfers between devices: 11 us -> 28.6 us  [to_chip(): return lax.ppermute(x, 'seq', pairs)]
    unnamed x137 -> x82, local copies, waits for them, and re-layouts: 42 us -> 27.5 us
    ppermute x27 -> x21, starting transfers between devices: 30.4 us -> 25.1 us  [to_group(): return lax.ppermute(x, 'grp', [(a, a ^ k) for a in range(groups)])]
    pallas_call x12 -> x11, Pallas kernels: 32.3 us -> 27 us  [call(): pl.pallas_call(kernel, out_shape=[jax.ShapeDtypeStruct(s, t) for s, t in...]
    all_to_all x1, starting transfers between devices: 3.55 us -> 8.42 us  [body(): lax.all_to_all(outgoing.reshape(owners, slot, width), 'seq', 0, 0, tiled=...]
    ppermute x16 -> x11, waiting for transfers between devices: 3.55 us -> 0.03 us  [to_core(): return lax.ppermute(x, 'seq', [(a, a ^ 1) for a in range(owners)])]
    slice x6 -> x4, local copies, waits for them, and re-layouts: 4.72 us -> 3.98 us  [gather_groups(): left, right = (to_group(one[:, :half], 2), to_group(two[:, half:], 1))]
  transfers between devices with their start and end apart: 53 -> 42, of which waited for: 22 -> 15; matrix products, arithmetic and copies ran while one was open for 3% -> 4% of each run, Pallas kernels for 14% -> 12%
where the time goes in v6:
time: 192 us; the launch traced here: 191 us
  starting transfers between devices  63.8 us (33%)
  waiting for transfers between devices  63.3 us (33%)
  local copies, waits for them, and re-layouts  32.9 us (17%)
  Pallas kernels  27 us (14%)
  other arithmetic  3.05 us (2%)
    ppermute x21, waiting for transfers between devices, to_group(): return lax.ppermute(x, 'grp', [(a, a ^ k) for a in range(groups)])  50.5 us
    ppermute x9, starting transfers between devices, to_chip(): return lax.ppermute(x, 'seq', pairs)  28.6 us
    unnamed x82, local copies, waits for them, and re-layouts  27.5 us
    pallas_call x11, Pallas kernels, call(): pl.pallas_call(kernel, out_shape=[jax.ShapeDtypeStruct(s, t) for s, t in...  27 us
    ppermute x21, starting transfers between devices, to_group(): return lax.ppermute(x, 'grp', [(a, a ^ k) for a in range(groups)])  25.1 us
    ppermute x9, waiting for transfers between devices, to_chip(): return lax.ppermute(x, 'seq', pairs)  12.8 us
    all_to_all x1, starting transfers between devices, body(): lax.all_to_all(outgoing.reshape(owners, slot, width), 'seq', 0, 0, tiled=...  8.42 us
    slice x4, local copies, waits for them, and re-layouts, gather_groups(): left, right = (to_group(one[:, :half], 2), to_group(two[:, half:], 1))  3.98 us
  transfers between devices with their start and end apart: 42, of which 15 were waited for; matrix products, arithmetic and copies ran while one was open for 4% of the time, Pallas kernels for 12%

profile of v6, /device:TPU:0, one launch (start us, length us, event | category | flops | bytes accessed | tf_op | source)
XLA Modules:
  0.0 191.0 jit_solution(13665992634259155388)
XLA Ops:
  3.3 2.6 %collective-permute-start = (bf16[128,1024]{1,0:T(8,128)(2,1)S(1)}, bf16[128,1024]{1,0:T(8,128)(2,1)S(1)}, u32[]{:S(2)}, u32[]{:S(2)}) collective-permute-start(bf16[128,1024]{1,0:T(8,128)(2,1)S(1)} %get-tuple-element.60), channel_id=1, source_target_pairs={{0,2},{1,3},{2,4},{3,5},{4,6},{5,7},{6,0},{7,1},{8,10},{9,11},{10,... | collective-permute-start | bytes 786440 | tf_op jit(solution)/shard_map/ppermute | solution.py:383
  5.9 2.6 %collective-permute-start.1 = (bf16[128,1024]{1,0:T(8,128)(2,1)S(1)}, bf16[128,1024]{1,0:T(8,128)(2,1)S(1)}, u32[]{:S(2)}, u32[]{:S(2)}) collective-permute-start(bf16[128,1024]{1,0:T(8,128)(2,1)S(1)} %get-tuple-element.60), channel_id=1, source_target_pairs={{0,4},{1,5},{2,6},{3,7},{4,0},{5,1},{6,2},{7,3},{8,12},{9,13},{10,... | collective-permute-start | bytes 786440 | tf_op jit(solution)/shard_map/ppermute | solution.py:383
  11.1 2.2 %copy-done.11 = bf16[1024,2048]{1,0:T(8,128)(2,1)S(1)} copy-done((bf16[1024,2048]{1,0:T(8,128)(2,1)S(1)}, bf16[1024,2048]{1,0:T(8,128)(2,1)}, u32[]{:S(2)}) %copy-start.11) | copy-done | bytes 4194328
  15.6 4.6 %shard_map.111 = (bf16[256,512]{1,0:T(8,128)(2,1)S(1)}, bf16[256,512]{1,0:T(8,128)(2,1)S(1)}, bf16[256,2048]{1,0:T(8,128)(2,1)S(1)}, bf16[256,2048]{1,0:T(8,128)...) custom-call(s32[1,8]{1,0:T(1,128)S(1)} %copy-done.30, ...), custom_call_target="tpu_custom_call" | custom-call | flops 1610612736 | bytes 11534336 | tf_op jit(solution)/shard_map/pallas_call | solution.py:53
  30.9 1.5 collective-permute-start.7
  32.4 8.4 %all-to-all-start = ((bf16[8,48,1024]{2,1,0:T(8,128)(2,1)}), bf16[8,48,1024]{2,1,0:T(8,128)(2,1)S(1)}, u32[]{:S(2)}, u32[]{:S(2)}) async-start(bf16[8,48,1024]{2,1,0:T(8,128)(2,1)} %bitcast.14), calls=%async_computation | async-start | bytes 1572864 | tf_op jit(solution)/shard_map/all_to_all | solution.py:431
  41.9 7.3 %collective-permute-done.6.refs_6_ = bf16[384,1024]{1,0:T(8,128)(2,1)} collective-permute-done((bf16[384,1024]{1,0:T(8,128)(2,1)}, bf16[384,1024]{1,0:T(8,128)(2,1)}, u32[]{:S(2)}, u32[]{:S(2)}) %collective-permute-start.6) | collective-permute-done | bytes 786464 | tf_op jit(solution)/shard_map/ppermute | solution.py:386
  50.4 1.5 collective-permute-start.8
  56.0 6.0 %collective-permute-done.8.refs_8_ = bf16[384,512]{1,0:T(8,128)(2,1)} collective-permute-done((bf16[384,512]{1,0:T(8,128)(2,1)S(1)}, bf16[384,512]{1,0:T(8,128)(2,1)}, u32[]{:S(2)}, u32[]{:S(2)}) %collective-permute-start.8) | collective-permute-done | bytes 393248 | tf_op jit(solution)/shard_map/ppermute | solution.py:386
  61.9 4.1 %collective-permute-done.9.refs_9_ = bf16[384,512]{1,0:T(8,128)(2,1)} collective-permute-done((bf16[384,512]{1,0:T(8,128)(2,1)S(1)}, bf16[384,512]{1,0:T(8,128)(2,1)}, u32[]{:S(2)}, u32[]{:S(2)}) %collective-permute-start.9) | collective-permute-done | bytes 393248 | tf_op jit(solution)/shard_map/ppermute | solution.py:386
  70.5 1.6 shard_map.113
  80.9 9.0 %shard_map.114 = (f32[16,256]{1,0:T(8,128)S(1)}, bf16[256,1024]{1,0:T(8,128)(2,1)S(1)}, bf16[256,512]{1,0:T(8,128)(2,1)S(1)}, bf16[256,512]{1,0:T(8,128)(2,1)S(1)}) custom-call(s32[256,4]{1,0:T(8,128)S(1)} %copy-done.8, f32[256,1]{1,0:T(8,128)S(1)} %copy-done.37, bf16[256,1024]{1,0:T(8,128)(2,1)S(1)} %copy-done.22, f32[256,1024]{1,0:T(8,128)S(1)} %copy-done.33, ...), custom_call_target="tpu_custom_call" | custom-call | flops 4294967296 | bytes 11534336 | tf_op jit(solution)/shard_map/pallas_call | solution.py:53
  90.0 1.6 shard_map.115.refs_4_
  92.7 1.6 collective-permute-start.19
  97.3 6.7 %collective-permute-done.21.refs_6_ = f32[16,256]{1,0:T(8,128)S(1)} collective-permute-done((f32[16,256]{1,0:T(8,128)S(1)}, f32[16,256]{1,0:T(8,128)S(1)}, u32[]{:S(2)}, u32[]{:S(2)}) %collective-permute-start.21) | collective-permute-done | bytes 16416 | tf_op jit(solution)/shard_map/ppermute | solution.py:386
  104.6 3.2 %collective-permute-done.22.refs_7_ = f32[16,256]{1,0:T(8,128)S(1)} collective-permute-done((f32[16,256]{1,0:T(8,128)S(1)}, f32[16,256]{1,0:T(8,128)S(1)}, u32[]{:S(2)}, u32[]{:S(2)}) %collective-permute-start.22) | collective-permute-done | bytes 16416 | tf_op jit(solution)/shard_map/ppermute | solution.py:386
  108.4 4.0 %collective-permute-done.23.refs_8_ = f32[16,256]{1,0:T(8,128)S(1)} collective-permute-done((f32[16,256]{1,0:T(8,128)S(1)}, f32[16,256]{1,0:T(8,128)S(1)}, u32[]{:S(2)}, u32[]{:S(2)}) %collective-permute-start.23) | collective-permute-done | bytes 16416 | tf_op jit(solution)/shard_map/ppermute | solution.py:386
  112.4 4.3 %shard_map.116 = (bf16[512,1024]{1,0:T(8,128)(2,1)S(1)}, bf16[512,1024]{1,0:T(8,128)(2,1)S(1)}) custom-call(bf16[256,1024]{1,0:T(8,128)(2,1)S(1)} %copy-done.22, bf16[256,1024]{1,0:T(8,128)(2,1)} %collective-permute-done.16.refs_1_, bf16[256,1024]{1,0:T(8,128)(2,1)} %collective-permute-done.17.refs_2_, bf16[256,512]{1,0:T(8,128)(2,1)S(1)} %collective-permute-done.19.refs_3_, ...), custom_call_target="tpu_custom_call" | custom-call | flops 2147483648 | bytes 4194304 | tf_op jit(solution)/shard_map/pallas_call | solution.py:53
  116.9 1.7 shard_map.117
  119.8 12.6 %collective-permute-done.27.by_two = bf16[2,4,32,1280]{3,2,1,0:T(8,128)(2,1)S(1)} collective-permute-done((bf16[2,4,32,1280]{3,2,1,0:T(8,128)(2,1)S(1)}, bf16[2,4,32,1280]{3,2,1,0:T(8,128)(2,1)S(1)}, u32[]{:S(2)}, u32[]{:S(2)}) %collective-permute-start.27) | collective-permute-done | bytes 655392 | tf_op jit(solution)/shard_map/ppermute | solution.py:386
  134.6 1.7 collective-permute-start.29
  137.2 6.9 %collective-permute-start.25 = (bf16[128,1024]{1,0:T(8,128)(2,1)}, bf16[128,1024]{1,0:T(8,128)(2,1)}, u32[]{:S(2)}, u32[]{:S(2)}) collective-permute-start(bf16[128,1024]{1,0:T(8,128)(2,1)} %get-tuple-element.98), channel_id=1, source_target_pairs={{0,6},{1,7},{2,0},{3,1},{4,2},{5,3},{6,4},{7,5},{8,14},{9,15},{10,... | collective-permute-start | bytes 786440 | tf_op jit(solution)/shard_map/ppermute | solution.py:383
  144.9 6.3 %collective-permute-done.25 = bf16[128,1024]{1,0:T(8,128)(2,1)} collective-permute-done((bf16[128,1024]{1,0:T(8,128)(2,1)}, bf16[128,1024]{1,0:T(8,128)(2,1)}, u32[]{:S(2)}, u32[]{:S(2)}) %collective-permute-start.25) | collective-permute-done | bytes 262176 | tf_op jit(solution)/shard_map/ppermute | solution.py:383
  151.4 4.5 %collective-permute-start.32 = (bf16[32,2560]{1,0:T(8,128)(2,1)S(1)}, bf16[32,2560]{1,0:T(8,128)(2,1)S(1)}, u32[]{:S(2)}, u32[]{:S(2)}) collective-permute-start(bf16[32,2560]{1,0:T(8,128)(2,1)S(1)} %get-tuple-element.107), channel_id=1, source_target_pairs={{0,6},{1,7},{2,0},{3,1},{4,2},{5,3},{6,4},{7,5},{8,14},{9,15},{10,... | collective-permute-start | bytes 491528 | tf_op jit(solution)/shard_map/ppermute | solution.py:383
  155.9 9.9 %collective-permute-start.31 = (bf16[32,2560]{1,0:T(8,128)(2,1)S(1)}, bf16[32,2560]{1,0:T(8,128)(2,1)S(1)}, u32[]{:S(2)}, u32[]{:S(2)}) collective-permute-start(bf16[32,2560]{1,0:T(8,128)(2,1)S(1)} %get-tuple-element.106), channel_id=1, source_target_pairs={{0,4},{1,5},{2,6},{3,7},{4,0},{5,1},{6,2},{7,3},{8,12},{9,13},{10,... | collective-permute-start | bytes 491528 | tf_op jit(solution)/shard_map/ppermute | solution.py:383
  165.9 5.1 %collective-permute-done.36 = bf16[128,1024]{1,0:T(8,128)(2,1)} collective-permute-done((bf16[128,1024]{1,0:T(8,128)(2,1)S(1)}, bf16[128,1024]{1,0:T(8,128)(2,1)}, u32[]{:S(2)}, u32[]{:S(2)}) %collective-permute-start.36) | collective-permute-done | bytes 262176 | tf_op jit(solution)/shard_map/ppermute | solution.py:383
  173.7 1.5 collective-permute-start.39
  178.1 1.5 collective-permute-start.34
  179.7 1.5 collective-permute-done.38.refs_1_
  181.2 2.3 %collective-permute-start.35 = (bf16[32,2560]{1,0:T(8,128)(2,1)S(1)}, bf16[32,2560]{1,0:T(8,128)(2,1)S(1)}, u32[]{:S(2)}, u32[]{:S(2)}) collective-permute-start(bf16[32,2560]{1,0:T(8,128)(2,1)S(1)} %add_convert_fusion.refs_0_), channel_id=1, source_target_pairs={{0,24},{8,16},{16,8},{24,0},{1,25},{9,17},{17,9},{25,1},{2,26},{10... | collective-permute-start | bytes 491528 | tf_op jit(solution)/shard_map/ppermute | solution.py:386
  183.5 2.8 %collective-permute-done.39.refs_2_ = bf16[128,1024]{1,0:T(8,128)(2,1)S(1)} collective-permute-done((bf16[128,1024]{1,0:T(8,128)(2,1)S(1)}, bf16[128,1024]{1,0:T(8,128)(2,1)S(1)}, u32[]{:S(2)}, u32[]{:S(2)}) %collective-permute-start.39) | collective-permute-done | bytes 262176 | tf_op jit(solution)/shard_map/ppermute | solution.py:386
  187.8 2.0 %collective-permute-done.34.refs_2_ = bf16[32,2560]{1,0:T(8,128)(2,1)S(1)} collective-permute-done((bf16[32,2560]{1,0:T(8,128)(2,1)S(1)}, bf16[32,2560]{1,0:T(8,128)(2,1)S(1)}, u32[]{:S(2)}, u32[]{:S(2)}) %collective-permute-start.34) | collective-permute-done | bytes 163872 | tf_op jit(solution)/shard_map/ppermute | solution.py:386
  (157 shorter events, 56.8 us)
Async XLA Ops:
  2.9 23.4 %collective-permute-start.3 = (bf16[512,1024]{1,0:T(8,128)(2,1)S(1)}, bf16[512,1024]{1,0:T(8,128)(2,1)S(1)}, u32[]{:S(2)}, u32[]{:S(2)}) collective-permute-start(bf16[512,1024]{1,0:T(8,128)(2,1)S(1)} %get-tuple-element.61.refs_4_.refs_9_), channel_id=1, source_target_pairs={{0,1},{1,0},{2,3},{3,2},{4,5},{5,4},{6,7},{7,6},{8,9},{9,8},{10,11... | collective-permute-start | bytes 3145736 | tf_op jit(solution)/shard_map/ppermute | solution.py:389
  3.3 22.3 %collective-permute-start = (bf16[128,1024]{1,0:T(8,128)(2,1)S(1)}, bf16[128,1024]{1,0:T(8,128)(2,1)S(1)}, u32[]{:S(2)}, u32[]{:S(2)}) collective-permute-start(bf16[128,1024]{1,0:T(8,128)(2,1)S(1)} %get-tuple-element.60), channel_id=1, source_target_pairs={{0,2},{1,3},{2,4},{3,5},{4,6},{5,7},{6,0},{7,1},{8,10},{9,11},{10,... | collective-permute-start | bytes 786440 | tf_op jit(solution)/shard_map/ppermute | solution.py:383
  5.9 20.3 %collective-permute-start.1 = (bf16[128,1024]{1,0:T(8,128)(2,1)S(1)}, bf16[128,1024]{1,0:T(8,128)(2,1)S(1)}, u32[]{:S(2)}, u32[]{:S(2)}) collective-permute-start(bf16[128,1024]{1,0:T(8,128)(2,1)S(1)} %get-tuple-element.60), channel_id=1, source_target_pairs={{0,4},{1,5},{2,6},{3,7},{4,0},{5,1},{6,2},{7,3},{8,12},{9,13},{10,... | collective-permute-start | bytes 786440 | tf_op jit(solution)/shard_map/ppermute | solution.py:383
  8.5 17.8 %collective-permute-start.2 = (bf16[128,1024]{1,0:T(8,128)(2,1)S(1)}, bf16[128,1024]{1,0:T(8,128)(2,1)S(1)}, u32[]{:S(2)}, u32[]{:S(2)}) collective-permute-start(bf16[128,1024]{1,0:T(8,128)(2,1)S(1)} %get-tuple-element.60), channel_id=1, source_target_pairs={{0,6},{1,7},{2,0},{3,1},{4,2},{5,3},{6,4},{7,5},{8,14},{9,15},{10,... | collective-permute-start | bytes 786440 | tf_op jit(solution)/shard_map/ppermute | solution.py:383
  29.4 19.7 %collective-permute-start.6 = (bf16[384,1024]{1,0:T(8,128)(2,1)}, bf16[384,1024]{1,0:T(8,128)(2,1)}, u32[]{:S(2)}, u32[]{:S(2)}) collective-permute-start(bf16[384,1024]{1,0:T(8,128)(2,1)} %constant_dynamic-update-slice_fusion.refs_5_.refs_10_), channel_id=1, source_target_pairs={{0,8},{8,0},{16,24},{24,16},{1,9},{9,1},{17,25},{25,17},{2,10},{10... | collective-permute-start | bytes 2359304 | tf_op jit(solution)/shard_map/ppermute | solution.py:386
  30.9 19.5 %collective-permute-start.7 = (bf16[384,1024]{1,0:T(8,128)(2,1)}, bf16[384,1024]{1,0:T(8,128)(2,1)}, u32[]{:S(2)}, u32[]{:S(2)}) collective-permute-start(bf16[384,1024]{1,0:T(8,128)(2,1)} %constant_dynamic-update-slice_fusion.refs_5_.refs_10_), channel_id=1, source_target_pairs={{0,16},{8,24},{16,0},{24,8},{1,17},{9,25},{17,1},{25,9},{2,18},{10... | collective-permute-start | bytes 2359304 | tf_op jit(solution)/shard_map/ppermute | solution.py:386
  32.4 38.1 %all-to-all-start = ((bf16[8,48,1024]{2,1,0:T(8,128)(2,1)}), bf16[8,48,1024]{2,1,0:T(8,128)(2,1)S(1)}, u32[]{:S(2)}, u32[]{:S(2)}) async-start(bf16[8,48,1024]{2,1,0:T(8,128)(2,1)} %bitcast.14), calls=%async_computation | async-start | bytes 1572864 | tf_op jit(solution)/shard_map/all_to_all | solution.py:431
  40.8 12.1 %collective-permute-start.4 = (bf16[256,512]{1,0:T(8,128)(2,1)}, bf16[256,512]{1,0:T(8,128)(2,1)S(1)}, u32[]{:S(2)}, u32[]{:S(2)}) collective-permute-start(bf16[256,512]{1,0:T(8,128)(2,1)} %copy-done.29), channel_id=1, source_target_pairs={{0,1},{1,0},{2,3},{3,2},{4,5},{5,4},{6,7},{7,6},{8,9},{9,8},{10,11... | collective-permute-start | bytes 786440 | tf_op jit(solution)/shard_map/ppermute | solution.py:389
  41.4 12.4 %collective-permute-start.5 = (bf16[256,512]{1,0:T(8,128)(2,1)}, bf16[256,512]{1,0:T(8,128)(2,1)S(1)}, u32[]{:S(2)}, u32[]{:S(2)}) collective-permute-start(bf16[256,512]{1,0:T(8,128)(2,1)} %copy-done.23), channel_id=1, source_target_pairs={{0,1},{1,0},{2,3},{3,2},{4,5},{5,4},{6,7},{7,6},{8,9},{9,8},{10,11... | collective-permute-start | bytes 786440 | tf_op jit(solution)/shard_map/ppermute | solution.py:389
  41.4 24.6 %collective-permute-start.10 = (bf16[384,1024]{1,0:T(8,128)(2,1)}, bf16[384,1024]{1,0:T(8,128)(2,1)S(1)}, u32[]{:S(2)}, u32[]{:S(2)}) collective-permute-start(bf16[384,1024]{1,0:T(8,128)(2,1)} %constant_dynamic-update-slice_fusion.refs_5_.refs_10_), channel_id=1, source_target_pairs={{0,1},{1,0},{2,3},{3,2},{4,5},{5,4},{6,7},{7,6},{8,9},{9,8},{10,11... | collective-permute-start | bytes 2359304 | tf_op jit(solution)/shard_map/ppermute | solution.py:389
  49.2 19.1 %collective-permute-start.11 = (bf16[384,1024]{1,0:T(8,128)(2,1)}, bf16[384,1024]{1,0:T(8,128)(2,1)S(1)}, u32[]{:S(2)}, u32[]{:S(2)}) collective-permute-start(bf16[384,1024]{1,0:T(8,128)(2,1)} %collective-permute-done.6.refs_6_), channel_id=1, source_target_pairs={{0,1},{1,0},{2,3},{3,2},{4,5},{5,4},{6,7},{7,6},{8,9},{9,8},{10,11... | collective-permute-start | bytes 2359304 | tf_op jit(solution)/shard_map/ppermute | solution.py:389
  50.4 11.6 %collective-permute-start.8 = (bf16[384,512]{1,0:T(8,128)(2,1)S(1)}, bf16[384,512]{1,0:T(8,128)(2,1)}, u32[]{:S(2)}, u32[]{:S(2)}) collective-permute-start(bf16[384,512]{1,0:T(8,128)(2,1)S(1)} %slice.24), channel_id=1, source_target_pairs={{0,16},{8,24},{16,0},{24,8},{1,17},{9,25},{17,1},{25,9},{2,18},{10... | collective-permute-start | bytes 1179656 | tf_op jit(solution)/shard_map/ppermute | solution.py:386
  53.6 18.5 %collective-permute-start.12 = (bf16[384,1024]{1,0:T(8,128)(2,1)}, bf16[384,1024]{1,0:T(8,128)(2,1)}, u32[]{:S(2)}, u32[]{:S(2)}) collective-permute-start(bf16[384,1024]{1,0:T(8,128)(2,1)} %collective-permute-done.7.refs_7_), channel_id=1, source_target_pairs={{0,1},{1,0},{2,3},{3,2},{4,5},{5,4},{6,7},{7,6},{8,9},{9,8},{10,11... | collective-permute-start | bytes 2359304 | tf_op jit(solution)/shard_map/ppermute | solution.py:389
  54.5 11.5 %collective-permute-start.9 = (bf16[384,512]{1,0:T(8,128)(2,1)S(1)}, bf16[384,512]{1,0:T(8,128)(2,1)}, u32[]{:S(2)}, u32[]{:S(2)}) collective-permute-start(bf16[384,512]{1,0:T(8,128)(2,1)S(1)} %slice.25), channel_id=1, source_target_pairs={{0,8},{8,0},{16,24},{24,16},{1,9},{9,1},{17,25},{25,17},{2,10},{10... | collective-permute-start | bytes 1179656 | tf_op jit(solution)/shard_map/ppermute | solution.py:386
  66.9 23.1 %collective-permute-start.16 = (bf16[256,1024]{1,0:T(8,128)(2,1)}, bf16[256,1024]{1,0:T(8,128)(2,1)}, u32[]{:S(2)}, u32[]{:S(2)}) collective-permute-start(bf16[256,1024]{1,0:T(8,128)(2,1)} %copy-done.21), channel_id=1, source_target_pairs={{0,8},{8,0},{16,24},{24,16},{1,9},{9,1},{17,25},{25,17},{2,10},{10... | collective-permute-start | bytes 1572872 | tf_op jit(solution)/shard_map/ppermute | solution.py:386
  69.2 20.8 %collective-permute-start.17 = (bf16[256,1024]{1,0:T(8,128)(2,1)}, bf16[256,1024]{1,0:T(8,128)(2,1)}, u32[]{:S(2)}, u32[]{:S(2)}) collective-permute-start(bf16[256,1024]{1,0:T(8,128)(2,1)} %copy-done.21), channel_id=1, source_target_pairs={{0,16},{8,24},{16,0},{24,8},{1,17},{9,25},{17,1},{25,9},{2,18},{10... | collective-permute-start | bytes 1572872 | tf_op jit(solution)/shard_map/ppermute | solution.py:386
  91.6 25.2 %collective-permute-start.18 = (bf16[256,2048]{1,0:T(8,128)(2,1)S(1)}, bf16[256,2048]{1,0:T(8,128)(2,1)S(1)}, u32[]{:S(2)}, u32[]{:S(2)}) collective-permute-start(bf16[256,2048]{1,0:T(8,128)(2,1)S(1)} %shard_map.115.refs_4_), channel_id=1, source_target_pairs={{0,1},{1,0},{2,3},{3,2},{4,5},{5,4},{6,7},{7,6},{8,9},{9,8},{10,11... | collective-permute-start | bytes 3145736 | tf_op jit(solution)/shard_map/ppermute | solution.py:389
  92.7 19.8 %collective-permute-start.19 = (bf16[256,512]{1,0:T(8,128)(2,1)S(1)}, bf16[256,512]{1,0:T(8,128)(2,1)S(1)}, u32[]{:S(2)}, u32[]{:S(2)}) collective-permute-start(bf16[256,512]{1,0:T(8,128)(2,1)S(1)} %slice.26), channel_id=1, source_target_pairs={{0,16},{8,24},{16,0},{24,8},{1,17},{9,25},{17,1},{25,9},{2,18},{10... | collective-permute-start | bytes 786440 | tf_op jit(solution)/shard_map/ppermute | solution.py:386
  95.2 17.2 %collective-permute-start.20 = (bf16[256,512]{1,0:T(8,128)(2,1)S(1)}, bf16[256,512]{1,0:T(8,128)(2,1)S(1)}, u32[]{:S(2)}, u32[]{:S(2)}) collective-permute-start(bf16[256,512]{1,0:T(8,128)(2,1)S(1)} %slice.27), channel_id=1, source_target_pairs={{0,8},{8,0},{16,24},{24,16},{1,9},{9,1},{17,25},{25,17},{2,10},{10... | collective-permute-start | bytes 786440 | tf_op jit(solution)/shard_map/ppermute | solution.py:386
  95.9 20.9 %collective-permute-start.15 = (bf16[256,512]{1,0:T(8,128)(2,1)S(1)}, bf16[256,512]{1,0:T(8,128)(2,1)S(1)}, u32[]{:S(2)}, u32[]{:S(2)}) collective-permute-start(bf16[256,512]{1,0:T(8,128)(2,1)S(1)} %get-tuple-element.77), channel_id=1, source_target_pairs={{0,1},{1,0},{2,3},{3,2},{4,5},{5,4},{6,7},{7,6},{8,9},{9,8},{10,11... | collective-permute-start | bytes 786440 | tf_op jit(solution)/shard_map/ppermute | solution.py:389
  118.6 13.8 %collective-permute-start.27 = (bf16[2,4,32,1280]{3,2,1,0:T(8,128)(2,1)S(1)}, bf16[2,4,32,1280]{3,2,1,0:T(8,128)(2,1)S(1)}, u32[]{:S(2)}, u32[]{:S(2)}) collective-permute-start(bf16[2,4,32,1280]{3,2,1,0:T(8,128)(2,1)S(1)} %get-tuple-element.101), channel_id=1, source_target_pairs={{0,16},{8,24},{16,0},{24,8},{1,17},{9,25},{17,1},{25,9},{2,18},{10... | collective-permute-start | bytes 1966088 | tf_op jit(solution)/shard_map/ppermute | solution.py:386
  119.1 14.7 %collective-permute-start.26 = (bf16[2,4,32,1280]{3,2,1,0:T(8,128)(2,1)S(1)}, bf16[2,4,32,1280]{3,2,1,0:T(8,128)(2,1)S(1)}, u32[]{:S(2)}, u32[]{:S(2)}) collective-permute-start(bf16[2,4,32,1280]{3,2,1,0:T(8,128)(2,1)S(1)} %get-tuple-element.100), channel_id=1, source_target_pairs={{0,8},{8,0},{16,24},{24,16},{1,9},{9,1},{17,25},{25,17},{2,10},{10... | collective-permute-start | bytes 1966088 | tf_op jit(solution)/shard_map/ppermute | solution.py:386
  119.8 16.5 %collective-permute-start.24 = (bf16[512,1024]{1,0:T(8,128)(2,1)S(1)}, bf16[512,1024]{1,0:T(8,128)(2,1)S(1)}, u32[]{:S(2)}, u32[]{:S(2)}) collective-permute-start(bf16[512,1024]{1,0:T(8,128)(2,1)S(1)} %get-tuple-element.97), channel_id=1, source_target_pairs={{0,1},{1,0},{2,3},{3,2},{4,5},{5,4},{6,7},{7,6},{8,9},{9,8},{10,11... | collective-permute-start | bytes 3145736 | tf_op jit(solution)/shard_map/ppermute | solution.py:389
  133.2 18.0 %collective-permute-start.28 = (bf16[4,32,1280]{2,1,0:T(8,128)(2,1)}, bf16[4,32,1280]{2,1,0:T(8,128)(2,1)S(1)}, u32[]{:S(2)}, u32[]{:S(2)}) collective-permute-start(bf16[4,32,1280]{2,1,0:T(8,128)(2,1)} %fusion.1), channel_id=1, source_target_pairs={{0,8},{8,0},{16,24},{24,16},{1,9},{9,1},{17,25},{25,17},{2,10},{10... | collective-permute-start | bytes 983048 | tf_op jit(solution)/shard_map/ppermute | solution.py:386
  134.6 16.6 %collective-permute-start.29 = (bf16[4,32,1280]{2,1,0:T(8,128)(2,1)}, bf16[4,32,1280]{2,1,0:T(8,128)(2,1)S(1)}, u32[]{:S(2)}, u32[]{:S(2)}) collective-permute-start(bf16[4,32,1280]{2,1,0:T(8,128)(2,1)} %fusion), channel_id=1, source_target_pairs={{0,16},{8,24},{16,0},{24,8},{1,17},{9,25},{17,1},{25,9},{2,18},{10... | collective-permute-start | bytes 983048 | tf_op jit(solution)/shard_map/ppermute | solution.py:386
  137.2 14.0 %collective-permute-start.25 = (bf16[128,1024]{1,0:T(8,128)(2,1)}, bf16[128,1024]{1,0:T(8,128)(2,1)}, u32[]{:S(2)}, u32[]{:S(2)}) collective-permute-start(bf16[128,1024]{1,0:T(8,128)(2,1)} %get-tuple-element.98), channel_id=1, source_target_pairs={{0,6},{1,7},{2,0},{3,1},{4,2},{5,3},{6,4},{7,5},{8,14},{9,15},{10,... | collective-permute-start | bytes 786440 | tf_op jit(solution)/shard_map/ppermute | solution.py:383
  144.1 21.8 %collective-permute-start.37 = (bf16[128,1024]{1,0:T(8,128)(2,1)S(1)}, bf16[128,1024]{1,0:T(8,128)(2,1)}, u32[]{:S(2)}, u32[]{:S(2)}) collective-permute-start(bf16[128,1024]{1,0:T(8,128)(2,1)S(1)} %get-tuple-element.112), channel_id=1, source_target_pairs={{0,2},{1,3},{2,4},{3,5},{4,6},{5,7},{6,0},{7,1},{8,10},{9,11},{10,... | collective-permute-start | bytes 786440 | tf_op jit(solution)/shard_map/ppermute | solution.py:383
  144.1 26.9 %collective-permute-start.36 = (bf16[128,1024]{1,0:T(8,128)(2,1)S(1)}, bf16[128,1024]{1,0:T(8,128)(2,1)}, u32[]{:S(2)}, u32[]{:S(2)}) collective-permute-start(bf16[128,1024]{1,0:T(8,128)(2,1)S(1)} %get-tuple-element.111), channel_id=1, source_target_pairs={{0,4},{1,5},{2,6},{3,7},{4,0},{5,1},{6,2},{7,3},{8,12},{9,13},{10,... | collective-permute-start | bytes 786440 | tf_op jit(solution)/shard_map/ppermute | solution.py:383
  151.4 23.7 %collective-permute-start.32 = (bf16[32,2560]{1,0:T(8,128)(2,1)S(1)}, bf16[32,2560]{1,0:T(8,128)(2,1)S(1)}, u32[]{:S(2)}, u32[]{:S(2)}) collective-permute-start(bf16[32,2560]{1,0:T(8,128)(2,1)S(1)} %get-tuple-element.107), channel_id=1, source_target_pairs={{0,6},{1,7},{2,0},{3,1},{4,2},{5,3},{6,4},{7,5},{8,14},{9,15},{10,... | collective-permute-start | bytes 491528 | tf_op jit(solution)/shard_map/ppermute | solution.py:383
  155.9 20.7 %collective-permute-start.31 = (bf16[32,2560]{1,0:T(8,128)(2,1)S(1)}, bf16[32,2560]{1,0:T(8,128)(2,1)S(1)}, u32[]{:S(2)}, u32[]{:S(2)}) collective-permute-start(bf16[32,2560]{1,0:T(8,128)(2,1)S(1)} %get-tuple-element.106), channel_id=1, source_target_pairs={{0,4},{1,5},{2,6},{3,7},{4,0},{5,1},{6,2},{7,3},{8,12},{9,13},{10,... | collective-permute-start | bytes 491528 | tf_op jit(solution)/shard_map/ppermute | solution.py:383
  173.7 12.7 %collective-permute-start.39 = (bf16[128,1024]{1,0:T(8,128)(2,1)S(1)}, bf16[128,1024]{1,0:T(8,128)(2,1)S(1)}, u32[]{:S(2)}, u32[]{:S(2)}) collective-permute-start(bf16[128,1024]{1,0:T(8,128)(2,1)S(1)} %multiply_convert_fusion.refs_0_), channel_id=1, source_target_pairs={{0,16},{8,24},{16,0},{24,8},{1,17},{9,25},{17,1},{25,9},{2,18},{10... | collective-permute-start | bytes 786440 | tf_op jit(solution)/shard_map/ppermute | solution.py:386
  178.1 11.7 %collective-permute-start.34 = (bf16[32,2560]{1,0:T(8,128)(2,1)S(1)}, bf16[32,2560]{1,0:T(8,128)(2,1)S(1)}, u32[]{:S(2)}, u32[]{:S(2)}) collective-permute-start(bf16[32,2560]{1,0:T(8,128)(2,1)S(1)} %add_convert_fusion.refs_0_), channel_id=1, source_target_pairs={{0,16},{8,24},{16,0},{24,8},{1,17},{9,25},{17,1},{25,9},{2,18},{10... | collective-permute-start | bytes 491528 | tf_op jit(solution)/shard_map/ppermute | solution.py:386
  (50 other events, 412.8 us)

commit v7 on v6

--- a/solution.py
+++ b/solution.py
@@ -126,11 +126,19 @@
     outgoing[...] = jnp.where(filled == 1, placed, EMPTY).astype(b16)
 
 
+def distances(chips):
+    order, bit = [0], chips // 2
+    while bit:
+        order += [x ^ bit for x in order]
+        bit //= 2
+    return order
+
+
 def owner_ids(owners):
     seq = lax.axis_index("seq")
     chip, core = seq // 2, seq % 2
     chips = owners // 2
-    return [2 * ((chip + chips - d) % chips) + (core ^ side) for side in range(2) for d in range(chips)]
+    return [2 * (chip ^ d) + (core ^ side) for side in range(2) for d in distances(chips)]
 
 
 def normalise_kernel(share, item_table, own, quarter, quarter_inv):
@@ -382,17 +390,21 @@
         pairs = [(2 * a + b, 2 * ((a + d) % chips) + b) for a in range(chips) for b in range(2)]
         return lax.ppermute(x, "seq", pairs)
 
+    def across(x, k):
+        pairs = [(2 * a + b, 2 * (a ^ k) + b) for a in range(chips) for b in range(2)]
+        return lax.ppermute(x, "seq", pairs)
+
     def to_group(x, k):
         return lax.ppermute(x, "grp", [(a, a ^ k) for a in range(groups)])
 
     def to_core(x):
         return lax.ppermute(x, "seq", [(a, a ^ 1) for a in range(owners)])
 
-    def gather_groups(x):
+    def gather_groups(x, near=None):
         wide = x.shape[1]
         if groups != 4:
             return [(k, 0, wide, to_group(x, k) if k else x) for k in range(groups)]
-        one, two = to_group(x, 1), to_group(x, 2)
+        one, two = near or [to_group(x, k) for k in (1, 2)]
         half = wide // 2
         left, right = to_group(one[:, :half], 2), to_group(two[:, half:], 1)
         return [(0, 0, wide, x), (1, 0, wide, one), (2, 0, wide, two), (3, 0, half, left), (3, half, half, right)]
@@ -403,8 +415,11 @@
         [VMEM], [item_table], flops=8 * vocab_dev * width, nbytes=5 * vocab_dev * width, room=8,
     )
     chunks = [list(range(1, chips))]
-    got = [to_chip(quarter, d) for d in chunks[0]]
-    far_own = to_core(own)
+    have, bit = {0: quarter}, chips // 2
+    while bit:
+        have.update({x ^ bit: across(have[x], bit) for x in have})
+        bit //= 2
+    got = [have[x] for x in distances(chips)[1:]]
     outs = [
         ((tok, width // 2), b16), ((tok, width // 2), b16), ((tok, 4 * hidden), b16), ((tok, 4 * hidden), b16),
         ((HEADS, tok, tok), b16), ((HEADS, tok, tok), b16), ((tok, hidden), f32), ((tok, 1), f32),
@@ -414,18 +429,19 @@
     (keep, give, proj, slope, attn, attn_slope, normed, inverse, gated, unit, unit_b, inv_len, outgoing) = call(
         lambda *refs: forward_kernel(owners, slot, *refs), outs, [SMEM, SMEM, VMEM, VMEM, VMEM],
         [lengths, destinations, events, in_weight, out_weight],
-        flops=2 * tok * width * 6 * hidden, nbytes=24 * tok * width + 10 * width * hidden, room=28,
-    )
-
-    got, far_own, unit_b = lax.optimization_barrier((got, far_own, unit_b))
+        room=63,
+    )
+
+    near_units = [to_group(unit_b, k) for k in (1, 2)]
+    got, near_units, own = lax.optimization_barrier((got, near_units, own))
+    far_own = to_core(own)
+    unit_sent = gather_groups(unit_b, near_units)
     others = [jnp.concatenate(got, 0)]
     pieces = [(0, -1, 0, 0, width, own)]
     for j, x in enumerate(others):
         pieces += [(0, j) + p for p in gather_groups(x)]
     pieces = pieces + [(1,) + p[1:5] + (to_core(p[5]) if p[1] >= 0 else far_own,) for p in pieces]
     near = [p[5] for p in pieces if p[2] == 0]
-    sent_unit, _ = lax.optimization_barrier((unit_b, [p[5] for p in pieces if p[0] == 0]))
-    unit_sent = gather_groups(sent_unit)
     outgoing, _ = lax.optimization_barrier((outgoing, others))
 
     arrived = lax.all_to_all(
@@ -433,43 +449,34 @@
     ).reshape(owners * slot, width)
     layer_out, = call(
         relay_kernel, [((tok, width), b16)], [VMEM], [arrived],
-        flops=3 * tok * tok * width, nbytes=6 * tok * width, room=8,
+        room=63,
     )
 
     candidates = jnp.concatenate([history[:, None], negatives], 1)
     vocab = vocab_dev * owners
     far_give, far_gated = to_core(give), to_core(gated)
-    layer_out, score_unit, far_give, far_gated = lax.optimization_barrier((layer_out, unit, far_give, far_gated))
+    units = [p[3] for p in unit_sent]
+    layer_out, score_unit, far_give, far_gated, units = lax.optimization_barrier(
+        (layer_out, unit, far_give, far_gated, units)
+    )
     tags, up, up_keep, up_give = call(
         lambda *refs: score_kernel(groups, owners, share, chunks, [p[:5] for p in pieces], *refs),
         [((2 * owners, tok), f32), ((tok, width), b16), ((tok, width // 2), b16), ((tok, width // 2), b16)],
         [VMEM] * 2 + [ANY] * (len(pieces) + 2), [candidates, inv_len, unit_b, score_unit] + [p[5] for p in pieces],
         [pltpu.VMEM((vocab, width), b16), pltpu.VMEM((tok, vocab), b16), pltpu.VMEM((tok, width), b16),
          pltpu.VMEM((tok, width), f32), pltpu.SemaphoreType.DMA((len(pieces) + 2,))],
-        flops=4 * tok * width * vocab, nbytes=2 * vocab * width + 12 * tok * width, room=24 if groups == 4 else 58,
-    )
-    units = [p[3] for p in unit_sent]
-
-    up, _ = lax.optimization_barrier((up, [p[3] for p in unit_sent[1:3]]))
+        room=63,
+    )
 
     grad, = call(
         backward_kernel, [((tok, 4 * hidden), b16)], [VMEM] * 8,
-        [up, out_weight, proj, slope, attn, attn_slope, normed, inverse],
-        flops=2 * tok * width * hidden, nbytes=20 * tok * width,
+        [up, out_weight, proj, slope, attn, attn_slope, normed, inverse], room=60,
     )
 
     all_tags = [to_group(tags, k) if k else tags for k in range(groups)]
-    far = [far_give, to_core(up_give), to_core(grad), far_gated]
-    mine, other = call(
-        lambda *refs: item_kernel(groups, owners, share, chunks, [p[:3] for p in unit_sent], *refs),
-        [((chips * share, width), b16)] * 2, [ANY] * len(units) + [VMEM] * groups + [ANY] * len(near),
-        units + all_tags + near,
-        [pltpu.VMEM((groups * tok, width), b16), pltpu.VMEM((2 * chips * share, width), b16),
-         pltpu.SemaphoreType.DMA((len(units) + 2 * chips,))],
-        flops=4 * groups * tok * width * chips * share, nbytes=4 * tok * groups * width, room=16 if groups == 4 else 48,
-    )
-    far_mine = to_core(other)
-    far, mine = lax.optimization_barrier((far, mine))
+    far = [far_give, to_core(up_give), None, far_gated]
+    grad, far[1], all_tags = lax.optimization_barrier((grad, far[1], all_tags))
+    far[2] = to_core(grad)
     half = 5 * hidden // 2
     if groups == 4:
         block = (chips, fine, 5 * hidden)
@@ -479,8 +486,9 @@
             [(block, b16)] + [((2,) + split, b16)] * 2 + [(split, b16)] * 2, [VMEM] * 8,
             [keep, far[0], up_keep, far[1], grad, far[2], gated, far[3]],
             [pltpu.VMEM((width // 2, 5 * hidden), b16)],
-            flops=2 * tok * width * 5 * hidden, nbytes=20 * tok * width, room=14,
+            flops=2 * tok * width * 5 * hidden, nbytes=20 * tok * width, room=60,
         )
+        after = parts[0]
         by_one, by_two = to_group(parts[1], 1), to_group(parts[2], 2)
         one_right = (parts[3].astype(f32) + by_two[0].astype(f32)).astype(b16)
         two_left = (parts[4].astype(f32) + by_one[0].astype(f32)).astype(b16)
@@ -493,16 +501,28 @@
         out_part = dot(both(up_keep, far[1]), both(gated, far[3]), TN)
         weight = jnp.concatenate([in_part, out_part], 1).astype(b16)
         weight = weight.reshape(chips, groups, fine, 5 * hidden)
+        after = weight
         sums = lax.dynamic_index_in_dim(weight, grp, 1, False).astype(f32)
         for k in range(1, groups):
             sums += to_group(lax.dynamic_index_in_dim(weight, grp ^ k, 1, False), k).astype(f32)
 
 
+    units[0], _ = lax.optimization_barrier((units[0], after))
+    mine, other = call(
+        lambda *refs: item_kernel(groups, owners, share, chunks, [p[:3] for p in unit_sent], *refs),
+        [((chips * share, width), b16)] * 2, [ANY] * len(units) + [VMEM] * groups + [ANY] * len(near),
+        units + all_tags + near,
+        [pltpu.VMEM((groups * tok, width), b16), pltpu.VMEM((2 * chips * share, width), b16),
+         pltpu.SemaphoreType.DMA((len(units) + 2 * chips,))],
+        flops=4 * groups * tok * width * chips * share, nbytes=4 * tok * groups * width, room=60,
+    )
+    far_mine = to_core(other)
+
     summed = call(
         pair_kernel, [((share, width), b16)] * chips, [VMEM] * 2, [mine, far_mine],
         flops=chips * share * width, nbytes=6 * chips * share * width, room=8,
     )
-    come = [to_chip(summed[d], -d) for d in range(1, chips)]
+    come = [across(summed[n], d) for n, d in enumerate(distances(chips)) if d]
     total = summed[0].astype(f32)
     for x in come:
         total += x.astype(f32)
@@ -514,7 +534,7 @@
     )
 
     if groups == 4:
-        base, _ = lax.optimization_barrier((parts[0], come[0]))
+        base = parts[0]
         sums = call(
             sum_kernel, [((fine, 5 * hidden), b16)] * chips, [VMEM] * 5, [base] + arrived,
             flops=chips * fine * 5 * hidden, nbytes=40 * chips * fine * hidden, room=10,

time: 192 us -> 191 us (level)
  the two profiles are of different devices: /device:TPU:0 before, /device:TPU:9 now
where the time goes in v7:
time: 191 us
  waiting for transfers between devices  79.1 us (41%)
  starting transfers between devices  53.9 us (28%)
  Pallas kernels  45.3 us (24%)
  local copies, waits for them, and re-layouts  8.17 us (4%)
  other arithmetic  3.36 us (2%)
    pallas_call x11, Pallas kernels, call(): pl.pallas_call(kernel, out_shape=[jax.ShapeDtypeStruct(s, t) for s, t in...  45.3 us
    ppermute x21, waiting for transfers between devices, to_group(): return lax.ppermute(x, 'grp', [(a, a ^ k) for a in range(groups)])  34.6 us
    ppermute x6, waiting for transfers between devices, across(): return lax.ppermute(x, 'seq', pairs)  25 us
    ppermute x11, starting transfers between devices, to_core(): return lax.ppermute(x, 'seq', [(a, a ^ 1) for a in range(owners)])  20.6 us
    ppermute x21, starting transfers between devices, to_group(): return lax.ppermute(x, 'grp', [(a, a ^ k) for a in range(groups)])  17.7 us
    ppermute x3, waiting for transfers between devices, to_chip(): return lax.ppermute(x, 'seq', pairs)  16.7 us
    ppermute x6, starting transfers between devices, across(): return lax.ppermute(x, 'seq', pairs)  6.48 us
    all_to_all x1, starting transfers between devices, body(): lax.all_to_all(outgoing.reshape(owners, slot, width), 'seq', 0, 0, tiled=...  4.95 us
  transfers between devices with their start and end apart: 42, of which 14 were waited for; matrix products, arithmetic and copies ran while one was open for 4% of the time, Pallas kernels for 14%

profile of v7, /device:TPU:9, one launch (start us, length us, event | category | flops | bytes accessed | tf_op | source)
XLA Modules:
  0.0 190.7 jit_solution(12088731848417765603)
XLA Ops:
  1.9 1.4 shard_map.112
  3.2 2.3 %collective-permute-start = (bf16[128,1024]{1,0:T(8,128)(2,1)S(1)}, bf16[128,1024]{1,0:T(8,128)(2,1)S(1)}, u32[]{:S(2)}, u32[]{:S(2)}) collective-permute-start(bf16[128,1024]{1,0:T(8,128)(2,1)S(1)} %get-tuple-element.65), channel_id=1, source_target_pairs={{0,4},{1,5},{2,6},{3,7},{4,0},{5,1},{6,2},{7,3},{8,12},{9,13},{10,... | collective-permute-start | bytes 786440 | tf_op jit(solution)/shard_map/ppermute | solution.py:395
  5.5 9.1 %shard_map.111 = (bf16[256,512]{1,0:T(8,128)(2,1)}, bf16[256,512]{1,0:T(8,128)(2,1)}, bf16[256,2048]{1,0:T(8,128)(2,1)}, bf16[256,2048]{1,0:T(8,128)(2,1)}, bf16...) custom-call(s32[1,8]{1,0:T(1,128)} %refs_0_.2, ...), custom_call_target="tpu_custom_call" | custom-call | tf_op jit(solution)/shard_map/pallas_call | solution.py:53
  14.7 1.3 collective-permute-start.4
  18.6 4.8 %collective-permute-done.1 = bf16[128,1024]{1,0:T(8,128)(2,1)S(1)} collective-permute-done((bf16[128,1024]{1,0:T(8,128)(2,1)S(1)}, bf16[128,1024]{1,0:T(8,128)(2,1)S(1)}, u32[]{:S(2)}, u32[]{:S(2)}) %collective-permute-start.1) | collective-permute-done | bytes 262176 | tf_op jit(solution)/shard_map/ppermute | solution.py:395
  23.5 5.6 %collective-permute-done.2 = bf16[128,1024]{1,0:T(8,128)(2,1)S(1)} collective-permute-done((bf16[128,1024]{1,0:T(8,128)(2,1)S(1)}, bf16[128,1024]{1,0:T(8,128)(2,1)S(1)}, u32[]{:S(2)}, u32[]{:S(2)}) %collective-permute-start.2) | collective-permute-done | bytes 262176 | tf_op jit(solution)/shard_map/ppermute | solution.py:395
  30.4 2.5 %collective-permute-start.14 = (bf16[384,1024]{1,0:T(8,128)(2,1)S(1)}, bf16[384,1024]{1,0:T(8,128)(2,1)S(1)}, u32[]{:S(2)}, u32[]{:S(2)}) collective-permute-start(bf16[384,1024]{1,0:T(8,128)(2,1)S(1)} %constant_dynamic-update-slice_fusion.refs_5_.refs_10_), channel_id=1, source_target_pairs={{0,1},{1,0},{2,3},{3,2},{4,5},{5,4},{6,7},{7,6},{8,9},{9,8},{10,11... | collective-permute-start | bytes 2359304 | tf_op jit(solution)/shard_map/ppermute | solution.py:401
  32.9 4.9 %all-to-all-start = ((bf16[8,48,1024]{2,1,0:T(8,128)(2,1)}), bf16[8,48,1024]{2,1,0:T(8,128)(2,1)S(1)}, u32[]{:S(2)}, u32[]{:S(2)}) async-start(bf16[8,48,1024]{2,1,0:T(8,128)(2,1)} %bitcast.14), calls=%async_computation | async-start | bytes 1572864 | tf_op jit(solution)/shard_map/all_to_all | solution.py:447
  39.9 6.1 %collective-permute-done.10.refs_7_ = bf16[384,1024]{1,0:T(8,128)(2,1)} collective-permute-done((bf16[384,1024]{1,0:T(8,128)(2,1)S(1)}, bf16[384,1024]{1,0:T(8,128)(2,1)}, u32[]{:S(2)}, u32[]{:S(2)}) %collective-permute-start.10) | collective-permute-done | bytes 786464 | tf_op jit(solution)/shard_map/ppermute | solution.py:398
  46.0 3.4 %collective-permute-start.13 = (bf16[512,1024]{1,0:T(8,128)(2,1)}, bf16[512,1024]{1,0:T(8,128)(2,1)}, u32[]{:S(2)}, u32[]{:S(2)}) collective-permute-start(bf16[512,1024]{1,0:T(8,128)(2,1)} %get-tuple-element.82.refs_4_.refs_9_), channel_id=1, source_target_pairs={{0,1},{1,0},{2,3},{3,2},{4,5},{5,4},{6,7},{7,6},{8,9},{9,8},{10,11... | collective-permute-start | bytes 3145736 | tf_op jit(solution)/shard_map/ppermute | solution.py:401
  53.5 1.4 collective-permute-done.7.refs_3_
  54.9 7.1 %collective-permute-start.16 = (bf16[384,1024]{1,0:T(8,128)(2,1)}, bf16[384,1024]{1,0:T(8,128)(2,1)}, u32[]{:S(2)}, u32[]{:S(2)}) collective-permute-start(bf16[384,1024]{1,0:T(8,128)(2,1)} %collective-permute-done.10.refs_7_), channel_id=1, source_target_pairs={{0,1},{1,0},{2,3},{3,2},{4,5},{5,4},{6,7},{7,6},{8,9},{9,8},{10,11... | collective-permute-start | bytes 2359304 | tf_op jit(solution)/shard_map/ppermute | solution.py:401
  62.1 2.0 %collective-permute-start.18 = (bf16[384,512]{1,0:T(8,128)(2,1)}, bf16[384,512]{1,0:T(8,128)(2,1)}, u32[]{:S(2)}, u32[]{:S(2)}) collective-permute-start(bf16[384,512]{1,0:T(8,128)(2,1)} %collective-permute-done.12.refs_9_), channel_id=1, source_target_pairs={{0,1},{1,0},{2,3},{3,2},{4,5},{5,4},{6,7},{7,6},{8,9},{9,8},{10,11... | collective-permute-start | bytes 1179656 | tf_op jit(solution)/shard_map/ppermute | solution.py:401
  64.0 2.7 %collective-permute-start.17 = (bf16[384,512]{1,0:T(8,128)(2,1)}, bf16[384,512]{1,0:T(8,128)(2,1)}, u32[]{:S(2)}, u32[]{:S(2)}) collective-permute-start(bf16[384,512]{1,0:T(8,128)(2,1)} %collective-permute-done.11.refs_8_), channel_id=1, source_target_pairs={{0,1},{1,0},{2,3},{3,2},{4,5},{5,4},{6,7},{7,6},{8,9},{9,8},{10,11... | collective-permute-start | bytes 1179656 | tf_op jit(solution)/shard_map/ppermute | solution.py:401
  68.5 2.7 %shard_map.113 = bf16[256,1024]{1,0:T(8,128)(2,1)} custom-call(bf16[384,1024]{1,0:T(8,128)(2,1)} %bitcast.13), custom_call_target="tpu_custom_call" | custom-call | tf_op jit(solution)/shard_map/pallas_call | solution.py:53
  71.3 11.3 %shard_map.114 = (f32[16,256]{1,0:T(8,128)}, bf16[256,1024]{1,0:T(8,128)(2,1)}, bf16[256,512]{1,0:T(8,128)(2,1)}, bf16[256,512]{1,0:T(8,128)(2,1)}) custom-call(s32[256,4]{1,0:T(8,128)} %copy.15.refs_0_, f32[256,1]{1,0:T(8,128)} %get-tuple-element.80.refs_1_, bf16[256,1024]{1,0:T(8,128)(2,1)} %get-tuple-element.108.refs_2_.refs_0_, ...), custom_call_target="tpu_custom_call" | custom-call | tf_op jit(solution)/shard_map/pallas_call | solution.py:53
  82.6 1.9 %collective-permute-start.22 = (f32[16,256]{1,0:T(8,128)}, f32[16,256]{1,0:T(8,128)S(1)}, u32[]{:S(2)}, u32[]{:S(2)}) collective-permute-start(f32[16,256]{1,0:T(8,128)} %get-tuple-element.113.refs_5_), channel_id=1, source_target_pairs={{0,24},{8,16},{16,8},{24,0},{1,25},{9,17},{17,9},{25,1},{2,26},{10... | collective-permute-start | bytes 49160 | tf_op jit(solution)/shard_map/ppermute | solution.py:398
  85.4 5.0 %shard_map.115.refs_4_ = bf16[256,2048]{1,0:T(8,128)(2,1)} custom-call(bf16[256,1024]{1,0:T(8,128)(2,1)} %get-tuple-element.84.up, bf16[1024,512]{1,0:T(8,128)(2,1)} %out_weight.1, bf16[256,2048]{1,0:T(8,128)(2,1)} %get-tuple-element.85.proj, bf16[256,2048]{1,0:T(8,128)(2,1)} %get-tuple-element.86.slope, bf16[4,256,256]{2,1,0:T(8,128)(2,1)} %get-tuple-element.87.attn, ...), custom_call_target="tpu_custom_call" | custom-call | tf_op jit(solution)/shard_map/pallas_call | solution.py:53
  90.4 1.3 collective-permute-start.23
  91.8 2.5 %collective-permute-done.23.refs_5_ = bf16[256,2048]{1,0:T(8,128)(2,1)S(1)} collective-permute-done((bf16[256,2048]{1,0:T(8,128)(2,1)}, bf16[256,2048]{1,0:T(8,128)(2,1)S(1)}, u32[]{:S(2)}, u32[]{:S(2)}) %collective-permute-start.23) | collective-permute-done | bytes 1048608 | tf_op jit(solution)/shard_map/ppermute | solution.py:401
  95.2 5.1 %shard_map.116 = (bf16[4,32,2560]{2,1,0:T(8,128)(2,1)}, bf16[2,4,32,1280]{3,2,1,0:T(8,128)(2,1)}, bf16[2,4,32,1280]{3,2,1,0:T(8,128)(2,1)}, bf16[4,32,1280]{2,1,0:T(8,128)(2,1)}, bf16[4,32,1280]{2,1,0:T(8,128)(2,1)}) custom-call(bf16[256,512]{1,0:T(8,128)(2,1)} %get-tuple-element.78.refs_0_, bf16[256,512]{1,0:T(8,128)(2,1)} %copy-done.13, ...), custom_call_target="tpu_custom_call" | custom-call | flops 1342177280 | bytes 5242880 | tf_op jit(solution)/shard_map/pallas_call | solution.py:53
  102.5 7.0 %shard_map.119 = (bf16[512,1024]{1,0:T(8,128)(2,1)}, bf16[512,1024]{1,0:T(8,128)(2,1)}) custom-call(bf16[256,1024]{1,0:T(8,128)(2,1)} %get-tuple-element.108.refs_2_.refs_0_, bf16[256,1024]{1,0:T(8,128)(2,1)} %copy-done.8, bf16[256,1024]{1,0:T(8,128)(2,1)} %copy-done.7, bf16[256,512]{1,0:T(8,128)(2,1)} %copy-done.15, bf16[256,512]{1,0:T(8,128)(2,1)} %copy-done.12, ...), custom_call_target="tpu_custom_call" | custom-call | flops 2147483648 | bytes 4194304 | tf_op jit(solution)/shard_map/pallas_call | solution.py:53
  110.5 6.0 %collective-permute-done.24.by_one = bf16[2,4,32,1280]{3,2,1,0:T(8,128)(2,1)S(1)} collective-permute-done((bf16[2,4,32,1280]{3,2,1,0:T(8,128)(2,1)}, bf16[2,4,32,1280]{3,2,1,0:T(8,128)(2,1)S(1)}, u32[]{:S(2)}, u32[]{:S(2)}) %collective-permute-start.24) | collective-permute-done | bytes 655392 | tf_op jit(solution)/shard_map/ppermute | solution.py:398
  120.9 4.7 %collective-permute-done.27.two_left = bf16[4,32,1280]{2,1,0:T(8,128)(2,1)S(1)} collective-permute-done((bf16[4,32,1280]{2,1,0:T(8,128)(2,1)S(1)}, bf16[4,32,1280]{2,1,0:T(8,128)(2,1)S(1)}, u32[]{:S(2)}, u32[]{:S(2)}) %collective-permute-start.27) | collective-permute-done | bytes 327712 | tf_op jit(solution)/shard_map/ppermute | solution.py:398
  125.6 2.0 %collective-permute-done.26.one_right = bf16[4,32,1280]{2,1,0:T(8,128)(2,1)S(1)} collective-permute-done((bf16[4,32,1280]{2,1,0:T(8,128)(2,1)S(1)}, bf16[4,32,1280]{2,1,0:T(8,128)(2,1)S(1)}, u32[]{:S(2)}, u32[]{:S(2)}) %collective-permute-start.26) | collective-permute-done | bytes 327712 | tf_op jit(solution)/shard_map/ppermute | solution.py:398
  129.4 2.4 %collective-permute-start.29 = (bf16[32,2560]{1,0:T(8,128)(2,1)}, bf16[32,2560]{1,0:T(8,128)(2,1)S(1)}, u32[]{:S(2)}, u32[]{:S(2)}) collective-permute-start(bf16[32,2560]{1,0:T(8,128)(2,1)} %get-tuple-element.103), channel_id=1, source_target_pairs={{0,4},{1,5},{2,6},{3,7},{4,0},{5,1},{6,2},{7,3},{8,12},{9,13},{10,... | collective-permute-start | bytes 491528 | tf_op jit(solution)/shard_map/ppermute | solution.py:391
  131.8 1.5 collective-permute-start.30
  134.9 1.5 collective-permute-start.37
  137.7 15.4 %collective-permute-done.30 = bf16[32,2560]{1,0:T(8,128)(2,1)S(1)} collective-permute-done((bf16[32,2560]{1,0:T(8,128)(2,1)}, bf16[32,2560]{1,0:T(8,128)(2,1)S(1)}, u32[]{:S(2)}, u32[]{:S(2)}) %collective-permute-start.30) | collective-permute-done | bytes 163872 | tf_op jit(solution)/shard_map/ppermute | solution.py:391
  155.8 14.0 %collective-permute-done.37 = bf16[128,1024]{1,0:T(8,128)(2,1)S(1)} collective-permute-done((bf16[128,1024]{1,0:T(8,128)(2,1)S(1)}, bf16[128,1024]{1,0:T(8,128)(2,1)S(1)}, u32[]{:S(2)}, u32[]{:S(2)}) %collective-permute-start.37) | collective-permute-done | bytes 262176 | tf_op jit(solution)/shard_map/ppermute | solution.py:395
  173.8 14.4 %collective-permute-done.32.refs_2_ = bf16[32,2560]{1,0:T(8,128)(2,1)S(1)} collective-permute-done((bf16[32,2560]{1,0:T(8,128)(2,1)S(1)}, bf16[32,2560]{1,0:T(8,128)(2,1)S(1)}, u32[]{:S(2)}, u32[]{:S(2)}) %collective-permute-start.32) | collective-permute-done | bytes 163872 | tf_op jit(solution)/shard_map/ppermute | solution.py:398
  189.3 1.5 shard_map.121
  (117 shorter events, 35.0 us)
Async XLA Ops:
  3.2 14.1 %collective-permute-start = (bf16[128,1024]{1,0:T(8,128)(2,1)S(1)}, bf16[128,1024]{1,0:T(8,128)(2,1)S(1)}, u32[]{:S(2)}, u32[]{:S(2)}) collective-permute-start(bf16[128,1024]{1,0:T(8,128)(2,1)S(1)} %get-tuple-element.65), channel_id=1, source_target_pairs={{0,4},{1,5},{2,6},{3,7},{4,0},{5,1},{6,2},{7,3},{8,12},{9,13},{10,... | collective-permute-start | bytes 786440 | tf_op jit(solution)/shard_map/ppermute | solution.py:395
  14.7 14.4 %collective-permute-start.4 = (bf16[256,1024]{1,0:T(8,128)(2,1)}, bf16[256,1024]{1,0:T(8,128)(2,1)S(1)}, u32[]{:S(2)}, u32[]{:S(2)}) collective-permute-start(bf16[256,1024]{1,0:T(8,128)(2,1)} %get-tuple-element.108.refs_2_.refs_0_), channel_id=1, source_target_pairs={{0,16},{8,24},{16,0},{24,8},{1,17},{9,25},{17,1},{25,9},{2,18},{10... | collective-permute-start | bytes 1572872 | tf_op jit(solution)/shard_map/ppermute | solution.py:398
  16.0 13.1 %collective-permute-start.3 = (bf16[256,1024]{1,0:T(8,128)(2,1)}, bf16[256,1024]{1,0:T(8,128)(2,1)S(1)}, u32[]{:S(2)}, u32[]{:S(2)}) collective-permute-start(bf16[256,1024]{1,0:T(8,128)(2,1)} %get-tuple-element.108.refs_2_.refs_0_), channel_id=1, source_target_pairs={{0,8},{8,0},{16,24},{24,16},{1,9},{9,1},{17,25},{25,17},{2,10},{10... | collective-permute-start | bytes 1572872 | tf_op jit(solution)/shard_map/ppermute | solution.py:398
  17.3 11.7 %collective-permute-start.2 = (bf16[128,1024]{1,0:T(8,128)(2,1)S(1)}, bf16[128,1024]{1,0:T(8,128)(2,1)S(1)}, u32[]{:S(2)}, u32[]{:S(2)}) collective-permute-start(bf16[128,1024]{1,0:T(8,128)(2,1)S(1)} %collective-permute-done), channel_id=1, source_target_pairs={{0,2},{1,3},{2,0},{3,1},{4,6},{5,7},{6,4},{7,5},{8,10},{9,11},{10,... | collective-permute-start | bytes 786440 | tf_op jit(solution)/shard_map/ppermute | solution.py:395
  29.2 16.8 %collective-permute-start.10 = (bf16[384,1024]{1,0:T(8,128)(2,1)S(1)}, bf16[384,1024]{1,0:T(8,128)(2,1)}, u32[]{:S(2)}, u32[]{:S(2)}) collective-permute-start(bf16[384,1024]{1,0:T(8,128)(2,1)S(1)} %constant_dynamic-update-slice_fusion.refs_5_.refs_10_), channel_id=1, source_target_pairs={{0,16},{8,24},{16,0},{24,8},{1,17},{9,25},{17,1},{25,9},{2,18},{10... | collective-permute-start | bytes 2359304 | tf_op jit(solution)/shard_map/ppermute | solution.py:398
  29.9 19.4 %collective-permute-start.9 = (bf16[384,1024]{1,0:T(8,128)(2,1)S(1)}, bf16[384,1024]{1,0:T(8,128)(2,1)}, u32[]{:S(2)}, u32[]{:S(2)}) collective-permute-start(bf16[384,1024]{1,0:T(8,128)(2,1)S(1)} %constant_dynamic-update-slice_fusion.refs_5_.refs_10_), channel_id=1, source_target_pairs={{0,8},{8,0},{16,24},{24,16},{1,9},{9,1},{17,25},{25,17},{2,10},{10... | collective-permute-start | bytes 2359304 | tf_op jit(solution)/shard_map/ppermute | solution.py:398
  30.4 31.6 %collective-permute-start.14 = (bf16[384,1024]{1,0:T(8,128)(2,1)S(1)}, bf16[384,1024]{1,0:T(8,128)(2,1)S(1)}, u32[]{:S(2)}, u32[]{:S(2)}) collective-permute-start(bf16[384,1024]{1,0:T(8,128)(2,1)S(1)} %constant_dynamic-update-slice_fusion.refs_5_.refs_10_), channel_id=1, source_target_pairs={{0,1},{1,0},{2,3},{3,2},{4,5},{5,4},{6,7},{7,6},{8,9},{9,8},{10,11... | collective-permute-start | bytes 2359304 | tf_op jit(solution)/shard_map/ppermute | solution.py:401
  32.9 34.7 %all-to-all-start = ((bf16[8,48,1024]{2,1,0:T(8,128)(2,1)}), bf16[8,48,1024]{2,1,0:T(8,128)(2,1)S(1)}, u32[]{:S(2)}, u32[]{:S(2)}) async-start(bf16[8,48,1024]{2,1,0:T(8,128)(2,1)} %bitcast.14), calls=%async_computation | async-start | bytes 1572864 | tf_op jit(solution)/shard_map/all_to_all | solution.py:447
  38.2 13.4 %collective-permute-start.6 = (bf16[256,512]{1,0:T(8,128)(2,1)}, bf16[256,512]{1,0:T(8,128)(2,1)S(1)}, u32[]{:S(2)}, u32[]{:S(2)}) collective-permute-start(bf16[256,512]{1,0:T(8,128)(2,1)} %get-tuple-element.74.refs_6_), channel_id=1, source_target_pairs={{0,1},{1,0},{2,3},{3,2},{4,5},{5,4},{6,7},{7,6},{8,9},{9,8},{10,11... | collective-permute-start | bytes 786440 | tf_op jit(solution)/shard_map/ppermute | solution.py:401
  39.6 12.7 %collective-permute-start.8 = (bf16[256,512]{1,0:T(8,128)(2,1)S(1)}, bf16[256,512]{1,0:T(8,128)(2,1)S(1)}, u32[]{:S(2)}, u32[]{:S(2)}) collective-permute-start(bf16[256,512]{1,0:T(8,128)(2,1)S(1)} %slice.19), channel_id=1, source_target_pairs={{0,8},{8,0},{16,24},{24,16},{1,9},{9,1},{17,25},{25,17},{2,10},{10... | collective-permute-start | bytes 786440 | tf_op jit(solution)/shard_map/ppermute | solution.py:398
  46.0 25.3 %collective-permute-start.13 = (bf16[512,1024]{1,0:T(8,128)(2,1)}, bf16[512,1024]{1,0:T(8,128)(2,1)}, u32[]{:S(2)}, u32[]{:S(2)}) collective-permute-start(bf16[512,1024]{1,0:T(8,128)(2,1)} %get-tuple-element.82.refs_4_.refs_9_), channel_id=1, source_target_pairs={{0,1},{1,0},{2,3},{3,2},{4,5},{5,4},{6,7},{7,6},{8,9},{9,8},{10,11... | collective-permute-start | bytes 3145736 | tf_op jit(solution)/shard_map/ppermute | solution.py:401
  51.7 10.4 %collective-permute-start.12 = (bf16[384,512]{1,0:T(8,128)(2,1)S(1)}, bf16[384,512]{1,0:T(8,128)(2,1)}, u32[]{:S(2)}, u32[]{:S(2)}) collective-permute-start(bf16[384,512]{1,0:T(8,128)(2,1)S(1)} %slice.25), channel_id=1, source_target_pairs={{0,8},{8,0},{16,24},{24,16},{1,9},{9,1},{17,25},{25,17},{2,10},{10... | collective-permute-start | bytes 1179656 | tf_op jit(solution)/shard_map/ppermute | solution.py:398
  52.3 11.8 %collective-permute-start.11 = (bf16[384,512]{1,0:T(8,128)(2,1)S(1)}, bf16[384,512]{1,0:T(8,128)(2,1)}, u32[]{:S(2)}, u32[]{:S(2)}) collective-permute-start(bf16[384,512]{1,0:T(8,128)(2,1)S(1)} %slice.24), channel_id=1, source_target_pairs={{0,16},{8,24},{16,0},{24,8},{1,17},{9,25},{17,1},{25,9},{2,18},{10... | collective-permute-start | bytes 1179656 | tf_op jit(solution)/shard_map/ppermute | solution.py:398
  54.9 16.3 %collective-permute-start.16 = (bf16[384,1024]{1,0:T(8,128)(2,1)}, bf16[384,1024]{1,0:T(8,128)(2,1)}, u32[]{:S(2)}, u32[]{:S(2)}) collective-permute-start(bf16[384,1024]{1,0:T(8,128)(2,1)} %collective-permute-done.10.refs_7_), channel_id=1, source_target_pairs={{0,1},{1,0},{2,3},{3,2},{4,5},{5,4},{6,7},{7,6},{8,9},{9,8},{10,11... | collective-permute-start | bytes 2359304 | tf_op jit(solution)/shard_map/ppermute | solution.py:401
  62.0 9.3 %collective-permute-start.15 = (bf16[384,1024]{1,0:T(8,128)(2,1)}, bf16[384,1024]{1,0:T(8,128)(2,1)}, u32[]{:S(2)}, u32[]{:S(2)}) collective-permute-start(bf16[384,1024]{1,0:T(8,128)(2,1)} %collective-permute-done.9.refs_6_), channel_id=1, source_target_pairs={{0,1},{1,0},{2,3},{3,2},{4,5},{5,4},{6,7},{7,6},{8,9},{9,8},{10,11... | collective-permute-start | bytes 2359304 | tf_op jit(solution)/shard_map/ppermute | solution.py:401
  62.1 9.1 %collective-permute-start.18 = (bf16[384,512]{1,0:T(8,128)(2,1)}, bf16[384,512]{1,0:T(8,128)(2,1)}, u32[]{:S(2)}, u32[]{:S(2)}) collective-permute-start(bf16[384,512]{1,0:T(8,128)(2,1)} %collective-permute-done.12.refs_9_), channel_id=1, source_target_pairs={{0,1},{1,0},{2,3},{3,2},{4,5},{5,4},{6,7},{7,6},{8,9},{9,8},{10,11... | collective-permute-start | bytes 1179656 | tf_op jit(solution)/shard_map/ppermute | solution.py:401
  82.6 7.9 %collective-permute-start.19 = (bf16[256,512]{1,0:T(8,128)(2,1)}, bf16[256,512]{1,0:T(8,128)(2,1)S(1)}, u32[]{:S(2)}, u32[]{:S(2)}) collective-permute-start(bf16[256,512]{1,0:T(8,128)(2,1)} %get-tuple-element.91), channel_id=1, source_target_pairs={{0,1},{1,0},{2,3},{3,2},{4,5},{5,4},{6,7},{7,6},{8,9},{9,8},{10,11... | collective-permute-start | bytes 786440 | tf_op jit(solution)/shard_map/ppermute | solution.py:401
  100.3 16.2 %collective-permute-start.24 = (bf16[2,4,32,1280]{3,2,1,0:T(8,128)(2,1)}, bf16[2,4,32,1280]{3,2,1,0:T(8,128)(2,1)S(1)}, u32[]{:S(2)}, u32[]{:S(2)}) collective-permute-start(bf16[2,4,32,1280]{3,2,1,0:T(8,128)(2,1)} %get-tuple-element.97), channel_id=1, source_target_pairs={{0,8},{8,0},{16,24},{24,16},{1,9},{9,1},{17,25},{25,17},{2,10},{10... | collective-permute-start | bytes 1966088 | tf_op jit(solution)/shard_map/ppermute | solution.py:398
  101.2 17.5 %collective-permute-start.25 = (bf16[2,4,32,1280]{3,2,1,0:T(8,128)(2,1)}, bf16[2,4,32,1280]{3,2,1,0:T(8,128)(2,1)S(1)}, u32[]{:S(2)}, u32[]{:S(2)}) collective-permute-start(bf16[2,4,32,1280]{3,2,1,0:T(8,128)(2,1)} %get-tuple-element.98), channel_id=1, source_target_pairs={{0,16},{8,24},{16,0},{24,8},{1,17},{9,25},{17,1},{25,9},{2,18},{10... | collective-permute-start | bytes 1966088 | tf_op jit(solution)/shard_map/ppermute | solution.py:398
  109.5 23.9 %collective-permute-start.34 = (bf16[512,1024]{1,0:T(8,128)(2,1)}, bf16[512,1024]{1,0:T(8,128)(2,1)S(1)}, u32[]{:S(2)}, u32[]{:S(2)}) collective-permute-start(bf16[512,1024]{1,0:T(8,128)(2,1)} %get-tuple-element.118), channel_id=1, source_target_pairs={{0,1},{1,0},{2,3},{3,2},{4,5},{5,4},{6,7},{7,6},{8,9},{9,8},{10,11... | collective-permute-start | bytes 3145736 | tf_op jit(solution)/shard_map/ppermute | solution.py:401
  117.5 8.1 %collective-permute-start.27 = (bf16[4,32,1280]{2,1,0:T(8,128)(2,1)S(1)}, bf16[4,32,1280]{2,1,0:T(8,128)(2,1)S(1)}, u32[]{:S(2)}, u32[]{:S(2)}) collective-permute-start(bf16[4,32,1280]{2,1,0:T(8,128)(2,1)S(1)} %fusion), channel_id=1, source_target_pairs={{0,16},{8,24},{16,0},{24,8},{1,17},{9,25},{17,1},{25,9},{2,18},{10... | collective-permute-start | bytes 983048 | tf_op jit(solution)/shard_map/ppermute | solution.py:398
  129.4 8.3 %collective-permute-start.29 = (bf16[32,2560]{1,0:T(8,128)(2,1)}, bf16[32,2560]{1,0:T(8,128)(2,1)S(1)}, u32[]{:S(2)}, u32[]{:S(2)}) collective-permute-start(bf16[32,2560]{1,0:T(8,128)(2,1)} %get-tuple-element.103), channel_id=1, source_target_pairs={{0,4},{1,5},{2,6},{3,7},{4,0},{5,1},{6,2},{7,3},{8,12},{9,13},{10,... | collective-permute-start | bytes 491528 | tf_op jit(solution)/shard_map/ppermute | solution.py:391
  131.8 21.3 %collective-permute-start.30 = (bf16[32,2560]{1,0:T(8,128)(2,1)}, bf16[32,2560]{1,0:T(8,128)(2,1)S(1)}, u32[]{:S(2)}, u32[]{:S(2)}) collective-permute-start(bf16[32,2560]{1,0:T(8,128)(2,1)} %get-tuple-element.104), channel_id=1, source_target_pairs={{0,6},{1,7},{2,0},{3,1},{4,2},{5,3},{6,4},{7,5},{8,14},{9,15},{10,... | collective-permute-start | bytes 491528 | tf_op jit(solution)/shard_map/ppermute | solution.py:391
  133.7 22.1 %collective-permute-start.35 = (bf16[128,1024]{1,0:T(8,128)(2,1)S(1)}, bf16[128,1024]{1,0:T(8,128)(2,1)S(1)}, u32[]{:S(2)}, u32[]{:S(2)}) collective-permute-start(bf16[128,1024]{1,0:T(8,128)(2,1)S(1)} %get-tuple-element.120), channel_id=1, source_target_pairs={{0,4},{1,5},{2,6},{3,7},{4,0},{5,1},{6,2},{7,3},{8,12},{9,13},{10,... | collective-permute-start | bytes 786440 | tf_op jit(solution)/shard_map/ppermute | solution.py:395
  133.8 22.0 %collective-permute-start.36 = (bf16[128,1024]{1,0:T(8,128)(2,1)S(1)}, bf16[128,1024]{1,0:T(8,128)(2,1)S(1)}, u32[]{:S(2)}, u32[]{:S(2)}) collective-permute-start(bf16[128,1024]{1,0:T(8,128)(2,1)S(1)} %get-tuple-element.121), channel_id=1, source_target_pairs={{0,2},{1,3},{2,0},{3,1},{4,6},{5,7},{6,4},{7,5},{8,10},{9,11},{10,... | collective-permute-start | bytes 786440 | tf_op jit(solution)/shard_map/ppermute | solution.py:395
  134.9 34.8 %collective-permute-start.37 = (bf16[128,1024]{1,0:T(8,128)(2,1)S(1)}, bf16[128,1024]{1,0:T(8,128)(2,1)S(1)}, u32[]{:S(2)}, u32[]{:S(2)}) collective-permute-start(bf16[128,1024]{1,0:T(8,128)(2,1)S(1)} %get-tuple-element.122), channel_id=1, source_target_pairs={{0,6},{1,7},{2,4},{3,5},{4,2},{5,3},{6,0},{7,1},{8,14},{9,15},{10,... | collective-permute-start | bytes 786440 | tf_op jit(solution)/shard_map/ppermute | solution.py:395
  154.1 18.5 %collective-permute-start.33 = (bf16[32,2560]{1,0:T(8,128)(2,1)S(1)}, bf16[32,2560]{1,0:T(8,128)(2,1)S(1)}, u32[]{:S(2)}, u32[]{:S(2)}) collective-permute-start(bf16[32,2560]{1,0:T(8,128)(2,1)S(1)} %add_convert_fusion.refs_0_), channel_id=1, source_target_pairs={{0,24},{8,16},{16,8},{24,0},{1,25},{9,17},{17,9},{25,1},{2,26},{10... | collective-permute-start | bytes 491528 | tf_op jit(solution)/shard_map/ppermute | solution.py:398
  169.9 19.3 %collective-permute-start.40 = (bf16[128,1024]{1,0:T(8,128)(2,1)S(1)}, bf16[128,1024]{1,0:T(8,128)(2,1)S(1)}, u32[]{:S(2)}, u32[]{:S(2)}) collective-permute-start(bf16[128,1024]{1,0:T(8,128)(2,1)S(1)} %multiply_convert_fusion.refs_0_), channel_id=1, source_target_pairs={{0,24},{8,16},{16,8},{24,0},{1,25},{9,17},{17,9},{25,1},{2,26},{10... | collective-permute-start | bytes 786440 | tf_op jit(solution)/shard_map/ppermute | solution.py:398
  170.8 18.4 %collective-permute-start.39 = (bf16[128,1024]{1,0:T(8,128)(2,1)S(1)}, bf16[128,1024]{1,0:T(8,128)(2,1)S(1)}, u32[]{:S(2)}, u32[]{:S(2)}) collective-permute-start(bf16[128,1024]{1,0:T(8,128)(2,1)S(1)} %multiply_convert_fusion.refs_0_), channel_id=1, source_target_pairs={{0,16},{8,24},{16,0},{24,8},{1,17},{9,25},{17,1},{25,9},{2,18},{10... | collective-permute-start | bytes 786440 | tf_op jit(solution)/shard_map/ppermute | solution.py:398
  172.0 17.3 %collective-permute-start.38 = (bf16[128,1024]{1,0:T(8,128)(2,1)S(1)}, bf16[128,1024]{1,0:T(8,128)(2,1)S(1)}, u32[]{:S(2)}, u32[]{:S(2)}) collective-permute-start(bf16[128,1024]{1,0:T(8,128)(2,1)S(1)} %multiply_convert_fusion.refs_0_), channel_id=1, source_target_pairs={{0,8},{8,0},{16,24},{24,16},{1,9},{9,1},{17,25},{25,17},{2,10},{10... | collective-permute-start | bytes 786440 | tf_op jit(solution)/shard_map/ppermute | solution.py:398
  172.6 15.5 %collective-permute-start.32 = (bf16[32,2560]{1,0:T(8,128)(2,1)S(1)}, bf16[32,2560]{1,0:T(8,128)(2,1)S(1)}, u32[]{:S(2)}, u32[]{:S(2)}) collective-permute-start(bf16[32,2560]{1,0:T(8,128)(2,1)S(1)} %add_convert_fusion.refs_0_), channel_id=1, source_target_pairs={{0,16},{8,24},{16,0},{24,8},{1,17},{9,25},{17,1},{25,9},{2,18},{10... | collective-permute-start | bytes 491528 | tf_op jit(solution)/shard_map/ppermute | solution.py:398
  172.6 15.5 %collective-permute-start.31 = (bf16[32,2560]{1,0:T(8,128)(2,1)S(1)}, bf16[32,2560]{1,0:T(8,128)(2,1)S(1)}, u32[]{:S(2)}, u32[]{:S(2)}) collective-permute-start(bf16[32,2560]{1,0:T(8,128)(2,1)S(1)} %add_convert_fusion.refs_0_), channel_id=1, source_target_pairs={{0,8},{8,0},{16,24},{24,16},{1,9},{9,1},{17,25},{25,17},{2,10},{10... | collective-permute-start | bytes 491528 | tf_op jit(solution)/shard_map/ppermute | solution.py:398
  (30 other events, 372.0 us)

commit v8 on v7

--- a/solution.py
+++ b/solution.py
@@ -151,33 +151,16 @@
     quarter_inv[...] = inverse
 
 
-def score_kernel(groups, owners, share, chunks, places, cand, inv_len, unit_hbm, yn_hbm, *refs):
+def score_kernel(groups, owners, share, chunks, places, cand, inv_len, unit_b, unit, *refs):
     count = len(places)
-    pieces, (tags, up, up_keep, up_give, table, spread, unit_b, unit, sems) = refs[:count], refs[count:]
+    pieces, (tags, up, up_keep, up_give, pulled) = refs[:count], refs[count:]
     chips = owners // 2
     vocab_dev = share * groups
     grp, core = lax.axis_index("grp"), lax.axis_index("seq") % 2
     tok = unit_b.shape[0]
-    block = vocab_dev + groups * (chips - 1) * share
-
-    def place(key):
-        side, chunk, k = key
-        if chunk < 0:
-            return side * block, vocab_dev
-        before = sum(len(ds) for ds in chunks[:chunk]) * groups * share
-        rows = len(chunks[chunk]) * share
-        return side * block + vocab_dev + before + k * rows, rows
-
-    load_unit = pltpu.make_async_copy(unit_hbm, unit_b, sems.at[count])
-    load_unit.start()
-    copies = {}
+    parts_of = {}
     for n, (*key, left, wide) in enumerate(places):
-        at, rows = place(key)
-        copy = pltpu.make_async_copy(pieces[n], table.at[pl.ds(at, rows), pl.ds(left, wide)], sems.at[n])
-        copy.start()
-        copies.setdefault(tuple(key), []).append(copy)
-    load_yn = pltpu.make_async_copy(yn_hbm, unit, sems.at[count + 1])
-    load_yn.start()
+        parts_of.setdefault(tuple(key), []).append((slice(left, left + wide), pieces[n]))
     ids = owner_ids(owners)
     lane = iota((1, 128), 1)
     owner = jnp.full((1, 128), -1, i32)
@@ -195,31 +178,25 @@
 
     def runs(key):
         side, chunk, k = key
-        at, rows = place(key)
         if chunk < 0:
-            return at, rows, [(side * chips, 0, vocab_dev, ids[side * chips] * vocab_dev)]
+            return [(side * chips, 0, vocab_dev, ids[side * chips] * vocab_dev)]
         begin = (grp ^ k) * share
-        return at, rows, [
+        return [
             (side * chips + d, i * share, share, ids[side * chips + d] * vocab_dev + begin)
             for i, d in enumerate(chunks[chunk])
         ]
 
     def tiles(key):
-        at, rows, here = runs(key)
-        for j, off, wide, base in here:
+        for j, off, wide, base in runs(key):
             step = min(wide, 128)
             for o in range(0, wide, step):
                 hit = wanted[j][:, :step] == base + o + iota((1, step), 1)
                 yield j, off + o, step, hit
 
-    load_unit.wait()
     yb = unit_b[...]
     value = [[] for _ in range(owners)]
-    for key in copies:
-        for copy in copies[key]:
-            copy.wait()
-        at, rows, _ = runs(key)
-        product = dot(yb, table[at : at + rows], NT)
+    for key, parts in parts_of.items():
+        product = sum(dot(yb[:, cols], part[...], NT) for cols, part in parts)
         for j, off, step, hit in tiles(key):
             value[j].append(jnp.where(hit, product[:, off : off + step], 0.0))
     logits = jnp.zeros((tok, 128), f32)
@@ -233,13 +210,14 @@
     tags[:owners] = coef.T[:owners]
     tags[owners:] = chosen.astype(f32).T[:owners]
     amount = [jnp.broadcast_to(coef[:, j : j + 1], (tok, 128)) for j in range(owners)]
-    for key in copies:
-        at = runs(key)[0]
-        for j, off, step, hit in tiles(key):
-            spread[:, at + off : at + off + step] = jnp.where(hit, amount[j][:, :step], 0.0).astype(b16)
-    pulled = dot(spread[...], table[...], NN)
-    load_yn.wait()
+    pulled[...] = jnp.zeros(pulled.shape, f32)
+    for key, parts in parts_of.items():
+        spread = [jnp.where(hit, amount[j][:, :step], 0.0).astype(b16) for j, off, step, hit in tiles(key)]
+        spread = jnp.concatenate(spread, 1) if len(spread) > 1 else spread[0]
+        for cols, part in parts:
+            pulled[:, cols] += dot(spread, part[...], NN)
     yn = unit[...]
+    pulled = pulled[...]
     upstream = (pulled - yn * jnp.sum(yn * pulled, -1, keepdims=True)) * inv_len[...]
     up[...] = upstream.astype(b16)
     mine, other = split_columns(upstream, owners, core)
@@ -329,17 +307,36 @@
         one_right[z], two_left[z] = piece[1][:, half:], piece[2][:, :half]
 
 
+def corner_kernel(by_one, by_two, one_right, two_left, right_out, left_out):
+    right_out[...] = (one_right[...].astype(f32) + by_two[0].astype(f32)).astype(b16)
+    left_out[...] = (two_left[...].astype(f32) + by_one[0].astype(f32)).astype(b16)
+
+
 def sum_kernel(base, by_one, by_two, one_right, two_left, *outs):
-    chips = len(outs)
+    chips, fine, wide = base.shape
     chip = lax.axis_index("seq") // 2
-    half = base.shape[2] // 2
-    for d in range(chips):
-        z = lax.rem(chip + d, chips)
+    half = wide // 2
+    for n, d in enumerate(distances(chips)):
+        z = chip ^ d
         own = base[z].astype(f32)
         left = own[:, :half] + by_one[1, z].astype(f32) + two_left[z].astype(f32)
         right = own[:, half:] + by_two[1, z].astype(f32) + one_right[z].astype(f32)
-        outs[d][:, :half] = left.astype(b16)
-        outs[d][:, half:] = right.astype(b16)
+        out = outs[2 * n // chips]
+        at = slice(n % (chips // 2) * fine, (n % (chips // 2) + 1) * fine)
+        out[at, :half] = left.astype(b16)
+        out[at, half:] = right.astype(b16)
+
+
+def join_kernel(*refs):
+    out, at = refs[-1], 0
+    for part in refs[:-1]:
+        rows = part.shape[0]
+        out[at : at + rows] = part[...]
+        at += rows
+
+
+def columns_kernel(first, x, out):
+    out[...] = x[:, first : first + out.shape[1]]
 
 
 def pair_kernel(x, y, *outs):
@@ -400,13 +397,30 @@
     def to_core(x):
         return lax.ppermute(x, "seq", [(a, a ^ 1) for a in range(owners)])
 
+    def columns(x, first, wide):
+        return call(lambda *refs: columns_kernel(first, *refs), [((x.shape[0], wide), b16)], [VMEM], [x], room=8)[0]
+
+    def join(parts):
+        rows = sum(x.shape[0] for x in parts)
+        return call(join_kernel, [((rows, parts[0].shape[1]), b16)], [VMEM] * len(parts), parts, room=8)[0]
+
+    def reduce_chips(low, high):
+        bit = 1
+        while True:
+            came = across(high, bit)
+            bit *= 2
+            if bit >= chips:
+                return low.astype(f32) + came.astype(f32)
+            shape = (low.shape[0] // 2, low.shape[1])
+            low, high = call(pair_kernel, [(shape, b16)] * 2, [VMEM] * 2, [low, came], room=8)
+
     def gather_groups(x, near=None):
         wide = x.shape[1]
         if groups != 4:
             return [(k, 0, wide, to_group(x, k) if k else x) for k in range(groups)]
         one, two = near or [to_group(x, k) for k in (1, 2)]
         half = wide // 2
-        left, right = to_group(one[:, :half], 2), to_group(two[:, half:], 1)
+        left, right = to_group(columns(one, 0, half), 2), to_group(columns(two, half, half), 1)
         return [(0, 0, wide, x), (1, 0, wide, one), (2, 0, wide, two), (3, 0, half, left), (3, half, half, right)]
 
     own, quarter, quarter_inv = call(
@@ -420,6 +434,8 @@
         have.update({x ^ bit: across(have[x], bit) for x in have})
         bit //= 2
     got = [have[x] for x in distances(chips)[1:]]
+    candidates = jnp.concatenate([history[:, None], negatives], 1)
+    events, candidates = lax.optimization_barrier((events, candidates))
     outs = [
         ((tok, width // 2), b16), ((tok, width // 2), b16), ((tok, 4 * hidden), b16), ((tok, 4 * hidden), b16),
         ((HEADS, tok, tok), b16), ((HEADS, tok, tok), b16), ((tok, hidden), f32), ((tok, 1), f32),
@@ -429,14 +445,14 @@
     (keep, give, proj, slope, attn, attn_slope, normed, inverse, gated, unit, unit_b, inv_len, outgoing) = call(
         lambda *refs: forward_kernel(owners, slot, *refs), outs, [SMEM, SMEM, VMEM, VMEM, VMEM],
         [lengths, destinations, events, in_weight, out_weight],
-        room=63,
+        flops=2 * tok * width * 6 * hidden, nbytes=24 * tok * width + 10 * width * hidden, room=28,
     )
 
     near_units = [to_group(unit_b, k) for k in (1, 2)]
     got, near_units, own = lax.optimization_barrier((got, near_units, own))
     far_own = to_core(own)
     unit_sent = gather_groups(unit_b, near_units)
-    others = [jnp.concatenate(got, 0)]
+    others = [join(got)]
     pieces = [(0, -1, 0, 0, width, own)]
     for j, x in enumerate(others):
         pieces += [(0, j) + p for p in gather_groups(x)]
@@ -449,10 +465,9 @@
     ).reshape(owners * slot, width)
     layer_out, = call(
         relay_kernel, [((tok, width), b16)], [VMEM], [arrived],
-        room=63,
-    )
-
-    candidates = jnp.concatenate([history[:, None], negatives], 1)
+        room=8,
+    )
+
     vocab = vocab_dev * owners
     far_give, far_gated = to_core(give), to_core(gated)
     units = [p[3] for p in unit_sent]
@@ -462,15 +477,14 @@
     tags, up, up_keep, up_give = call(
         lambda *refs: score_kernel(groups, owners, share, chunks, [p[:5] for p in pieces], *refs),
         [((2 * owners, tok), f32), ((tok, width), b16), ((tok, width // 2), b16), ((tok, width // 2), b16)],
-        [VMEM] * 2 + [ANY] * (len(pieces) + 2), [candidates, inv_len, unit_b, score_unit] + [p[5] for p in pieces],
-        [pltpu.VMEM((vocab, width), b16), pltpu.VMEM((tok, vocab), b16), pltpu.VMEM((tok, width), b16),
-         pltpu.VMEM((tok, width), f32), pltpu.SemaphoreType.DMA((len(pieces) + 2,))],
-        room=63,
+        [VMEM] * (len(pieces) + 4), [candidates, inv_len, unit_b, score_unit] + [p[5] for p in pieces],
+        [pltpu.VMEM((tok, width), f32)],
+        flops=4 * tok * width * vocab, nbytes=2 * vocab * width + 12 * tok * width, room=20 if groups == 4 else 40,
     )
 
     grad, = call(
         backward_kernel, [((tok, 4 * hidden), b16)], [VMEM] * 8,
-        [up, out_weight, proj, slope, attn, attn_slope, normed, inverse], room=60,
+        [up, out_weight, proj, slope, attn, attn_slope, normed, inverse],
     )
 
     all_tags = [to_group(tags, k) if k else tags for k in range(groups)]
@@ -486,13 +500,11 @@
             [(block, b16)] + [((2,) + split, b16)] * 2 + [(split, b16)] * 2, [VMEM] * 8,
             [keep, far[0], up_keep, far[1], grad, far[2], gated, far[3]],
             [pltpu.VMEM((width // 2, 5 * hidden), b16)],
-            flops=2 * tok * width * 5 * hidden, nbytes=20 * tok * width, room=60,
+            flops=2 * tok * width * 5 * hidden, nbytes=20 * tok * width,
         )
         after = parts[0]
         by_one, by_two = to_group(parts[1], 1), to_group(parts[2], 2)
-        one_right = (parts[3].astype(f32) + by_two[0].astype(f32)).astype(b16)
-        two_left = (parts[4].astype(f32) + by_one[0].astype(f32)).astype(b16)
-        arrived = [by_one, by_two, to_group(one_right, 1), to_group(two_left, 2)]
+        corner = (by_one, by_two)
     else:
         def both(x, y):
             return jnp.concatenate([x, y], 0)
@@ -514,18 +526,21 @@
         units + all_tags + near,
         [pltpu.VMEM((groups * tok, width), b16), pltpu.VMEM((2 * chips * share, width), b16),
          pltpu.SemaphoreType.DMA((len(units) + 2 * chips,))],
-        flops=4 * groups * tok * width * chips * share, nbytes=4 * tok * groups * width, room=60,
+        room=16 if groups == 4 else 48,
     )
     far_mine = to_core(other)
 
-    summed = call(
-        pair_kernel, [((share, width), b16)] * chips, [VMEM] * 2, [mine, far_mine],
+    low, high = call(
+        pair_kernel, [((chips // 2 * share, width), b16)] * 2, [VMEM] * 2, [mine, far_mine],
         flops=chips * share * width, nbytes=6 * chips * share * width, room=8,
     )
-    come = [across(summed[n], d) for n, d in enumerate(distances(chips)) if d]
-    total = summed[0].astype(f32)
-    for x in come:
-        total += x.astype(f32)
+    if groups == 4:
+        by_one, by_two, low, high = lax.optimization_barrier(corner + (low, high))
+        one_right, two_left = call(
+            corner_kernel, [(split, b16)] * 2, [VMEM] * 4, [by_one, by_two, parts[3], parts[4]], room=8,
+        )
+        arrived = [by_one, by_two, to_group(one_right, 1), to_group(two_left, 2)]
+    total = reduce_chips(low, high)
     total = (total * quarter_inv).astype(b16)
     table_grad, = call(
         lambda *refs: assemble_kernel(groups, [width], *refs), [((vocab_dev, width), f32)], [VMEM] * groups,
@@ -534,18 +549,16 @@
     )
 
     if groups == 4:
-        base = parts[0]
-        sums = call(
-            sum_kernel, [((fine, 5 * hidden), b16)] * chips, [VMEM] * 5, [base] + arrived,
+        low, high = call(
+            sum_kernel, [((chips // 2 * fine, 5 * hidden), b16)] * 2, [VMEM] * 5, [parts[0]] + arrived,
             flops=chips * fine * 5 * hidden, nbytes=40 * chips * fine * hidden, room=10,
         )
+        line = reduce_chips(low, high)
     else:
-        sums = [
-            lax.dynamic_index_in_dim(sums, (chip + d) % chips, 0, False).astype(b16) for d in range(chips)
-        ]
-    line = sums[0].astype(f32)
-    for d in range(1, chips):
-        line += to_chip(sums[d], d).astype(f32)
+        blocks = [lax.dynamic_index_in_dim(sums, (chip + d) % chips, 0, False).astype(b16) for d in range(chips)]
+        line = blocks[0].astype(f32)
+        for d in range(1, chips):
+            line += to_chip(blocks[d], d).astype(f32)
     line = line.astype(b16)
     lines = [to_group(line, k) if k else line for k in range(groups)]
     if fine % 16 == 0:

time: 191 us -> 191 us (level)
  the two profiles are of different devices: /device:TPU:9 before, /device:TPU:0 now
where the time goes in v8:
time: 191 us; the launch traced here: 190 us
  waiting for transfers between devices  93.6 us (49%)
  starting transfers between devices  41.1 us (22%)
  Pallas kernels  29 us (15%)
  local copies, waits for them, and re-layouts  24.7 us (13%)
    ppermute x21, waiting for transfers between devices, to_group(): return lax.ppermute(x, 'grp', [(a, a ^ k) for a in range(groups)])  53.1 us
    ppermute x7, waiting for transfers between devices, across(): return lax.ppermute(x, 'seq', pairs)  36.5 us
    pallas_call x19, Pallas kernels, call(): pl.pallas_call(kernel, out_shape=[jax.ShapeDtypeStruct(s, t) for s, t in...  29 us
    unnamed x82, local copies, waits for them, and re-layouts  23.9 us
    ppermute x21, starting transfers between devices, to_group(): return lax.ppermute(x, 'grp', [(a, a ^ k) for a in range(groups)])  23.2 us
    ppermute x7, starting transfers between devices, across(): return lax.ppermute(x, 'seq', pairs)  12.3 us
    ppermute x11, waiting for transfers between devices, to_core(): return lax.ppermute(x, 'seq', [(a, a ^ 1) for a in range(owners)])  3.98 us
  transfers between devices with their start and end apart: 40, of which 20 were waited for; matrix products, arithmetic and copies ran while one was open for 1% of the time, Pallas kernels for 6%

profile of v8, /device:TPU:0, one launch (start us, length us, event | category | flops | bytes accessed | tf_op | source)
XLA Modules:
  0.0 190.4 jit_solution(6878697549920163553)
XLA Ops:
  3.9 4.0 %collective-permute-start = (bf16[128,1024]{1,0:T(8,128)(2,1)S(1)}, bf16[128,1024]{1,0:T(8,128)(2,1)S(1)}, u32[]{:S(2)}, u32[]{:S(2)}) collective-permute-start(bf16[128,1024]{1,0:T(8,128)(2,1)S(1)} %get-tuple-element.74), channel_id=1, source_target_pairs={{0,4},{1,5},{2,6},{3,7},{4,0},{5,1},{6,2},{7,3},{8,12},{9,13},{10,... | collective-permute-start | bytes 786440 | tf_op jit(solution)/shard_map/ppermute | solution.py:392
  9.8 2.2 %copy-done.24 = bf16[1024,2048]{1,0:T(8,128)(2,1)S(1)} copy-done((bf16[1024,2048]{1,0:T(8,128)(2,1)S(1)}, bf16[1024,2048]{1,0:T(8,128)(2,1)}, u32[]{:S(2)}) %copy-start.24) | copy-done | bytes 4194328
  14.4 5.5 %shard_map.111 = (bf16[256,512]{1,0:T(8,128)(2,1)S(1)}, bf16[256,512]{1,0:T(8,128)(2,1)S(1)}, bf16[256,2048]{1,0:T(8,128)(2,1)S(1)}, bf16[256,2048]{1,0:T(8,128)...) custom-call(s32[1,8]{1,0:T(1,128)S(1)} %copy-done.33, ...), custom_call_target="tpu_custom_call" | custom-call | flops 1610612736 | bytes 11534336 | tf_op jit(solution)/shard_map/pallas_call | solution.py:53
  27.1 1.5 collective-permute-start.4
  28.6 1.5 collective-permute-start.3
  30.1 1.6 collective-permute-start.1
  32.1 7.2 %collective-permute-done.1.refs_1_ = bf16[128,1024]{1,0:T(8,128)(2,1)S(1)} collective-permute-done((bf16[128,1024]{1,0:T(8,128)(2,1)S(1)}, bf16[128,1024]{1,0:T(8,128)(2,1)S(1)}, u32[]{:S(2)}, u32[]{:S(2)}) %collective-permute-start.1) | collective-permute-done | bytes 262176 | tf_op jit(solution)/shard_map/ppermute | solution.py:392
  39.4 3.6 %collective-permute-done.2.refs_2_ = bf16[128,1024]{1,0:T(8,128)(2,1)S(1)} collective-permute-done((bf16[128,1024]{1,0:T(8,128)(2,1)S(1)}, bf16[128,1024]{1,0:T(8,128)(2,1)S(1)}, u32[]{:S(2)}, u32[]{:S(2)}) %collective-permute-start.2) | collective-permute-done | bytes 262176 | tf_op jit(solution)/shard_map/ppermute | solution.py:392
  44.1 3.7 %all-to-all-start = ((bf16[8,48,1024]{2,1,0:T(8,128)(2,1)}), bf16[8,48,1024]{2,1,0:T(8,128)(2,1)S(1)}, u32[]{:S(2)}, u32[]{:S(2)}) async-start(bf16[8,48,1024]{2,1,0:T(8,128)(2,1)} %bitcast.1), calls=%async_computation | async-start | bytes 1572864 | tf_op jit(solution)/shard_map/all_to_all | solution.py:463
  50.5 1.5 collective-permute-start.8
  52.0 8.6 %collective-permute-done.10.refs_0_.refs_7_ = bf16[384,1024]{1,0:T(8,128)(2,1)S(1)} collective-permute-done((bf16[384,1024]{1,0:T(8,128)(2,1)S(1)}, bf16[384,1024]{1,0:T(8,128)(2,1)S(1)}, u32[]{:S(2)}, u32[]{:S(2)}) %collective-permute-start.10) | collective-permute-done | bytes 786464 | tf_op jit(solution)/shard_map/ppermute | solution.py:395
  60.6 3.1 %collective-permute-done.9.refs_0_.refs_6_ = bf16[384,1024]{1,0:T(8,128)(2,1)} collective-permute-done((bf16[384,1024]{1,0:T(8,128)(2,1)S(1)}, bf16[384,1024]{1,0:T(8,128)(2,1)}, u32[]{:S(2)}, u32[]{:S(2)}) %collective-permute-start.9) | collective-permute-done | bytes 786464 | tf_op jit(solution)/shard_map/ppermute | solution.py:395
  63.7 1.5 collective-permute-start.7
  69.2 3.6 %collective-permute-done.7.refs_3_ = bf16[256,512]{1,0:T(8,128)(2,1)S(1)} collective-permute-done((bf16[256,512]{1,0:T(8,128)(2,1)S(1)}, bf16[256,512]{1,0:T(8,128)(2,1)S(1)}, u32[]{:S(2)}, u32[]{:S(2)}) %collective-permute-start.7) | collective-permute-done | bytes 262176 | tf_op jit(solution)/shard_map/ppermute | solution.py:395
  75.0 3.2 %collective-permute-done.11.refs_8_ = bf16[384,512]{1,0:T(8,128)(2,1)} collective-permute-done((bf16[384,512]{1,0:T(8,128)(2,1)S(1)}, bf16[384,512]{1,0:T(8,128)(2,1)}, u32[]{:S(2)}, u32[]{:S(2)}) %collective-permute-start.11) | collective-permute-done | bytes 393248 | tf_op jit(solution)/shard_map/ppermute | solution.py:395
  79.0 1.6 shard_map.114
  86.0 9.0 %shard_map.119 = (f32[16,256]{1,0:T(8,128)S(1)}, bf16[256,1024]{1,0:T(8,128)(2,1)S(1)}, bf16[256,512]{1,0:T(8,128)(2,1)S(1)}, bf16[256,512]{1,0:T(8,128)(2,1)S(1)}) custom-call(s32[256,4]{1,0:T(8,128)S(1)} %copy-done.21, f32[256,1]{1,0:T(8,128)S(1)} %copy-done.40, bf16[256,1024]{1,0:T(8,128)(2,1)S(1)} %copy-done.10, f32[256,1024]{1,0:T(8,128)S(1)} %copy-done.36, ...), custom_call_target="tpu_custom_call" | custom-call | flops 4294967296 | bytes 11534336 | tf_op jit(solution)/shard_map/pallas_call | solution.py:53
  95.6 1.9 %collective-permute-start.22 = (f32[16,256]{1,0:T(8,128)S(1)}, f32[16,256]{1,0:T(8,128)S(1)}, u32[]{:S(2)}, u32[]{:S(2)}) collective-permute-start(f32[16,256]{1,0:T(8,128)S(1)} %get-tuple-element.115.refs_5_), channel_id=1, source_target_pairs={{0,24},{8,16},{16,8},{24,0},{1,25},{9,17},{17,9},{25,1},{2,26},{10... | collective-permute-start | bytes 49160 | tf_op jit(solution)/shard_map/ppermute | solution.py:395
  99.2 1.6 shard_map.120.refs_4_
  101.9 2.7 %collective-permute-done.23.refs_5_ = bf16[256,2048]{1,0:T(8,128)(2,1)S(1)} collective-permute-done((bf16[256,2048]{1,0:T(8,128)(2,1)S(1)}, bf16[256,2048]{1,0:T(8,128)(2,1)S(1)}, u32[]{:S(2)}, u32[]{:S(2)}) %collective-permute-start.23) | collective-permute-done | bytes 1048608 | tf_op jit(solution)/shard_map/ppermute | solution.py:398
  104.6 1.7 shard_map.121
  106.3 4.5 %shard_map.122 = (bf16[512,1024]{1,0:T(8,128)(2,1)S(1)}, bf16[512,1024]{1,0:T(8,128)(2,1)S(1)}) custom-call(bf16[256,1024]{1,0:T(8,128)(2,1)S(1)} %copy-done.10, bf16[256,1024]{1,0:T(8,128)(2,1)S(1)} %collective-permute-done.3.refs_0_.refs_1_, bf16[256,1024]{1,0:T(8,128)(2,1)S(1)} %collective-permute-done.4.refs_0_.refs_2_, bf16[256,512]{1,0:T(8,128)(2,1)S(1)} %copy-done.20, ...), custom_call_target="tpu_custom_call" | custom-call | tf_op jit(solution)/shard_map/pallas_call | solution.py:53
  113.8 14.2 %collective-permute-done.24.by_one = bf16[2,4,32,1280]{3,2,1,0:T(8,128)(2,1)S(1)} collective-permute-done((bf16[2,4,32,1280]{3,2,1,0:T(8,128)(2,1)S(1)}, bf16[2,4,32,1280]{3,2,1,0:T(8,128)(2,1)S(1)}, u32[]{:S(2)}, u32[]{:S(2)}) %collective-permute-start.24) | collective-permute-done | bytes 655392 | tf_op jit(solution)/shard_map/ppermute | solution.py:395
  131.4 1.6 collective-permute-start.34
  133.0 4.8 %collective-permute-done.27.one_right = bf16[4,32,1280]{2,1,0:T(8,128)(2,1)S(1)} collective-permute-done((bf16[4,32,1280]{2,1,0:T(8,128)(2,1)S(1)}, bf16[4,32,1280]{2,1,0:T(8,128)(2,1)S(1)}, u32[]{:S(2)}, u32[]{:S(2)}) %collective-permute-start.27) | collective-permute-done | bytes 327712 | tf_op jit(solution)/shard_map/ppermute | solution.py:395
  138.8 1.6 collective-permute-start.29
  140.4 10.5 %collective-permute-done.29.y = bf16[64,2560]{1,0:T(8,128)(2,1)S(1)} collective-permute-done((bf16[64,2560]{1,0:T(8,128)(2,1)S(1)}, bf16[64,2560]{1,0:T(8,128)(2,1)S(1)}, u32[]{:S(2)}, u32[]{:S(2)}) %collective-permute-start.29) | collective-permute-done | bytes 327712 | tf_op jit(solution)/shard_map/ppermute | solution.py:392
  151.7 2.6 %collective-permute-start.35 = (bf16[128,1024]{1,0:T(8,128)(2,1)S(1)}, bf16[128,1024]{1,0:T(8,128)(2,1)S(1)}, u32[]{:S(2)}, u32[]{:S(2)}) collective-permute-start(bf16[128,1024]{1,0:T(8,128)(2,1)S(1)} %get-tuple-element.138), channel_id=1, source_target_pairs={{0,4},{1,5},{2,6},{3,7},{4,0},{5,1},{6,2},{7,3},{8,12},{9,13},{10,... | collective-permute-start | bytes 786440 | tf_op jit(solution)/shard_map/ppermute | solution.py:392
  154.4 11.8 %collective-permute-done.30 = bf16[32,2560]{1,0:T(8,128)(2,1)S(1)} collective-permute-done((bf16[32,2560]{1,0:T(8,128)(2,1)S(1)}, bf16[32,2560]{1,0:T(8,128)(2,1)S(1)}, u32[]{:S(2)}, u32[]{:S(2)}) %collective-permute-start.30) | collective-permute-done | bytes 163872 | tf_op jit(solution)/shard_map/ppermute | solution.py:392
  167.3 3.3 %collective-permute-done.35 = bf16[128,1024]{1,0:T(8,128)(2,1)S(1)} collective-permute-done((bf16[128,1024]{1,0:T(8,128)(2,1)S(1)}, bf16[128,1024]{1,0:T(8,128)(2,1)S(1)}, u32[]{:S(2)}, u32[]{:S(2)}) %collective-permute-start.35) | collective-permute-done | bytes 262176 | tf_op jit(solution)/shard_map/ppermute | solution.py:392
  175.9 11.9 %collective-permute-done.32.refs_2_ = bf16[32,2560]{1,0:T(8,128)(2,1)S(1)} collective-permute-done((bf16[32,2560]{1,0:T(8,128)(2,1)S(1)}, bf16[32,2560]{1,0:T(8,128)(2,1)S(1)}, u32[]{:S(2)}, u32[]{:S(2)}) %collective-permute-start.32) | collective-permute-done | bytes 163872 | tf_op jit(solution)/shard_map/ppermute | solution.py:395
  189.0 1.5 shard_map.129
  (154 shorter events, 50.0 us)
Async XLA Ops:
  3.9 27.8 %collective-permute-start = (bf16[128,1024]{1,0:T(8,128)(2,1)S(1)}, bf16[128,1024]{1,0:T(8,128)(2,1)S(1)}, u32[]{:S(2)}, u32[]{:S(2)}) collective-permute-start(bf16[128,1024]{1,0:T(8,128)(2,1)S(1)} %get-tuple-element.74), channel_id=1, source_target_pairs={{0,4},{1,5},{2,6},{3,7},{4,0},{5,1},{6,2},{7,3},{8,12},{9,13},{10,... | collective-permute-start | bytes 786440 | tf_op jit(solution)/shard_map/ppermute | solution.py:392
  27.1 15.8 %collective-permute-start.4 = (bf16[256,1024]{1,0:T(8,128)(2,1)S(1)}, bf16[256,1024]{1,0:T(8,128)(2,1)S(1)}, u32[]{:S(2)}, u32[]{:S(2)}) collective-permute-start(bf16[256,1024]{1,0:T(8,128)(2,1)S(1)} %get-tuple-element.110.refs_2_.refs_0_), channel_id=1, source_target_pairs={{0,16},{8,24},{16,0},{24,8},{1,17},{9,25},{17,1},{25,9},{2,18},{10... | collective-permute-start | bytes 1572872 | tf_op jit(solution)/shard_map/ppermute | solution.py:395
  28.6 14.3 %collective-permute-start.3 = (bf16[256,1024]{1,0:T(8,128)(2,1)S(1)}, bf16[256,1024]{1,0:T(8,128)(2,1)S(1)}, u32[]{:S(2)}, u32[]{:S(2)}) collective-permute-start(bf16[256,1024]{1,0:T(8,128)(2,1)S(1)} %get-tuple-element.110.refs_2_.refs_0_), channel_id=1, source_target_pairs={{0,8},{8,0},{16,24},{24,16},{1,9},{9,1},{17,25},{25,17},{2,10},{10... | collective-permute-start | bytes 1572872 | tf_op jit(solution)/shard_map/ppermute | solution.py:395
  30.1 9.2 %collective-permute-start.1 = (bf16[128,1024]{1,0:T(8,128)(2,1)S(1)}, bf16[128,1024]{1,0:T(8,128)(2,1)S(1)}, u32[]{:S(2)}, u32[]{:S(2)}) collective-permute-start(bf16[128,1024]{1,0:T(8,128)(2,1)S(1)} %get-tuple-element.74), channel_id=1, source_target_pairs={{0,2},{1,3},{2,0},{3,1},{4,6},{5,7},{6,4},{7,5},{8,10},{9,11},{10,... | collective-permute-start | bytes 786440 | tf_op jit(solution)/shard_map/ppermute | solution.py:392
  31.7 11.2 %collective-permute-start.2 = (bf16[128,1024]{1,0:T(8,128)(2,1)S(1)}, bf16[128,1024]{1,0:T(8,128)(2,1)S(1)}, u32[]{:S(2)}, u32[]{:S(2)}) collective-permute-start(bf16[128,1024]{1,0:T(8,128)(2,1)S(1)} %collective-permute-done.refs_0_), channel_id=1, source_target_pairs={{0,2},{1,3},{2,0},{3,1},{4,6},{5,7},{6,4},{7,5},{8,10},{9,11},{10,... | collective-permute-start | bytes 786440 | tf_op jit(solution)/shard_map/ppermute | solution.py:392
  43.0 17.6 %collective-permute-start.10 = (bf16[384,1024]{1,0:T(8,128)(2,1)S(1)}, bf16[384,1024]{1,0:T(8,128)(2,1)S(1)}, u32[]{:S(2)}, u32[]{:S(2)}) collective-permute-start(bf16[384,1024]{1,0:T(8,128)(2,1)S(1)} %shard_map.113.refs_5_.refs_10_), channel_id=1, source_target_pairs={{0,16},{8,24},{16,0},{24,8},{1,17},{9,25},{17,1},{25,9},{2,18},{10... | collective-permute-start | bytes 2359304 | tf_op jit(solution)/shard_map/ppermute | solution.py:395
  43.6 20.1 %collective-permute-start.9 = (bf16[384,1024]{1,0:T(8,128)(2,1)S(1)}, bf16[384,1024]{1,0:T(8,128)(2,1)}, u32[]{:S(2)}, u32[]{:S(2)}) collective-permute-start(bf16[384,1024]{1,0:T(8,128)(2,1)S(1)} %shard_map.113.refs_5_.refs_10_), channel_id=1, source_target_pairs={{0,8},{8,0},{16,24},{24,16},{1,9},{9,1},{17,25},{25,17},{2,10},{10... | collective-permute-start | bytes 2359304 | tf_op jit(solution)/shard_map/ppermute | solution.py:395
  44.1 29.4 %collective-permute-start.14 = (bf16[384,1024]{1,0:T(8,128)(2,1)S(1)}, bf16[384,1024]{1,0:T(8,128)(2,1)}, u32[]{:S(2)}, u32[]{:S(2)}) collective-permute-start(bf16[384,1024]{1,0:T(8,128)(2,1)S(1)} %shard_map.113.refs_5_.refs_10_), channel_id=1, source_target_pairs={{0,1},{1,0},{2,3},{3,2},{4,5},{5,4},{6,7},{7,6},{8,9},{9,8},{10,11... | collective-permute-start | bytes 2359304 | tf_op jit(solution)/shard_map/ppermute | solution.py:398
  44.1 34.9 %all-to-all-start = ((bf16[8,48,1024]{2,1,0:T(8,128)(2,1)}), bf16[8,48,1024]{2,1,0:T(8,128)(2,1)S(1)}, u32[]{:S(2)}, u32[]{:S(2)}) async-start(bf16[8,48,1024]{2,1,0:T(8,128)(2,1)} %bitcast.1), calls=%async_computation | async-start | bytes 1572864 | tf_op jit(solution)/shard_map/all_to_all | solution.py:463
  48.4 18.1 %collective-permute-start.6 = (bf16[256,512]{1,0:T(8,128)(2,1)}, bf16[256,512]{1,0:T(8,128)(2,1)S(1)}, u32[]{:S(2)}, u32[]{:S(2)}) collective-permute-start(bf16[256,512]{1,0:T(8,128)(2,1)} %copy-done.26), channel_id=1, source_target_pairs={{0,1},{1,0},{2,3},{3,2},{4,5},{5,4},{6,7},{7,6},{8,9},{9,8},{10,11... | collective-permute-start | bytes 786440 | tf_op jit(solution)/shard_map/ppermute | solution.py:398
  50.5 17.2 %collective-permute-start.8 = (bf16[256,512]{1,0:T(8,128)(2,1)S(1)}, bf16[256,512]{1,0:T(8,128)(2,1)S(1)}, u32[]{:S(2)}, u32[]{:S(2)}) collective-permute-start(bf16[256,512]{1,0:T(8,128)(2,1)S(1)} %shard_map.116), channel_id=1, source_target_pairs={{0,8},{8,0},{16,24},{24,16},{1,9},{9,1},{17,25},{25,17},{2,10},{10... | collective-permute-start | bytes 786440 | tf_op jit(solution)/shard_map/ppermute | solution.py:395
  60.6 20.0 %collective-permute-start.13 = (bf16[512,1024]{1,0:T(8,128)(2,1)}, bf16[512,1024]{1,0:T(8,128)(2,1)}, u32[]{:S(2)}, u32[]{:S(2)}) collective-permute-start(bf16[512,1024]{1,0:T(8,128)(2,1)} %copy-done.7), channel_id=1, source_target_pairs={{0,1},{1,0},{2,3},{3,2},{4,5},{5,4},{6,7},{7,6},{8,9},{9,8},{10,11... | collective-permute-start | bytes 3145736 | tf_op jit(solution)/shard_map/ppermute | solution.py:398
  63.7 9.1 %collective-permute-start.7 = (bf16[256,512]{1,0:T(8,128)(2,1)S(1)}, bf16[256,512]{1,0:T(8,128)(2,1)S(1)}, u32[]{:S(2)}, u32[]{:S(2)}) collective-permute-start(bf16[256,512]{1,0:T(8,128)(2,1)S(1)} %shard_map.115), channel_id=1, source_target_pairs={{0,16},{8,24},{16,0},{24,8},{1,17},{9,25},{17,1},{25,9},{2,18},{10... | collective-permute-start | bytes 786440 | tf_op jit(solution)/shard_map/ppermute | solution.py:395
  67.1 7.9 %collective-permute-start.12 = (bf16[384,512]{1,0:T(8,128)(2,1)S(1)}, bf16[384,512]{1,0:T(8,128)(2,1)}, u32[]{:S(2)}, u32[]{:S(2)}) collective-permute-start(bf16[384,512]{1,0:T(8,128)(2,1)S(1)} %shard_map.118), channel_id=1, source_target_pairs={{0,8},{8,0},{16,24},{24,16},{1,9},{9,1},{17,25},{25,17},{2,10},{10... | collective-permute-start | bytes 1179656 | tf_op jit(solution)/shard_map/ppermute | solution.py:395
  68.4 9.8 %collective-permute-start.11 = (bf16[384,512]{1,0:T(8,128)(2,1)S(1)}, bf16[384,512]{1,0:T(8,128)(2,1)}, u32[]{:S(2)}, u32[]{:S(2)}) collective-permute-start(bf16[384,512]{1,0:T(8,128)(2,1)S(1)} %shard_map.117), channel_id=1, source_target_pairs={{0,16},{8,24},{16,0},{24,8},{1,17},{9,25},{17,1},{25,9},{2,18},{10... | collective-permute-start | bytes 1179656 | tf_op jit(solution)/shard_map/ppermute | solution.py:395
  73.5 7.1 %collective-permute-start.16 = (bf16[384,1024]{1,0:T(8,128)(2,1)S(1)}, bf16[384,1024]{1,0:T(8,128)(2,1)}, u32[]{:S(2)}, u32[]{:S(2)}) collective-permute-start(bf16[384,1024]{1,0:T(8,128)(2,1)S(1)} %collective-permute-done.10.refs_0_.refs_7_), channel_id=1, source_target_pairs={{0,1},{1,0},{2,3},{3,2},{4,5},{5,4},{6,7},{7,6},{8,9},{9,8},{10,11... | collective-permute-start | bytes 2359304 | tf_op jit(solution)/shard_map/ppermute | solution.py:398
  73.5 7.1 %collective-permute-start.15 = (bf16[384,1024]{1,0:T(8,128)(2,1)}, bf16[384,1024]{1,0:T(8,128)(2,1)}, u32[]{:S(2)}, u32[]{:S(2)}) collective-permute-start(bf16[384,1024]{1,0:T(8,128)(2,1)} %collective-permute-done.9.refs_0_.refs_6_), channel_id=1, source_target_pairs={{0,1},{1,0},{2,3},{3,2},{4,5},{5,4},{6,7},{7,6},{8,9},{9,8},{10,11... | collective-permute-start | bytes 2359304 | tf_op jit(solution)/shard_map/ppermute | solution.py:398
  95.1 6.8 %collective-permute-start.19 = (bf16[256,512]{1,0:T(8,128)(2,1)S(1)}, bf16[256,512]{1,0:T(8,128)(2,1)S(1)}, u32[]{:S(2)}, u32[]{:S(2)}) collective-permute-start(bf16[256,512]{1,0:T(8,128)(2,1)S(1)} %get-tuple-element.101), channel_id=1, source_target_pairs={{0,1},{1,0},{2,3},{3,2},{4,5},{5,4},{6,7},{7,6},{8,9},{9,8},{10,11... | collective-permute-start | bytes 786440 | tf_op jit(solution)/shard_map/ppermute | solution.py:398
  111.0 17.0 %collective-permute-start.24 = (bf16[2,4,32,1280]{3,2,1,0:T(8,128)(2,1)S(1)}, bf16[2,4,32,1280]{3,2,1,0:T(8,128)(2,1)S(1)}, u32[]{:S(2)}, u32[]{:S(2)}) collective-permute-start(bf16[2,4,32,1280]{3,2,1,0:T(8,128)(2,1)S(1)} %get-tuple-element.107), channel_id=1, source_target_pairs={{0,8},{8,0},{16,24},{24,16},{1,9},{9,1},{17,25},{25,17},{2,10},{10... | collective-permute-start | bytes 1966088 | tf_op jit(solution)/shard_map/ppermute | solution.py:395
  112.0 16.7 %collective-permute-start.25 = (bf16[2,4,32,1280]{3,2,1,0:T(8,128)(2,1)S(1)}, bf16[2,4,32,1280]{3,2,1,0:T(8,128)(2,1)S(1)}, u32[]{:S(2)}, u32[]{:S(2)}) collective-permute-start(bf16[2,4,32,1280]{3,2,1,0:T(8,128)(2,1)S(1)} %get-tuple-element.108), channel_id=1, source_target_pairs={{0,16},{8,24},{16,0},{24,8},{1,17},{9,25},{17,1},{25,9},{2,18},{10... | collective-permute-start | bytes 1966088 | tf_op jit(solution)/shard_map/ppermute | solution.py:395
  128.9 8.9 %collective-permute-start.27 = (bf16[4,32,1280]{2,1,0:T(8,128)(2,1)S(1)}, bf16[4,32,1280]{2,1,0:T(8,128)(2,1)S(1)}, u32[]{:S(2)}, u32[]{:S(2)}) collective-permute-start(bf16[4,32,1280]{2,1,0:T(8,128)(2,1)S(1)} %get-tuple-element.127), channel_id=1, source_target_pairs={{0,8},{8,0},{16,24},{24,16},{1,9},{9,1},{17,25},{25,17},{2,10},{10... | collective-permute-start | bytes 983048 | tf_op jit(solution)/shard_map/ppermute | solution.py:395
  130.0 8.6 %collective-permute-start.28 = (bf16[4,32,1280]{2,1,0:T(8,128)(2,1)S(1)}, bf16[4,32,1280]{2,1,0:T(8,128)(2,1)S(1)}, u32[]{:S(2)}, u32[]{:S(2)}) collective-permute-start(bf16[4,32,1280]{2,1,0:T(8,128)(2,1)S(1)} %get-tuple-element.128), channel_id=1, source_target_pairs={{0,16},{8,24},{16,0},{24,8},{1,17},{9,25},{17,1},{25,9},{2,18},{10... | collective-permute-start | bytes 983048 | tf_op jit(solution)/shard_map/ppermute | solution.py:395
  131.4 20.2 %collective-permute-start.34 = (bf16[256,1024]{1,0:T(8,128)(2,1)S(1)}, bf16[256,1024]{1,0:T(8,128)(2,1)S(1)}, u32[]{:S(2)}, u32[]{:S(2)}) collective-permute-start(bf16[256,1024]{1,0:T(8,128)(2,1)S(1)} %get-tuple-element.136), channel_id=1, source_target_pairs={{0,2},{1,3},{2,0},{3,1},{4,6},{5,7},{6,4},{7,5},{8,10},{9,11},{10,... | collective-permute-start | bytes 1572872 | tf_op jit(solution)/shard_map/ppermute | solution.py:392
  138.8 12.2 %collective-permute-start.29 = (bf16[64,2560]{1,0:T(8,128)(2,1)S(1)}, bf16[64,2560]{1,0:T(8,128)(2,1)S(1)}, u32[]{:S(2)}, u32[]{:S(2)}) collective-permute-start(bf16[64,2560]{1,0:T(8,128)(2,1)S(1)} %get-tuple-element.130), channel_id=1, source_target_pairs={{0,2},{1,3},{2,0},{3,1},{4,6},{5,7},{6,4},{7,5},{8,10},{9,11},{10,... | collective-permute-start | bytes 983048 | tf_op jit(solution)/shard_map/ppermute | solution.py:392
  151.1 15.1 %collective-permute-start.30 = (bf16[32,2560]{1,0:T(8,128)(2,1)S(1)}, bf16[32,2560]{1,0:T(8,128)(2,1)S(1)}, u32[]{:S(2)}, u32[]{:S(2)}) collective-permute-start(bf16[32,2560]{1,0:T(8,128)(2,1)S(1)} %get-tuple-element.132), channel_id=1, source_target_pairs={{0,4},{1,5},{2,6},{3,7},{4,0},{5,1},{6,2},{7,3},{8,12},{9,13},{10,... | collective-permute-start | bytes 491528 | tf_op jit(solution)/shard_map/ppermute | solution.py:392
  151.7 18.9 %collective-permute-start.35 = (bf16[128,1024]{1,0:T(8,128)(2,1)S(1)}, bf16[128,1024]{1,0:T(8,128)(2,1)S(1)}, u32[]{:S(2)}, u32[]{:S(2)}) collective-permute-start(bf16[128,1024]{1,0:T(8,128)(2,1)S(1)} %get-tuple-element.138), channel_id=1, source_target_pairs={{0,4},{1,5},{2,6},{3,7},{4,0},{5,1},{6,2},{7,3},{8,12},{9,13},{10,... | collective-permute-start | bytes 786440 | tf_op jit(solution)/shard_map/ppermute | solution.py:392
  166.2 8.6 %collective-permute-start.33 = (bf16[32,2560]{1,0:T(8,128)(2,1)S(1)}, bf16[32,2560]{1,0:T(8,128)(2,1)S(1)}, u32[]{:S(2)}, u32[]{:S(2)}) collective-permute-start(bf16[32,2560]{1,0:T(8,128)(2,1)S(1)} %add_convert_fusion.refs_0_), channel_id=1, source_target_pairs={{0,24},{8,16},{16,8},{24,0},{1,25},{9,17},{17,9},{25,1},{2,26},{10... | collective-permute-start | bytes 491528 | tf_op jit(solution)/shard_map/ppermute | solution.py:395
  170.7 18.2 %collective-permute-start.38 = (bf16[128,1024]{1,0:T(8,128)(2,1)S(1)}, bf16[128,1024]{1,0:T(8,128)(2,1)S(1)}, u32[]{:S(2)}, u32[]{:S(2)}) collective-permute-start(bf16[128,1024]{1,0:T(8,128)(2,1)S(1)} %multiply_convert_fusion.refs_0_), channel_id=1, source_target_pairs={{0,24},{8,16},{16,8},{24,0},{1,25},{9,17},{17,9},{25,1},{2,26},{10... | collective-permute-start | bytes 786440 | tf_op jit(solution)/shard_map/ppermute | solution.py:395
  171.8 17.2 %collective-permute-start.37 = (bf16[128,1024]{1,0:T(8,128)(2,1)S(1)}, bf16[128,1024]{1,0:T(8,128)(2,1)S(1)}, u32[]{:S(2)}, u32[]{:S(2)}) collective-permute-start(bf16[128,1024]{1,0:T(8,128)(2,1)S(1)} %multiply_convert_fusion.refs_0_), channel_id=1, source_target_pairs={{0,16},{8,24},{16,0},{24,8},{1,17},{9,25},{17,1},{25,9},{2,18},{10... | collective-permute-start | bytes 786440 | tf_op jit(solution)/shard_map/ppermute | solution.py:395
  173.3 15.7 %collective-permute-start.36 = (bf16[128,1024]{1,0:T(8,128)(2,1)S(1)}, bf16[128,1024]{1,0:T(8,128)(2,1)S(1)}, u32[]{:S(2)}, u32[]{:S(2)}) collective-permute-start(bf16[128,1024]{1,0:T(8,128)(2,1)S(1)} %multiply_convert_fusion.refs_0_), channel_id=1, source_target_pairs={{0,8},{8,0},{16,24},{24,16},{1,9},{9,1},{17,25},{25,17},{2,10},{10... | collective-permute-start | bytes 786440 | tf_op jit(solution)/shard_map/ppermute | solution.py:395
  174.3 13.5 %collective-permute-start.32 = (bf16[32,2560]{1,0:T(8,128)(2,1)S(1)}, bf16[32,2560]{1,0:T(8,128)(2,1)S(1)}, u32[]{:S(2)}, u32[]{:S(2)}) collective-permute-start(bf16[32,2560]{1,0:T(8,128)(2,1)S(1)} %add_convert_fusion.refs_0_), channel_id=1, source_target_pairs={{0,16},{8,24},{16,0},{24,8},{1,17},{9,25},{17,1},{25,9},{2,18},{10... | collective-permute-start | bytes 491528 | tf_op jit(solution)/shard_map/ppermute | solution.py:395
  174.9 12.9 %collective-permute-start.31 = (bf16[32,2560]{1,0:T(8,128)(2,1)S(1)}, bf16[32,2560]{1,0:T(8,128)(2,1)S(1)}, u32[]{:S(2)}, u32[]{:S(2)}) collective-permute-start(bf16[32,2560]{1,0:T(8,128)(2,1)S(1)} %add_convert_fusion.refs_0_), channel_id=1, source_target_pairs={{0,8},{8,0},{16,24},{24,16},{1,9},{9,1},{17,25},{25,17},{2,10},{10... | collective-permute-start | bytes 491528 | tf_op jit(solution)/shard_map/ppermute | solution.py:395
  (49 other events, 257.3 us)

commit v9 on v8

--- a/solution.py
+++ b/solution.py
@@ -62,13 +62,14 @@
 
 
 def forward_kernel(
-    owners, slot, lengths, dests, events, in_weight, out_weight,
+    owners, slot, lengths, dests, events, in_weight, out_weight, cand, cand_out,
     keep, give, proj, slope, attn, attn_slope, normed_out, inv_out, gated_out, unit, unit_b, inv_len, outgoing,
 ):
     tok = events.shape[0]
     hidden = out_weight.shape[1]
     scale = HEAD_DIM ** (-0.5)
     core = lax.axis_index("seq") % 2
+    cand_out[...] = cand[...]
     x = events[...].astype(f32)
     normed_in = center_scale(x)[0]
     mine, other = split_columns(normed_in, owners, core)
@@ -404,15 +405,16 @@
         rows = sum(x.shape[0] for x in parts)
         return call(join_kernel, [((rows, parts[0].shape[1]), b16)], [VMEM] * len(parts), parts, room=8)[0]
 
-    def reduce_chips(low, high):
+    def fold(low, high):
         bit = 1
-        while True:
-            came = across(high, bit)
+        while bit < chips // 2:
+            shape = (low.shape[0] // 2, low.shape[1])
+            low, high = call(pair_kernel, [(shape, b16)] * 2, [VMEM] * 2, [low, across(high, bit)], room=8)
             bit *= 2
-            if bit >= chips:
-                return low.astype(f32) + came.astype(f32)
-            shape = (low.shape[0] // 2, low.shape[1])
-            low, high = call(pair_kernel, [(shape, b16)] * 2, [VMEM] * 2, [low, came], room=8)
+        return low, high
+
+    def finish(low, high):
+        return low.astype(f32) + across(high, chips // 2).astype(f32)
 
     def gather_groups(x, near=None):
         wide = x.shape[1]
@@ -435,16 +437,16 @@
         bit //= 2
     got = [have[x] for x in distances(chips)[1:]]
     candidates = jnp.concatenate([history[:, None], negatives], 1)
-    events, candidates = lax.optimization_barrier((events, candidates))
+    events, candidates, _ = lax.optimization_barrier((events, candidates, [have[x] for x in have if x and not x & (x - 1)]))
     outs = [
-        ((tok, width // 2), b16), ((tok, width // 2), b16), ((tok, 4 * hidden), b16), ((tok, 4 * hidden), b16),
+        ((tok, NCAND), i32), ((tok, width // 2), b16), ((tok, width // 2), b16), ((tok, 4 * hidden), b16), ((tok, 4 * hidden), b16),
         ((HEADS, tok, tok), b16), ((HEADS, tok, tok), b16), ((tok, hidden), f32), ((tok, 1), f32),
         ((tok, hidden), b16), ((tok, width), f32), ((tok, width), b16), ((tok, 1), f32),
         ((owners * slot, width), b16),
     ]
-    (keep, give, proj, slope, attn, attn_slope, normed, inverse, gated, unit, unit_b, inv_len, outgoing) = call(
-        lambda *refs: forward_kernel(owners, slot, *refs), outs, [SMEM, SMEM, VMEM, VMEM, VMEM],
-        [lengths, destinations, events, in_weight, out_weight],
+    (candidates, keep, give, proj, slope, attn, attn_slope, normed, inverse, gated, unit, unit_b, inv_len, outgoing) = call(
+        lambda *refs: forward_kernel(owners, slot, *refs), outs, [SMEM, SMEM, VMEM, VMEM, VMEM, VMEM],
+        [lengths, destinations, events, in_weight, out_weight, candidates],
         flops=2 * tok * width * 6 * hidden, nbytes=24 * tok * width + 10 * width * hidden, room=28,
     )
 
@@ -491,6 +493,16 @@
     far = [far_give, to_core(up_give), None, far_gated]
     grad, far[1], all_tags = lax.optimization_barrier((grad, far[1], all_tags))
     far[2] = to_core(grad)
+    mine, other = call(
+        lambda *refs: item_kernel(groups, owners, share, chunks, [p[:3] for p in unit_sent], *refs),
+        [((chips * share, width), b16)] * 2, [ANY] * len(units) + [VMEM] * groups + [ANY] * len(near),
+        units + all_tags + near,
+        [pltpu.VMEM((groups * tok, width), b16), pltpu.VMEM((2 * chips * share, width), b16),
+         pltpu.SemaphoreType.DMA((len(units) + 2 * chips,))],
+        room=16 if groups == 4 else 48,
+    )
+    far_mine = to_core(other)
+    far, mine = lax.optimization_barrier((far, mine))
     half = 5 * hidden // 2
     if groups == 4:
         block = (chips, fine, 5 * hidden)
@@ -502,7 +514,6 @@
             [pltpu.VMEM((width // 2, 5 * hidden), b16)],
             flops=2 * tok * width * 5 * hidden, nbytes=20 * tok * width,
         )
-        after = parts[0]
         by_one, by_two = to_group(parts[1], 1), to_group(parts[2], 2)
         corner = (by_one, by_two)
     else:
@@ -513,34 +524,23 @@
         out_part = dot(both(up_keep, far[1]), both(gated, far[3]), TN)
         weight = jnp.concatenate([in_part, out_part], 1).astype(b16)
         weight = weight.reshape(chips, groups, fine, 5 * hidden)
-        after = weight
         sums = lax.dynamic_index_in_dim(weight, grp, 1, False).astype(f32)
         for k in range(1, groups):
             sums += to_group(lax.dynamic_index_in_dim(weight, grp ^ k, 1, False), k).astype(f32)
 
 
-    units[0], _ = lax.optimization_barrier((units[0], after))
-    mine, other = call(
-        lambda *refs: item_kernel(groups, owners, share, chunks, [p[:3] for p in unit_sent], *refs),
-        [((chips * share, width), b16)] * 2, [ANY] * len(units) + [VMEM] * groups + [ANY] * len(near),
-        units + all_tags + near,
-        [pltpu.VMEM((groups * tok, width), b16), pltpu.VMEM((2 * chips * share, width), b16),
-         pltpu.SemaphoreType.DMA((len(units) + 2 * chips,))],
-        room=16 if groups == 4 else 48,
-    )
-    far_mine = to_core(other)
-
     low, high = call(
         pair_kernel, [((chips // 2 * share, width), b16)] * 2, [VMEM] * 2, [mine, far_mine],
         flops=chips * share * width, nbytes=6 * chips * share * width, room=8,
     )
+    low, high = fold(low, high)
     if groups == 4:
         by_one, by_two, low, high = lax.optimization_barrier(corner + (low, high))
         one_right, two_left = call(
             corner_kernel, [(split, b16)] * 2, [VMEM] * 4, [by_one, by_two, parts[3], parts[4]], room=8,
         )
         arrived = [by_one, by_two, to_group(one_right, 1), to_group(two_left, 2)]
-    total = reduce_chips(low, high)
+    total = finish(low, high)
     total = (total * quarter_inv).astype(b16)
     table_grad, = call(
         lambda *refs: assemble_kernel(groups, [width], *refs), [((vocab_dev, width), f32)], [VMEM] * groups,
@@ -549,11 +549,12 @@
     )
 
     if groups == 4:
+        base, _ = lax.optimization_barrier((parts[0], total))
         low, high = call(
-            sum_kernel, [((chips // 2 * fine, 5 * hidden), b16)] * 2, [VMEM] * 5, [parts[0]] + arrived,
+            sum_kernel, [((chips // 2 * fine, 5 * hidden), b16)] * 2, [VMEM] * 5, [base] + arrived,
             flops=chips * fine * 5 * hidden, nbytes=40 * chips * fine * hidden, room=10,
         )
-        line = reduce_chips(low, high)
+        line = finish(*fold(low, high))
     else:
         blocks = [lax.dynamic_index_in_dim(sums, (chip + d) % chips, 0, False).astype(b16) for d in range(chips)]
         line = blocks[0].astype(f32)

time: 191 us -> 181 us (0.948)
  waiting for transfers between devices: 93.6 us -> 78.3 us
  starting transfers between devices: 41.1 us -> 45.1 us
    ppermute x21, waiting for transfers between devices: 53.1 us -> 30.1 us  [to_group(): return lax.ppermute(x, 'grp', [(a, a ^ k) for a in range(groups)])]
    ppermute x7, waiting for transfers between devices: 36.5 us -> 46.4 us  [across(): return lax.ppermute(x, 'seq', pairs)]
    ppermute x7, starting transfers between devices: 12.3 us -> 15.4 us  [across(): return lax.ppermute(x, 'seq', pairs)]
    ppermute x11, waiting for transfers between devices: 3.98 us -> 1.76 us  [to_core(): return lax.ppermute(x, 'seq', [(a, a ^ 1) for a in range(owners)])]
    unnamed x82 -> x84, local copies, waits for them, and re-layouts: 23.9 us -> 24.5 us
  transfers between devices with their start and end apart: 40 -> 40, of which waited for: 20 -> 23; matrix products, arithmetic and copies ran while one was open for 1% -> 1% of each run, Pallas kernels for 6% -> 7%
where the time goes in v9:
time: 181 us
  waiting for transfers between devices  78.3 us (43%)
  starting transfers between devices  45.1 us (25%)
  Pallas kernels  29.7 us (16%)
  local copies, waits for them, and re-layouts  24.6 us (14%)
  other arithmetic  1.9 us (1%)
    ppermute x7, waiting for transfers between devices, across(): return lax.ppermute(x, 'seq', pairs)  46.4 us
    ppermute x21, waiting for transfers between devices, to_group(): return lax.ppermute(x, 'grp', [(a, a ^ k) for a in range(groups)])  30.1 us
    pallas_call x19, Pallas kernels, call(): pl.pallas_call(kernel, out_shape=[jax.ShapeDtypeStruct(s, t) for s, t in...  29.7 us
    unnamed x84, local copies, waits for them, and re-layouts  24.5 us
    ppermute x21, starting transfers between devices, to_group(): return lax.ppermute(x, 'grp', [(a, a ^ k) for a in range(groups)])  24 us
    ppermute x7, starting transfers between devices, across(): return lax.ppermute(x, 'seq', pairs)  15.4 us
    all_to_all x1, starting transfers between devices, body(): lax.all_to_all(outgoing.reshape(owners, slot, width), 'seq', 0, 0, tiled=...  3.85 us
  transfers between devices with their start and end apart: 40, of which 23 were waited for; matrix products, arithmetic and copies ran while one was open for 1% of the time, Pallas kernels for 7%

profile of v9, /device:TPU:0, one launch (start us, length us, event | category | flops | bytes accessed | tf_op | source)
XLA Modules:
  0.0 180.6 jit_solution(10015663299503161524)
XLA Ops:
  3.9 3.0 %collective-permute-start.1 = (bf16[128,1024]{1,0:T(8,128)(2,1)S(1)}, bf16[128,1024]{1,0:T(8,128)(2,1)S(1)}, u32[]{:S(2)}, u32[]{:S(2)}) collective-permute-start(bf16[128,1024]{1,0:T(8,128)(2,1)S(1)} %get-tuple-element.78), channel_id=1, source_target_pairs={{0,2},{1,3},{2,0},{3,1},{4,6},{5,7},{6,4},{7,5},{8,10},{9,11},{10,... | collective-permute-start | bytes 786440 | tf_op jit(solution)/shard_map/ppermute | solution.py:393
  6.9 2.6 %collective-permute-start = (bf16[128,1024]{1,0:T(8,128)(2,1)S(1)}, bf16[128,1024]{1,0:T(8,128)(2,1)S(1)}, u32[]{:S(2)}, u32[]{:S(2)}) collective-permute-start(bf16[128,1024]{1,0:T(8,128)(2,1)S(1)} %get-tuple-element.78), channel_id=1, source_target_pairs={{0,4},{1,5},{2,6},{3,7},{4,0},{5,1},{6,2},{7,3},{8,12},{9,13},{10,... | collective-permute-start | bytes 786440 | tf_op jit(solution)/shard_map/ppermute | solution.py:393
  10.2 8.5 %collective-permute-done.1.refs_1_ = bf16[128,1024]{1,0:T(8,128)(2,1)S(1)} collective-permute-done((bf16[128,1024]{1,0:T(8,128)(2,1)S(1)}, bf16[128,1024]{1,0:T(8,128)(2,1)S(1)}, u32[]{:S(2)}, u32[]{:S(2)}) %collective-permute-start.1) | collective-permute-done | bytes 262176 | tf_op jit(solution)/shard_map/ppermute | solution.py:393
  18.7 2.5 %collective-permute-done.refs_0_ = bf16[128,1024]{1,0:T(8,128)(2,1)S(1)} collective-permute-done((bf16[128,1024]{1,0:T(8,128)(2,1)S(1)}, bf16[128,1024]{1,0:T(8,128)(2,1)S(1)}, u32[]{:S(2)}, u32[]{:S(2)}) %collective-permute-start) | collective-permute-done | bytes 262176 | tf_op jit(solution)/shard_map/ppermute | solution.py:393
  22.6 2.2 %copy-done.23 = bf16[1024,2048]{1,0:T(8,128)(2,1)S(1)} copy-done((bf16[1024,2048]{1,0:T(8,128)(2,1)S(1)}, bf16[1024,2048]{1,0:T(8,128)(2,1)}, u32[]{:S(2)}) %copy-start.23) | copy-done | bytes 4194328
  27.1 5.5 %shard_map.112 = (s32[256,4]{1,0:T(8,128)S(1)}, bf16[256,512]{1,0:T(8,128)(2,1)S(1)}, bf16[256,512]{1,0:T(8,128)(2,1)S(1)}, bf16[256,2048]{1,0:T(8,128)(2,1)S(1)...) custom-call(s32[1,8]{1,0:T(1,128)S(1)} %copy-done.32, ...), custom_call_target="tpu_custom_call" | custom-call | flops 1610612736 | bytes 11534336 | tf_op jit(solution)/shard_map/pallas_call | solution.py:53
  43.9 5.9 %collective-permute-done.2.refs_2_ = bf16[128,1024]{1,0:T(8,128)(2,1)S(1)} collective-permute-done((bf16[128,1024]{1,0:T(8,128)(2,1)S(1)}, bf16[128,1024]{1,0:T(8,128)(2,1)S(1)}, u32[]{:S(2)}, u32[]{:S(2)}) %collective-permute-start.2) | collective-permute-done | bytes 262176 | tf_op jit(solution)/shard_map/ppermute | solution.py:393
  49.8 1.9 %collective-permute-done.4.refs_0_.refs_2_ = bf16[256,1024]{1,0:T(8,128)(2,1)S(1)} collective-permute-done((bf16[256,1024]{1,0:T(8,128)(2,1)S(1)}, bf16[256,1024]{1,0:T(8,128)(2,1)S(1)}, u32[]{:S(2)}, u32[]{:S(2)}) %collective-permute-start.4) | collective-permute-done | bytes 524320 | tf_op jit(solution)/shard_map/ppermute | solution.py:396
  51.8 1.6 collective-permute-done.3.refs_0_.refs_1_
  53.8 1.8 collective-permute-start.9
  55.6 3.8 %all-to-all-start = ((bf16[8,48,1024]{2,1,0:T(8,128)(2,1)}), bf16[8,48,1024]{2,1,0:T(8,128)(2,1)S(1)}, u32[]{:S(2)}, u32[]{:S(2)}) async-start(bf16[8,48,1024]{2,1,0:T(8,128)(2,1)} %bitcast.1), calls=%async_computation | async-start | bytes 1572864 | tf_op jit(solution)/shard_map/all_to_all | solution.py:465
  62.5 5.3 %collective-permute-done.10.refs_0_.refs_7_ = bf16[384,1024]{1,0:T(8,128)(2,1)S(1)} collective-permute-done((bf16[384,1024]{1,0:T(8,128)(2,1)S(1)}, bf16[384,1024]{1,0:T(8,128)(2,1)S(1)}, u32[]{:S(2)}, u32[]{:S(2)}) %collective-permute-start.10) | collective-permute-done | bytes 786464 | tf_op jit(solution)/shard_map/ppermute | solution.py:396
  67.9 4.0 %collective-permute-done.9.refs_0_.refs_6_ = bf16[384,1024]{1,0:T(8,128)(2,1)} collective-permute-done((bf16[384,1024]{1,0:T(8,128)(2,1)S(1)}, bf16[384,1024]{1,0:T(8,128)(2,1)}, u32[]{:S(2)}, u32[]{:S(2)}) %collective-permute-start.9) | collective-permute-done | bytes 786464 | tf_op jit(solution)/shard_map/ppermute | solution.py:396
  78.0 2.6 %collective-permute-done.7.refs_3_ = bf16[256,512]{1,0:T(8,128)(2,1)S(1)} collective-permute-done((bf16[256,512]{1,0:T(8,128)(2,1)S(1)}, bf16[256,512]{1,0:T(8,128)(2,1)S(1)}, u32[]{:S(2)}, u32[]{:S(2)}) %collective-permute-start.7) | collective-permute-done | bytes 262176 | tf_op jit(solution)/shard_map/ppermute | solution.py:396
  83.1 3.7 %collective-permute-done.11.refs_8_ = bf16[384,512]{1,0:T(8,128)(2,1)} collective-permute-done((bf16[384,512]{1,0:T(8,128)(2,1)S(1)}, bf16[384,512]{1,0:T(8,128)(2,1)}, u32[]{:S(2)}, u32[]{:S(2)}) %collective-permute-start.11) | collective-permute-done | bytes 393248 | tf_op jit(solution)/shard_map/ppermute | solution.py:396
  86.8 1.6 shard_map.114
  94.2 9.0 %shard_map.119 = (f32[16,256]{1,0:T(8,128)S(1)}, bf16[256,1024]{1,0:T(8,128)(2,1)S(1)}, bf16[256,512]{1,0:T(8,128)(2,1)S(1)}, bf16[256,512]{1,0:T(8,128)(2,1)S(1)}) custom-call(s32[256,4]{1,0:T(8,128)S(1)} %copy-done.39, f32[256,1]{1,0:T(8,128)S(1)} %copy-done.41, bf16[256,1024]{1,0:T(8,128)(2,1)S(1)} %copy-done.10, f32[256,1024]{1,0:T(8,128)S(1)} %copy-done.35, ...), custom_call_target="tpu_custom_call" | custom-call | flops 4294967296 | bytes 11534336 | tf_op jit(solution)/shard_map/pallas_call | solution.py:53
  107.0 1.6 shard_map.120.refs_4_
  109.7 4.5 %shard_map.121 = (bf16[512,1024]{1,0:T(8,128)(2,1)S(1)}, bf16[512,1024]{1,0:T(8,128)(2,1)S(1)}) custom-call(bf16[256,1024]{1,0:T(8,128)(2,1)S(1)} %copy-done.10, bf16[256,1024]{1,0:T(8,128)(2,1)S(1)} %collective-permute-done.3.refs_0_.refs_1_, bf16[256,1024]{1,0:T(8,128)(2,1)S(1)} %collective-permute-done.4.refs_0_.refs_2_, bf16[256,512]{1,0:T(8,128)(2,1)S(1)} %copy-done.20, ...), custom_call_target="tpu_custom_call" | custom-call | tf_op jit(solution)/shard_map/pallas_call | solution.py:53
  114.8 1.7 shard_map.122
  118.5 4.3 %collective-permute-start.27 = (bf16[256,1024]{1,0:T(8,128)(2,1)S(1)}, bf16[256,1024]{1,0:T(8,128)(2,1)S(1)}, u32[]{:S(2)}, u32[]{:S(2)}) collective-permute-start(bf16[256,1024]{1,0:T(8,128)(2,1)S(1)} %get-tuple-element.133), channel_id=1, source_target_pairs={{0,2},{1,3},{2,0},{3,1},{4,6},{5,7},{6,4},{7,5},{8,10},{9,11},{10,... | collective-permute-start | bytes 1572872 | tf_op jit(solution)/shard_map/ppermute | solution.py:393
  122.8 11.6 %collective-permute-done.27.y = bf16[256,1024]{1,0:T(8,128)(2,1)S(1)} collective-permute-done((bf16[256,1024]{1,0:T(8,128)(2,1)S(1)}, bf16[256,1024]{1,0:T(8,128)(2,1)S(1)}, u32[]{:S(2)}, u32[]{:S(2)}) %collective-permute-start.27) | collective-permute-done | bytes 524320 | tf_op jit(solution)/shard_map/ppermute | solution.py:393
  134.5 2.8 %collective-permute-start.28 = (bf16[128,1024]{1,0:T(8,128)(2,1)S(1)}, bf16[128,1024]{1,0:T(8,128)(2,1)}, u32[]{:S(2)}, u32[]{:S(2)}) collective-permute-start(bf16[128,1024]{1,0:T(8,128)(2,1)S(1)} %get-tuple-element.137), channel_id=1, source_target_pairs={{0,4},{1,5},{2,6},{3,7},{4,0},{5,1},{6,2},{7,3},{8,12},{9,13},{10,... | collective-permute-start | bytes 786440 | tf_op jit(solution)/shard_map/ppermute | solution.py:393
  140.7 7.7 %collective-permute-done.28 = bf16[128,1024]{1,0:T(8,128)(2,1)} collective-permute-done((bf16[128,1024]{1,0:T(8,128)(2,1)S(1)}, bf16[128,1024]{1,0:T(8,128)(2,1)}, u32[]{:S(2)}, u32[]{:S(2)}) %collective-permute-start.28) | collective-permute-done | bytes 262176 | tf_op jit(solution)/shard_map/ppermute | solution.py:393
  149.8 7.6 %collective-permute-done.31.y = bf16[64,2560]{1,0:T(8,128)(2,1)S(1)} collective-permute-done((bf16[64,2560]{1,0:T(8,128)(2,1)S(1)}, bf16[64,2560]{1,0:T(8,128)(2,1)S(1)}, u32[]{:S(2)}, u32[]{:S(2)}) %collective-permute-start.31) | collective-permute-done | bytes 327712 | tf_op jit(solution)/shard_map/ppermute | solution.py:393
  157.5 2.2 %collective-permute-start.32 = (bf16[32,2560]{1,0:T(8,128)(2,1)S(1)}, bf16[32,2560]{1,0:T(8,128)(2,1)S(1)}, u32[]{:S(2)}, u32[]{:S(2)}) collective-permute-start(bf16[32,2560]{1,0:T(8,128)(2,1)S(1)} %get-tuple-element.149), channel_id=1, source_target_pairs={{0,4},{1,5},{2,6},{3,7},{4,0},{5,1},{6,2},{7,3},{8,12},{9,13},{10,... | collective-permute-start | bytes 491528 | tf_op jit(solution)/shard_map/ppermute | solution.py:393
  159.7 1.9 %collective-permute-start.38 = (bf16[128,1024]{1,0:T(8,128)(2,1)S(1)}, bf16[128,1024]{1,0:T(8,128)(2,1)S(1)}, u32[]{:S(2)}, u32[]{:S(2)}) collective-permute-start(bf16[128,1024]{1,0:T(8,128)(2,1)S(1)} %multiply_convert_fusion.refs_0_), channel_id=1, source_target_pairs={{0,24},{8,16},{16,8},{24,0},{1,25},{9,17},{17,9},{25,1},{2,26},{10... | collective-permute-start | bytes 786440 | tf_op jit(solution)/shard_map/ppermute | solution.py:396
  163.2 2.6 %collective-permute-done.32 = bf16[32,2560]{1,0:T(8,128)(2,1)S(1)} collective-permute-done((bf16[32,2560]{1,0:T(8,128)(2,1)S(1)}, bf16[32,2560]{1,0:T(8,128)(2,1)S(1)}, u32[]{:S(2)}, u32[]{:S(2)}) %collective-permute-start.32) | collective-permute-done | bytes 163872 | tf_op jit(solution)/shard_map/ppermute | solution.py:393
  165.8 1.9 %collective-permute-start.35 = (bf16[32,2560]{1,0:T(8,128)(2,1)S(1)}, bf16[32,2560]{1,0:T(8,128)(2,1)S(1)}, u32[]{:S(2)}, u32[]{:S(2)}) collective-permute-start(bf16[32,2560]{1,0:T(8,128)(2,1)S(1)} %add_convert_fusion.refs_0_), channel_id=1, source_target_pairs={{0,24},{8,16},{16,8},{24,0},{1,25},{9,17},{17,9},{25,1},{2,26},{10... | collective-permute-start | bytes 491528 | tf_op jit(solution)/shard_map/ppermute | solution.py:396
  168.4 1.5 collective-permute-done.38.refs_3_
  170.9 4.0 %collective-permute-done.37.refs_2_ = bf16[128,1024]{1,0:T(8,128)(2,1)S(1)} collective-permute-done((bf16[128,1024]{1,0:T(8,128)(2,1)S(1)}, bf16[128,1024]{1,0:T(8,128)(2,1)S(1)}, u32[]{:S(2)}, u32[]{:S(2)}) %collective-permute-start.37) | collective-permute-done | bytes 262176 | tf_op jit(solution)/shard_map/ppermute | solution.py:396
  177.8 1.6 collective-permute-done.34.refs_2_
  (156 shorter events, 56.4 us)
Async XLA Ops:
  3.9 14.8 %collective-permute-start.1 = (bf16[128,1024]{1,0:T(8,128)(2,1)S(1)}, bf16[128,1024]{1,0:T(8,128)(2,1)S(1)}, u32[]{:S(2)}, u32[]{:S(2)}) collective-permute-start(bf16[128,1024]{1,0:T(8,128)(2,1)S(1)} %get-tuple-element.78), channel_id=1, source_target_pairs={{0,2},{1,3},{2,0},{3,1},{4,6},{5,7},{6,4},{7,5},{8,10},{9,11},{10,... | collective-permute-start | bytes 786440 | tf_op jit(solution)/shard_map/ppermute | solution.py:393
  6.9 14.3 %collective-permute-start = (bf16[128,1024]{1,0:T(8,128)(2,1)S(1)}, bf16[128,1024]{1,0:T(8,128)(2,1)S(1)}, u32[]{:S(2)}, u32[]{:S(2)}) collective-permute-start(bf16[128,1024]{1,0:T(8,128)(2,1)S(1)} %get-tuple-element.78), channel_id=1, source_target_pairs={{0,4},{1,5},{2,6},{3,7},{4,0},{5,1},{6,2},{7,3},{8,12},{9,13},{10,... | collective-permute-start | bytes 786440 | tf_op jit(solution)/shard_map/ppermute | solution.py:393
  40.4 11.3 %collective-permute-start.4 = (bf16[256,1024]{1,0:T(8,128)(2,1)S(1)}, bf16[256,1024]{1,0:T(8,128)(2,1)S(1)}, u32[]{:S(2)}, u32[]{:S(2)}) collective-permute-start(bf16[256,1024]{1,0:T(8,128)(2,1)S(1)} %get-tuple-element.112.refs_2_.refs_0_), channel_id=1, source_target_pairs={{0,16},{8,24},{16,0},{24,8},{1,17},{9,25},{17,1},{25,9},{2,18},{10... | collective-permute-start | bytes 1572872 | tf_op jit(solution)/shard_map/ppermute | solution.py:396
  42.0 11.4 %collective-permute-start.3 = (bf16[256,1024]{1,0:T(8,128)(2,1)S(1)}, bf16[256,1024]{1,0:T(8,128)(2,1)S(1)}, u32[]{:S(2)}, u32[]{:S(2)}) collective-permute-start(bf16[256,1024]{1,0:T(8,128)(2,1)S(1)} %get-tuple-element.112.refs_2_.refs_0_), channel_id=1, source_target_pairs={{0,8},{8,0},{16,24},{24,16},{1,9},{9,1},{17,25},{25,17},{2,10},{10... | collective-permute-start | bytes 1572872 | tf_op jit(solution)/shard_map/ppermute | solution.py:396
  43.5 6.4 %collective-permute-start.2 = (bf16[128,1024]{1,0:T(8,128)(2,1)S(1)}, bf16[128,1024]{1,0:T(8,128)(2,1)S(1)}, u32[]{:S(2)}, u32[]{:S(2)}) collective-permute-start(bf16[128,1024]{1,0:T(8,128)(2,1)S(1)} %collective-permute-done.refs_0_), channel_id=1, source_target_pairs={{0,2},{1,3},{2,0},{3,1},{4,6},{5,7},{6,4},{7,5},{8,10},{9,11},{10,... | collective-permute-start | bytes 786440 | tf_op jit(solution)/shard_map/ppermute | solution.py:393
  53.4 14.5 %collective-permute-start.10 = (bf16[384,1024]{1,0:T(8,128)(2,1)S(1)}, bf16[384,1024]{1,0:T(8,128)(2,1)S(1)}, u32[]{:S(2)}, u32[]{:S(2)}) collective-permute-start(bf16[384,1024]{1,0:T(8,128)(2,1)S(1)} %shard_map.113.refs_5_.refs_10_), channel_id=1, source_target_pairs={{0,16},{8,24},{16,0},{24,8},{1,17},{9,25},{17,1},{25,9},{2,18},{10... | collective-permute-start | bytes 2359304 | tf_op jit(solution)/shard_map/ppermute | solution.py:396
  53.8 18.1 %collective-permute-start.9 = (bf16[384,1024]{1,0:T(8,128)(2,1)S(1)}, bf16[384,1024]{1,0:T(8,128)(2,1)}, u32[]{:S(2)}, u32[]{:S(2)}) collective-permute-start(bf16[384,1024]{1,0:T(8,128)(2,1)S(1)} %shard_map.113.refs_5_.refs_10_), channel_id=1, source_target_pairs={{0,8},{8,0},{16,24},{24,16},{1,9},{9,1},{17,25},{25,17},{2,10},{10... | collective-permute-start | bytes 2359304 | tf_op jit(solution)/shard_map/ppermute | solution.py:396
  55.6 25.8 %collective-permute-start.14 = (bf16[384,1024]{1,0:T(8,128)(2,1)S(1)}, bf16[384,1024]{1,0:T(8,128)(2,1)}, u32[]{:S(2)}, u32[]{:S(2)}) collective-permute-start(bf16[384,1024]{1,0:T(8,128)(2,1)S(1)} %shard_map.113.refs_5_.refs_10_), channel_id=1, source_target_pairs={{0,1},{1,0},{2,3},{3,2},{4,5},{5,4},{6,7},{7,6},{8,9},{9,8},{10,11... | collective-permute-start | bytes 2359304 | tf_op jit(solution)/shard_map/ppermute | solution.py:399
  55.6 31.2 %all-to-all-start = ((bf16[8,48,1024]{2,1,0:T(8,128)(2,1)}), bf16[8,48,1024]{2,1,0:T(8,128)(2,1)S(1)}, u32[]{:S(2)}, u32[]{:S(2)}) async-start(bf16[8,48,1024]{2,1,0:T(8,128)(2,1)} %bitcast.1), calls=%async_computation | async-start | bytes 1572864 | tf_op jit(solution)/shard_map/all_to_all | solution.py:465
  59.9 13.8 %collective-permute-start.6 = (bf16[256,512]{1,0:T(8,128)(2,1)}, bf16[256,512]{1,0:T(8,128)(2,1)S(1)}, u32[]{:S(2)}, u32[]{:S(2)}) collective-permute-start(bf16[256,512]{1,0:T(8,128)(2,1)} %copy-done.25), channel_id=1, source_target_pairs={{0,1},{1,0},{2,3},{3,2},{4,5},{5,4},{6,7},{7,6},{8,9},{9,8},{10,11... | collective-permute-start | bytes 786440 | tf_op jit(solution)/shard_map/ppermute | solution.py:399
  62.0 13.8 %collective-permute-start.8 = (bf16[256,512]{1,0:T(8,128)(2,1)S(1)}, bf16[256,512]{1,0:T(8,128)(2,1)S(1)}, u32[]{:S(2)}, u32[]{:S(2)}) collective-permute-start(bf16[256,512]{1,0:T(8,128)(2,1)S(1)} %shard_map.116), channel_id=1, source_target_pairs={{0,8},{8,0},{16,24},{24,16},{1,9},{9,1},{17,25},{25,17},{2,10},{10... | collective-permute-start | bytes 786440 | tf_op jit(solution)/shard_map/ppermute | solution.py:396
  67.9 20.5 %collective-permute-start.13 = (bf16[512,1024]{1,0:T(8,128)(2,1)}, bf16[512,1024]{1,0:T(8,128)(2,1)}, u32[]{:S(2)}, u32[]{:S(2)}) collective-permute-start(bf16[512,1024]{1,0:T(8,128)(2,1)} %copy-done.7), channel_id=1, source_target_pairs={{0,1},{1,0},{2,3},{3,2},{4,5},{5,4},{6,7},{7,6},{8,9},{9,8},{10,11... | collective-permute-start | bytes 3145736 | tf_op jit(solution)/shard_map/ppermute | solution.py:399
  71.9 8.8 %collective-permute-start.7 = (bf16[256,512]{1,0:T(8,128)(2,1)S(1)}, bf16[256,512]{1,0:T(8,128)(2,1)S(1)}, u32[]{:S(2)}, u32[]{:S(2)}) collective-permute-start(bf16[256,512]{1,0:T(8,128)(2,1)S(1)} %shard_map.115), channel_id=1, source_target_pairs={{0,16},{8,24},{16,0},{24,8},{1,17},{9,25},{17,1},{25,9},{2,18},{10... | collective-permute-start | bytes 786440 | tf_op jit(solution)/shard_map/ppermute | solution.py:396
  74.5 8.7 %collective-permute-start.12 = (bf16[384,512]{1,0:T(8,128)(2,1)S(1)}, bf16[384,512]{1,0:T(8,128)(2,1)}, u32[]{:S(2)}, u32[]{:S(2)}) collective-permute-start(bf16[384,512]{1,0:T(8,128)(2,1)S(1)} %shard_map.118), channel_id=1, source_target_pairs={{0,8},{8,0},{16,24},{24,16},{1,9},{9,1},{17,25},{25,17},{2,10},{10... | collective-permute-start | bytes 1179656 | tf_op jit(solution)/shard_map/ppermute | solution.py:396
  76.5 10.3 %collective-permute-start.11 = (bf16[384,512]{1,0:T(8,128)(2,1)S(1)}, bf16[384,512]{1,0:T(8,128)(2,1)}, u32[]{:S(2)}, u32[]{:S(2)}) collective-permute-start(bf16[384,512]{1,0:T(8,128)(2,1)S(1)} %shard_map.117), channel_id=1, source_target_pairs={{0,16},{8,24},{16,0},{24,8},{1,17},{9,25},{17,1},{25,9},{2,18},{10... | collective-permute-start | bytes 1179656 | tf_op jit(solution)/shard_map/ppermute | solution.py:396
  81.3 7.1 %collective-permute-start.16 = (bf16[384,1024]{1,0:T(8,128)(2,1)S(1)}, bf16[384,1024]{1,0:T(8,128)(2,1)}, u32[]{:S(2)}, u32[]{:S(2)}) collective-permute-start(bf16[384,1024]{1,0:T(8,128)(2,1)S(1)} %collective-permute-done.10.refs_0_.refs_7_), channel_id=1, source_target_pairs={{0,1},{1,0},{2,3},{3,2},{4,5},{5,4},{6,7},{7,6},{8,9},{9,8},{10,11... | collective-permute-start | bytes 2359304 | tf_op jit(solution)/shard_map/ppermute | solution.py:399
  81.3 7.5 %collective-permute-start.15 = (bf16[384,1024]{1,0:T(8,128)(2,1)}, bf16[384,1024]{1,0:T(8,128)(2,1)}, u32[]{:S(2)}, u32[]{:S(2)}) collective-permute-start(bf16[384,1024]{1,0:T(8,128)(2,1)} %collective-permute-done.9.refs_0_.refs_6_), channel_id=1, source_target_pairs={{0,1},{1,0},{2,3},{3,2},{4,5},{5,4},{6,7},{7,6},{8,9},{9,8},{10,11... | collective-permute-start | bytes 2359304 | tf_op jit(solution)/shard_map/ppermute | solution.py:399
  103.2 6.4 %collective-permute-start.19 = (bf16[256,512]{1,0:T(8,128)(2,1)S(1)}, bf16[256,512]{1,0:T(8,128)(2,1)S(1)}, u32[]{:S(2)}, u32[]{:S(2)}) collective-permute-start(bf16[256,512]{1,0:T(8,128)(2,1)S(1)} %get-tuple-element.107), channel_id=1, source_target_pairs={{0,1},{1,0},{2,3},{3,2},{4,5},{5,4},{6,7},{7,6},{8,9},{9,8},{10,11... | collective-permute-start | bytes 786440 | tf_op jit(solution)/shard_map/ppermute | solution.py:399
  116.5 18.0 %collective-permute-start.24 = (bf16[2,4,32,1280]{3,2,1,0:T(8,128)(2,1)S(1)}, bf16[2,4,32,1280]{3,2,1,0:T(8,128)(2,1)S(1)}, u32[]{:S(2)}, u32[]{:S(2)}) collective-permute-start(bf16[2,4,32,1280]{3,2,1,0:T(8,128)(2,1)S(1)} %get-tuple-element.128), channel_id=1, source_target_pairs={{0,8},{8,0},{16,24},{24,16},{1,9},{9,1},{17,25},{25,17},{2,10},{10... | collective-permute-start | bytes 1966088 | tf_op jit(solution)/shard_map/ppermute | solution.py:396
  117.6 17.0 %collective-permute-start.25 = (bf16[2,4,32,1280]{3,2,1,0:T(8,128)(2,1)S(1)}, bf16[2,4,32,1280]{3,2,1,0:T(8,128)(2,1)S(1)}, u32[]{:S(2)}, u32[]{:S(2)}) collective-permute-start(bf16[2,4,32,1280]{3,2,1,0:T(8,128)(2,1)S(1)} %get-tuple-element.129), channel_id=1, source_target_pairs={{0,16},{8,24},{16,0},{24,8},{1,17},{9,25},{17,1},{25,9},{2,18},{10... | collective-permute-start | bytes 1966088 | tf_op jit(solution)/shard_map/ppermute | solution.py:396
  118.5 15.9 %collective-permute-start.27 = (bf16[256,1024]{1,0:T(8,128)(2,1)S(1)}, bf16[256,1024]{1,0:T(8,128)(2,1)S(1)}, u32[]{:S(2)}, u32[]{:S(2)}) collective-permute-start(bf16[256,1024]{1,0:T(8,128)(2,1)S(1)} %get-tuple-element.133), channel_id=1, source_target_pairs={{0,2},{1,3},{2,0},{3,1},{4,6},{5,7},{6,4},{7,5},{8,10},{9,11},{10,... | collective-permute-start | bytes 1572872 | tf_op jit(solution)/shard_map/ppermute | solution.py:393
  134.5 13.9 %collective-permute-start.28 = (bf16[128,1024]{1,0:T(8,128)(2,1)S(1)}, bf16[128,1024]{1,0:T(8,128)(2,1)}, u32[]{:S(2)}, u32[]{:S(2)}) collective-permute-start(bf16[128,1024]{1,0:T(8,128)(2,1)S(1)} %get-tuple-element.137), channel_id=1, source_target_pairs={{0,4},{1,5},{2,6},{3,7},{4,0},{5,1},{6,2},{7,3},{8,12},{9,13},{10,... | collective-permute-start | bytes 786440 | tf_op jit(solution)/shard_map/ppermute | solution.py:393
  138.1 11.3 %collective-permute-start.29 = (bf16[4,32,1280]{2,1,0:T(8,128)(2,1)}, bf16[4,32,1280]{2,1,0:T(8,128)(2,1)S(1)}, u32[]{:S(2)}, u32[]{:S(2)}) collective-permute-start(bf16[4,32,1280]{2,1,0:T(8,128)(2,1)} %get-tuple-element.144), channel_id=1, source_target_pairs={{0,8},{8,0},{16,24},{24,16},{1,9},{9,1},{17,25},{25,17},{2,10},{10... | collective-permute-start | bytes 983048 | tf_op jit(solution)/shard_map/ppermute | solution.py:396
  139.1 10.3 %collective-permute-start.30 = (bf16[4,32,1280]{2,1,0:T(8,128)(2,1)S(1)}, bf16[4,32,1280]{2,1,0:T(8,128)(2,1)S(1)}, u32[]{:S(2)}, u32[]{:S(2)}) collective-permute-start(bf16[4,32,1280]{2,1,0:T(8,128)(2,1)S(1)} %get-tuple-element.145), channel_id=1, source_target_pairs={{0,16},{8,24},{16,0},{24,8},{1,17},{9,25},{17,1},{25,9},{2,18},{10... | collective-permute-start | bytes 983048 | tf_op jit(solution)/shard_map/ppermute | solution.py:396
  149.7 7.7 %collective-permute-start.31 = (bf16[64,2560]{1,0:T(8,128)(2,1)S(1)}, bf16[64,2560]{1,0:T(8,128)(2,1)S(1)}, u32[]{:S(2)}, u32[]{:S(2)}) collective-permute-start(bf16[64,2560]{1,0:T(8,128)(2,1)S(1)} %get-tuple-element.147), channel_id=1, source_target_pairs={{0,2},{1,3},{2,0},{3,1},{4,6},{5,7},{6,4},{7,5},{8,10},{9,11},{10,... | collective-permute-start | bytes 983048 | tf_op jit(solution)/shard_map/ppermute | solution.py:393
  157.5 8.3 %collective-permute-start.32 = (bf16[32,2560]{1,0:T(8,128)(2,1)S(1)}, bf16[32,2560]{1,0:T(8,128)(2,1)S(1)}, u32[]{:S(2)}, u32[]{:S(2)}) collective-permute-start(bf16[32,2560]{1,0:T(8,128)(2,1)S(1)} %get-tuple-element.149), channel_id=1, source_target_pairs={{0,4},{1,5},{2,6},{3,7},{4,0},{5,1},{6,2},{7,3},{8,12},{9,13},{10,... | collective-permute-start | bytes 491528 | tf_op jit(solution)/shard_map/ppermute | solution.py:393
  159.7 10.2 %collective-permute-start.38 = (bf16[128,1024]{1,0:T(8,128)(2,1)S(1)}, bf16[128,1024]{1,0:T(8,128)(2,1)S(1)}, u32[]{:S(2)}, u32[]{:S(2)}) collective-permute-start(bf16[128,1024]{1,0:T(8,128)(2,1)S(1)} %multiply_convert_fusion.refs_0_), channel_id=1, source_target_pairs={{0,24},{8,16},{16,8},{24,0},{1,25},{9,17},{17,9},{25,1},{2,26},{10... | collective-permute-start | bytes 786440 | tf_op jit(solution)/shard_map/ppermute | solution.py:396
  161.6 13.3 %collective-permute-start.37 = (bf16[128,1024]{1,0:T(8,128)(2,1)S(1)}, bf16[128,1024]{1,0:T(8,128)(2,1)S(1)}, u32[]{:S(2)}, u32[]{:S(2)}) collective-permute-start(bf16[128,1024]{1,0:T(8,128)(2,1)S(1)} %multiply_convert_fusion.refs_0_), channel_id=1, source_target_pairs={{0,16},{8,24},{16,0},{24,8},{1,17},{9,25},{17,1},{25,9},{2,18},{10... | collective-permute-start | bytes 786440 | tf_op jit(solution)/shard_map/ppermute | solution.py:396
  162.2 13.3 %collective-permute-start.36 = (bf16[128,1024]{1,0:T(8,128)(2,1)S(1)}, bf16[128,1024]{1,0:T(8,128)(2,1)S(1)}, u32[]{:S(2)}, u32[]{:S(2)}) collective-permute-start(bf16[128,1024]{1,0:T(8,128)(2,1)S(1)} %multiply_convert_fusion.refs_0_), channel_id=1, source_target_pairs={{0,8},{8,0},{16,24},{24,16},{1,9},{9,1},{17,25},{25,17},{2,10},{10... | collective-permute-start | bytes 786440 | tf_op jit(solution)/shard_map/ppermute | solution.py:396
  165.8 11.9 %collective-permute-start.35 = (bf16[32,2560]{1,0:T(8,128)(2,1)S(1)}, bf16[32,2560]{1,0:T(8,128)(2,1)S(1)}, u32[]{:S(2)}, u32[]{:S(2)}) collective-permute-start(bf16[32,2560]{1,0:T(8,128)(2,1)S(1)} %add_convert_fusion.refs_0_), channel_id=1, source_target_pairs={{0,24},{8,16},{16,8},{24,0},{1,25},{9,17},{17,9},{25,1},{2,26},{10... | collective-permute-start | bytes 491528 | tf_op jit(solution)/shard_map/ppermute | solution.py:396
  167.8 11.6 %collective-permute-start.34 = (bf16[32,2560]{1,0:T(8,128)(2,1)S(1)}, bf16[32,2560]{1,0:T(8,128)(2,1)S(1)}, u32[]{:S(2)}, u32[]{:S(2)}) collective-permute-start(bf16[32,2560]{1,0:T(8,128)(2,1)S(1)} %add_convert_fusion.refs_0_), channel_id=1, source_target_pairs={{0,16},{8,24},{16,0},{24,8},{1,17},{9,25},{17,1},{25,9},{2,18},{10... | collective-permute-start | bytes 491528 | tf_op jit(solution)/shard_map/ppermute | solution.py:396
  169.9 9.6 %collective-permute-start.33 = (bf16[32,2560]{1,0:T(8,128)(2,1)S(1)}, bf16[32,2560]{1,0:T(8,128)(2,1)S(1)}, u32[]{:S(2)}, u32[]{:S(2)}) collective-permute-start(bf16[32,2560]{1,0:T(8,128)(2,1)S(1)} %add_convert_fusion.refs_0_), channel_id=1, source_target_pairs={{0,8},{8,0},{16,24},{24,16},{1,9},{9,1},{17,25},{25,17},{2,10},{10... | collective-permute-start | bytes 491528 | tf_op jit(solution)/shard_map/ppermute | solution.py:396
  (50 other events, 224.6 us)

commit v10 on v7

--- a/solution.py
+++ b/solution.py
@@ -151,9 +151,32 @@
     quarter_inv[...] = inverse
 
 
-def score_kernel(groups, owners, share, chunks, places, cand, inv_len, unit_hbm, yn_hbm, *refs):
+def backward(up, inverse, out_weight, proj, slope, attn, attn_slope, normed_ref, grad):
+    hidden = out_weight.shape[1]
+    normed = normed_ref[...]
+    grad_gated = dot(up, out_weight[...], NN)
+    grad[:, :hidden] = (grad_gated * normed * slope[:, :hidden].astype(f32)).astype(b16)
+    grad_normed = grad_gated * proj[:, :hidden].astype(f32)
+    grad_attended = inverse[...] * (
+        grad_normed
+        - jnp.mean(grad_normed, -1, keepdims=True)
+        - normed * jnp.mean(grad_normed * normed, -1, keepdims=True)
+    )
+    grad_attended = grad_attended.astype(b16)
+    for h in range(HEADS):
+        cv, cq, ck = [slice(i * hidden + h * HEAD_DIM, i * hidden + (h + 1) * HEAD_DIM) for i in (1, 2, 3)]
+        part = grad_attended[:, h * HEAD_DIM : (h + 1) * HEAD_DIM]
+        grad_attn = dot(part, proj[:, cv], NT)
+        grad_score = (grad_attn * attn_slope[h].astype(f32)).astype(b16)
+        grad[:, cv] = (dot(attn[h], part, TN) * slope[:, cv].astype(f32)).astype(b16)
+        grad[:, cq] = (dot(grad_score, proj[:, ck], NN) * slope[:, cq].astype(f32)).astype(b16)
+        grad[:, ck] = (dot(grad_score, proj[:, cq], TN) * slope[:, ck].astype(f32)).astype(b16)
+
+
+def score_kernel(groups, owners, share, chunks, places, cand, inv_len, inverse, unit_hbm, yn_hbm, *refs):
     count = len(places)
-    pieces, (tags, up, up_keep, up_give, table, spread, unit_b, unit, sems) = refs[:count], refs[count:]
+    pieces, saved_hbm, refs = refs[:count], refs[count : count + 6], refs[count + 6 :]
+    tags, up_keep, up_give, grad, table, spread, unit_b, unit, *saved, sems = refs
     chips = owners // 2
     vocab_dev = share * groups
     grp, core = lax.axis_index("grp"), lax.axis_index("seq") % 2
@@ -178,6 +201,11 @@
         copies.setdefault(tuple(key), []).append(copy)
     load_yn = pltpu.make_async_copy(yn_hbm, unit, sems.at[count + 1])
     load_yn.start()
+    load_saved = [
+        pltpu.make_async_copy(x, y, sems.at[count + 2 + n]) for n, (x, y) in enumerate(zip(saved_hbm, saved))
+    ]
+    for copy in load_saved:
+        copy.start()
     ids = owner_ids(owners)
     lane = iota((1, 128), 1)
     owner = jnp.full((1, 128), -1, i32)
@@ -241,32 +269,12 @@
     load_yn.wait()
     yn = unit[...]
     upstream = (pulled - yn * jnp.sum(yn * pulled, -1, keepdims=True)) * inv_len[...]
-    up[...] = upstream.astype(b16)
     mine, other = split_columns(upstream, owners, core)
     up_keep[...] = mine.astype(b16)
     up_give[...] = other.astype(b16)
-
-
-def backward_kernel(up, out_weight, proj, slope, attn, attn_slope, normed_ref, inverse, grad):
-    hidden = out_weight.shape[1]
-    normed = normed_ref[...]
-    grad_gated = dot(up[...], out_weight[...], NN)
-    grad[:, :hidden] = (grad_gated * normed * slope[:, :hidden].astype(f32)).astype(b16)
-    grad_normed = grad_gated * proj[:, :hidden].astype(f32)
-    grad_attended = inverse[...] * (
-        grad_normed
-        - jnp.mean(grad_normed, -1, keepdims=True)
-        - normed * jnp.mean(grad_normed * normed, -1, keepdims=True)
-    )
-    grad_attended = grad_attended.astype(b16)
-    for h in range(HEADS):
-        cv, cq, ck = [slice(i * hidden + h * HEAD_DIM, i * hidden + (h + 1) * HEAD_DIM) for i in (1, 2, 3)]
-        part = grad_attended[:, h * HEAD_DIM : (h + 1) * HEAD_DIM]
-        grad_attn = dot(part, proj[:, cv], NT)
-        grad_score = (grad_attn * attn_slope[h].astype(f32)).astype(b16)
-        grad[:, cv] = (dot(attn[h], part, TN) * slope[:, cv].astype(f32)).astype(b16)
-        grad[:, cq] = (dot(grad_score, proj[:, ck], NN) * slope[:, cq].astype(f32)).astype(b16)
-        grad[:, ck] = (dot(grad_score, proj[:, cq], TN) * slope[:, ck].astype(f32)).astype(b16)
+    for copy in load_saved:
+        copy.wait()
+    backward(upstream.astype(b16), inverse, *saved, grad)
 
 
 def item_kernel(groups, owners, share, chunks, places, *refs):
@@ -329,17 +337,24 @@
         one_right[z], two_left[z] = piece[1][:, half:], piece[2][:, :half]
 
 
+def corner_kernel(by_one, by_two, one_right, two_left, right_out, left_out):
+    right_out[...] = (one_right[...].astype(f32) + by_two[0].astype(f32)).astype(b16)
+    left_out[...] = (two_left[...].astype(f32) + by_one[0].astype(f32)).astype(b16)
+
+
 def sum_kernel(base, by_one, by_two, one_right, two_left, *outs):
-    chips = len(outs)
+    chips, fine, wide = base.shape
     chip = lax.axis_index("seq") // 2
-    half = base.shape[2] // 2
-    for d in range(chips):
-        z = lax.rem(chip + d, chips)
+    half = wide // 2
+    for n, d in enumerate(distances(chips)):
+        z = chip ^ d
         own = base[z].astype(f32)
         left = own[:, :half] + by_one[1, z].astype(f32) + two_left[z].astype(f32)
         right = own[:, half:] + by_two[1, z].astype(f32) + one_right[z].astype(f32)
-        outs[d][:, :half] = left.astype(b16)
-        outs[d][:, half:] = right.astype(b16)
+        out = outs[2 * n // chips]
+        at = slice(n % (chips // 2) * fine, (n % (chips // 2) + 1) * fine)
+        out[at, :half] = left.astype(b16)
+        out[at, half:] = right.astype(b16)
 
 
 def pair_kernel(x, y, *outs):
@@ -400,6 +415,17 @@
     def to_core(x):
         return lax.ppermute(x, "seq", [(a, a ^ 1) for a in range(owners)])
 
+    def fold(low, high):
+        bit = 1
+        while bit < chips // 2:
+            shape = (low.shape[0] // 2, low.shape[1])
+            low, high = call(pair_kernel, [(shape, b16)] * 2, [VMEM] * 2, [low, across(high, bit)], room=8)
+            bit *= 2
+        return low, high
+
+    def finish(low, high):
+        return low.astype(f32) + across(high, chips // 2).astype(f32)
+
     def gather_groups(x, near=None):
         wide = x.shape[1]
         if groups != 4:
@@ -420,6 +446,7 @@
         have.update({x ^ bit: across(have[x], bit) for x in have})
         bit //= 2
     got = [have[x] for x in distances(chips)[1:]]
+    candidates = jnp.concatenate([history[:, None], negatives], 1)
     outs = [
         ((tok, width // 2), b16), ((tok, width // 2), b16), ((tok, 4 * hidden), b16), ((tok, 4 * hidden), b16),
         ((HEADS, tok, tok), b16), ((HEADS, tok, tok), b16), ((tok, hidden), f32), ((tok, 1), f32),
@@ -452,31 +479,38 @@
         room=63,
     )
 
-    candidates = jnp.concatenate([history[:, None], negatives], 1)
     vocab = vocab_dev * owners
     far_give, far_gated = to_core(give), to_core(gated)
     units = [p[3] for p in unit_sent]
     layer_out, score_unit, far_give, far_gated, units = lax.optimization_barrier(
         (layer_out, unit, far_give, far_gated, units)
     )
-    tags, up, up_keep, up_give = call(
+    saved = [out_weight, proj, slope, attn, attn_slope, normed]
+    tags, up_keep, up_give, grad = call(
         lambda *refs: score_kernel(groups, owners, share, chunks, [p[:5] for p in pieces], *refs),
-        [((2 * owners, tok), f32), ((tok, width), b16), ((tok, width // 2), b16), ((tok, width // 2), b16)],
-        [VMEM] * 2 + [ANY] * (len(pieces) + 2), [candidates, inv_len, unit_b, score_unit] + [p[5] for p in pieces],
+        [((2 * owners, tok), f32), ((tok, width // 2), b16), ((tok, width // 2), b16), ((tok, 4 * hidden), b16)],
+        [VMEM] * 3 + [ANY] * (len(pieces) + 8),
+        [candidates, inv_len, inverse, unit_b, score_unit] + [p[5] for p in pieces] + saved,
         [pltpu.VMEM((vocab, width), b16), pltpu.VMEM((tok, vocab), b16), pltpu.VMEM((tok, width), b16),
-         pltpu.VMEM((tok, width), f32), pltpu.SemaphoreType.DMA((len(pieces) + 2,))],
+         pltpu.VMEM((tok, width), f32)] + [pltpu.VMEM(x.shape, x.dtype) for x in saved]
+        + [pltpu.SemaphoreType.DMA((len(pieces) + 8,))],
         room=63,
-    )
-
-    grad, = call(
-        backward_kernel, [((tok, 4 * hidden), b16)], [VMEM] * 8,
-        [up, out_weight, proj, slope, attn, attn_slope, normed, inverse], room=60,
     )
 
     all_tags = [to_group(tags, k) if k else tags for k in range(groups)]
     far = [far_give, to_core(up_give), None, far_gated]
     grad, far[1], all_tags = lax.optimization_barrier((grad, far[1], all_tags))
     far[2] = to_core(grad)
+    mine, other = call(
+        lambda *refs: item_kernel(groups, owners, share, chunks, [p[:3] for p in unit_sent], *refs),
+        [((chips * share, width), b16)] * 2, [ANY] * len(units) + [VMEM] * groups + [ANY] * len(near),
+        units + all_tags + near,
+        [pltpu.VMEM((groups * tok, width), b16), pltpu.VMEM((2 * chips * share, width), b16),
+         pltpu.SemaphoreType.DMA((len(units) + 2 * chips,))],
+        room=63,
+    )
+    far_mine = to_core(other)
+    far, mine = lax.optimization_barrier((far, mine))
     half = 5 * hidden // 2
     if groups == 4:
         block = (chips, fine, 5 * hidden)
@@ -488,11 +522,8 @@
             [pltpu.VMEM((width // 2, 5 * hidden), b16)],
             flops=2 * tok * width * 5 * hidden, nbytes=20 * tok * width, room=60,
         )
-        after = parts[0]
         by_one, by_two = to_group(parts[1], 1), to_group(parts[2], 2)
-        one_right = (parts[3].astype(f32) + by_two[0].astype(f32)).astype(b16)
-        two_left = (parts[4].astype(f32) + by_one[0].astype(f32)).astype(b16)
-        arrived = [by_one, by_two, to_group(one_right, 1), to_group(two_left, 2)]
+        corner = (by_one, by_two)
     else:
         def both(x, y):
             return jnp.concatenate([x, y], 0)
@@ -501,31 +532,23 @@
         out_part = dot(both(up_keep, far[1]), both(gated, far[3]), TN)
         weight = jnp.concatenate([in_part, out_part], 1).astype(b16)
         weight = weight.reshape(chips, groups, fine, 5 * hidden)
-        after = weight
         sums = lax.dynamic_index_in_dim(weight, grp, 1, False).astype(f32)
         for k in range(1, groups):
             sums += to_group(lax.dynamic_index_in_dim(weight, grp ^ k, 1, False), k).astype(f32)
 
 
-    units[0], _ = lax.optimization_barrier((units[0], after))
-    mine, other = call(
-        lambda *refs: item_kernel(groups, owners, share, chunks, [p[:3] for p in unit_sent], *refs),
-        [((chips * share, width), b16)] * 2, [ANY] * len(units) + [VMEM] * groups + [ANY] * len(near),
-        units + all_tags + near,
-        [pltpu.VMEM((groups * tok, width), b16), pltpu.VMEM((2 * chips * share, width), b16),
-         pltpu.SemaphoreType.DMA((len(units) + 2 * chips,))],
-        flops=4 * groups * tok * width * chips * share, nbytes=4 * tok * groups * width, room=60,
-    )
-    far_mine = to_core(other)
-
-    summed = call(
-        pair_kernel, [((share, width), b16)] * chips, [VMEM] * 2, [mine, far_mine],
+    low, high = call(
+        pair_kernel, [((chips // 2 * share, width), b16)] * 2, [VMEM] * 2, [mine, far_mine],
         flops=chips * share * width, nbytes=6 * chips * share * width, room=8,
     )
-    come = [across(summed[n], d) for n, d in enumerate(distances(chips)) if d]
-    total = summed[0].astype(f32)
-    for x in come:
-        total += x.astype(f32)
+    low, high = fold(low, high)
+    if groups == 4:
+        by_one, by_two, low, high = lax.optimization_barrier(corner + (low, high))
+        one_right, two_left = call(
+            corner_kernel, [(split, b16)] * 2, [VMEM] * 4, [by_one, by_two, parts[3], parts[4]], room=8,
+        )
+        arrived = [by_one, by_two, to_group(one_right, 1), to_group(two_left, 2)]
+    total = finish(low, high)
     total = (total * quarter_inv).astype(b16)
     table_grad, = call(
         lambda *refs: assemble_kernel(groups, [width], *refs), [((vocab_dev, width), f32)], [VMEM] * groups,
@@ -534,18 +557,17 @@
     )
 
     if groups == 4:
-        base = parts[0]
-        sums = call(
-            sum_kernel, [((fine, 5 * hidden), b16)] * chips, [VMEM] * 5, [base] + arrived,
+        base, _ = lax.optimization_barrier((parts[0], total))
+        low, high = call(
+            sum_kernel, [((chips // 2 * fine, 5 * hidden), b16)] * 2, [VMEM] * 5, [base] + arrived,
             flops=chips * fine * 5 * hidden, nbytes=40 * chips * fine * hidden, room=10,
         )
+        line = finish(*fold(low, high))
     else:
-        sums = [
-            lax.dynamic_index_in_dim(sums, (chip + d) % chips, 0, False).astype(b16) for d in range(chips)
-        ]
-    line = sums[0].astype(f32)
-    for d in range(1, chips):
-        line += to_chip(sums[d], d).astype(f32)
+        blocks = [lax.dynamic_index_in_dim(sums, (chip + d) % chips, 0, False).astype(b16) for d in range(chips)]
+        line = blocks[0].astype(f32)
+        for d in range(1, chips):
+            line += to_chip(blocks[d], d).astype(f32)
     line = line.astype(b16)
     lines = [to_group(line, k) if k else line for k in range(groups)]
     if fine % 16 == 0:

time: 191 us -> 173 us (0.906)
  the two profiles are of different devices: /device:TPU:9 before, /device:TPU:0 now
where the time goes in v10:
time: 173 us; the launch traced here: 172 us
  waiting for transfers between devices  73.7 us (43%)
  starting transfers between devices  44.7 us (26%)
  Pallas kernels  43 us (25%)
  local copies, waits for them, and re-layouts  8.77 us (5%)
    pallas_call x13, Pallas kernels, call(): pl.pallas_call(kernel, out_shape=[jax.ShapeDtypeStruct(s, t) for s, t in...  43 us
    ppermute x7, waiting for transfers between devices, across(): return lax.ppermute(x, 'seq', pairs)  40.9 us
    ppermute x21, waiting for transfers between devices, to_group(): return lax.ppermute(x, 'grp', [(a, a ^ k) for a in range(groups)])  31.5 us
    ppermute x21, starting transfers between devices, to_group(): return lax.ppermute(x, 'grp', [(a, a ^ k) for a in range(groups)])  24.5 us
    ppermute x7, starting transfers between devices, across(): return lax.ppermute(x, 'seq', pairs)  13.6 us
    unnamed x40, local copies, waits for them, and re-layouts  5.87 us
    all_to_all x1, starting transfers between devices, body(): lax.all_to_all(outgoing.reshape(owners, slot, width), 'seq', 0, 0, tiled=...  4.88 us
  transfers between devices with their start and end apart: 40, of which 20 were waited for; matrix products, arithmetic and copies ran while one was open for 2% of the time, Pallas kernels for 16%

profile of v10, /device:TPU:0, one launch (start us, length us, event | category | flops | bytes accessed | tf_op | source)
XLA Modules:
  0.0 172.3 jit_solution(16764004847871580750)
XLA Ops:
  3.2 4.0 %collective-permute-start = (bf16[128,1024]{1,0:T(8,128)(2,1)S(1)}, bf16[128,1024]{1,0:T(8,128)(2,1)}, u32[]{:S(2)}, u32[]{:S(2)}) collective-permute-start(bf16[128,1024]{1,0:T(8,128)(2,1)S(1)} %get-tuple-element.76), channel_id=1, source_target_pairs={{0,4},{1,5},{2,6},{3,7},{4,0},{5,1},{6,2},{7,3},{8,12},{9,13},{10,... | collective-permute-start | bytes 786440 | tf_op jit(solution)/shard_map/ppermute | solution.py:410
  7.3 9.1 %shard_map.111 = (bf16[256,512]{1,0:T(8,128)(2,1)}, bf16[256,512]{1,0:T(8,128)(2,1)}, bf16[256,2048]{1,0:T(8,128)(2,1)}, bf16[256,2048]{1,0:T(8,128)(2,1)}, bf16...) custom-call(s32[1,8]{1,0:T(1,128)} %refs_0_.2, ...), custom_call_target="tpu_custom_call" | custom-call | tf_op jit(solution)/shard_map/pallas_call | solution.py:53
  16.4 1.6 collective-permute-start.4
  18.0 1.5 collective-permute-start.3
  19.4 1.6 collective-permute-start.1
  21.5 7.2 %collective-permute-done.1 = bf16[128,1024]{1,0:T(8,128)(2,1)S(1)} collective-permute-done((bf16[128,1024]{1,0:T(8,128)(2,1)S(1)}, bf16[128,1024]{1,0:T(8,128)(2,1)S(1)}, u32[]{:S(2)}, u32[]{:S(2)}) %collective-permute-start.1) | collective-permute-done | bytes 262176 | tf_op jit(solution)/shard_map/ppermute | solution.py:410
  28.7 3.6 %collective-permute-done.2 = bf16[128,1024]{1,0:T(8,128)(2,1)S(1)} collective-permute-done((bf16[128,1024]{1,0:T(8,128)(2,1)}, bf16[128,1024]{1,0:T(8,128)(2,1)S(1)}, u32[]{:S(2)}, u32[]{:S(2)}) %collective-permute-start.2) | collective-permute-done | bytes 262176 | tf_op jit(solution)/shard_map/ppermute | solution.py:410
  34.8 4.9 %all-to-all-start = ((bf16[8,48,1024]{2,1,0:T(8,128)(2,1)}), bf16[8,48,1024]{2,1,0:T(8,128)(2,1)}, u32[]{:S(2)}, u32[]{:S(2)}) async-start(bf16[8,48,1024]{2,1,0:T(8,128)(2,1)} %bitcast.3), calls=%async_computation | async-start | bytes 1572864 | tf_op jit(solution)/shard_map/all_to_all | solution.py:474
  42.4 8.8 %collective-permute-done.10.refs_8_ = bf16[384,1024]{1,0:T(8,128)(2,1)} collective-permute-done((bf16[384,1024]{1,0:T(8,128)(2,1)S(1)}, bf16[384,1024]{1,0:T(8,128)(2,1)}, u32[]{:S(2)}, u32[]{:S(2)}) %collective-permute-start.10) | collective-permute-done | bytes 786464 | tf_op jit(solution)/shard_map/ppermute | solution.py:413
  51.2 3.0 %collective-permute-done.9.refs_7_ = bf16[384,1024]{1,0:T(8,128)(2,1)} collective-permute-done((bf16[384,1024]{1,0:T(8,128)(2,1)S(1)}, bf16[384,1024]{1,0:T(8,128)(2,1)}, u32[]{:S(2)}, u32[]{:S(2)}) %collective-permute-start.9) | collective-permute-done | bytes 786464 | tf_op jit(solution)/shard_map/ppermute | solution.py:413
  54.2 1.5 collective-permute-start.7
  59.3 4.0 %collective-permute-done.7.refs_3_ = bf16[256,512]{1,0:T(8,128)(2,1)S(1)} collective-permute-done((bf16[256,512]{1,0:T(8,128)(2,1)S(1)}, bf16[256,512]{1,0:T(8,128)(2,1)S(1)}, u32[]{:S(2)}, u32[]{:S(2)}) %collective-permute-start.7) | collective-permute-done | bytes 262176 | tf_op jit(solution)/shard_map/ppermute | solution.py:413
  65.8 2.9 %collective-permute-done.11.refs_9_ = bf16[384,512]{1,0:T(8,128)(2,1)} collective-permute-done((bf16[384,512]{1,0:T(8,128)(2,1)S(1)}, bf16[384,512]{1,0:T(8,128)(2,1)}, u32[]{:S(2)}, u32[]{:S(2)}) %collective-permute-start.11) | collective-permute-done | bytes 393248 | tf_op jit(solution)/shard_map/ppermute | solution.py:413
  69.5 2.7 %shard_map.113 = bf16[256,1024]{1,0:T(8,128)(2,1)} custom-call(bf16[384,1024]{1,0:T(8,128)(2,1)} %bitcast.1.arrived), custom_call_target="tpu_custom_call" | custom-call | tf_op jit(solution)/shard_map/pallas_call | solution.py:53
  72.3 12.9 %shard_map.114 = (f32[16,256]{1,0:T(8,128)}, bf16[256,512]{1,0:T(8,128)(2,1)}, bf16[256,512]{1,0:T(8,128)(2,1)}, bf16[256,2048]{1,0:T(8,128)(2,1)}) custom-call(s32[256,4]{1,0:T(8,128)} %copy.15.refs_0_, f32[256,1]{1,0:T(8,128)} %get-tuple-element.91.refs_1_, f32[256,1]{1,0:T(8,128)} %get-tuple-element.92.refs_2_, ...), custom_call_target="tpu_custom_call" | custom-call | tf_op jit(solution)/shard_map/pallas_call | solution.py:53
  85.8 2.1 %collective-permute-start.22 = (f32[16,256]{1,0:T(8,128)}, f32[16,256]{1,0:T(8,128)S(1)}, u32[]{:S(2)}, u32[]{:S(2)}) collective-permute-start(f32[16,256]{1,0:T(8,128)} %get-tuple-element.111.refs_5_), channel_id=1, source_target_pairs={{0,24},{8,16},{16,8},{24,0},{1,25},{9,17},{17,9},{25,1},{2,26},{10... | collective-permute-start | bytes 49160 | tf_op jit(solution)/shard_map/ppermute | solution.py:413
  89.3 1.5 collective-permute-done.22.refs_8_
  92.9 6.9 %shard_map.115 = (bf16[512,1024]{1,0:T(8,128)(2,1)}, bf16[512,1024]{1,0:T(8,128)(2,1)}) custom-call(bf16[256,1024]{1,0:T(8,128)(2,1)} %get-tuple-element.106.refs_3_.refs_0_, bf16[256,1024]{1,0:T(8,128)(2,1)} %copy-done.8, bf16[256,1024]{1,0:T(8,128)(2,1)} %copy-done.7, bf16[256,512]{1,0:T(8,128)(2,1)} %copy-done.10, bf16[256,512]{1,0:T(8,128)(2,1)} %copy-done.9, ...), custom_call_target="tpu_custom_call" | custom-call | tf_op jit(solution)/shard_map/pallas_call | solution.py:53
  100.0 5.2 %shard_map.116 = (bf16[4,32,2560]{2,1,0:T(8,128)(2,1)}, bf16[2,4,32,1280]{3,2,1,0:T(8,128)(2,1)}, bf16[2,4,32,1280]{3,2,1,0:T(8,128)(2,1)}, bf16[4,32,1280]{2,1,0:T(8,128)(2,1)}, bf16[4,32,1280]{2,1,0:T(8,128)(2,1)}) custom-call(bf16[256,512]{1,0:T(8,128)(2,1)} %get-tuple-element.89.refs_0_, bf16[256,512]{1,0:T(8,128)(2,1)} %copy-done.16, ...), custom_call_target="tpu_custom_call" | custom-call | flops 1342177280 | bytes 5242880 | tf_op jit(solution)/shard_map/pallas_call | solution.py:53
  107.6 1.6 collective-permute-start.27
  109.3 12.1 %collective-permute-done.27.y = bf16[256,1024]{1,0:T(8,128)(2,1)S(1)} collective-permute-done((bf16[256,1024]{1,0:T(8,128)(2,1)S(1)}, bf16[256,1024]{1,0:T(8,128)(2,1)S(1)}, u32[]{:S(2)}, u32[]{:S(2)}) %collective-permute-start.27) | collective-permute-done | bytes 524320 | tf_op jit(solution)/shard_map/ppermute | solution.py:410
  123.1 1.8 %collective-permute-start.28 = (bf16[128,1024]{1,0:T(8,128)(2,1)}, bf16[128,1024]{1,0:T(8,128)(2,1)}, u32[]{:S(2)}, u32[]{:S(2)}) collective-permute-start(bf16[128,1024]{1,0:T(8,128)(2,1)} %get-tuple-element.131), channel_id=1, source_target_pairs={{0,4},{1,5},{2,6},{3,7},{4,0},{5,1},{6,2},{7,3},{8,12},{9,13},{10,... | collective-permute-start | bytes 786440 | tf_op jit(solution)/shard_map/ppermute | solution.py:410
  127.6 1.5 collective-permute-start.29
  130.5 6.9 %collective-permute-done.28 = bf16[128,1024]{1,0:T(8,128)(2,1)} collective-permute-done((bf16[128,1024]{1,0:T(8,128)(2,1)}, bf16[128,1024]{1,0:T(8,128)(2,1)}, u32[]{:S(2)}, u32[]{:S(2)}) %collective-permute-start.28) | collective-permute-done | bytes 262176 | tf_op jit(solution)/shard_map/ppermute | solution.py:410
  140.1 7.2 %collective-permute-done.31.y = bf16[64,2560]{1,0:T(8,128)(2,1)S(1)} collective-permute-done((bf16[64,2560]{1,0:T(8,128)(2,1)S(1)}, bf16[64,2560]{1,0:T(8,128)(2,1)S(1)}, u32[]{:S(2)}, u32[]{:S(2)}) %collective-permute-start.31) | collective-permute-done | bytes 327712 | tf_op jit(solution)/shard_map/ppermute | solution.py:410
  147.4 2.7 %collective-permute-start.32 = (bf16[32,2560]{1,0:T(8,128)(2,1)S(1)}, bf16[32,2560]{1,0:T(8,128)(2,1)S(1)}, u32[]{:S(2)}, u32[]{:S(2)}) collective-permute-start(bf16[32,2560]{1,0:T(8,128)(2,1)S(1)} %get-tuple-element.143), channel_id=1, source_target_pairs={{0,4},{1,5},{2,6},{3,7},{4,0},{5,1},{6,2},{7,3},{8,12},{9,13},{10,... | collective-permute-start | bytes 491528 | tf_op jit(solution)/shard_map/ppermute | solution.py:410
  150.2 2.2 %collective-permute-start.38 = (bf16[128,1024]{1,0:T(8,128)(2,1)S(1)}, bf16[128,1024]{1,0:T(8,128)(2,1)S(1)}, u32[]{:S(2)}, u32[]{:S(2)}) collective-permute-start(bf16[128,1024]{1,0:T(8,128)(2,1)S(1)} %multiply_convert_fusion.refs_0_), channel_id=1, source_target_pairs={{0,24},{8,16},{16,8},{24,0},{1,25},{9,17},{17,9},{25,1},{2,26},{10... | collective-permute-start | bytes 786440 | tf_op jit(solution)/shard_map/ppermute | solution.py:413
  153.7 3.9 %collective-permute-done.32 = bf16[32,2560]{1,0:T(8,128)(2,1)S(1)} collective-permute-done((bf16[32,2560]{1,0:T(8,128)(2,1)S(1)}, bf16[32,2560]{1,0:T(8,128)(2,1)S(1)}, u32[]{:S(2)}, u32[]{:S(2)}) %collective-permute-start.32) | collective-permute-done | bytes 163872 | tf_op jit(solution)/shard_map/ppermute | solution.py:410
  157.6 2.3 %collective-permute-start.35 = (bf16[32,2560]{1,0:T(8,128)(2,1)S(1)}, bf16[32,2560]{1,0:T(8,128)(2,1)S(1)}, u32[]{:S(2)}, u32[]{:S(2)}) collective-permute-start(bf16[32,2560]{1,0:T(8,128)(2,1)S(1)} %add_convert_fusion.refs_0_), channel_id=1, source_target_pairs={{0,24},{8,16},{16,8},{24,0},{1,25},{9,17},{17,9},{25,1},{2,26},{10... | collective-permute-start | bytes 491528 | tf_op jit(solution)/shard_map/ppermute | solution.py:413
  161.8 4.2 %collective-permute-done.37.refs_2_ = bf16[128,1024]{1,0:T(8,128)(2,1)S(1)} collective-permute-done((bf16[128,1024]{1,0:T(8,128)(2,1)S(1)}, bf16[128,1024]{1,0:T(8,128)(2,1)S(1)}, u32[]{:S(2)}, u32[]{:S(2)}) %collective-permute-start.37) | collective-permute-done | bytes 262176 | tf_op jit(solution)/shard_map/ppermute | solution.py:413
  167.4 2.1 %collective-permute-done.35.refs_3_ = bf16[32,2560]{1,0:T(8,128)(2,1)S(1)} collective-permute-done((bf16[32,2560]{1,0:T(8,128)(2,1)S(1)}, bf16[32,2560]{1,0:T(8,128)(2,1)S(1)}, u32[]{:S(2)}, u32[]{:S(2)}) %collective-permute-start.35) | collective-permute-done | bytes 163872 | tf_op jit(solution)/shard_map/ppermute | solution.py:413
  169.5 1.6 collective-permute-done.34.refs_2_
  (111 shorter events, 36.2 us)
Async XLA Ops:
  3.2 17.8 %collective-permute-start = (bf16[128,1024]{1,0:T(8,128)(2,1)S(1)}, bf16[128,1024]{1,0:T(8,128)(2,1)}, u32[]{:S(2)}, u32[]{:S(2)}) collective-permute-start(bf16[128,1024]{1,0:T(8,128)(2,1)S(1)} %get-tuple-element.76), channel_id=1, source_target_pairs={{0,4},{1,5},{2,6},{3,7},{4,0},{5,1},{6,2},{7,3},{8,12},{9,13},{10,... | collective-permute-start | bytes 786440 | tf_op jit(solution)/shard_map/ppermute | solution.py:410
  16.4 15.9 %collective-permute-start.4 = (bf16[256,1024]{1,0:T(8,128)(2,1)}, bf16[256,1024]{1,0:T(8,128)(2,1)S(1)}, u32[]{:S(2)}, u32[]{:S(2)}) collective-permute-start(bf16[256,1024]{1,0:T(8,128)(2,1)} %get-tuple-element.106.refs_3_.refs_0_), channel_id=1, source_target_pairs={{0,16},{8,24},{16,0},{24,8},{1,17},{9,25},{17,1},{25,9},{2,18},{10... | collective-permute-start | bytes 1572872 | tf_op jit(solution)/shard_map/ppermute | solution.py:413
  18.0 14.3 %collective-permute-start.3 = (bf16[256,1024]{1,0:T(8,128)(2,1)}, bf16[256,1024]{1,0:T(8,128)(2,1)S(1)}, u32[]{:S(2)}, u32[]{:S(2)}) collective-permute-start(bf16[256,1024]{1,0:T(8,128)(2,1)} %get-tuple-element.106.refs_3_.refs_0_), channel_id=1, source_target_pairs={{0,8},{8,0},{16,24},{24,16},{1,9},{9,1},{17,25},{25,17},{2,10},{10... | collective-permute-start | bytes 1572872 | tf_op jit(solution)/shard_map/ppermute | solution.py:413
  19.4 9.2 %collective-permute-start.1 = (bf16[128,1024]{1,0:T(8,128)(2,1)S(1)}, bf16[128,1024]{1,0:T(8,128)(2,1)S(1)}, u32[]{:S(2)}, u32[]{:S(2)}) collective-permute-start(bf16[128,1024]{1,0:T(8,128)(2,1)S(1)} %get-tuple-element.76), channel_id=1, source_target_pairs={{0,2},{1,3},{2,0},{3,1},{4,6},{5,7},{6,4},{7,5},{8,10},{9,11},{10,... | collective-permute-start | bytes 786440 | tf_op jit(solution)/shard_map/ppermute | solution.py:410
  21.0 11.2 %collective-permute-start.2 = (bf16[128,1024]{1,0:T(8,128)(2,1)}, bf16[128,1024]{1,0:T(8,128)(2,1)S(1)}, u32[]{:S(2)}, u32[]{:S(2)}) collective-permute-start(bf16[128,1024]{1,0:T(8,128)(2,1)} %collective-permute-done), channel_id=1, source_target_pairs={{0,2},{1,3},{2,0},{3,1},{4,6},{5,7},{6,4},{7,5},{8,10},{9,11},{10,... | collective-permute-start | bytes 786440 | tf_op jit(solution)/shard_map/ppermute | solution.py:410
  33.5 17.7 %collective-permute-start.10 = (bf16[384,1024]{1,0:T(8,128)(2,1)S(1)}, bf16[384,1024]{1,0:T(8,128)(2,1)}, u32[]{:S(2)}, u32[]{:S(2)}) collective-permute-start(bf16[384,1024]{1,0:T(8,128)(2,1)S(1)} %constant_dynamic-update-slice_fusion.refs_6_.refs_10_), channel_id=1, source_target_pairs={{0,16},{8,24},{16,0},{24,8},{1,17},{9,25},{17,1},{25,9},{2,18},{10... | collective-permute-start | bytes 2359304 | tf_op jit(solution)/shard_map/ppermute | solution.py:413
  34.1 20.1 %collective-permute-start.9 = (bf16[384,1024]{1,0:T(8,128)(2,1)S(1)}, bf16[384,1024]{1,0:T(8,128)(2,1)}, u32[]{:S(2)}, u32[]{:S(2)}) collective-permute-start(bf16[384,1024]{1,0:T(8,128)(2,1)S(1)} %constant_dynamic-update-slice_fusion.refs_6_.refs_10_), channel_id=1, source_target_pairs={{0,8},{8,0},{16,24},{24,16},{1,9},{9,1},{17,25},{25,17},{2,10},{10... | collective-permute-start | bytes 2359304 | tf_op jit(solution)/shard_map/ppermute | solution.py:413
  34.8 28.5 %collective-permute-start.14 = (bf16[384,1024]{1,0:T(8,128)(2,1)S(1)}, bf16[384,1024]{1,0:T(8,128)(2,1)S(1)}, u32[]{:S(2)}, u32[]{:S(2)}) collective-permute-start(bf16[384,1024]{1,0:T(8,128)(2,1)S(1)} %constant_dynamic-update-slice_fusion.refs_6_.refs_10_), channel_id=1, source_target_pairs={{0,1},{1,0},{2,3},{3,2},{4,5},{5,4},{6,7},{7,6},{8,9},{9,8},{10,11... | collective-permute-start | bytes 2359304 | tf_op jit(solution)/shard_map/ppermute | solution.py:416
  34.8 34.7 %all-to-all-start = ((bf16[8,48,1024]{2,1,0:T(8,128)(2,1)}), bf16[8,48,1024]{2,1,0:T(8,128)(2,1)}, u32[]{:S(2)}, u32[]{:S(2)}) async-start(bf16[8,48,1024]{2,1,0:T(8,128)(2,1)} %bitcast.3), calls=%async_computation | async-start | bytes 1572864 | tf_op jit(solution)/shard_map/all_to_all | solution.py:474
  40.2 17.6 %collective-permute-start.6 = (bf16[256,512]{1,0:T(8,128)(2,1)}, bf16[256,512]{1,0:T(8,128)(2,1)S(1)}, u32[]{:S(2)}, u32[]{:S(2)}) collective-permute-start(bf16[256,512]{1,0:T(8,128)(2,1)} %get-tuple-element.85.refs_6_), channel_id=1, source_target_pairs={{0,1},{1,0},{2,3},{3,2},{4,5},{5,4},{6,7},{7,6},{8,9},{9,8},{10,11... | collective-permute-start | bytes 786440 | tf_op jit(solution)/shard_map/ppermute | solution.py:416
  41.6 17.0 %collective-permute-start.8 = (bf16[256,512]{1,0:T(8,128)(2,1)S(1)}, bf16[256,512]{1,0:T(8,128)(2,1)S(1)}, u32[]{:S(2)}, u32[]{:S(2)}) collective-permute-start(bf16[256,512]{1,0:T(8,128)(2,1)S(1)} %slice.13), channel_id=1, source_target_pairs={{0,8},{8,0},{16,24},{24,16},{1,9},{9,1},{17,25},{25,17},{2,10},{10... | collective-permute-start | bytes 786440 | tf_op jit(solution)/shard_map/ppermute | solution.py:413
  51.2 21.0 %collective-permute-start.13 = (bf16[512,1024]{1,0:T(8,128)(2,1)}, bf16[512,1024]{1,0:T(8,128)(2,1)}, u32[]{:S(2)}, u32[]{:S(2)}) collective-permute-start(bf16[512,1024]{1,0:T(8,128)(2,1)} %get-tuple-element.94.refs_5_.refs_9_), channel_id=1, source_target_pairs={{0,1},{1,0},{2,3},{3,2},{4,5},{5,4},{6,7},{7,6},{8,9},{9,8},{10,11... | collective-permute-start | bytes 3145736 | tf_op jit(solution)/shard_map/ppermute | solution.py:416
  54.2 9.1 %collective-permute-start.7 = (bf16[256,512]{1,0:T(8,128)(2,1)S(1)}, bf16[256,512]{1,0:T(8,128)(2,1)S(1)}, u32[]{:S(2)}, u32[]{:S(2)}) collective-permute-start(bf16[256,512]{1,0:T(8,128)(2,1)S(1)} %slice.12), channel_id=1, source_target_pairs={{0,16},{8,24},{16,0},{24,8},{1,17},{9,25},{17,1},{25,9},{2,18},{10... | collective-permute-start | bytes 786440 | tf_op jit(solution)/shard_map/ppermute | solution.py:413
  57.8 7.9 %collective-permute-start.12 = (bf16[384,512]{1,0:T(8,128)(2,1)S(1)}, bf16[384,512]{1,0:T(8,128)(2,1)}, u32[]{:S(2)}, u32[]{:S(2)}) collective-permute-start(bf16[384,512]{1,0:T(8,128)(2,1)S(1)} %slice.17), channel_id=1, source_target_pairs={{0,8},{8,0},{16,24},{24,16},{1,9},{9,1},{17,25},{25,17},{2,10},{10... | collective-permute-start | bytes 1179656 | tf_op jit(solution)/shard_map/ppermute | solution.py:413
  58.6 10.0 %collective-permute-start.11 = (bf16[384,512]{1,0:T(8,128)(2,1)S(1)}, bf16[384,512]{1,0:T(8,128)(2,1)}, u32[]{:S(2)}, u32[]{:S(2)}) collective-permute-start(bf16[384,512]{1,0:T(8,128)(2,1)S(1)} %slice.16), channel_id=1, source_target_pairs={{0,16},{8,24},{16,0},{24,8},{1,17},{9,25},{17,1},{25,9},{2,18},{10... | collective-permute-start | bytes 1179656 | tf_op jit(solution)/shard_map/ppermute | solution.py:413
  63.3 8.9 %collective-permute-start.16 = (bf16[384,1024]{1,0:T(8,128)(2,1)}, bf16[384,1024]{1,0:T(8,128)(2,1)}, u32[]{:S(2)}, u32[]{:S(2)}) collective-permute-start(bf16[384,1024]{1,0:T(8,128)(2,1)} %collective-permute-done.10.refs_8_), channel_id=1, source_target_pairs={{0,1},{1,0},{2,3},{3,2},{4,5},{5,4},{6,7},{7,6},{8,9},{9,8},{10,11... | collective-permute-start | bytes 2359304 | tf_op jit(solution)/shard_map/ppermute | solution.py:416
  64.3 7.9 %collective-permute-start.15 = (bf16[384,1024]{1,0:T(8,128)(2,1)}, bf16[384,1024]{1,0:T(8,128)(2,1)}, u32[]{:S(2)}, u32[]{:S(2)}) collective-permute-start(bf16[384,1024]{1,0:T(8,128)(2,1)} %collective-permute-done.9.refs_7_), channel_id=1, source_target_pairs={{0,1},{1,0},{2,3},{3,2},{4,5},{5,4},{6,7},{7,6},{8,9},{9,8},{10,11... | collective-permute-start | bytes 2359304 | tf_op jit(solution)/shard_map/ppermute | solution.py:416
  92.3 7.7 %collective-permute-start.23 = (bf16[256,2048]{1,0:T(8,128)(2,1)}, bf16[256,2048]{1,0:T(8,128)(2,1)}, u32[]{:S(2)}, u32[]{:S(2)}) collective-permute-start(bf16[256,2048]{1,0:T(8,128)(2,1)} %get-tuple-element.104.refs_4_), channel_id=1, source_target_pairs={{0,1},{1,0},{2,3},{3,2},{4,5},{5,4},{6,7},{7,6},{8,9},{9,8},{10,11... | collective-permute-start | bytes 3145736 | tf_op jit(solution)/shard_map/ppermute | solution.py:416
  105.1 17.3 %collective-permute-start.24 = (bf16[2,4,32,1280]{3,2,1,0:T(8,128)(2,1)}, bf16[2,4,32,1280]{3,2,1,0:T(8,128)(2,1)S(1)}, u32[]{:S(2)}, u32[]{:S(2)}) collective-permute-start(bf16[2,4,32,1280]{3,2,1,0:T(8,128)(2,1)} %get-tuple-element.122), channel_id=1, source_target_pairs={{0,8},{8,0},{16,24},{24,16},{1,9},{9,1},{17,25},{25,17},{2,10},{10... | collective-permute-start | bytes 1966088 | tf_op jit(solution)/shard_map/ppermute | solution.py:413
  106.1 17.0 %collective-permute-start.25 = (bf16[2,4,32,1280]{3,2,1,0:T(8,128)(2,1)}, bf16[2,4,32,1280]{3,2,1,0:T(8,128)(2,1)S(1)}, u32[]{:S(2)}, u32[]{:S(2)}) collective-permute-start(bf16[2,4,32,1280]{3,2,1,0:T(8,128)(2,1)} %get-tuple-element.123), channel_id=1, source_target_pairs={{0,16},{8,24},{16,0},{24,8},{1,17},{9,25},{17,1},{25,9},{2,18},{10... | collective-permute-start | bytes 1966088 | tf_op jit(solution)/shard_map/ppermute | solution.py:413
  107.6 13.8 %collective-permute-start.27 = (bf16[256,1024]{1,0:T(8,128)(2,1)S(1)}, bf16[256,1024]{1,0:T(8,128)(2,1)S(1)}, u32[]{:S(2)}, u32[]{:S(2)}) collective-permute-start(bf16[256,1024]{1,0:T(8,128)(2,1)S(1)} %get-tuple-element.127), channel_id=1, source_target_pairs={{0,2},{1,3},{2,0},{3,1},{4,6},{5,7},{6,4},{7,5},{8,10},{9,11},{10,... | collective-permute-start | bytes 1572872 | tf_op jit(solution)/shard_map/ppermute | solution.py:410
  123.1 14.4 %collective-permute-start.28 = (bf16[128,1024]{1,0:T(8,128)(2,1)}, bf16[128,1024]{1,0:T(8,128)(2,1)}, u32[]{:S(2)}, u32[]{:S(2)}) collective-permute-start(bf16[128,1024]{1,0:T(8,128)(2,1)} %get-tuple-element.131), channel_id=1, source_target_pairs={{0,4},{1,5},{2,6},{3,7},{4,0},{5,1},{6,2},{7,3},{8,12},{9,13},{10,... | collective-permute-start | bytes 786440 | tf_op jit(solution)/shard_map/ppermute | solution.py:410
  127.6 10.9 %collective-permute-start.29 = (bf16[4,32,1280]{2,1,0:T(8,128)(2,1)}, bf16[4,32,1280]{2,1,0:T(8,128)(2,1)S(1)}, u32[]{:S(2)}, u32[]{:S(2)}) collective-permute-start(bf16[4,32,1280]{2,1,0:T(8,128)(2,1)} %get-tuple-element.138), channel_id=1, source_target_pairs={{0,8},{8,0},{16,24},{24,16},{1,9},{9,1},{17,25},{25,17},{2,10},{10... | collective-permute-start | bytes 983048 | tf_op jit(solution)/shard_map/ppermute | solution.py:413
  129.1 9.4 %collective-permute-start.30 = (bf16[4,32,1280]{2,1,0:T(8,128)(2,1)S(1)}, bf16[4,32,1280]{2,1,0:T(8,128)(2,1)S(1)}, u32[]{:S(2)}, u32[]{:S(2)}) collective-permute-start(bf16[4,32,1280]{2,1,0:T(8,128)(2,1)S(1)} %get-tuple-element.139), channel_id=1, source_target_pairs={{0,16},{8,24},{16,0},{24,8},{1,17},{9,25},{17,1},{25,9},{2,18},{10... | collective-permute-start | bytes 983048 | tf_op jit(solution)/shard_map/ppermute | solution.py:413
  138.8 8.6 %collective-permute-start.31 = (bf16[64,2560]{1,0:T(8,128)(2,1)S(1)}, bf16[64,2560]{1,0:T(8,128)(2,1)S(1)}, u32[]{:S(2)}, u32[]{:S(2)}) collective-permute-start(bf16[64,2560]{1,0:T(8,128)(2,1)S(1)} %get-tuple-element.141), channel_id=1, source_target_pairs={{0,2},{1,3},{2,0},{3,1},{4,6},{5,7},{6,4},{7,5},{8,10},{9,11},{10,... | collective-permute-start | bytes 983048 | tf_op jit(solution)/shard_map/ppermute | solution.py:410
  147.4 10.1 %collective-permute-start.32 = (bf16[32,2560]{1,0:T(8,128)(2,1)S(1)}, bf16[32,2560]{1,0:T(8,128)(2,1)S(1)}, u32[]{:S(2)}, u32[]{:S(2)}) collective-permute-start(bf16[32,2560]{1,0:T(8,128)(2,1)S(1)} %get-tuple-element.143), channel_id=1, source_target_pairs={{0,4},{1,5},{2,6},{3,7},{4,0},{5,1},{6,2},{7,3},{8,12},{9,13},{10,... | collective-permute-start | bytes 491528 | tf_op jit(solution)/shard_map/ppermute | solution.py:410
  150.2 10.4 %collective-permute-start.38 = (bf16[128,1024]{1,0:T(8,128)(2,1)S(1)}, bf16[128,1024]{1,0:T(8,128)(2,1)S(1)}, u32[]{:S(2)}, u32[]{:S(2)}) collective-permute-start(bf16[128,1024]{1,0:T(8,128)(2,1)S(1)} %multiply_convert_fusion.refs_0_), channel_id=1, source_target_pairs={{0,24},{8,16},{16,8},{24,0},{1,25},{9,17},{17,9},{25,1},{2,26},{10... | collective-permute-start | bytes 786440 | tf_op jit(solution)/shard_map/ppermute | solution.py:413
  152.4 13.6 %collective-permute-start.37 = (bf16[128,1024]{1,0:T(8,128)(2,1)S(1)}, bf16[128,1024]{1,0:T(8,128)(2,1)S(1)}, u32[]{:S(2)}, u32[]{:S(2)}) collective-permute-start(bf16[128,1024]{1,0:T(8,128)(2,1)S(1)} %multiply_convert_fusion.refs_0_), channel_id=1, source_target_pairs={{0,16},{8,24},{16,0},{24,8},{1,17},{9,25},{17,1},{25,9},{2,18},{10... | collective-permute-start | bytes 786440 | tf_op jit(solution)/shard_map/ppermute | solution.py:413
  153.1 12.9 %collective-permute-start.36 = (bf16[128,1024]{1,0:T(8,128)(2,1)S(1)}, bf16[128,1024]{1,0:T(8,128)(2,1)S(1)}, u32[]{:S(2)}, u32[]{:S(2)}) collective-permute-start(bf16[128,1024]{1,0:T(8,128)(2,1)S(1)} %multiply_convert_fusion.refs_0_), channel_id=1, source_target_pairs={{0,8},{8,0},{16,24},{24,16},{1,9},{9,1},{17,25},{25,17},{2,10},{10... | collective-permute-start | bytes 786440 | tf_op jit(solution)/shard_map/ppermute | solution.py:413
  157.6 11.9 %collective-permute-start.35 = (bf16[32,2560]{1,0:T(8,128)(2,1)S(1)}, bf16[32,2560]{1,0:T(8,128)(2,1)S(1)}, u32[]{:S(2)}, u32[]{:S(2)}) collective-permute-start(bf16[32,2560]{1,0:T(8,128)(2,1)S(1)} %add_convert_fusion.refs_0_), channel_id=1, source_target_pairs={{0,24},{8,16},{16,8},{24,0},{1,25},{9,17},{17,9},{25,1},{2,26},{10... | collective-permute-start | bytes 491528 | tf_op jit(solution)/shard_map/ppermute | solution.py:413
  159.9 11.3 %collective-permute-start.34 = (bf16[32,2560]{1,0:T(8,128)(2,1)S(1)}, bf16[32,2560]{1,0:T(8,128)(2,1)S(1)}, u32[]{:S(2)}, u32[]{:S(2)}) collective-permute-start(bf16[32,2560]{1,0:T(8,128)(2,1)S(1)} %add_convert_fusion.refs_0_), channel_id=1, source_target_pairs={{0,16},{8,24},{16,0},{24,8},{1,17},{9,25},{17,1},{25,9},{2,18},{10... | collective-permute-start | bytes 491528 | tf_op jit(solution)/shard_map/ppermute | solution.py:413
  160.5 10.6 %collective-permute-start.33 = (bf16[32,2560]{1,0:T(8,128)(2,1)S(1)}, bf16[32,2560]{1,0:T(8,128)(2,1)S(1)}, u32[]{:S(2)}, u32[]{:S(2)}) collective-permute-start(bf16[32,2560]{1,0:T(8,128)(2,1)S(1)} %add_convert_fusion.refs_0_), channel_id=1, source_target_pairs={{0,8},{8,0},{16,24},{24,16},{1,9},{9,1},{17,25},{25,17},{2,10},{10... | collective-permute-start | bytes 491528 | tf_op jit(solution)/shard_map/ppermute | solution.py:413
  (27 other events, 342.2 us)

commit v11 on v10

--- a/solution.py
+++ b/solution.py
@@ -300,7 +300,7 @@
     ids = owner_ids(owners)
     amounts = jnp.concatenate([t[:owners] for t in tags], 1)
     chosen = jnp.concatenate([t[owners:] for t in tags], 1).astype(i32)
-    for copy in copies:
+    for copy in copies[:count]:
         copy.wait()
     for side, out in ((0, keep), (1, give)):
         parts = []
@@ -309,22 +309,35 @@
             hit = ids[j] * vocab_dev + grp * share + iota((share, 1), 0) == chosen[j : j + 1]
             parts.append(jnp.where(hit, amounts[j : j + 1], 0.0).astype(b16))
         summed = dot(jnp.concatenate(parts, 0), gathered[...], NN)
+        for copy in copies[count + side * chips : count + (side + 1) * chips]:
+            copy.wait()
         row = near[side * chips * share : (side + 1) * chips * share].astype(f32)
         out[...] = (summed - row * jnp.sum(row * summed, -1, keepdims=True)).astype(b16)
 
 
-def weight_kernel(groups, owners, keep, give, up_keep, up_give, grad, far_grad, gated, far_gated, *refs):
-    outs, whole = refs[:-1], refs[-1]
+def weight_kernel(groups, owners, *refs):
+    given, outs, loaded, (own, whole, sems) = refs[:8], refs[8:13], refs[13:21], refs[21:]
+    copies = [pltpu.make_async_copy(x, y, sems.at[n]) for n, (x, y) in enumerate(zip(given, loaded))]
+    for copy in copies:
+        copy.start()
+    keep, grad, up_keep, gated, up_give, far_gated, give, far_grad = loaded
     chips = owners // 2
     grp = lax.axis_index("grp")
     wide = grad.shape[1]
     step = gated.shape[1]
+    for copy in copies[:2]:
+        copy.wait()
+    for i in range(0, wide, step):
+        own[:, i : i + step] = dot(keep[...], grad[:, i : i + step], TN)
+    for copy in copies[2:6]:
+        copy.wait()
+    part = dot(up_keep[...], gated[...], TN) + dot(up_give[...], far_gated[...], TN)
+    whole[:, wide:] = part.astype(b16)
+    for copy in copies[6:]:
+        copy.wait()
     for i in range(0, wide, step):
         cols = slice(i, i + step)
-        part = dot(keep[...], grad[:, cols], TN) + dot(give[...], far_grad[:, cols], TN)
-        whole[:, cols] = part.astype(b16)
-    part = dot(up_keep[...], gated[...], TN) + dot(up_give[...], far_gated[...], TN)
-    whole[:, wide:] = part.astype(b16)
+        whole[:, cols] = (own[:, cols] + dot(give[...], far_grad[:, cols], TN)).astype(b16)
     rows = whole.shape[0] // chips
     fine = rows // groups
     half = whole.shape[1] // 2
@@ -415,11 +428,12 @@
     def to_core(x):
         return lax.ppermute(x, "seq", [(a, a ^ 1) for a in range(owners)])
 
-    def fold(low, high):
+    def fold(low, high, gate=()):
         bit = 1
         while bit < chips // 2:
             shape = (low.shape[0] // 2, low.shape[1])
-            low, high = call(pair_kernel, [(shape, b16)] * 2, [VMEM] * 2, [low, across(high, bit)], room=8)
+            came, _ = lax.optimization_barrier((across(high, bit), gate))
+            low, high = call(pair_kernel, [(shape, b16)] * 2, [VMEM] * 2, [low, came], room=8)
             bit *= 2
         return low, high
 
@@ -446,7 +460,6 @@
         have.update({x ^ bit: across(have[x], bit) for x in have})
         bit //= 2
     got = [have[x] for x in distances(chips)[1:]]
-    candidates = jnp.concatenate([history[:, None], negatives], 1)
     outs = [
         ((tok, width // 2), b16), ((tok, width // 2), b16), ((tok, 4 * hidden), b16), ((tok, 4 * hidden), b16),
         ((HEADS, tok, tok), b16), ((HEADS, tok, tok), b16), ((tok, hidden), f32), ((tok, 1), f32),
@@ -460,7 +473,8 @@
     )
 
     near_units = [to_group(unit_b, k) for k in (1, 2)]
-    got, near_units, own = lax.optimization_barrier((got, near_units, own))
+    candidates = jnp.concatenate([history[:, None], negatives], 1)
+    got, near_units, own, candidates = lax.optimization_barrier((got, near_units, own, candidates))
     far_own = to_core(own)
     unit_sent = gather_groups(unit_b, near_units)
     others = [jnp.concatenate(got, 0)]
@@ -474,14 +488,10 @@
     arrived = lax.all_to_all(
         outgoing.reshape(owners, slot, width), "seq", 0, 0, tiled=True
     ).reshape(owners * slot, width)
-    layer_out, = call(
-        relay_kernel, [((tok, width), b16)], [VMEM], [arrived],
-        room=63,
-    )
-
     vocab = vocab_dev * owners
     far_give, far_gated = to_core(give), to_core(gated)
     units = [p[3] for p in unit_sent]
+    layer_out, = call(relay_kernel, [((tok, width), b16)], [VMEM], [arrived], room=63)
     layer_out, score_unit, far_give, far_gated, units = lax.optimization_barrier(
         (layer_out, unit, far_give, far_gated, units)
     )
@@ -517,9 +527,11 @@
         split = (chips, fine, half)
         parts = call(
             lambda *refs: weight_kernel(groups, owners, *refs),
-            [(block, b16)] + [((2,) + split, b16)] * 2 + [(split, b16)] * 2, [VMEM] * 8,
-            [keep, far[0], up_keep, far[1], grad, far[2], gated, far[3]],
-            [pltpu.VMEM((width // 2, 5 * hidden), b16)],
+            [(block, b16)] + [((2,) + split, b16)] * 2 + [(split, b16)] * 2, [ANY] * 8,
+            [keep, grad, up_keep, gated, far[1], far[3], far[0], far[2]],
+            [pltpu.VMEM(x.shape, b16) for x in (keep, grad, up_keep, gated, up_keep, gated, keep, grad)]
+            + [pltpu.VMEM((width // 2, 4 * hidden), f32), pltpu.VMEM((width // 2, 5 * hidden), b16),
+               pltpu.SemaphoreType.DMA((8,))],
             flops=2 * tok * width * 5 * hidden, nbytes=20 * tok * width, room=60,
         )
         by_one, by_two = to_group(parts[1], 1), to_group(parts[2], 2)
@@ -550,9 +562,9 @@
         arrived = [by_one, by_two, to_group(one_right, 1), to_group(two_left, 2)]
     total = finish(low, high)
     total = (total * quarter_inv).astype(b16)
+    totals = [to_group(total, k) if k else total for k in range(groups)]
     table_grad, = call(
-        lambda *refs: assemble_kernel(groups, [width], *refs), [((vocab_dev, width), f32)], [VMEM] * groups,
-        [to_group(total, k) if k else total for k in range(groups)],
+        lambda *refs: assemble_kernel(groups, [width], *refs), [((vocab_dev, width), f32)], [VMEM] * groups, totals,
         flops=vocab_dev * width, nbytes=6 * vocab_dev * width, room=8,
     )
 
@@ -562,7 +574,7 @@
             sum_kernel, [((chips // 2 * fine, 5 * hidden), b16)] * 2, [VMEM] * 5, [base] + arrived,
             flops=chips * fine * 5 * hidden, nbytes=40 * chips * fine * hidden, room=10,
         )
-        line = finish(*fold(low, high))
+        line = finish(*fold(low, high, totals))
     else:
         blocks = [lax.dynamic_index_in_dim(sums, (chip + d) % chips, 0, False).astype(b16) for d in range(chips)]
         line = blocks[0].astype(f32)

time: 173 us -> 177 us (1.023)
  waiting for transfers between devices: 73.7 us -> 77.7 us
    ppermute x21, waiting for transfers between devices: 31.5 us -> 38.8 us  [to_group(): return lax.ppermute(x, 'grp', [(a, a ^ k) for a in range(groups)])]
    ppermute x7, waiting for transfers between devices: 40.9 us -> 37.6 us  [across(): return lax.ppermute(x, 'seq', pairs)]
  transfers between devices with their start and end apart: 40 -> 40, of which waited for: 20 -> 21; matrix products, arithmetic and copies ran while one was open for 2% -> 2% of each run, Pallas kernels for 16% -> 15%
where the time goes in v11:
time: 177 us; the launch traced here: 176 us
  waiting for transfers between devices  77.7 us (44%)
  starting transfers between devices  44.8 us (25%)
  Pallas kernels  42.5 us (24%)
  local copies, waits for them, and re-layouts  8.74 us (5%)
    pallas_call x13, Pallas kernels, call(): pl.pallas_call(kernel, out_shape=[jax.ShapeDtypeStruct(s, t) for s, t in...  42.5 us
    ppermute x21, waiting for transfers between devices, to_group(): return lax.ppermute(x, 'grp', [(a, a ^ k) for a in range(groups)])  38.8 us
    ppermute x7, waiting for transfers between devices, across(): return lax.ppermute(x, 'seq', pairs)  37.6 us
    ppermute x21, starting transfers between devices, to_group(): return lax.ppermute(x, 'grp', [(a, a ^ k) for a in range(groups)])  24 us
    ppermute x7, starting transfers between devices, across(): return lax.ppermute(x, 'seq', pairs)  14.2 us
    unnamed x40, local copies, waits for them, and re-layouts  5.85 us
    all_to_all x1, starting transfers between devices, body(): lax.all_to_all(outgoing.reshape(owners, slot, width), 'seq', 0, 0, tiled=...  4.88 us
  transfers between devices with their start and end apart: 40, of which 21 were waited for; matrix products, arithmetic and copies ran while one was open for 2% of the time, Pallas kernels for 15%

profile of v11, /device:TPU:0, one launch (start us, length us, event | category | flops | bytes accessed | tf_op | source)
XLA Modules:
  0.0 175.9 jit_solution(108211682167280474)
XLA Ops:
  3.2 4.0 %collective-permute-start = (bf16[128,1024]{1,0:T(8,128)(2,1)S(1)}, bf16[128,1024]{1,0:T(8,128)(2,1)}, u32[]{:S(2)}, u32[]{:S(2)}) collective-permute-start(bf16[128,1024]{1,0:T(8,128)(2,1)S(1)} %get-tuple-element.78), channel_id=1, source_target_pairs={{0,4},{1,5},{2,6},{3,7},{4,0},{5,1},{6,2},{7,3},{8,12},{9,13},{10,... | collective-permute-start | bytes 786440 | tf_op jit(solution)/shard_map/ppermute | solution.py:423
  7.3 9.1 %shard_map.111 = (bf16[256,512]{1,0:T(8,128)(2,1)}, bf16[256,512]{1,0:T(8,128)(2,1)}, bf16[256,2048]{1,0:T(8,128)(2,1)}, bf16[256,2048]{1,0:T(8,128)(2,1)}, bf16...) custom-call(s32[1,8]{1,0:T(1,128)} %refs_0_.2, ...), custom_call_target="tpu_custom_call" | custom-call | tf_op jit(solution)/shard_map/pallas_call | solution.py:53
  16.4 1.5 collective-permute-start.4
  17.9 1.5 collective-permute-start.3
  19.4 1.6 collective-permute-start.1
  21.4 7.2 %collective-permute-done.1 = bf16[128,1024]{1,0:T(8,128)(2,1)S(1)} collective-permute-done((bf16[128,1024]{1,0:T(8,128)(2,1)S(1)}, bf16[128,1024]{1,0:T(8,128)(2,1)S(1)}, u32[]{:S(2)}, u32[]{:S(2)}) %collective-permute-start.1) | collective-permute-done | bytes 262176 | tf_op jit(solution)/shard_map/ppermute | solution.py:423
  28.6 3.6 %collective-permute-done.2 = bf16[128,1024]{1,0:T(8,128)(2,1)S(1)} collective-permute-done((bf16[128,1024]{1,0:T(8,128)(2,1)}, bf16[128,1024]{1,0:T(8,128)(2,1)S(1)}, u32[]{:S(2)}, u32[]{:S(2)}) %collective-permute-start.2) | collective-permute-done | bytes 262176 | tf_op jit(solution)/shard_map/ppermute | solution.py:423
  34.8 4.9 %all-to-all-start = ((bf16[8,48,1024]{2,1,0:T(8,128)(2,1)}), bf16[8,48,1024]{2,1,0:T(8,128)(2,1)}, u32[]{:S(2)}, u32[]{:S(2)}) async-start(bf16[8,48,1024]{2,1,0:T(8,128)(2,1)} %bitcast.3), calls=%async_computation | async-start | bytes 1572864 | tf_op jit(solution)/shard_map/all_to_all | solution.py:488
  42.4 8.8 %collective-permute-done.10.refs_8_ = bf16[384,1024]{1,0:T(8,128)(2,1)} collective-permute-done((bf16[384,1024]{1,0:T(8,128)(2,1)S(1)}, bf16[384,1024]{1,0:T(8,128)(2,1)}, u32[]{:S(2)}, u32[]{:S(2)}) %collective-permute-start.10) | collective-permute-done | bytes 786464 | tf_op jit(solution)/shard_map/ppermute | solution.py:426
  51.1 3.0 %collective-permute-done.9.refs_7_ = bf16[384,1024]{1,0:T(8,128)(2,1)} collective-permute-done((bf16[384,1024]{1,0:T(8,128)(2,1)S(1)}, bf16[384,1024]{1,0:T(8,128)(2,1)}, u32[]{:S(2)}, u32[]{:S(2)}) %collective-permute-start.9) | collective-permute-done | bytes 786464 | tf_op jit(solution)/shard_map/ppermute | solution.py:426
  54.2 1.5 collective-permute-start.7
  59.4 3.9 %collective-permute-done.7.refs_3_ = bf16[256,512]{1,0:T(8,128)(2,1)S(1)} collective-permute-done((bf16[256,512]{1,0:T(8,128)(2,1)S(1)}, bf16[256,512]{1,0:T(8,128)(2,1)S(1)}, u32[]{:S(2)}, u32[]{:S(2)}) %collective-permute-start.7) | collective-permute-done | bytes 262176 | tf_op jit(solution)/shard_map/ppermute | solution.py:426
  65.7 3.0 %collective-permute-done.11.refs_9_ = bf16[384,512]{1,0:T(8,128)(2,1)} collective-permute-done((bf16[384,512]{1,0:T(8,128)(2,1)S(1)}, bf16[384,512]{1,0:T(8,128)(2,1)}, u32[]{:S(2)}, u32[]{:S(2)}) %collective-permute-start.11) | collective-permute-done | bytes 393248 | tf_op jit(solution)/shard_map/ppermute | solution.py:426
  69.6 2.7 %shard_map.113 = bf16[256,1024]{1,0:T(8,128)(2,1)} custom-call(bf16[384,1024]{1,0:T(8,128)(2,1)} %bitcast.2.arrived), custom_call_target="tpu_custom_call" | custom-call | tf_op jit(solution)/shard_map/pallas_call | solution.py:53
  72.4 13.0 %shard_map.114 = (f32[16,256]{1,0:T(8,128)}, bf16[256,512]{1,0:T(8,128)(2,1)}, bf16[256,512]{1,0:T(8,128)(2,1)}, bf16[256,2048]{1,0:T(8,128)(2,1)}) custom-call(s32[256,4]{1,0:T(8,128)} %copy.15.refs_0_, f32[256,1]{1,0:T(8,128)} %get-tuple-element.93.refs_1_, f32[256,1]{1,0:T(8,128)} %get-tuple-element.94.refs_2_, ...), custom_call_target="tpu_custom_call" | custom-call | tf_op jit(solution)/shard_map/pallas_call | solution.py:53
  85.9 1.9 %collective-permute-start.22 = (f32[16,256]{1,0:T(8,128)}, f32[16,256]{1,0:T(8,128)S(1)}, u32[]{:S(2)}, u32[]{:S(2)}) collective-permute-start(f32[16,256]{1,0:T(8,128)} %get-tuple-element.115.refs_5_), channel_id=1, source_target_pairs={{0,24},{8,16},{16,8},{24,0},{1,25},{9,17},{17,9},{25,1},{2,26},{10... | collective-permute-start | bytes 49160 | tf_op jit(solution)/shard_map/ppermute | solution.py:426
  92.9 6.7 %shard_map.115 = (bf16[512,1024]{1,0:T(8,128)(2,1)}, bf16[512,1024]{1,0:T(8,128)(2,1)}) custom-call(bf16[256,1024]{1,0:T(8,128)(2,1)} %get-tuple-element.110.refs_3_.refs_0_, bf16[256,1024]{1,0:T(8,128)(2,1)} %copy-done.8, bf16[256,1024]{1,0:T(8,128)(2,1)} %copy-done.7, bf16[256,512]{1,0:T(8,128)(2,1)} %copy-done.10, bf16[256,512]{1,0:T(8,128)(2,1)} %copy-done.9, ...), custom_call_target="tpu_custom_call" | custom-call | tf_op jit(solution)/shard_map/pallas_call | solution.py:53
  99.7 5.0 %shard_map.116 = (bf16[4,32,2560]{2,1,0:T(8,128)(2,1)}, bf16[2,4,32,1280]{3,2,1,0:T(8,128)(2,1)}, bf16[2,4,32,1280]{3,2,1,0:T(8,128)(2,1)}, bf16[4,32,1280]{2,1,0:T(8,128)(2,1)}, bf16[4,32,1280]{2,1,0:T(8,128)(2,1)}) custom-call(bf16[256,512]{1,0:T(8,128)(2,1)} %get-tuple-element.91.refs_0_, bf16[256,2048]{1,0:T(8,128)(2,1)} %get-tuple-element.105.refs_1_, ...), custom_call_target="tpu_custom_call" | custom-call | flops 1342177280 | bytes 5242880 | tf_op jit(solution)/shard_map/pallas_call | solution.py:53
  107.2 1.6 collective-permute-start.27
  108.9 12.1 %collective-permute-done.27.y = bf16[256,1024]{1,0:T(8,128)(2,1)S(1)} collective-permute-done((bf16[256,1024]{1,0:T(8,128)(2,1)S(1)}, bf16[256,1024]{1,0:T(8,128)(2,1)S(1)}, u32[]{:S(2)}, u32[]{:S(2)}) %collective-permute-start.27) | collective-permute-done | bytes 524320 | tf_op jit(solution)/shard_map/ppermute | solution.py:423
  122.8 1.7 collective-permute-start.28
  127.3 1.5 collective-permute-start.29
  130.2 6.9 %collective-permute-done.28 = bf16[128,1024]{1,0:T(8,128)(2,1)} collective-permute-done((bf16[128,1024]{1,0:T(8,128)(2,1)}, bf16[128,1024]{1,0:T(8,128)(2,1)}, u32[]{:S(2)}, u32[]{:S(2)}) %collective-permute-start.28) | collective-permute-done | bytes 262176 | tf_op jit(solution)/shard_map/ppermute | solution.py:423
  139.8 1.5 collective-permute-start.34
  143.3 6.7 %collective-permute-done.34.refs_3_ = bf16[128,1024]{1,0:T(8,128)(2,1)S(1)} collective-permute-done((bf16[128,1024]{1,0:T(8,128)(2,1)S(1)}, bf16[128,1024]{1,0:T(8,128)(2,1)S(1)}, u32[]{:S(2)}, u32[]{:S(2)}) %collective-permute-start.34) | collective-permute-done | bytes 262176 | tf_op jit(solution)/shard_map/ppermute | solution.py:426
  150.0 2.9 %collective-permute-done.33.refs_2_ = bf16[128,1024]{1,0:T(8,128)(2,1)S(1)} collective-permute-done((bf16[128,1024]{1,0:T(8,128)(2,1)S(1)}, bf16[128,1024]{1,0:T(8,128)(2,1)S(1)}, u32[]{:S(2)}, u32[]{:S(2)}) %collective-permute-start.33) | collective-permute-done | bytes 262176 | tf_op jit(solution)/shard_map/ppermute | solution.py:426
  153.0 3.4 %collective-permute-start.35 = (bf16[32,2560]{1,0:T(8,128)(2,1)S(1)}, bf16[32,2560]{1,0:T(8,128)(2,1)S(1)}, u32[]{:S(2)}, u32[]{:S(2)}) collective-permute-start(bf16[32,2560]{1,0:T(8,128)(2,1)S(1)} %get-tuple-element.147), channel_id=1, source_target_pairs={{0,4},{1,5},{2,6},{3,7},{4,0},{5,1},{6,2},{7,3},{8,12},{9,13},{10,... | collective-permute-start | bytes 491528 | tf_op jit(solution)/shard_map/ppermute | solution.py:423
  156.4 7.7 %collective-permute-done.35 = bf16[32,2560]{1,0:T(8,128)(2,1)S(1)} collective-permute-done((bf16[32,2560]{1,0:T(8,128)(2,1)S(1)}, bf16[32,2560]{1,0:T(8,128)(2,1)S(1)}, u32[]{:S(2)}, u32[]{:S(2)}) %collective-permute-start.35) | collective-permute-done | bytes 163872 | tf_op jit(solution)/shard_map/ppermute | solution.py:423
  165.6 1.5 collective-permute-start.37
  167.7 1.5 shard_map.123
  169.2 3.0 %collective-permute-done.38.refs_3_ = bf16[32,2560]{1,0:T(8,128)(2,1)S(1)} collective-permute-done((bf16[32,2560]{1,0:T(8,128)(2,1)S(1)}, bf16[32,2560]{1,0:T(8,128)(2,1)S(1)}, u32[]{:S(2)}, u32[]{:S(2)}) %collective-permute-start.38) | collective-permute-done | bytes 163872 | tf_op jit(solution)/shard_map/ppermute | solution.py:426
  172.2 2.5 %collective-permute-done.37.refs_2_ = bf16[32,2560]{1,0:T(8,128)(2,1)S(1)} collective-permute-done((bf16[32,2560]{1,0:T(8,128)(2,1)S(1)}, bf16[32,2560]{1,0:T(8,128)(2,1)S(1)}, u32[]{:S(2)}, u32[]{:S(2)}) %collective-permute-start.37) | collective-permute-done | bytes 163872 | tf_op jit(solution)/shard_map/ppermute | solution.py:426
  (111 shorter events, 37.6 us)
Async XLA Ops:
  3.2 17.7 %collective-permute-start = (bf16[128,1024]{1,0:T(8,128)(2,1)S(1)}, bf16[128,1024]{1,0:T(8,128)(2,1)}, u32[]{:S(2)}, u32[]{:S(2)}) collective-permute-start(bf16[128,1024]{1,0:T(8,128)(2,1)S(1)} %get-tuple-element.78), channel_id=1, source_target_pairs={{0,4},{1,5},{2,6},{3,7},{4,0},{5,1},{6,2},{7,3},{8,12},{9,13},{10,... | collective-permute-start | bytes 786440 | tf_op jit(solution)/shard_map/ppermute | solution.py:423
  16.4 15.8 %collective-permute-start.4 = (bf16[256,1024]{1,0:T(8,128)(2,1)}, bf16[256,1024]{1,0:T(8,128)(2,1)S(1)}, u32[]{:S(2)}, u32[]{:S(2)}) collective-permute-start(bf16[256,1024]{1,0:T(8,128)(2,1)} %get-tuple-element.110.refs_3_.refs_0_), channel_id=1, source_target_pairs={{0,16},{8,24},{16,0},{24,8},{1,17},{9,25},{17,1},{25,9},{2,18},{10... | collective-permute-start | bytes 1572872 | tf_op jit(solution)/shard_map/ppermute | solution.py:426
  17.9 14.3 %collective-permute-start.3 = (bf16[256,1024]{1,0:T(8,128)(2,1)}, bf16[256,1024]{1,0:T(8,128)(2,1)S(1)}, u32[]{:S(2)}, u32[]{:S(2)}) collective-permute-start(bf16[256,1024]{1,0:T(8,128)(2,1)} %get-tuple-element.110.refs_3_.refs_0_), channel_id=1, source_target_pairs={{0,8},{8,0},{16,24},{24,16},{1,9},{9,1},{17,25},{25,17},{2,10},{10... | collective-permute-start | bytes 1572872 | tf_op jit(solution)/shard_map/ppermute | solution.py:426
  19.4 9.2 %collective-permute-start.1 = (bf16[128,1024]{1,0:T(8,128)(2,1)S(1)}, bf16[128,1024]{1,0:T(8,128)(2,1)S(1)}, u32[]{:S(2)}, u32[]{:S(2)}) collective-permute-start(bf16[128,1024]{1,0:T(8,128)(2,1)S(1)} %get-tuple-element.78), channel_id=1, source_target_pairs={{0,2},{1,3},{2,0},{3,1},{4,6},{5,7},{6,4},{7,5},{8,10},{9,11},{10,... | collective-permute-start | bytes 786440 | tf_op jit(solution)/shard_map/ppermute | solution.py:423
  20.9 11.2 %collective-permute-start.2 = (bf16[128,1024]{1,0:T(8,128)(2,1)}, bf16[128,1024]{1,0:T(8,128)(2,1)S(1)}, u32[]{:S(2)}, u32[]{:S(2)}) collective-permute-start(bf16[128,1024]{1,0:T(8,128)(2,1)} %collective-permute-done), channel_id=1, source_target_pairs={{0,2},{1,3},{2,0},{3,1},{4,6},{5,7},{6,4},{7,5},{8,10},{9,11},{10,... | collective-permute-start | bytes 786440 | tf_op jit(solution)/shard_map/ppermute | solution.py:423
  33.4 17.7 %collective-permute-start.10 = (bf16[384,1024]{1,0:T(8,128)(2,1)S(1)}, bf16[384,1024]{1,0:T(8,128)(2,1)}, u32[]{:S(2)}, u32[]{:S(2)}) collective-permute-start(bf16[384,1024]{1,0:T(8,128)(2,1)S(1)} %constant_dynamic-update-slice_fusion.refs_6_.refs_10_), channel_id=1, source_target_pairs={{0,16},{8,24},{16,0},{24,8},{1,17},{9,25},{17,1},{25,9},{2,18},{10... | collective-permute-start | bytes 2359304 | tf_op jit(solution)/shard_map/ppermute | solution.py:426
  34.0 20.2 %collective-permute-start.9 = (bf16[384,1024]{1,0:T(8,128)(2,1)S(1)}, bf16[384,1024]{1,0:T(8,128)(2,1)}, u32[]{:S(2)}, u32[]{:S(2)}) collective-permute-start(bf16[384,1024]{1,0:T(8,128)(2,1)S(1)} %constant_dynamic-update-slice_fusion.refs_6_.refs_10_), channel_id=1, source_target_pairs={{0,8},{8,0},{16,24},{24,16},{1,9},{9,1},{17,25},{25,17},{2,10},{10... | collective-permute-start | bytes 2359304 | tf_op jit(solution)/shard_map/ppermute | solution.py:426
  34.8 28.5 %collective-permute-start.14 = (bf16[384,1024]{1,0:T(8,128)(2,1)S(1)}, bf16[384,1024]{1,0:T(8,128)(2,1)S(1)}, u32[]{:S(2)}, u32[]{:S(2)}) collective-permute-start(bf16[384,1024]{1,0:T(8,128)(2,1)S(1)} %constant_dynamic-update-slice_fusion.refs_6_.refs_10_), channel_id=1, source_target_pairs={{0,1},{1,0},{2,3},{3,2},{4,5},{5,4},{6,7},{7,6},{8,9},{9,8},{10,11... | collective-permute-start | bytes 2359304 | tf_op jit(solution)/shard_map/ppermute | solution.py:429
  34.8 34.8 %all-to-all-start = ((bf16[8,48,1024]{2,1,0:T(8,128)(2,1)}), bf16[8,48,1024]{2,1,0:T(8,128)(2,1)}, u32[]{:S(2)}, u32[]{:S(2)}) async-start(bf16[8,48,1024]{2,1,0:T(8,128)(2,1)} %bitcast.3), calls=%async_computation | async-start | bytes 1572864 | tf_op jit(solution)/shard_map/all_to_all | solution.py:488
  40.2 17.5 %collective-permute-start.6 = (bf16[256,512]{1,0:T(8,128)(2,1)}, bf16[256,512]{1,0:T(8,128)(2,1)S(1)}, u32[]{:S(2)}, u32[]{:S(2)}) collective-permute-start(bf16[256,512]{1,0:T(8,128)(2,1)} %get-tuple-element.87.refs_3_), channel_id=1, source_target_pairs={{0,1},{1,0},{2,3},{3,2},{4,5},{5,4},{6,7},{7,6},{8,9},{9,8},{10,11... | collective-permute-start | bytes 786440 | tf_op jit(solution)/shard_map/ppermute | solution.py:429
  41.6 17.0 %collective-permute-start.8 = (bf16[256,512]{1,0:T(8,128)(2,1)S(1)}, bf16[256,512]{1,0:T(8,128)(2,1)S(1)}, u32[]{:S(2)}, u32[]{:S(2)}) collective-permute-start(bf16[256,512]{1,0:T(8,128)(2,1)S(1)} %slice.13), channel_id=1, source_target_pairs={{0,8},{8,0},{16,24},{24,16},{1,9},{9,1},{17,25},{25,17},{2,10},{10... | collective-permute-start | bytes 786440 | tf_op jit(solution)/shard_map/ppermute | solution.py:426
  51.1 21.2 %collective-permute-start.13 = (bf16[512,1024]{1,0:T(8,128)(2,1)}, bf16[512,1024]{1,0:T(8,128)(2,1)}, u32[]{:S(2)}, u32[]{:S(2)}) collective-permute-start(bf16[512,1024]{1,0:T(8,128)(2,1)} %get-tuple-element.96.refs_5_.refs_9_), channel_id=1, source_target_pairs={{0,1},{1,0},{2,3},{3,2},{4,5},{5,4},{6,7},{7,6},{8,9},{9,8},{10,11... | collective-permute-start | bytes 3145736 | tf_op jit(solution)/shard_map/ppermute | solution.py:429
  54.2 9.1 %collective-permute-start.7 = (bf16[256,512]{1,0:T(8,128)(2,1)S(1)}, bf16[256,512]{1,0:T(8,128)(2,1)S(1)}, u32[]{:S(2)}, u32[]{:S(2)}) collective-permute-start(bf16[256,512]{1,0:T(8,128)(2,1)S(1)} %slice.12), channel_id=1, source_target_pairs={{0,16},{8,24},{16,0},{24,8},{1,17},{9,25},{17,1},{25,9},{2,18},{10... | collective-permute-start | bytes 786440 | tf_op jit(solution)/shard_map/ppermute | solution.py:426
  57.8 7.9 %collective-permute-start.12 = (bf16[384,512]{1,0:T(8,128)(2,1)S(1)}, bf16[384,512]{1,0:T(8,128)(2,1)}, u32[]{:S(2)}, u32[]{:S(2)}) collective-permute-start(bf16[384,512]{1,0:T(8,128)(2,1)S(1)} %slice.17), channel_id=1, source_target_pairs={{0,8},{8,0},{16,24},{24,16},{1,9},{9,1},{17,25},{25,17},{2,10},{10... | collective-permute-start | bytes 1179656 | tf_op jit(solution)/shard_map/ppermute | solution.py:426
  58.6 10.2 %collective-permute-start.11 = (bf16[384,512]{1,0:T(8,128)(2,1)S(1)}, bf16[384,512]{1,0:T(8,128)(2,1)}, u32[]{:S(2)}, u32[]{:S(2)}) collective-permute-start(bf16[384,512]{1,0:T(8,128)(2,1)S(1)} %slice.16), channel_id=1, source_target_pairs={{0,16},{8,24},{16,0},{24,8},{1,17},{9,25},{17,1},{25,9},{2,18},{10... | collective-permute-start | bytes 1179656 | tf_op jit(solution)/shard_map/ppermute | solution.py:426
  63.3 9.1 %collective-permute-start.16 = (bf16[384,1024]{1,0:T(8,128)(2,1)}, bf16[384,1024]{1,0:T(8,128)(2,1)}, u32[]{:S(2)}, u32[]{:S(2)}) collective-permute-start(bf16[384,1024]{1,0:T(8,128)(2,1)} %collective-permute-done.10.refs_8_), channel_id=1, source_target_pairs={{0,1},{1,0},{2,3},{3,2},{4,5},{5,4},{6,7},{7,6},{8,9},{9,8},{10,11... | collective-permute-start | bytes 2359304 | tf_op jit(solution)/shard_map/ppermute | solution.py:429
  64.2 8.1 %collective-permute-start.15 = (bf16[384,1024]{1,0:T(8,128)(2,1)}, bf16[384,1024]{1,0:T(8,128)(2,1)}, u32[]{:S(2)}, u32[]{:S(2)}) collective-permute-start(bf16[384,1024]{1,0:T(8,128)(2,1)} %collective-permute-done.9.refs_7_), channel_id=1, source_target_pairs={{0,1},{1,0},{2,3},{3,2},{4,5},{5,4},{6,7},{7,6},{8,9},{9,8},{10,11... | collective-permute-start | bytes 2359304 | tf_op jit(solution)/shard_map/ppermute | solution.py:429
  99.6 7.4 %collective-permute-start.26 = (bf16[512,1024]{1,0:T(8,128)(2,1)}, bf16[512,1024]{1,0:T(8,128)(2,1)S(1)}, u32[]{:S(2)}, u32[]{:S(2)}) collective-permute-start(bf16[512,1024]{1,0:T(8,128)(2,1)} %get-tuple-element.128), channel_id=1, source_target_pairs={{0,1},{1,0},{2,3},{3,2},{4,5},{5,4},{6,7},{7,6},{8,9},{9,8},{10,11... | collective-permute-start | bytes 3145736 | tf_op jit(solution)/shard_map/ppermute | solution.py:429
  104.6 17.4 %collective-permute-start.24 = (bf16[2,4,32,1280]{3,2,1,0:T(8,128)(2,1)}, bf16[2,4,32,1280]{3,2,1,0:T(8,128)(2,1)S(1)}, u32[]{:S(2)}, u32[]{:S(2)}) collective-permute-start(bf16[2,4,32,1280]{3,2,1,0:T(8,128)(2,1)} %get-tuple-element.125), channel_id=1, source_target_pairs={{0,8},{8,0},{16,24},{24,16},{1,9},{9,1},{17,25},{25,17},{2,10},{10... | collective-permute-start | bytes 1966088 | tf_op jit(solution)/shard_map/ppermute | solution.py:426
  105.8 17.0 %collective-permute-start.25 = (bf16[2,4,32,1280]{3,2,1,0:T(8,128)(2,1)}, bf16[2,4,32,1280]{3,2,1,0:T(8,128)(2,1)S(1)}, u32[]{:S(2)}, u32[]{:S(2)}) collective-permute-start(bf16[2,4,32,1280]{3,2,1,0:T(8,128)(2,1)} %get-tuple-element.126), channel_id=1, source_target_pairs={{0,16},{8,24},{16,0},{24,8},{1,17},{9,25},{17,1},{25,9},{2,18},{10... | collective-permute-start | bytes 1966088 | tf_op jit(solution)/shard_map/ppermute | solution.py:426
  107.2 13.8 %collective-permute-start.27 = (bf16[256,1024]{1,0:T(8,128)(2,1)S(1)}, bf16[256,1024]{1,0:T(8,128)(2,1)S(1)}, u32[]{:S(2)}, u32[]{:S(2)}) collective-permute-start(bf16[256,1024]{1,0:T(8,128)(2,1)S(1)} %get-tuple-element.130), channel_id=1, source_target_pairs={{0,2},{1,3},{2,0},{3,1},{4,6},{5,7},{6,4},{7,5},{8,10},{9,11},{10,... | collective-permute-start | bytes 1572872 | tf_op jit(solution)/shard_map/ppermute | solution.py:423
  122.8 14.4 %collective-permute-start.28 = (bf16[128,1024]{1,0:T(8,128)(2,1)}, bf16[128,1024]{1,0:T(8,128)(2,1)}, u32[]{:S(2)}, u32[]{:S(2)}) collective-permute-start(bf16[128,1024]{1,0:T(8,128)(2,1)} %get-tuple-element.134), channel_id=1, source_target_pairs={{0,4},{1,5},{2,6},{3,7},{4,0},{5,1},{6,2},{7,3},{8,12},{9,13},{10,... | collective-permute-start | bytes 786440 | tf_op jit(solution)/shard_map/ppermute | solution.py:423
  127.3 10.9 %collective-permute-start.29 = (bf16[4,32,1280]{2,1,0:T(8,128)(2,1)}, bf16[4,32,1280]{2,1,0:T(8,128)(2,1)S(1)}, u32[]{:S(2)}, u32[]{:S(2)}) collective-permute-start(bf16[4,32,1280]{2,1,0:T(8,128)(2,1)} %get-tuple-element.141), channel_id=1, source_target_pairs={{0,8},{8,0},{16,24},{24,16},{1,9},{9,1},{17,25},{25,17},{2,10},{10... | collective-permute-start | bytes 983048 | tf_op jit(solution)/shard_map/ppermute | solution.py:426
  128.7 9.5 %collective-permute-start.30 = (bf16[4,32,1280]{2,1,0:T(8,128)(2,1)S(1)}, bf16[4,32,1280]{2,1,0:T(8,128)(2,1)S(1)}, u32[]{:S(2)}, u32[]{:S(2)}) collective-permute-start(bf16[4,32,1280]{2,1,0:T(8,128)(2,1)S(1)} %get-tuple-element.142), channel_id=1, source_target_pairs={{0,16},{8,24},{16,0},{24,8},{1,17},{9,25},{17,1},{25,9},{2,18},{10... | collective-permute-start | bytes 983048 | tf_op jit(solution)/shard_map/ppermute | solution.py:426
  138.5 14.4 %collective-permute-start.31 = (bf16[64,2560]{1,0:T(8,128)(2,1)S(1)}, bf16[64,2560]{1,0:T(8,128)(2,1)S(1)}, u32[]{:S(2)}, u32[]{:S(2)}) collective-permute-start(bf16[64,2560]{1,0:T(8,128)(2,1)S(1)} %get-tuple-element.144), channel_id=1, source_target_pairs={{0,2},{1,3},{2,0},{3,1},{4,6},{5,7},{6,4},{7,5},{8,10},{9,11},{10,... | collective-permute-start | bytes 983048 | tf_op jit(solution)/shard_map/ppermute | solution.py:423
  139.8 10.2 %collective-permute-start.34 = (bf16[128,1024]{1,0:T(8,128)(2,1)S(1)}, bf16[128,1024]{1,0:T(8,128)(2,1)S(1)}, u32[]{:S(2)}, u32[]{:S(2)}) collective-permute-start(bf16[128,1024]{1,0:T(8,128)(2,1)S(1)} %multiply_convert_fusion.refs_0_), channel_id=1, source_target_pairs={{0,24},{8,16},{16,8},{24,0},{1,25},{9,17},{17,9},{25,1},{2,26},{10... | collective-permute-start | bytes 786440 | tf_op jit(solution)/shard_map/ppermute | solution.py:426
  141.3 11.6 %collective-permute-start.33 = (bf16[128,1024]{1,0:T(8,128)(2,1)S(1)}, bf16[128,1024]{1,0:T(8,128)(2,1)S(1)}, u32[]{:S(2)}, u32[]{:S(2)}) collective-permute-start(bf16[128,1024]{1,0:T(8,128)(2,1)S(1)} %multiply_convert_fusion.refs_0_), channel_id=1, source_target_pairs={{0,16},{8,24},{16,0},{24,8},{1,17},{9,25},{17,1},{25,9},{2,18},{10... | collective-permute-start | bytes 786440 | tf_op jit(solution)/shard_map/ppermute | solution.py:426
  141.9 11.0 %collective-permute-start.32 = (bf16[128,1024]{1,0:T(8,128)(2,1)S(1)}, bf16[128,1024]{1,0:T(8,128)(2,1)S(1)}, u32[]{:S(2)}, u32[]{:S(2)}) collective-permute-start(bf16[128,1024]{1,0:T(8,128)(2,1)S(1)} %multiply_convert_fusion.refs_0_), channel_id=1, source_target_pairs={{0,8},{8,0},{16,24},{24,16},{1,9},{9,1},{17,25},{25,17},{2,10},{10... | collective-permute-start | bytes 786440 | tf_op jit(solution)/shard_map/ppermute | solution.py:426
  153.0 11.1 %collective-permute-start.35 = (bf16[32,2560]{1,0:T(8,128)(2,1)S(1)}, bf16[32,2560]{1,0:T(8,128)(2,1)S(1)}, u32[]{:S(2)}, u32[]{:S(2)}) collective-permute-start(bf16[32,2560]{1,0:T(8,128)(2,1)S(1)} %get-tuple-element.147), channel_id=1, source_target_pairs={{0,4},{1,5},{2,6},{3,7},{4,0},{5,1},{6,2},{7,3},{8,12},{9,13},{10,... | collective-permute-start | bytes 491528 | tf_op jit(solution)/shard_map/ppermute | solution.py:423
  164.2 8.1 %collective-permute-start.38 = (bf16[32,2560]{1,0:T(8,128)(2,1)S(1)}, bf16[32,2560]{1,0:T(8,128)(2,1)S(1)}, u32[]{:S(2)}, u32[]{:S(2)}) collective-permute-start(bf16[32,2560]{1,0:T(8,128)(2,1)S(1)} %add_convert_fusion.refs_0_), channel_id=1, source_target_pairs={{0,24},{8,16},{16,8},{24,0},{1,25},{9,17},{17,9},{25,1},{2,26},{10... | collective-permute-start | bytes 491528 | tf_op jit(solution)/shard_map/ppermute | solution.py:426
  165.6 9.1 %collective-permute-start.37 = (bf16[32,2560]{1,0:T(8,128)(2,1)S(1)}, bf16[32,2560]{1,0:T(8,128)(2,1)S(1)}, u32[]{:S(2)}, u32[]{:S(2)}) collective-permute-start(bf16[32,2560]{1,0:T(8,128)(2,1)S(1)} %add_convert_fusion.refs_0_), channel_id=1, source_target_pairs={{0,16},{8,24},{16,0},{24,8},{1,17},{9,25},{17,1},{25,9},{2,18},{10... | collective-permute-start | bytes 491528 | tf_op jit(solution)/shard_map/ppermute | solution.py:426
  167.1 7.7 %collective-permute-start.36 = (bf16[32,2560]{1,0:T(8,128)(2,1)S(1)}, bf16[32,2560]{1,0:T(8,128)(2,1)S(1)}, u32[]{:S(2)}, u32[]{:S(2)}) collective-permute-start(bf16[32,2560]{1,0:T(8,128)(2,1)S(1)} %add_convert_fusion.refs_0_), channel_id=1, source_target_pairs={{0,8},{8,0},{16,24},{24,16},{1,9},{9,1},{17,25},{25,17},{2,10},{10... | collective-permute-start | bytes 491528 | tf_op jit(solution)/shard_map/ppermute | solution.py:426
  (27 other events, 276.6 us)

commit v12 on v11

--- a/solution.py
+++ b/solution.py
@@ -508,9 +508,8 @@
     )
 
     all_tags = [to_group(tags, k) if k else tags for k in range(groups)]
-    far = [far_give, to_core(up_give), None, far_gated]
-    grad, far[1], all_tags = lax.optimization_barrier((grad, far[1], all_tags))
-    far[2] = to_core(grad)
+    far = [far_give, to_core(up_give), to_core(grad), far_gated]
+    far[1], all_tags = lax.optimization_barrier((far[1], all_tags))
     mine, other = call(
         lambda *refs: item_kernel(groups, owners, share, chunks, [p[:3] for p in unit_sent], *refs),
         [((chips * share, width), b16)] * 2, [ANY] * len(units) + [VMEM] * groups + [ANY] * len(near),
@@ -574,7 +573,7 @@
             sum_kernel, [((chips // 2 * fine, 5 * hidden), b16)] * 2, [VMEM] * 5, [base] + arrived,
             flops=chips * fine * 5 * hidden, nbytes=40 * chips * fine * hidden, room=10,
         )
-        line = finish(*fold(low, high, totals))
+        line = finish(*fold(low, high, totals[1]))
     else:
         blocks = [lax.dynamic_index_in_dim(sums, (chip + d) % chips, 0, False).astype(b16) for d in range(chips)]
         line = blocks[0].astype(f32)

time: 177 us -> 173 us (0.977)
  waiting for transfers between devices: 77.7 us -> 74.5 us
    ppermute x7, waiting for transfers between devices: 37.6 us -> 35.1 us  [across(): return lax.ppermute(x, 'seq', pairs)]
  transfers between devices with their start and end apart: 40 -> 40, of which waited for: 21 -> 20; matrix products, arithmetic and copies ran while one was open for 2% -> 2% of each run, Pallas kernels for 15% -> 16%
where the time goes in v12:
time: 173 us; the launch traced here: 172 us
  waiting for transfers between devices  74.5 us (43%)
  starting transfers between devices  44.1 us (25%)
  Pallas kernels  42.6 us (25%)
  local copies, waits for them, and re-layouts  8.83 us (5%)
    pallas_call x13, Pallas kernels, call(): pl.pallas_call(kernel, out_shape=[jax.ShapeDtypeStruct(s, t) for s, t in...  42.6 us
    ppermute x21, waiting for transfers between devices, to_group(): return lax.ppermute(x, 'grp', [(a, a ^ k) for a in range(groups)])  38.1 us
    ppermute x7, waiting for transfers between devices, across(): return lax.ppermute(x, 'seq', pairs)  35.1 us
    ppermute x21, starting transfers between devices, to_group(): return lax.ppermute(x, 'grp', [(a, a ^ k) for a in range(groups)])  24 us
    ppermute x7, starting transfers between devices, across(): return lax.ppermute(x, 'seq', pairs)  13.4 us
    unnamed x40, local copies, waits for them, and re-layouts  5.93 us
    all_to_all x1, starting transfers between devices, body(): lax.all_to_all(outgoing.reshape(owners, slot, width), 'seq', 0, 0, tiled=...  4.88 us
  transfers between devices with their start and end apart: 40, of which 20 were waited for; matrix products, arithmetic and copies ran while one was open for 2% of the time, Pallas kernels for 16%

profile of v12, /device:TPU:0, one launch (start us, length us, event | category | flops | bytes accessed | tf_op | source)
XLA Modules:
  0.0 172.1 jit_solution(2411219765947633602)
XLA Ops:
  1.9 1.4 shard_map.112
  3.2 4.0 %collective-permute-start = (bf16[128,1024]{1,0:T(8,128)(2,1)S(1)}, bf16[128,1024]{1,0:T(8,128)(2,1)}, u32[]{:S(2)}, u32[]{:S(2)}) collective-permute-start(bf16[128,1024]{1,0:T(8,128)(2,1)S(1)} %get-tuple-element.77), channel_id=1, source_target_pairs={{0,4},{1,5},{2,6},{3,7},{4,0},{5,1},{6,2},{7,3},{8,12},{9,13},{10,... | collective-permute-start | bytes 786440 | tf_op jit(solution)/shard_map/ppermute | solution.py:423
  7.3 9.1 %shard_map.111 = (bf16[256,512]{1,0:T(8,128)(2,1)}, bf16[256,512]{1,0:T(8,128)(2,1)}, bf16[256,2048]{1,0:T(8,128)(2,1)}, bf16[256,2048]{1,0:T(8,128)(2,1)}, bf16...) custom-call(s32[1,8]{1,0:T(1,128)} %refs_0_.2, ...), custom_call_target="tpu_custom_call" | custom-call | tf_op jit(solution)/shard_map/pallas_call | solution.py:53
  16.4 1.5 collective-permute-start.4
  17.9 1.5 collective-permute-start.3
  19.4 1.6 collective-permute-start.1
  21.4 7.2 %collective-permute-done.1 = bf16[128,1024]{1,0:T(8,128)(2,1)S(1)} collective-permute-done((bf16[128,1024]{1,0:T(8,128)(2,1)S(1)}, bf16[128,1024]{1,0:T(8,128)(2,1)S(1)}, u32[]{:S(2)}, u32[]{:S(2)}) %collective-permute-start.1) | collective-permute-done | bytes 262176 | tf_op jit(solution)/shard_map/ppermute | solution.py:423
  28.6 3.6 %collective-permute-done.2 = bf16[128,1024]{1,0:T(8,128)(2,1)S(1)} collective-permute-done((bf16[128,1024]{1,0:T(8,128)(2,1)}, bf16[128,1024]{1,0:T(8,128)(2,1)S(1)}, u32[]{:S(2)}, u32[]{:S(2)}) %collective-permute-start.2) | collective-permute-done | bytes 262176 | tf_op jit(solution)/shard_map/ppermute | solution.py:423
  34.8 4.9 %all-to-all-start = ((bf16[8,48,1024]{2,1,0:T(8,128)(2,1)}), bf16[8,48,1024]{2,1,0:T(8,128)(2,1)}, u32[]{:S(2)}, u32[]{:S(2)}) async-start(bf16[8,48,1024]{2,1,0:T(8,128)(2,1)} %bitcast.3), calls=%async_computation | async-start | bytes 1572864 | tf_op jit(solution)/shard_map/all_to_all | solution.py:488
  42.4 8.8 %collective-permute-done.10.refs_8_ = bf16[384,1024]{1,0:T(8,128)(2,1)} collective-permute-done((bf16[384,1024]{1,0:T(8,128)(2,1)S(1)}, bf16[384,1024]{1,0:T(8,128)(2,1)}, u32[]{:S(2)}, u32[]{:S(2)}) %collective-permute-start.10) | collective-permute-done | bytes 786464 | tf_op jit(solution)/shard_map/ppermute | solution.py:426
  51.1 3.0 %collective-permute-done.9.refs_7_ = bf16[384,1024]{1,0:T(8,128)(2,1)} collective-permute-done((bf16[384,1024]{1,0:T(8,128)(2,1)S(1)}, bf16[384,1024]{1,0:T(8,128)(2,1)}, u32[]{:S(2)}, u32[]{:S(2)}) %collective-permute-start.9) | collective-permute-done | bytes 786464 | tf_op jit(solution)/shard_map/ppermute | solution.py:426
  54.2 1.5 collective-permute-start.7
  59.4 3.9 %collective-permute-done.7.refs_3_ = bf16[256,512]{1,0:T(8,128)(2,1)S(1)} collective-permute-done((bf16[256,512]{1,0:T(8,128)(2,1)S(1)}, bf16[256,512]{1,0:T(8,128)(2,1)S(1)}, u32[]{:S(2)}, u32[]{:S(2)}) %collective-permute-start.7) | collective-permute-done | bytes 262176 | tf_op jit(solution)/shard_map/ppermute | solution.py:426
  65.7 3.0 %collective-permute-done.11.refs_9_ = bf16[384,512]{1,0:T(8,128)(2,1)} collective-permute-done((bf16[384,512]{1,0:T(8,128)(2,1)S(1)}, bf16[384,512]{1,0:T(8,128)(2,1)}, u32[]{:S(2)}, u32[]{:S(2)}) %collective-permute-start.11) | collective-permute-done | bytes 393248 | tf_op jit(solution)/shard_map/ppermute | solution.py:426
  69.6 2.7 %shard_map.113 = bf16[256,1024]{1,0:T(8,128)(2,1)} custom-call(bf16[384,1024]{1,0:T(8,128)(2,1)} %bitcast.2.arrived), custom_call_target="tpu_custom_call" | custom-call | tf_op jit(solution)/shard_map/pallas_call | solution.py:53
  72.4 13.0 %shard_map.114 = (f32[16,256]{1,0:T(8,128)}, bf16[256,512]{1,0:T(8,128)(2,1)}, bf16[256,512]{1,0:T(8,128)(2,1)}, bf16[256,2048]{1,0:T(8,128)(2,1)}) custom-call(s32[256,4]{1,0:T(8,128)} %copy.15.refs_0_, f32[256,1]{1,0:T(8,128)} %get-tuple-element.92.refs_1_, f32[256,1]{1,0:T(8,128)} %get-tuple-element.93.refs_2_, ...), custom_call_target="tpu_custom_call" | custom-call | tf_op jit(solution)/shard_map/pallas_call | solution.py:53
  86.0 1.9 %collective-permute-start.22 = (f32[16,256]{1,0:T(8,128)}, f32[16,256]{1,0:T(8,128)S(1)}, u32[]{:S(2)}, u32[]{:S(2)}) collective-permute-start(f32[16,256]{1,0:T(8,128)} %get-tuple-element.113.refs_5_), channel_id=1, source_target_pairs={{0,24},{8,16},{16,8},{24,0},{1,25},{9,17},{17,9},{25,1},{2,26},{10... | collective-permute-start | bytes 49160 | tf_op jit(solution)/shard_map/ppermute | solution.py:426
  93.0 6.8 %shard_map.115 = (bf16[512,1024]{1,0:T(8,128)(2,1)}, bf16[512,1024]{1,0:T(8,128)(2,1)}) custom-call(bf16[256,1024]{1,0:T(8,128)(2,1)} %get-tuple-element.108.refs_3_.refs_0_, bf16[256,1024]{1,0:T(8,128)(2,1)} %copy-done.8, bf16[256,1024]{1,0:T(8,128)(2,1)} %copy-done.7, bf16[256,512]{1,0:T(8,128)(2,1)} %copy-done.10, bf16[256,512]{1,0:T(8,128)(2,1)} %copy-done.9, ...), custom_call_target="tpu_custom_call" | custom-call | tf_op jit(solution)/shard_map/pallas_call | solution.py:53
  99.9 5.0 %shard_map.116 = (bf16[4,32,2560]{2,1,0:T(8,128)(2,1)}, bf16[2,4,32,1280]{3,2,1,0:T(8,128)(2,1)}, bf16[2,4,32,1280]{3,2,1,0:T(8,128)(2,1)}, bf16[4,32,1280]{2,1,0:T(8,128)(2,1)}, bf16[4,32,1280]{2,1,0:T(8,128)(2,1)}) custom-call(bf16[256,512]{1,0:T(8,128)(2,1)} %get-tuple-element.90.refs_0_, bf16[256,2048]{1,0:T(8,128)(2,1)} %get-tuple-element.101.refs_1_, ...), custom_call_target="tpu_custom_call" | custom-call | flops 1342177280 | bytes 5242880 | tf_op jit(solution)/shard_map/pallas_call | solution.py:53
  107.4 1.6 collective-permute-start.27
  109.1 12.1 %collective-permute-done.27.y = bf16[256,1024]{1,0:T(8,128)(2,1)S(1)} collective-permute-done((bf16[256,1024]{1,0:T(8,128)(2,1)S(1)}, bf16[256,1024]{1,0:T(8,128)(2,1)S(1)}, u32[]{:S(2)}, u32[]{:S(2)}) %collective-permute-start.27) | collective-permute-done | bytes 524320 | tf_op jit(solution)/shard_map/ppermute | solution.py:423
  123.0 1.7 %collective-permute-start.28 = (bf16[128,1024]{1,0:T(8,128)(2,1)}, bf16[128,1024]{1,0:T(8,128)(2,1)}, u32[]{:S(2)}, u32[]{:S(2)}) collective-permute-start(bf16[128,1024]{1,0:T(8,128)(2,1)} %get-tuple-element.132), channel_id=1, source_target_pairs={{0,4},{1,5},{2,6},{3,7},{4,0},{5,1},{6,2},{7,3},{8,12},{9,13},{10,... | collective-permute-start | bytes 786440 | tf_op jit(solution)/shard_map/ppermute | solution.py:423
  127.5 1.5 collective-permute-start.29
  130.4 6.9 %collective-permute-done.28 = bf16[128,1024]{1,0:T(8,128)(2,1)} collective-permute-done((bf16[128,1024]{1,0:T(8,128)(2,1)}, bf16[128,1024]{1,0:T(8,128)(2,1)}, u32[]{:S(2)}, u32[]{:S(2)}) %collective-permute-start.28) | collective-permute-done | bytes 262176 | tf_op jit(solution)/shard_map/ppermute | solution.py:423
  140.6 6.0 %collective-permute-done.32.refs_1_ = bf16[128,1024]{1,0:T(8,128)(2,1)S(1)} collective-permute-done((bf16[128,1024]{1,0:T(8,128)(2,1)S(1)}, bf16[128,1024]{1,0:T(8,128)(2,1)S(1)}, u32[]{:S(2)}, u32[]{:S(2)}) %collective-permute-start.32) | collective-permute-done | bytes 262176 | tf_op jit(solution)/shard_map/ppermute | solution.py:426
  147.4 2.7 %collective-permute-start.33 = (bf16[32,2560]{1,0:T(8,128)(2,1)S(1)}, bf16[32,2560]{1,0:T(8,128)(2,1)S(1)}, u32[]{:S(2)}, u32[]{:S(2)}) collective-permute-start(bf16[32,2560]{1,0:T(8,128)(2,1)S(1)} %get-tuple-element.145), channel_id=1, source_target_pairs={{0,4},{1,5},{2,6},{3,7},{4,0},{5,1},{6,2},{7,3},{8,12},{9,13},{10,... | collective-permute-start | bytes 491528 | tf_op jit(solution)/shard_map/ppermute | solution.py:423
  150.1 2.2 %collective-permute-start.38 = (bf16[128,1024]{1,0:T(8,128)(2,1)S(1)}, bf16[128,1024]{1,0:T(8,128)(2,1)S(1)}, u32[]{:S(2)}, u32[]{:S(2)}) collective-permute-start(bf16[128,1024]{1,0:T(8,128)(2,1)S(1)} %multiply_convert_fusion.refs_0_), channel_id=1, source_target_pairs={{0,24},{8,16},{16,8},{24,0},{1,25},{9,17},{17,9},{25,1},{2,26},{10... | collective-permute-start | bytes 786440 | tf_op jit(solution)/shard_map/ppermute | solution.py:426
  153.0 4.4 %collective-permute-done.33 = bf16[32,2560]{1,0:T(8,128)(2,1)S(1)} collective-permute-done((bf16[32,2560]{1,0:T(8,128)(2,1)S(1)}, bf16[32,2560]{1,0:T(8,128)(2,1)S(1)}, u32[]{:S(2)}, u32[]{:S(2)}) %collective-permute-start.33) | collective-permute-done | bytes 163872 | tf_op jit(solution)/shard_map/ppermute | solution.py:423
  157.4 2.3 %collective-permute-start.36 = (bf16[32,2560]{1,0:T(8,128)(2,1)S(1)}, bf16[32,2560]{1,0:T(8,128)(2,1)S(1)}, u32[]{:S(2)}, u32[]{:S(2)}) collective-permute-start(bf16[32,2560]{1,0:T(8,128)(2,1)S(1)} %add_convert_fusion.refs_0_), channel_id=1, source_target_pairs={{0,24},{8,16},{16,8},{24,0},{1,25},{9,17},{17,9},{25,1},{2,26},{10... | collective-permute-start | bytes 491528 | tf_op jit(solution)/shard_map/ppermute | solution.py:426
  161.0 6.6 %collective-permute-done.37.refs_2_ = bf16[128,1024]{1,0:T(8,128)(2,1)S(1)} collective-permute-done((bf16[128,1024]{1,0:T(8,128)(2,1)S(1)}, bf16[128,1024]{1,0:T(8,128)(2,1)S(1)}, u32[]{:S(2)}, u32[]{:S(2)}) %collective-permute-start.37) | collective-permute-done | bytes 262176 | tf_op jit(solution)/shard_map/ppermute | solution.py:426
  167.6 1.5 shard_map.123
  169.0 1.9 %collective-permute-done.35.refs_2_ = bf16[32,2560]{1,0:T(8,128)(2,1)S(1)} collective-permute-done((bf16[32,2560]{1,0:T(8,128)(2,1)S(1)}, bf16[32,2560]{1,0:T(8,128)(2,1)S(1)}, u32[]{:S(2)}, u32[]{:S(2)}) %collective-permute-start.35) | collective-permute-done | bytes 163872 | tf_op jit(solution)/shard_map/ppermute | solution.py:426
  (111 shorter events, 35.4 us)
Async XLA Ops:
  3.2 17.7 %collective-permute-start = (bf16[128,1024]{1,0:T(8,128)(2,1)S(1)}, bf16[128,1024]{1,0:T(8,128)(2,1)}, u32[]{:S(2)}, u32[]{:S(2)}) collective-permute-start(bf16[128,1024]{1,0:T(8,128)(2,1)S(1)} %get-tuple-element.77), channel_id=1, source_target_pairs={{0,4},{1,5},{2,6},{3,7},{4,0},{5,1},{6,2},{7,3},{8,12},{9,13},{10,... | collective-permute-start | bytes 786440 | tf_op jit(solution)/shard_map/ppermute | solution.py:423
  16.4 15.8 %collective-permute-start.4 = (bf16[256,1024]{1,0:T(8,128)(2,1)}, bf16[256,1024]{1,0:T(8,128)(2,1)S(1)}, u32[]{:S(2)}, u32[]{:S(2)}) collective-permute-start(bf16[256,1024]{1,0:T(8,128)(2,1)} %get-tuple-element.108.refs_3_.refs_0_), channel_id=1, source_target_pairs={{0,16},{8,24},{16,0},{24,8},{1,17},{9,25},{17,1},{25,9},{2,18},{10... | collective-permute-start | bytes 1572872 | tf_op jit(solution)/shard_map/ppermute | solution.py:426
  17.9 14.3 %collective-permute-start.3 = (bf16[256,1024]{1,0:T(8,128)(2,1)}, bf16[256,1024]{1,0:T(8,128)(2,1)S(1)}, u32[]{:S(2)}, u32[]{:S(2)}) collective-permute-start(bf16[256,1024]{1,0:T(8,128)(2,1)} %get-tuple-element.108.refs_3_.refs_0_), channel_id=1, source_target_pairs={{0,8},{8,0},{16,24},{24,16},{1,9},{9,1},{17,25},{25,17},{2,10},{10... | collective-permute-start | bytes 1572872 | tf_op jit(solution)/shard_map/ppermute | solution.py:426
  19.4 9.2 %collective-permute-start.1 = (bf16[128,1024]{1,0:T(8,128)(2,1)S(1)}, bf16[128,1024]{1,0:T(8,128)(2,1)S(1)}, u32[]{:S(2)}, u32[]{:S(2)}) collective-permute-start(bf16[128,1024]{1,0:T(8,128)(2,1)S(1)} %get-tuple-element.77), channel_id=1, source_target_pairs={{0,2},{1,3},{2,0},{3,1},{4,6},{5,7},{6,4},{7,5},{8,10},{9,11},{10,... | collective-permute-start | bytes 786440 | tf_op jit(solution)/shard_map/ppermute | solution.py:423
  20.9 11.2 %collective-permute-start.2 = (bf16[128,1024]{1,0:T(8,128)(2,1)}, bf16[128,1024]{1,0:T(8,128)(2,1)S(1)}, u32[]{:S(2)}, u32[]{:S(2)}) collective-permute-start(bf16[128,1024]{1,0:T(8,128)(2,1)} %collective-permute-done), channel_id=1, source_target_pairs={{0,2},{1,3},{2,0},{3,1},{4,6},{5,7},{6,4},{7,5},{8,10},{9,11},{10,... | collective-permute-start | bytes 786440 | tf_op jit(solution)/shard_map/ppermute | solution.py:423
  33.4 17.7 %collective-permute-start.10 = (bf16[384,1024]{1,0:T(8,128)(2,1)S(1)}, bf16[384,1024]{1,0:T(8,128)(2,1)}, u32[]{:S(2)}, u32[]{:S(2)}) collective-permute-start(bf16[384,1024]{1,0:T(8,128)(2,1)S(1)} %constant_dynamic-update-slice_fusion.refs_6_.refs_10_), channel_id=1, source_target_pairs={{0,16},{8,24},{16,0},{24,8},{1,17},{9,25},{17,1},{25,9},{2,18},{10... | collective-permute-start | bytes 2359304 | tf_op jit(solution)/shard_map/ppermute | solution.py:426
  34.0 20.2 %collective-permute-start.9 = (bf16[384,1024]{1,0:T(8,128)(2,1)S(1)}, bf16[384,1024]{1,0:T(8,128)(2,1)}, u32[]{:S(2)}, u32[]{:S(2)}) collective-permute-start(bf16[384,1024]{1,0:T(8,128)(2,1)S(1)} %constant_dynamic-update-slice_fusion.refs_6_.refs_10_), channel_id=1, source_target_pairs={{0,8},{8,0},{16,24},{24,16},{1,9},{9,1},{17,25},{25,17},{2,10},{10... | collective-permute-start | bytes 2359304 | tf_op jit(solution)/shard_map/ppermute | solution.py:426
  34.8 28.5 %collective-permute-start.14 = (bf16[384,1024]{1,0:T(8,128)(2,1)S(1)}, bf16[384,1024]{1,0:T(8,128)(2,1)S(1)}, u32[]{:S(2)}, u32[]{:S(2)}) collective-permute-start(bf16[384,1024]{1,0:T(8,128)(2,1)S(1)} %constant_dynamic-update-slice_fusion.refs_6_.refs_10_), channel_id=1, source_target_pairs={{0,1},{1,0},{2,3},{3,2},{4,5},{5,4},{6,7},{7,6},{8,9},{9,8},{10,11... | collective-permute-start | bytes 2359304 | tf_op jit(solution)/shard_map/ppermute | solution.py:429
  34.8 34.8 %all-to-all-start = ((bf16[8,48,1024]{2,1,0:T(8,128)(2,1)}), bf16[8,48,1024]{2,1,0:T(8,128)(2,1)}, u32[]{:S(2)}, u32[]{:S(2)}) async-start(bf16[8,48,1024]{2,1,0:T(8,128)(2,1)} %bitcast.3), calls=%async_computation | async-start | bytes 1572864 | tf_op jit(solution)/shard_map/all_to_all | solution.py:488
  40.2 17.5 %collective-permute-start.6 = (bf16[256,512]{1,0:T(8,128)(2,1)}, bf16[256,512]{1,0:T(8,128)(2,1)S(1)}, u32[]{:S(2)}, u32[]{:S(2)}) collective-permute-start(bf16[256,512]{1,0:T(8,128)(2,1)} %get-tuple-element.86.refs_3_), channel_id=1, source_target_pairs={{0,1},{1,0},{2,3},{3,2},{4,5},{5,4},{6,7},{7,6},{8,9},{9,8},{10,11... | collective-permute-start | bytes 786440 | tf_op jit(solution)/shard_map/ppermute | solution.py:429
  41.6 17.0 %collective-permute-start.8 = (bf16[256,512]{1,0:T(8,128)(2,1)S(1)}, bf16[256,512]{1,0:T(8,128)(2,1)S(1)}, u32[]{:S(2)}, u32[]{:S(2)}) collective-permute-start(bf16[256,512]{1,0:T(8,128)(2,1)S(1)} %slice.13), channel_id=1, source_target_pairs={{0,8},{8,0},{16,24},{24,16},{1,9},{9,1},{17,25},{25,17},{2,10},{10... | collective-permute-start | bytes 786440 | tf_op jit(solution)/shard_map/ppermute | solution.py:426
  51.1 21.2 %collective-permute-start.13 = (bf16[512,1024]{1,0:T(8,128)(2,1)}, bf16[512,1024]{1,0:T(8,128)(2,1)}, u32[]{:S(2)}, u32[]{:S(2)}) collective-permute-start(bf16[512,1024]{1,0:T(8,128)(2,1)} %get-tuple-element.95.refs_5_.refs_9_), channel_id=1, source_target_pairs={{0,1},{1,0},{2,3},{3,2},{4,5},{5,4},{6,7},{7,6},{8,9},{9,8},{10,11... | collective-permute-start | bytes 3145736 | tf_op jit(solution)/shard_map/ppermute | solution.py:429
  54.2 9.1 %collective-permute-start.7 = (bf16[256,512]{1,0:T(8,128)(2,1)S(1)}, bf16[256,512]{1,0:T(8,128)(2,1)S(1)}, u32[]{:S(2)}, u32[]{:S(2)}) collective-permute-start(bf16[256,512]{1,0:T(8,128)(2,1)S(1)} %slice.12), channel_id=1, source_target_pairs={{0,16},{8,24},{16,0},{24,8},{1,17},{9,25},{17,1},{25,9},{2,18},{10... | collective-permute-start | bytes 786440 | tf_op jit(solution)/shard_map/ppermute | solution.py:426
  57.8 7.9 %collective-permute-start.12 = (bf16[384,512]{1,0:T(8,128)(2,1)S(1)}, bf16[384,512]{1,0:T(8,128)(2,1)}, u32[]{:S(2)}, u32[]{:S(2)}) collective-permute-start(bf16[384,512]{1,0:T(8,128)(2,1)S(1)} %slice.17), channel_id=1, source_target_pairs={{0,8},{8,0},{16,24},{24,16},{1,9},{9,1},{17,25},{25,17},{2,10},{10... | collective-permute-start | bytes 1179656 | tf_op jit(solution)/shard_map/ppermute | solution.py:426
  58.6 10.2 %collective-permute-start.11 = (bf16[384,512]{1,0:T(8,128)(2,1)S(1)}, bf16[384,512]{1,0:T(8,128)(2,1)}, u32[]{:S(2)}, u32[]{:S(2)}) collective-permute-start(bf16[384,512]{1,0:T(8,128)(2,1)S(1)} %slice.16), channel_id=1, source_target_pairs={{0,16},{8,24},{16,0},{24,8},{1,17},{9,25},{17,1},{25,9},{2,18},{10... | collective-permute-start | bytes 1179656 | tf_op jit(solution)/shard_map/ppermute | solution.py:426
  63.3 9.1 %collective-permute-start.16 = (bf16[384,1024]{1,0:T(8,128)(2,1)}, bf16[384,1024]{1,0:T(8,128)(2,1)}, u32[]{:S(2)}, u32[]{:S(2)}) collective-permute-start(bf16[384,1024]{1,0:T(8,128)(2,1)} %collective-permute-done.10.refs_8_), channel_id=1, source_target_pairs={{0,1},{1,0},{2,3},{3,2},{4,5},{5,4},{6,7},{7,6},{8,9},{9,8},{10,11... | collective-permute-start | bytes 2359304 | tf_op jit(solution)/shard_map/ppermute | solution.py:429
  64.2 8.1 %collective-permute-start.15 = (bf16[384,1024]{1,0:T(8,128)(2,1)}, bf16[384,1024]{1,0:T(8,128)(2,1)}, u32[]{:S(2)}, u32[]{:S(2)}) collective-permute-start(bf16[384,1024]{1,0:T(8,128)(2,1)} %collective-permute-done.9.refs_7_), channel_id=1, source_target_pairs={{0,1},{1,0},{2,3},{3,2},{4,5},{5,4},{6,7},{7,6},{8,9},{9,8},{10,11... | collective-permute-start | bytes 2359304 | tf_op jit(solution)/shard_map/ppermute | solution.py:429
  85.9 14.0 %collective-permute-start.23 = (bf16[256,2048]{1,0:T(8,128)(2,1)}, bf16[256,2048]{1,0:T(8,128)(2,1)}, u32[]{:S(2)}, u32[]{:S(2)}) collective-permute-start(bf16[256,2048]{1,0:T(8,128)(2,1)} %get-tuple-element.101.refs_1_), channel_id=1, source_target_pairs={{0,1},{1,0},{2,3},{3,2},{4,5},{5,4},{6,7},{7,6},{8,9},{9,8},{10,11... | collective-permute-start | bytes 3145736 | tf_op jit(solution)/shard_map/ppermute | solution.py:429
  99.8 7.4 %collective-permute-start.26 = (bf16[512,1024]{1,0:T(8,128)(2,1)}, bf16[512,1024]{1,0:T(8,128)(2,1)S(1)}, u32[]{:S(2)}, u32[]{:S(2)}) collective-permute-start(bf16[512,1024]{1,0:T(8,128)(2,1)} %get-tuple-element.126), channel_id=1, source_target_pairs={{0,1},{1,0},{2,3},{3,2},{4,5},{5,4},{6,7},{7,6},{8,9},{9,8},{10,11... | collective-permute-start | bytes 3145736 | tf_op jit(solution)/shard_map/ppermute | solution.py:429
  104.8 17.4 %collective-permute-start.24 = (bf16[2,4,32,1280]{3,2,1,0:T(8,128)(2,1)}, bf16[2,4,32,1280]{3,2,1,0:T(8,128)(2,1)S(1)}, u32[]{:S(2)}, u32[]{:S(2)}) collective-permute-start(bf16[2,4,32,1280]{3,2,1,0:T(8,128)(2,1)} %get-tuple-element.123), channel_id=1, source_target_pairs={{0,8},{8,0},{16,24},{24,16},{1,9},{9,1},{17,25},{25,17},{2,10},{10... | collective-permute-start | bytes 1966088 | tf_op jit(solution)/shard_map/ppermute | solution.py:426
  105.9 17.0 %collective-permute-start.25 = (bf16[2,4,32,1280]{3,2,1,0:T(8,128)(2,1)}, bf16[2,4,32,1280]{3,2,1,0:T(8,128)(2,1)S(1)}, u32[]{:S(2)}, u32[]{:S(2)}) collective-permute-start(bf16[2,4,32,1280]{3,2,1,0:T(8,128)(2,1)} %get-tuple-element.124), channel_id=1, source_target_pairs={{0,16},{8,24},{16,0},{24,8},{1,17},{9,25},{17,1},{25,9},{2,18},{10... | collective-permute-start | bytes 1966088 | tf_op jit(solution)/shard_map/ppermute | solution.py:426
  107.4 13.8 %collective-permute-start.27 = (bf16[256,1024]{1,0:T(8,128)(2,1)S(1)}, bf16[256,1024]{1,0:T(8,128)(2,1)S(1)}, u32[]{:S(2)}, u32[]{:S(2)}) collective-permute-start(bf16[256,1024]{1,0:T(8,128)(2,1)S(1)} %get-tuple-element.128), channel_id=1, source_target_pairs={{0,2},{1,3},{2,0},{3,1},{4,6},{5,7},{6,4},{7,5},{8,10},{9,11},{10,... | collective-permute-start | bytes 1572872 | tf_op jit(solution)/shard_map/ppermute | solution.py:423
  123.0 14.4 %collective-permute-start.28 = (bf16[128,1024]{1,0:T(8,128)(2,1)}, bf16[128,1024]{1,0:T(8,128)(2,1)}, u32[]{:S(2)}, u32[]{:S(2)}) collective-permute-start(bf16[128,1024]{1,0:T(8,128)(2,1)} %get-tuple-element.132), channel_id=1, source_target_pairs={{0,4},{1,5},{2,6},{3,7},{4,0},{5,1},{6,2},{7,3},{8,12},{9,13},{10,... | collective-permute-start | bytes 786440 | tf_op jit(solution)/shard_map/ppermute | solution.py:423
  127.5 10.9 %collective-permute-start.29 = (bf16[4,32,1280]{2,1,0:T(8,128)(2,1)}, bf16[4,32,1280]{2,1,0:T(8,128)(2,1)S(1)}, u32[]{:S(2)}, u32[]{:S(2)}) collective-permute-start(bf16[4,32,1280]{2,1,0:T(8,128)(2,1)} %get-tuple-element.139), channel_id=1, source_target_pairs={{0,8},{8,0},{16,24},{24,16},{1,9},{9,1},{17,25},{25,17},{2,10},{10... | collective-permute-start | bytes 983048 | tf_op jit(solution)/shard_map/ppermute | solution.py:426
  128.9 9.5 %collective-permute-start.30 = (bf16[4,32,1280]{2,1,0:T(8,128)(2,1)S(1)}, bf16[4,32,1280]{2,1,0:T(8,128)(2,1)S(1)}, u32[]{:S(2)}, u32[]{:S(2)}) collective-permute-start(bf16[4,32,1280]{2,1,0:T(8,128)(2,1)S(1)} %get-tuple-element.140), channel_id=1, source_target_pairs={{0,16},{8,24},{16,0},{24,8},{1,17},{9,25},{17,1},{25,9},{2,18},{10... | collective-permute-start | bytes 983048 | tf_op jit(solution)/shard_map/ppermute | solution.py:426
  138.7 8.7 %collective-permute-start.31 = (bf16[64,2560]{1,0:T(8,128)(2,1)S(1)}, bf16[64,2560]{1,0:T(8,128)(2,1)S(1)}, u32[]{:S(2)}, u32[]{:S(2)}) collective-permute-start(bf16[64,2560]{1,0:T(8,128)(2,1)S(1)} %get-tuple-element.142), channel_id=1, source_target_pairs={{0,2},{1,3},{2,0},{3,1},{4,6},{5,7},{6,4},{7,5},{8,10},{9,11},{10,... | collective-permute-start | bytes 983048 | tf_op jit(solution)/shard_map/ppermute | solution.py:423
  147.4 10.0 %collective-permute-start.33 = (bf16[32,2560]{1,0:T(8,128)(2,1)S(1)}, bf16[32,2560]{1,0:T(8,128)(2,1)S(1)}, u32[]{:S(2)}, u32[]{:S(2)}) collective-permute-start(bf16[32,2560]{1,0:T(8,128)(2,1)S(1)} %get-tuple-element.145), channel_id=1, source_target_pairs={{0,4},{1,5},{2,6},{3,7},{4,0},{5,1},{6,2},{7,3},{8,12},{9,13},{10,... | collective-permute-start | bytes 491528 | tf_op jit(solution)/shard_map/ppermute | solution.py:423
  150.1 10.9 %collective-permute-start.38 = (bf16[128,1024]{1,0:T(8,128)(2,1)S(1)}, bf16[128,1024]{1,0:T(8,128)(2,1)S(1)}, u32[]{:S(2)}, u32[]{:S(2)}) collective-permute-start(bf16[128,1024]{1,0:T(8,128)(2,1)S(1)} %multiply_convert_fusion.refs_0_), channel_id=1, source_target_pairs={{0,24},{8,16},{16,8},{24,0},{1,25},{9,17},{17,9},{25,1},{2,26},{10... | collective-permute-start | bytes 786440 | tf_op jit(solution)/shard_map/ppermute | solution.py:426
  152.3 15.3 %collective-permute-start.37 = (bf16[128,1024]{1,0:T(8,128)(2,1)S(1)}, bf16[128,1024]{1,0:T(8,128)(2,1)S(1)}, u32[]{:S(2)}, u32[]{:S(2)}) collective-permute-start(bf16[128,1024]{1,0:T(8,128)(2,1)S(1)} %multiply_convert_fusion.refs_0_), channel_id=1, source_target_pairs={{0,16},{8,24},{16,0},{24,8},{1,17},{9,25},{17,1},{25,9},{2,18},{10... | collective-permute-start | bytes 786440 | tf_op jit(solution)/shard_map/ppermute | solution.py:426
  157.4 11.6 %collective-permute-start.36 = (bf16[32,2560]{1,0:T(8,128)(2,1)S(1)}, bf16[32,2560]{1,0:T(8,128)(2,1)S(1)}, u32[]{:S(2)}, u32[]{:S(2)}) collective-permute-start(bf16[32,2560]{1,0:T(8,128)(2,1)S(1)} %add_convert_fusion.refs_0_), channel_id=1, source_target_pairs={{0,24},{8,16},{16,8},{24,0},{1,25},{9,17},{17,9},{25,1},{2,26},{10... | collective-permute-start | bytes 491528 | tf_op jit(solution)/shard_map/ppermute | solution.py:426
  159.7 11.3 %collective-permute-start.35 = (bf16[32,2560]{1,0:T(8,128)(2,1)S(1)}, bf16[32,2560]{1,0:T(8,128)(2,1)S(1)}, u32[]{:S(2)}, u32[]{:S(2)}) collective-permute-start(bf16[32,2560]{1,0:T(8,128)(2,1)S(1)} %add_convert_fusion.refs_0_), channel_id=1, source_target_pairs={{0,16},{8,24},{16,0},{24,8},{1,17},{9,25},{17,1},{25,9},{2,18},{10... | collective-permute-start | bytes 491528 | tf_op jit(solution)/shard_map/ppermute | solution.py:426
  160.4 10.6 %collective-permute-start.34 = (bf16[32,2560]{1,0:T(8,128)(2,1)S(1)}, bf16[32,2560]{1,0:T(8,128)(2,1)S(1)}, u32[]{:S(2)}, u32[]{:S(2)}) collective-permute-start(bf16[32,2560]{1,0:T(8,128)(2,1)S(1)} %add_convert_fusion.refs_0_), channel_id=1, source_target_pairs={{0,8},{8,0},{16,24},{24,16},{1,9},{9,1},{17,25},{25,17},{2,10},{10... | collective-permute-start | bytes 491528 | tf_op jit(solution)/shard_map/ppermute | solution.py:426
  (27 other events, 275.3 us)

commit v13 on v12

--- a/solution.py
+++ b/solution.py
@@ -316,7 +316,7 @@
 
 
 def weight_kernel(groups, owners, *refs):
-    given, outs, loaded, (own, whole, sems) = refs[:8], refs[8:13], refs[13:21], refs[21:]
+    given, outs, loaded, (own, whole, sems) = refs[:8], refs[8:15], refs[15:23], refs[23:]
     copies = [pltpu.make_async_copy(x, y, sems.at[n]) for n, (x, y) in enumerate(zip(given, loaded))]
     for copy in copies:
         copy.start()
@@ -341,29 +341,31 @@
     rows = whole.shape[0] // chips
     fine = rows // groups
     half = whole.shape[1] // 2
-    base, by_one, by_two, one_right, two_left = outs
+    base = outs[0]
     for z in range(chips):
-        piece = [whole[pl.ds(pl.multiple_of(z * rows + (grp ^ k) * fine, fine), fine)] for k in range(groups)]
-        base[z] = piece[0]
-        by_one[0, z], by_one[1, z] = piece[3][:, :half], piece[1][:, :half]
-        by_two[0, z], by_two[1, z] = piece[3][:, half:], piece[2][:, half:]
-        one_right[z], two_left[z] = piece[1][:, half:], piece[2][:, :half]
-
-
-def corner_kernel(by_one, by_two, one_right, two_left, right_out, left_out):
-    right_out[...] = (one_right[...].astype(f32) + by_two[0].astype(f32)).astype(b16)
-    left_out[...] = (two_left[...].astype(f32) + by_one[0].astype(f32)).astype(b16)
-
-
-def sum_kernel(base, by_one, by_two, one_right, two_left, *outs):
+        for k in range(groups):
+            piece = whole[pl.ds(pl.multiple_of(z * rows + (grp ^ k) * fine, fine), fine)]
+            if k == 0:
+                base[z] = piece
+            else:
+                outs[2 * k - 1][z] = piece[:, :half]
+                outs[2 * k][z] = piece[:, half:]
+
+
+def corner_kernel(left, right, one_right, two_left, right_out, left_out):
+    right_out[...] = (one_right[...].astype(f32) + right[...].astype(f32)).astype(b16)
+    left_out[...] = (two_left[...].astype(f32) + left[...].astype(f32)).astype(b16)
+
+
+def sum_kernel(base, one_left, one_right, two_left, two_right, *outs):
     chips, fine, wide = base.shape
     chip = lax.axis_index("seq") // 2
     half = wide // 2
     for n, d in enumerate(distances(chips)):
         z = chip ^ d
         own = base[z].astype(f32)
-        left = own[:, :half] + by_one[1, z].astype(f32) + two_left[z].astype(f32)
-        right = own[:, half:] + by_two[1, z].astype(f32) + one_right[z].astype(f32)
+        left = own[:, :half] + one_left[z].astype(f32) + two_left[z].astype(f32)
+        right = own[:, half:] + two_right[z].astype(f32) + one_right[z].astype(f32)
         out = outs[2 * n // chips]
         at = slice(n % (chips // 2) * fine, (n % (chips // 2) + 1) * fine)
         out[at, :half] = left.astype(b16)
@@ -509,7 +511,42 @@
 
     all_tags = [to_group(tags, k) if k else tags for k in range(groups)]
     far = [far_give, to_core(up_give), to_core(grad), far_gated]
-    far[1], all_tags = lax.optimization_barrier((far[1], all_tags))
+    far, all_tags = lax.optimization_barrier((far, all_tags))
+    half = 5 * hidden // 2
+    if groups == 4:
+        block = (chips, fine, 5 * hidden)
+        split = (chips, fine, half)
+        parts = call(
+            lambda *refs: weight_kernel(groups, owners, *refs),
+            [(block, b16)] + [(split, b16)] * 6, [ANY] * 8,
+            [keep, grad, up_keep, gated, far[1], far[3], far[0], far[2]],
+            [pltpu.VMEM(x.shape, b16) for x in (keep, grad, up_keep, gated, up_keep, gated, keep, grad)]
+            + [pltpu.VMEM((width // 2, 4 * hidden), f32), pltpu.VMEM((width // 2, 5 * hidden), b16),
+               pltpu.SemaphoreType.DMA((8,))],
+            flops=2 * tok * width * 5 * hidden, nbytes=20 * tok * width, room=60,
+        )
+        left, right = to_group(parts[5], 1), to_group(parts[6], 2)
+        one_left, two_right = to_group(parts[1], 1), to_group(parts[4], 2)
+        one_right, two_left = call(
+            corner_kernel, [(split, b16)] * 2, [VMEM] * 4, [left, right, parts[2], parts[3]], room=8,
+        )
+        arrived = [one_left, to_group(one_right, 1), to_group(two_left, 2), two_right]
+        after = one_right
+    else:
+        def both(x, y):
+            return jnp.concatenate([x, y], 0)
+
+        in_part = dot(both(keep, far[0]), both(grad, far[2]), TN)
+        out_part = dot(both(up_keep, far[1]), both(gated, far[3]), TN)
+        weight = jnp.concatenate([in_part, out_part], 1).astype(b16)
+        weight = weight.reshape(chips, groups, fine, 5 * hidden)
+        after = weight
+        sums = lax.dynamic_index_in_dim(weight, grp, 1, False).astype(f32)
+        for k in range(1, groups):
+            sums += to_group(lax.dynamic_index_in_dim(weight, grp ^ k, 1, False), k).astype(f32)
+
+
+    units[0], _ = lax.optimization_barrier((units[0], after))
     mine, other = call(
         lambda *refs: item_kernel(groups, owners, share, chunks, [p[:3] for p in unit_sent], *refs),
         [((chips * share, width), b16)] * 2, [ANY] * len(units) + [VMEM] * groups + [ANY] * len(near),
@@ -519,46 +556,12 @@
         room=63,
     )
     far_mine = to_core(other)
-    far, mine = lax.optimization_barrier((far, mine))
-    half = 5 * hidden // 2
-    if groups == 4:
-        block = (chips, fine, 5 * hidden)
-        split = (chips, fine, half)
-        parts = call(
-            lambda *refs: weight_kernel(groups, owners, *refs),
-            [(block, b16)] + [((2,) + split, b16)] * 2 + [(split, b16)] * 2, [ANY] * 8,
-            [keep, grad, up_keep, gated, far[1], far[3], far[0], far[2]],
-            [pltpu.VMEM(x.shape, b16) for x in (keep, grad, up_keep, gated, up_keep, gated, keep, grad)]
-            + [pltpu.VMEM((width // 2, 4 * hidden), f32), pltpu.VMEM((width // 2, 5 * hidden), b16),
-               pltpu.SemaphoreType.DMA((8,))],
-            flops=2 * tok * width * 5 * hidden, nbytes=20 * tok * width, room=60,
-        )
-        by_one, by_two = to_group(parts[1], 1), to_group(parts[2], 2)
-        corner = (by_one, by_two)
-    else:
-        def both(x, y):
-            return jnp.concatenate([x, y], 0)
-
-        in_part = dot(both(keep, far[0]), both(grad, far[2]), TN)
-        out_part = dot(both(up_keep, far[1]), both(gated, far[3]), TN)
-        weight = jnp.concatenate([in_part, out_part], 1).astype(b16)
-        weight = weight.reshape(chips, groups, fine, 5 * hidden)
-        sums = lax.dynamic_index_in_dim(weight, grp, 1, False).astype(f32)
-        for k in range(1, groups):
-            sums += to_group(lax.dynamic_index_in_dim(weight, grp ^ k, 1, False), k).astype(f32)
-
 
     low, high = call(
         pair_kernel, [((chips // 2 * share, width), b16)] * 2, [VMEM] * 2, [mine, far_mine],
         flops=chips * share * width, nbytes=6 * chips * share * width, room=8,
     )
     low, high = fold(low, high)
-    if groups == 4:
-        by_one, by_two, low, high = lax.optimization_barrier(corner + (low, high))
-        one_right, two_left = call(
-            corner_kernel, [(split, b16)] * 2, [VMEM] * 4, [by_one, by_two, parts[3], parts[4]], room=8,
-        )
-        arrived = [by_one, by_two, to_group(one_right, 1), to_group(two_left, 2)]
     total = finish(low, high)
     total = (total * quarter_inv).astype(b16)
     totals = [to_group(total, k) if k else total for k in range(groups)]
@@ -568,12 +571,12 @@
     )
 
     if groups == 4:
-        base, _ = lax.optimization_barrier((parts[0], total))
+        base = parts[0]
         low, high = call(
             sum_kernel, [((chips // 2 * fine, 5 * hidden), b16)] * 2, [VMEM] * 5, [base] + arrived,
             flops=chips * fine * 5 * hidden, nbytes=40 * chips * fine * hidden, room=10,
         )
-        line = finish(*fold(low, high, totals[1]))
+        line = finish(*fold(low, high))
     else:
         blocks = [lax.dynamic_index_in_dim(sums, (chip + d) % chips, 0, False).astype(b16) for d in range(chips)]
         line = blocks[0].astype(f32)

time: 173 us -> 187 us (1.081)
  waiting for transfers between devices: 74.5 us -> 88.3 us
  local copies, waits for them, and re-layouts: 8.83 us -> 11.9 us
    ppermute x21 -> x23, waiting for transfers between devices: 38.1 us -> 52.5 us  [to_group(): return lax.ppermute(x, 'grp', [(a, a ^ k) for a in range(groups)])]
    unnamed x40 -> x46, local copies, waits for them, and re-layouts: 5.93 us -> 9.02 us
    ppermute x21 -> x23, starting transfers between devices: 24 us -> 24.9 us  [to_group(): return lax.ppermute(x, 'grp', [(a, a ^ k) for a in range(groups)])]
  transfers between devices with their start and end apart: 40 -> 42, of which waited for: 20 -> 20; matrix products, arithmetic and copies ran while one was open for 2% -> 2% of each run, Pallas kernels for 16% -> 7%
where the time goes in v13:
time: 187 us; the launch traced here: 186 us
  waiting for transfers between devices  88.3 us (47%)
  starting transfers between devices  43.8 us (23%)
  Pallas kernels  41.2 us (22%)
  local copies, waits for them, and re-layouts  11.9 us (6%)
    ppermute x23, waiting for transfers between devices, to_group(): return lax.ppermute(x, 'grp', [(a, a ^ k) for a in range(groups)])  52.5 us
    pallas_call x13, Pallas kernels, call(): pl.pallas_call(kernel, out_shape=[jax.ShapeDtypeStruct(s, t) for s, t in...  41.2 us
    ppermute x7, waiting for transfers between devices, across(): return lax.ppermute(x, 'seq', pairs)  34.1 us
    ppermute x23, starting transfers between devices, to_group(): return lax.ppermute(x, 'grp', [(a, a ^ k) for a in range(groups)])  24.9 us
    ppermute x7, starting transfers between devices, across(): return lax.ppermute(x, 'seq', pairs)  12.2 us
    unnamed x46, local copies, waits for them, and re-layouts  9.02 us
    all_to_all x1, starting transfers between devices, body(): lax.all_to_all(outgoing.reshape(owners, slot, width), 'seq', 0, 0, tiled=...  4.88 us
  transfers between devices with their start and end apart: 42, of which 20 were waited for; matrix products, arithmetic and copies ran while one was open for 2% of the time, Pallas kernels for 7%

profile of v13, /device:TPU:0, one launch (start us, length us, event | category | flops | bytes accessed | tf_op | source)
XLA Modules:
  0.0 186.3 jit_solution(10621367355720022930)
XLA Ops:
  3.3 4.0 %collective-permute-start = (bf16[128,1024]{1,0:T(8,128)(2,1)S(1)}, bf16[128,1024]{1,0:T(8,128)(2,1)S(1)}, u32[]{:S(2)}, u32[]{:S(2)}) collective-permute-start(bf16[128,1024]{1,0:T(8,128)(2,1)S(1)} %get-tuple-element.72), channel_id=1, source_target_pairs={{0,4},{1,5},{2,6},{3,7},{4,0},{5,1},{6,2},{7,3},{8,12},{9,13},{10,... | collective-permute-start | bytes 786440 | tf_op jit(solution)/shard_map/ppermute | solution.py:425
  7.3 9.1 %shard_map.111 = (bf16[256,512]{1,0:T(8,128)(2,1)}, bf16[256,512]{1,0:T(8,128)(2,1)}, bf16[256,2048]{1,0:T(8,128)(2,1)}, bf16[256,2048]{1,0:T(8,128)(2,1)}, bf16...) custom-call(s32[1,8]{1,0:T(1,128)} %refs_0_.2, ...), custom_call_target="tpu_custom_call" | custom-call | tf_op jit(solution)/shard_map/pallas_call | solution.py:53
  16.4 1.5 collective-permute-start.4
  17.9 1.5 collective-permute-start.3
  19.4 1.6 collective-permute-start.1
  21.4 7.2 %collective-permute-done.1 = bf16[128,1024]{1,0:T(8,128)(2,1)S(1)} collective-permute-done((bf16[128,1024]{1,0:T(8,128)(2,1)S(1)}, bf16[128,1024]{1,0:T(8,128)(2,1)S(1)}, u32[]{:S(2)}, u32[]{:S(2)}) %collective-permute-start.1) | collective-permute-done | bytes 262176 | tf_op jit(solution)/shard_map/ppermute | solution.py:425
  28.6 3.6 %collective-permute-done.2 = bf16[128,1024]{1,0:T(8,128)(2,1)S(1)} collective-permute-done((bf16[128,1024]{1,0:T(8,128)(2,1)S(1)}, bf16[128,1024]{1,0:T(8,128)(2,1)S(1)}, u32[]{:S(2)}, u32[]{:S(2)}) %collective-permute-start.2) | collective-permute-done | bytes 262176 | tf_op jit(solution)/shard_map/ppermute | solution.py:425
  34.9 4.9 %all-to-all-start = ((bf16[8,48,1024]{2,1,0:T(8,128)(2,1)}), bf16[8,48,1024]{2,1,0:T(8,128)(2,1)}, u32[]{:S(2)}, u32[]{:S(2)}) async-start(bf16[8,48,1024]{2,1,0:T(8,128)(2,1)} %bitcast.3), calls=%async_computation | async-start | bytes 1572864 | tf_op jit(solution)/shard_map/all_to_all | solution.py:490
  40.3 1.8 collective-permute-done.5.refs_6_
  42.5 8.6 %collective-permute-done.10.refs_8_ = bf16[384,1024]{1,0:T(8,128)(2,1)} collective-permute-done((bf16[384,1024]{1,0:T(8,128)(2,1)S(1)}, bf16[384,1024]{1,0:T(8,128)(2,1)}, u32[]{:S(2)}, u32[]{:S(2)}) %collective-permute-start.10) | collective-permute-done | bytes 786464 | tf_op jit(solution)/shard_map/ppermute | solution.py:428
  51.2 3.0 %collective-permute-done.9.refs_7_ = bf16[384,1024]{1,0:T(8,128)(2,1)} collective-permute-done((bf16[384,1024]{1,0:T(8,128)(2,1)S(1)}, bf16[384,1024]{1,0:T(8,128)(2,1)}, u32[]{:S(2)}, u32[]{:S(2)}) %collective-permute-start.9) | collective-permute-done | bytes 786464 | tf_op jit(solution)/shard_map/ppermute | solution.py:428
  54.2 1.5 collective-permute-start.7
  59.4 3.9 %collective-permute-done.7.refs_3_ = bf16[256,512]{1,0:T(8,128)(2,1)S(1)} collective-permute-done((bf16[256,512]{1,0:T(8,128)(2,1)S(1)}, bf16[256,512]{1,0:T(8,128)(2,1)S(1)}, u32[]{:S(2)}, u32[]{:S(2)}) %collective-permute-start.7) | collective-permute-done | bytes 262176 | tf_op jit(solution)/shard_map/ppermute | solution.py:428
  65.8 3.0 %collective-permute-done.11.refs_9_ = bf16[384,512]{1,0:T(8,128)(2,1)} collective-permute-done((bf16[384,512]{1,0:T(8,128)(2,1)S(1)}, bf16[384,512]{1,0:T(8,128)(2,1)}, u32[]{:S(2)}, u32[]{:S(2)}) %collective-permute-start.11) | collective-permute-done | bytes 393248 | tf_op jit(solution)/shard_map/ppermute | solution.py:428
  69.6 2.7 %shard_map.113 = bf16[256,1024]{1,0:T(8,128)(2,1)} custom-call(bf16[384,1024]{1,0:T(8,128)(2,1)} %bitcast.2.arrived), custom_call_target="tpu_custom_call" | custom-call | tf_op jit(solution)/shard_map/pallas_call | solution.py:53
  72.4 12.9 %shard_map.114 = (f32[16,256]{1,0:T(8,128)}, bf16[256,512]{1,0:T(8,128)(2,1)}, bf16[256,512]{1,0:T(8,128)(2,1)}, bf16[256,2048]{1,0:T(8,128)(2,1)}) custom-call(s32[256,4]{1,0:T(8,128)} %copy.15.refs_0_, f32[256,1]{1,0:T(8,128)} %get-tuple-element.87.refs_1_, f32[256,1]{1,0:T(8,128)} %get-tuple-element.88.refs_2_, ...), custom_call_target="tpu_custom_call" | custom-call | tf_op jit(solution)/shard_map/pallas_call | solution.py:53
  86.0 2.0 %collective-permute-start.23 = (f32[16,256]{1,0:T(8,128)}, f32[16,256]{1,0:T(8,128)S(1)}, u32[]{:S(2)}, u32[]{:S(2)}) collective-permute-start(f32[16,256]{1,0:T(8,128)} %get-tuple-element.127.refs_5_), channel_id=1, source_target_pairs={{0,24},{8,16},{16,8},{24,0},{1,25},{9,17},{17,9},{25,1},{2,26},{10... | collective-permute-start | bytes 49160 | tf_op jit(solution)/shard_map/ppermute | solution.py:428
  93.4 4.9 %shard_map.115 = (bf16[4,32,2560]{2,1,0:T(8,128)(2,1)}, bf16[4,32,1280]{2,1,0:T(8,128)(2,1)}, bf16[4,32,1280]{2,1,0:T(8,128)(2,1)}, bf16[4,32,1280]{2,1,0:T(8,12...) custom-call(bf16[256,512]{1,0:T(8,128)(2,1)} %get-tuple-element.85.refs_0_, ...), custom_call_target="tpu_custom_call" | custom-call | flops 1342177280 | bytes 5242880 | tf_op jit(solution)/shard_map/pallas_call | solution.py:53
  100.6 6.3 %collective-permute-done.25.left = bf16[4,32,1280]{2,1,0:T(8,128)(2,1)S(1)} collective-permute-done((bf16[4,32,1280]{2,1,0:T(8,128)(2,1)}, bf16[4,32,1280]{2,1,0:T(8,128)(2,1)S(1)}, u32[]{:S(2)}, u32[]{:S(2)}) %collective-permute-start.25) | collective-permute-done | bytes 327712 | tf_op jit(solution)/shard_map/ppermute | solution.py:428
  111.4 6.5 %shard_map.120 = (bf16[512,1024]{1,0:T(8,128)(2,1)}, bf16[512,1024]{1,0:T(8,128)(2,1)}) custom-call(bf16[256,1024]{1,0:T(8,128)(2,1)} %get-tuple-element.122.refs_3_.refs_0_, bf16[256,1024]{1,0:T(8,128)(2,1)} %copy-done.10, bf16[256,1024]{1,0:T(8,128)(2,1)} %copy-done.9, bf16[256,512]{1,0:T(8,128)(2,1)} %copy-done.12, bf16[256,512]{1,0:T(8,128)(2,1)} %copy-done.11, ...), custom_call_target="tpu_custom_call" | custom-call | tf_op jit(solution)/shard_map/pallas_call | solution.py:53
  119.1 1.6 collective-permute-start.29
  125.1 3.7 %collective-permute-done.24.one_left = bf16[4,32,1280]{2,1,0:T(8,128)(2,1)S(1)} collective-permute-done((bf16[4,32,1280]{2,1,0:T(8,128)(2,1)}, bf16[4,32,1280]{2,1,0:T(8,128)(2,1)S(1)}, u32[]{:S(2)}, u32[]{:S(2)}) %collective-permute-start.24) | collective-permute-done | bytes 327712 | tf_op jit(solution)/shard_map/ppermute | solution.py:428
  129.9 6.2 %collective-permute-done.28.two_left = bf16[4,32,1280]{2,1,0:T(8,128)(2,1)S(1)} collective-permute-done((bf16[4,32,1280]{2,1,0:T(8,128)(2,1)}, bf16[4,32,1280]{2,1,0:T(8,128)(2,1)S(1)}, u32[]{:S(2)}, u32[]{:S(2)}) %collective-permute-start.28) | collective-permute-done | bytes 327712 | tf_op jit(solution)/shard_map/ppermute | solution.py:428
  136.4 1.6 collective-permute-start.30
  138.0 7.4 %collective-permute-done.30.y = bf16[64,2560]{1,0:T(8,128)(2,1)S(1)} collective-permute-done((bf16[64,2560]{1,0:T(8,128)(2,1)S(1)}, bf16[64,2560]{1,0:T(8,128)(2,1)S(1)}, u32[]{:S(2)}, u32[]{:S(2)}) %collective-permute-start.30) | collective-permute-done | bytes 327712 | tf_op jit(solution)/shard_map/ppermute | solution.py:425
  145.5 2.9 %collective-permute-start.31 = (bf16[32,2560]{1,0:T(8,128)(2,1)S(1)}, bf16[32,2560]{1,0:T(8,128)(2,1)S(1)}, u32[]{:S(2)}, u32[]{:S(2)}) collective-permute-start(bf16[32,2560]{1,0:T(8,128)(2,1)S(1)} %get-tuple-element.118), channel_id=1, source_target_pairs={{0,4},{1,5},{2,6},{3,7},{4,0},{5,1},{6,2},{7,3},{8,12},{9,13},{10,... | collective-permute-start | bytes 491528 | tf_op jit(solution)/shard_map/ppermute | solution.py:425
  148.8 12.9 %collective-permute-done.31 = bf16[32,2560]{1,0:T(8,128)(2,1)S(1)} collective-permute-done((bf16[32,2560]{1,0:T(8,128)(2,1)S(1)}, bf16[32,2560]{1,0:T(8,128)(2,1)S(1)}, u32[]{:S(2)}, u32[]{:S(2)}) %collective-permute-start.31) | collective-permute-done | bytes 163872 | tf_op jit(solution)/shard_map/ppermute | solution.py:425
  161.7 1.5 collective-permute-start.34
  163.2 3.0 %collective-permute-done.37 = bf16[128,1024]{1,0:T(8,128)(2,1)S(1)} collective-permute-done((bf16[128,1024]{1,0:T(8,128)(2,1)S(1)}, bf16[128,1024]{1,0:T(8,128)(2,1)S(1)}, u32[]{:S(2)}, u32[]{:S(2)}) %collective-permute-start.37) | collective-permute-done | bytes 262176 | tf_op jit(solution)/shard_map/ppermute | solution.py:425
  166.3 1.5 collective-permute-start.40
  171.9 11.8 %collective-permute-done.33.refs_2_ = bf16[32,2560]{1,0:T(8,128)(2,1)S(1)} collective-permute-done((bf16[32,2560]{1,0:T(8,128)(2,1)S(1)}, bf16[32,2560]{1,0:T(8,128)(2,1)S(1)}, u32[]{:S(2)}, u32[]{:S(2)}) %collective-permute-start.33) | collective-permute-done | bytes 163872 | tf_op jit(solution)/shard_map/ppermute | solution.py:428
  184.9 1.5 shard_map.123
  (121 shorter events, 39.2 us)
Async XLA Ops:
  3.3 17.7 %collective-permute-start = (bf16[128,1024]{1,0:T(8,128)(2,1)S(1)}, bf16[128,1024]{1,0:T(8,128)(2,1)S(1)}, u32[]{:S(2)}, u32[]{:S(2)}) collective-permute-start(bf16[128,1024]{1,0:T(8,128)(2,1)S(1)} %get-tuple-element.72), channel_id=1, source_target_pairs={{0,4},{1,5},{2,6},{3,7},{4,0},{5,1},{6,2},{7,3},{8,12},{9,13},{10,... | collective-permute-start | bytes 786440 | tf_op jit(solution)/shard_map/ppermute | solution.py:425
  16.4 15.8 %collective-permute-start.4 = (bf16[256,1024]{1,0:T(8,128)(2,1)}, bf16[256,1024]{1,0:T(8,128)(2,1)S(1)}, u32[]{:S(2)}, u32[]{:S(2)}) collective-permute-start(bf16[256,1024]{1,0:T(8,128)(2,1)} %get-tuple-element.122.refs_3_.refs_0_), channel_id=1, source_target_pairs={{0,16},{8,24},{16,0},{24,8},{1,17},{9,25},{17,1},{25,9},{2,18},{10... | collective-permute-start | bytes 1572872 | tf_op jit(solution)/shard_map/ppermute | solution.py:428
  17.9 14.3 %collective-permute-start.3 = (bf16[256,1024]{1,0:T(8,128)(2,1)}, bf16[256,1024]{1,0:T(8,128)(2,1)S(1)}, u32[]{:S(2)}, u32[]{:S(2)}) collective-permute-start(bf16[256,1024]{1,0:T(8,128)(2,1)} %get-tuple-element.122.refs_3_.refs_0_), channel_id=1, source_target_pairs={{0,8},{8,0},{16,24},{24,16},{1,9},{9,1},{17,25},{25,17},{2,10},{10... | collective-permute-start | bytes 1572872 | tf_op jit(solution)/shard_map/ppermute | solution.py:428
  19.4 9.2 %collective-permute-start.1 = (bf16[128,1024]{1,0:T(8,128)(2,1)S(1)}, bf16[128,1024]{1,0:T(8,128)(2,1)S(1)}, u32[]{:S(2)}, u32[]{:S(2)}) collective-permute-start(bf16[128,1024]{1,0:T(8,128)(2,1)S(1)} %get-tuple-element.72), channel_id=1, source_target_pairs={{0,2},{1,3},{2,0},{3,1},{4,6},{5,7},{6,4},{7,5},{8,10},{9,11},{10,... | collective-permute-start | bytes 786440 | tf_op jit(solution)/shard_map/ppermute | solution.py:425
  21.0 11.2 %collective-permute-start.2 = (bf16[128,1024]{1,0:T(8,128)(2,1)S(1)}, bf16[128,1024]{1,0:T(8,128)(2,1)S(1)}, u32[]{:S(2)}, u32[]{:S(2)}) collective-permute-start(bf16[128,1024]{1,0:T(8,128)(2,1)S(1)} %collective-permute-done), channel_id=1, source_target_pairs={{0,2},{1,3},{2,0},{3,1},{4,6},{5,7},{6,4},{7,5},{8,10},{9,11},{10,... | collective-permute-start | bytes 786440 | tf_op jit(solution)/shard_map/ppermute | solution.py:425
  33.5 17.7 %collective-permute-start.10 = (bf16[384,1024]{1,0:T(8,128)(2,1)S(1)}, bf16[384,1024]{1,0:T(8,128)(2,1)}, u32[]{:S(2)}, u32[]{:S(2)}) collective-permute-start(bf16[384,1024]{1,0:T(8,128)(2,1)S(1)} %constant_dynamic-update-slice_fusion.refs_6_.refs_10_), channel_id=1, source_target_pairs={{0,16},{8,24},{16,0},{24,8},{1,17},{9,25},{17,1},{25,9},{2,18},{10... | collective-permute-start | bytes 2359304 | tf_op jit(solution)/shard_map/ppermute | solution.py:428
  34.1 20.1 %collective-permute-start.9 = (bf16[384,1024]{1,0:T(8,128)(2,1)S(1)}, bf16[384,1024]{1,0:T(8,128)(2,1)}, u32[]{:S(2)}, u32[]{:S(2)}) collective-permute-start(bf16[384,1024]{1,0:T(8,128)(2,1)S(1)} %constant_dynamic-update-slice_fusion.refs_6_.refs_10_), channel_id=1, source_target_pairs={{0,8},{8,0},{16,24},{24,16},{1,9},{9,1},{17,25},{25,17},{2,10},{10... | collective-permute-start | bytes 2359304 | tf_op jit(solution)/shard_map/ppermute | solution.py:428
  34.9 28.5 %collective-permute-start.14 = (bf16[384,1024]{1,0:T(8,128)(2,1)S(1)}, bf16[384,1024]{1,0:T(8,128)(2,1)S(1)}, u32[]{:S(2)}, u32[]{:S(2)}) collective-permute-start(bf16[384,1024]{1,0:T(8,128)(2,1)S(1)} %constant_dynamic-update-slice_fusion.refs_6_.refs_10_), channel_id=1, source_target_pairs={{0,1},{1,0},{2,3},{3,2},{4,5},{5,4},{6,7},{7,6},{8,9},{9,8},{10,11... | collective-permute-start | bytes 2359304 | tf_op jit(solution)/shard_map/ppermute | solution.py:431
  34.9 34.8 %all-to-all-start = ((bf16[8,48,1024]{2,1,0:T(8,128)(2,1)}), bf16[8,48,1024]{2,1,0:T(8,128)(2,1)}, u32[]{:S(2)}, u32[]{:S(2)}) async-start(bf16[8,48,1024]{2,1,0:T(8,128)(2,1)} %bitcast.3), calls=%async_computation | async-start | bytes 1572864 | tf_op jit(solution)/shard_map/all_to_all | solution.py:490
  40.2 17.5 %collective-permute-start.6 = (bf16[256,512]{1,0:T(8,128)(2,1)}, bf16[256,512]{1,0:T(8,128)(2,1)S(1)}, u32[]{:S(2)}, u32[]{:S(2)}) collective-permute-start(bf16[256,512]{1,0:T(8,128)(2,1)} %get-tuple-element.81.refs_3_), channel_id=1, source_target_pairs={{0,1},{1,0},{2,3},{3,2},{4,5},{5,4},{6,7},{7,6},{8,9},{9,8},{10,11... | collective-permute-start | bytes 786440 | tf_op jit(solution)/shard_map/ppermute | solution.py:431
  42.1 16.5 %collective-permute-start.8 = (bf16[256,512]{1,0:T(8,128)(2,1)S(1)}, bf16[256,512]{1,0:T(8,128)(2,1)S(1)}, u32[]{:S(2)}, u32[]{:S(2)}) collective-permute-start(bf16[256,512]{1,0:T(8,128)(2,1)S(1)} %slice.13), channel_id=1, source_target_pairs={{0,8},{8,0},{16,24},{24,16},{1,9},{9,1},{17,25},{25,17},{2,10},{10... | collective-permute-start | bytes 786440 | tf_op jit(solution)/shard_map/ppermute | solution.py:428
  51.2 21.2 %collective-permute-start.13 = (bf16[512,1024]{1,0:T(8,128)(2,1)}, bf16[512,1024]{1,0:T(8,128)(2,1)}, u32[]{:S(2)}, u32[]{:S(2)}) collective-permute-start(bf16[512,1024]{1,0:T(8,128)(2,1)} %get-tuple-element.90.refs_5_.refs_9_), channel_id=1, source_target_pairs={{0,1},{1,0},{2,3},{3,2},{4,5},{5,4},{6,7},{7,6},{8,9},{9,8},{10,11... | collective-permute-start | bytes 3145736 | tf_op jit(solution)/shard_map/ppermute | solution.py:431
  54.2 9.1 %collective-permute-start.7 = (bf16[256,512]{1,0:T(8,128)(2,1)S(1)}, bf16[256,512]{1,0:T(8,128)(2,1)S(1)}, u32[]{:S(2)}, u32[]{:S(2)}) collective-permute-start(bf16[256,512]{1,0:T(8,128)(2,1)S(1)} %slice.12), channel_id=1, source_target_pairs={{0,16},{8,24},{16,0},{24,8},{1,17},{9,25},{17,1},{25,9},{2,18},{10... | collective-permute-start | bytes 786440 | tf_op jit(solution)/shard_map/ppermute | solution.py:428
  58.6 10.2 %collective-permute-start.11 = (bf16[384,512]{1,0:T(8,128)(2,1)S(1)}, bf16[384,512]{1,0:T(8,128)(2,1)}, u32[]{:S(2)}, u32[]{:S(2)}) collective-permute-start(bf16[384,512]{1,0:T(8,128)(2,1)S(1)} %slice.16), channel_id=1, source_target_pairs={{0,16},{8,24},{16,0},{24,8},{1,17},{9,25},{17,1},{25,9},{2,18},{10... | collective-permute-start | bytes 1179656 | tf_op jit(solution)/shard_map/ppermute | solution.py:428
  63.3 9.1 %collective-permute-start.16 = (bf16[384,1024]{1,0:T(8,128)(2,1)}, bf16[384,1024]{1,0:T(8,128)(2,1)}, u32[]{:S(2)}, u32[]{:S(2)}) collective-permute-start(bf16[384,1024]{1,0:T(8,128)(2,1)} %collective-permute-done.10.refs_8_), channel_id=1, source_target_pairs={{0,1},{1,0},{2,3},{3,2},{4,5},{5,4},{6,7},{7,6},{8,9},{9,8},{10,11... | collective-permute-start | bytes 2359304 | tf_op jit(solution)/shard_map/ppermute | solution.py:431
  64.2 8.1 %collective-permute-start.15 = (bf16[384,1024]{1,0:T(8,128)(2,1)}, bf16[384,1024]{1,0:T(8,128)(2,1)}, u32[]{:S(2)}, u32[]{:S(2)}) collective-permute-start(bf16[384,1024]{1,0:T(8,128)(2,1)} %collective-permute-done.9.refs_7_), channel_id=1, source_target_pairs={{0,1},{1,0},{2,3},{3,2},{4,5},{5,4},{6,7},{7,6},{8,9},{9,8},{10,11... | collective-permute-start | bytes 2359304 | tf_op jit(solution)/shard_map/ppermute | solution.py:431
  98.3 8.6 %collective-permute-start.25 = (bf16[4,32,1280]{2,1,0:T(8,128)(2,1)}, bf16[4,32,1280]{2,1,0:T(8,128)(2,1)S(1)}, u32[]{:S(2)}, u32[]{:S(2)}) collective-permute-start(bf16[4,32,1280]{2,1,0:T(8,128)(2,1)} %get-tuple-element.108), channel_id=1, source_target_pairs={{0,8},{8,0},{16,24},{24,16},{1,9},{9,1},{17,25},{25,17},{2,10},{10... | collective-permute-start | bytes 983048 | tf_op jit(solution)/shard_map/ppermute | solution.py:428
  99.4 8.3 %collective-permute-start.26 = (bf16[4,32,1280]{2,1,0:T(8,128)(2,1)}, bf16[4,32,1280]{2,1,0:T(8,128)(2,1)S(1)}, u32[]{:S(2)}, u32[]{:S(2)}) collective-permute-start(bf16[4,32,1280]{2,1,0:T(8,128)(2,1)} %get-tuple-element.109), channel_id=1, source_target_pairs={{0,16},{8,24},{16,0},{24,8},{1,17},{9,25},{17,1},{25,9},{2,18},{10... | collective-permute-start | bytes 983048 | tf_op jit(solution)/shard_map/ppermute | solution.py:428
  118.1 10.8 %collective-permute-start.24 = (bf16[4,32,1280]{2,1,0:T(8,128)(2,1)}, bf16[4,32,1280]{2,1,0:T(8,128)(2,1)S(1)}, u32[]{:S(2)}, u32[]{:S(2)}) collective-permute-start(bf16[4,32,1280]{2,1,0:T(8,128)(2,1)} %get-tuple-element.107), channel_id=1, source_target_pairs={{0,8},{8,0},{16,24},{24,16},{1,9},{9,1},{17,25},{25,17},{2,10},{10... | collective-permute-start | bytes 983048 | tf_op jit(solution)/shard_map/ppermute | solution.py:428
  119.1 10.8 %collective-permute-start.29 = (bf16[4,32,1280]{2,1,0:T(8,128)(2,1)}, bf16[4,32,1280]{2,1,0:T(8,128)(2,1)S(1)}, u32[]{:S(2)}, u32[]{:S(2)}) collective-permute-start(bf16[4,32,1280]{2,1,0:T(8,128)(2,1)} %get-tuple-element.114), channel_id=1, source_target_pairs={{0,16},{8,24},{16,0},{24,8},{1,17},{9,25},{17,1},{25,9},{2,18},{10... | collective-permute-start | bytes 983048 | tf_op jit(solution)/shard_map/ppermute | solution.py:428
  120.7 15.5 %collective-permute-start.28 = (bf16[4,32,1280]{2,1,0:T(8,128)(2,1)}, bf16[4,32,1280]{2,1,0:T(8,128)(2,1)S(1)}, u32[]{:S(2)}, u32[]{:S(2)}) collective-permute-start(bf16[4,32,1280]{2,1,0:T(8,128)(2,1)} %copy-done.6), channel_id=1, source_target_pairs={{0,16},{8,24},{16,0},{24,8},{1,17},{9,25},{17,1},{25,9},{2,18},{10... | collective-permute-start | bytes 983048 | tf_op jit(solution)/shard_map/ppermute | solution.py:428
  121.1 15.0 %collective-permute-start.27 = (bf16[4,32,1280]{2,1,0:T(8,128)(2,1)}, bf16[4,32,1280]{2,1,0:T(8,128)(2,1)S(1)}, u32[]{:S(2)}, u32[]{:S(2)}) collective-permute-start(bf16[4,32,1280]{2,1,0:T(8,128)(2,1)} %copy-done.5), channel_id=1, source_target_pairs={{0,8},{8,0},{16,24},{24,16},{1,9},{9,1},{17,25},{25,17},{2,10},{10... | collective-permute-start | bytes 983048 | tf_op jit(solution)/shard_map/ppermute | solution.py:428
  123.6 24.9 %collective-permute-start.36 = (bf16[256,1024]{1,0:T(8,128)(2,1)S(1)}, bf16[256,1024]{1,0:T(8,128)(2,1)S(1)}, u32[]{:S(2)}, u32[]{:S(2)}) collective-permute-start(bf16[256,1024]{1,0:T(8,128)(2,1)S(1)} %get-tuple-element.134), channel_id=1, source_target_pairs={{0,2},{1,3},{2,0},{3,1},{4,6},{5,7},{6,4},{7,5},{8,10},{9,11},{10,... | collective-permute-start | bytes 1572872 | tf_op jit(solution)/shard_map/ppermute | solution.py:425
  136.4 9.0 %collective-permute-start.30 = (bf16[64,2560]{1,0:T(8,128)(2,1)S(1)}, bf16[64,2560]{1,0:T(8,128)(2,1)S(1)}, u32[]{:S(2)}, u32[]{:S(2)}) collective-permute-start(bf16[64,2560]{1,0:T(8,128)(2,1)S(1)} %get-tuple-element.116), channel_id=1, source_target_pairs={{0,2},{1,3},{2,0},{3,1},{4,6},{5,7},{6,4},{7,5},{8,10},{9,11},{10,... | collective-permute-start | bytes 983048 | tf_op jit(solution)/shard_map/ppermute | solution.py:425
  145.5 16.2 %collective-permute-start.31 = (bf16[32,2560]{1,0:T(8,128)(2,1)S(1)}, bf16[32,2560]{1,0:T(8,128)(2,1)S(1)}, u32[]{:S(2)}, u32[]{:S(2)}) collective-permute-start(bf16[32,2560]{1,0:T(8,128)(2,1)S(1)} %get-tuple-element.118), channel_id=1, source_target_pairs={{0,4},{1,5},{2,6},{3,7},{4,0},{5,1},{6,2},{7,3},{8,12},{9,13},{10,... | collective-permute-start | bytes 491528 | tf_op jit(solution)/shard_map/ppermute | solution.py:425
  148.7 17.6 %collective-permute-start.37 = (bf16[128,1024]{1,0:T(8,128)(2,1)S(1)}, bf16[128,1024]{1,0:T(8,128)(2,1)S(1)}, u32[]{:S(2)}, u32[]{:S(2)}) collective-permute-start(bf16[128,1024]{1,0:T(8,128)(2,1)S(1)} %get-tuple-element.136), channel_id=1, source_target_pairs={{0,4},{1,5},{2,6},{3,7},{4,0},{5,1},{6,2},{7,3},{8,12},{9,13},{10,... | collective-permute-start | bytes 786440 | tf_op jit(solution)/shard_map/ppermute | solution.py:425
  161.7 9.6 %collective-permute-start.34 = (bf16[32,2560]{1,0:T(8,128)(2,1)S(1)}, bf16[32,2560]{1,0:T(8,128)(2,1)S(1)}, u32[]{:S(2)}, u32[]{:S(2)}) collective-permute-start(bf16[32,2560]{1,0:T(8,128)(2,1)S(1)} %add_convert_fusion.refs_0_), channel_id=1, source_target_pairs={{0,24},{8,16},{16,8},{24,0},{1,25},{9,17},{17,9},{25,1},{2,26},{10... | collective-permute-start | bytes 491528 | tf_op jit(solution)/shard_map/ppermute | solution.py:428
  166.3 18.5 %collective-permute-start.40 = (bf16[128,1024]{1,0:T(8,128)(2,1)S(1)}, bf16[128,1024]{1,0:T(8,128)(2,1)S(1)}, u32[]{:S(2)}, u32[]{:S(2)}) collective-permute-start(bf16[128,1024]{1,0:T(8,128)(2,1)S(1)} %multiply_convert_fusion.refs_0_), channel_id=1, source_target_pairs={{0,24},{8,16},{16,8},{24,0},{1,25},{9,17},{17,9},{25,1},{2,26},{10... | collective-permute-start | bytes 786440 | tf_op jit(solution)/shard_map/ppermute | solution.py:428
  167.8 17.0 %collective-permute-start.39 = (bf16[128,1024]{1,0:T(8,128)(2,1)S(1)}, bf16[128,1024]{1,0:T(8,128)(2,1)S(1)}, u32[]{:S(2)}, u32[]{:S(2)}) collective-permute-start(bf16[128,1024]{1,0:T(8,128)(2,1)S(1)} %multiply_convert_fusion.refs_0_), channel_id=1, source_target_pairs={{0,16},{8,24},{16,0},{24,8},{1,17},{9,25},{17,1},{25,9},{2,18},{10... | collective-permute-start | bytes 786440 | tf_op jit(solution)/shard_map/ppermute | solution.py:428
  168.8 16.1 %collective-permute-start.38 = (bf16[128,1024]{1,0:T(8,128)(2,1)S(1)}, bf16[128,1024]{1,0:T(8,128)(2,1)S(1)}, u32[]{:S(2)}, u32[]{:S(2)}) collective-permute-start(bf16[128,1024]{1,0:T(8,128)(2,1)S(1)} %multiply_convert_fusion.refs_0_), channel_id=1, source_target_pairs={{0,8},{8,0},{16,24},{24,16},{1,9},{9,1},{17,25},{25,17},{2,10},{10... | collective-permute-start | bytes 786440 | tf_op jit(solution)/shard_map/ppermute | solution.py:428
  169.9 13.8 %collective-permute-start.33 = (bf16[32,2560]{1,0:T(8,128)(2,1)S(1)}, bf16[32,2560]{1,0:T(8,128)(2,1)S(1)}, u32[]{:S(2)}, u32[]{:S(2)}) collective-permute-start(bf16[32,2560]{1,0:T(8,128)(2,1)S(1)} %add_convert_fusion.refs_0_), channel_id=1, source_target_pairs={{0,16},{8,24},{16,0},{24,8},{1,17},{9,25},{17,1},{25,9},{2,18},{10... | collective-permute-start | bytes 491528 | tf_op jit(solution)/shard_map/ppermute | solution.py:428
  171.3 12.4 %collective-permute-start.32 = (bf16[32,2560]{1,0:T(8,128)(2,1)S(1)}, bf16[32,2560]{1,0:T(8,128)(2,1)S(1)}, u32[]{:S(2)}, u32[]{:S(2)}) collective-permute-start(bf16[32,2560]{1,0:T(8,128)(2,1)S(1)} %add_convert_fusion.refs_0_), channel_id=1, source_target_pairs={{0,8},{8,0},{16,24},{24,16},{1,9},{9,1},{17,25},{25,17},{2,10},{10... | collective-permute-start | bytes 491528 | tf_op jit(solution)/shard_map/ppermute | solution.py:428
  (32 other events, 325.4 us)

commit v14 on v12

--- a/solution.py
+++ b/solution.py
@@ -474,13 +474,14 @@
 
     near_units = [to_group(unit_b, k) for k in (1, 2)]
     candidates = jnp.concatenate([history[:, None], negatives], 1)
-    got, near_units, own, candidates = lax.optimization_barrier((got, near_units, own, candidates))
-    far_own = to_core(own)
+    got, near_units, candidates = lax.optimization_barrier((got, near_units, candidates))
     unit_sent = gather_groups(unit_b, near_units)
     others = [jnp.concatenate(got, 0)]
     pieces = [(0, -1, 0, 0, width, own)]
     for j, x in enumerate(others):
         pieces += [(0, j) + p for p in gather_groups(x)]
+    later, _ = lax.optimization_barrier((own, [p[5] for p in pieces[1:4]]))
+    far_own = to_core(later)
     pieces = pieces + [(1,) + p[1:5] + (to_core(p[5]) if p[1] >= 0 else far_own,) for p in pieces]
     near = [p[5] for p in pieces if p[2] == 0]
     outgoing, _ = lax.optimization_barrier((outgoing, others))

time: 173 us -> 172 us (level)
  transfers between devices with their start and end apart: 40 -> 40, of which waited for: 20 -> 19; matrix products, arithmetic and copies ran while one was open for 2% -> 2% of each run, Pallas kernels for 16% -> 16%
where the time goes in v14:
time: 172 us
  waiting for transfers between devices  73.9 us (43%)
  starting transfers between devices  43.8 us (25%)
  Pallas kernels  42.6 us (25%)
  local copies, waits for them, and re-layouts  9.51 us (6%)
    pallas_call x13, Pallas kernels, call(): pl.pallas_call(kernel, out_shape=[jax.ShapeDtypeStruct(s, t) for s, t in...  42.6 us
    ppermute x21, waiting for transfers between devices, to_group(): return lax.ppermute(x, 'grp', [(a, a ^ k) for a in range(groups)])  38.7 us
    ppermute x7, waiting for transfers between devices, across(): return lax.ppermute(x, 'seq', pairs)  35.2 us
    ppermute x21, starting transfers between devices, to_group(): return lax.ppermute(x, 'grp', [(a, a ^ k) for a in range(groups)])  23.1 us
    ppermute x7, starting transfers between devices, across(): return lax.ppermute(x, 'seq', pairs)  13.7 us
    unnamed x40, local copies, waits for them, and re-layouts  6.62 us
    all_to_all x1, starting transfers between devices, body(): lax.all_to_all(outgoing.reshape(owners, slot, width), 'seq', 0, 0, tiled=...  4.88 us
  transfers between devices with their start and end apart: 40, of which 19 were waited for; matrix products, arithmetic and copies ran while one was open for 2% of the time, Pallas kernels for 16%

profile of v14, /device:TPU:0, one launch (start us, length us, event | category | flops | bytes accessed | tf_op | source)
XLA Modules:
  0.0 171.9 jit_solution(13532401170498366321)
XLA Ops:
  1.9 1.4 shard_map.112
  3.2 4.0 %collective-permute-start = (bf16[128,1024]{1,0:T(8,128)(2,1)S(1)}, bf16[128,1024]{1,0:T(8,128)(2,1)}, u32[]{:S(2)}, u32[]{:S(2)}) collective-permute-start(bf16[128,1024]{1,0:T(8,128)(2,1)S(1)} %get-tuple-element.77), channel_id=1, source_target_pairs={{0,4},{1,5},{2,6},{3,7},{4,0},{5,1},{6,2},{7,3},{8,12},{9,13},{10,... | collective-permute-start | bytes 786440 | tf_op jit(solution)/shard_map/ppermute | solution.py:423
  7.3 9.1 %shard_map.111 = (bf16[256,512]{1,0:T(8,128)(2,1)}, bf16[256,512]{1,0:T(8,128)(2,1)}, bf16[256,2048]{1,0:T(8,128)(2,1)}, bf16[256,2048]{1,0:T(8,128)(2,1)}, bf16...) custom-call(s32[1,8]{1,0:T(1,128)} %refs_0_.2, ...), custom_call_target="tpu_custom_call" | custom-call | tf_op jit(solution)/shard_map/pallas_call | solution.py:53
  16.4 1.5 collective-permute-start.4
  17.9 1.5 collective-permute-start.3
  19.4 1.6 collective-permute-start.1
  21.4 7.2 %collective-permute-done.1 = bf16[128,1024]{1,0:T(8,128)(2,1)S(1)} collective-permute-done((bf16[128,1024]{1,0:T(8,128)(2,1)S(1)}, bf16[128,1024]{1,0:T(8,128)(2,1)S(1)}, u32[]{:S(2)}, u32[]{:S(2)}) %collective-permute-start.1) | collective-permute-done | bytes 262176 | tf_op jit(solution)/shard_map/ppermute | solution.py:423
  28.6 3.6 %collective-permute-done.2 = bf16[128,1024]{1,0:T(8,128)(2,1)S(1)} collective-permute-done((bf16[128,1024]{1,0:T(8,128)(2,1)}, bf16[128,1024]{1,0:T(8,128)(2,1)S(1)}, u32[]{:S(2)}, u32[]{:S(2)}) %collective-permute-start.2) | collective-permute-done | bytes 262176 | tf_op jit(solution)/shard_map/ppermute | solution.py:423
  34.8 4.9 %all-to-all-start = ((bf16[8,48,1024]{2,1,0:T(8,128)(2,1)}), bf16[8,48,1024]{2,1,0:T(8,128)(2,1)}, u32[]{:S(2)}, u32[]{:S(2)}) async-start(bf16[8,48,1024]{2,1,0:T(8,128)(2,1)} %bitcast.3), calls=%async_computation | async-start | bytes 1572864 | tf_op jit(solution)/shard_map/all_to_all | solution.py:489
  40.3 10.9 %collective-permute-done.10.refs_8_ = bf16[384,1024]{1,0:T(8,128)(2,1)} collective-permute-done((bf16[384,1024]{1,0:T(8,128)(2,1)S(1)}, bf16[384,1024]{1,0:T(8,128)(2,1)}, u32[]{:S(2)}, u32[]{:S(2)}) %collective-permute-start.10) | collective-permute-done | bytes 786464 | tf_op jit(solution)/shard_map/ppermute | solution.py:426
  51.9 2.3 %collective-permute-start.7 = (bf16[256,512]{1,0:T(8,128)(2,1)S(1)}, bf16[256,512]{1,0:T(8,128)(2,1)S(1)}, u32[]{:S(2)}, u32[]{:S(2)}) collective-permute-start(bf16[256,512]{1,0:T(8,128)(2,1)S(1)} %slice.12), channel_id=1, source_target_pairs={{0,16},{8,24},{16,0},{24,8},{1,17},{9,25},{17,1},{25,9},{2,18},{10... | collective-permute-start | bytes 786440 | tf_op jit(solution)/shard_map/ppermute | solution.py:426
  60.0 8.0 %collective-permute-done.12.refs_10_ = bf16[384,512]{1,0:T(8,128)(2,1)} collective-permute-done((bf16[384,512]{1,0:T(8,128)(2,1)S(1)}, bf16[384,512]{1,0:T(8,128)(2,1)}, u32[]{:S(2)}, u32[]{:S(2)}) %collective-permute-start.12) | collective-permute-done | bytes 393248 | tf_op jit(solution)/shard_map/ppermute | solution.py:426
  69.4 2.7 %shard_map.113 = bf16[256,1024]{1,0:T(8,128)(2,1)} custom-call(bf16[384,1024]{1,0:T(8,128)(2,1)} %bitcast.2.arrived), custom_call_target="tpu_custom_call" | custom-call | tf_op jit(solution)/shard_map/pallas_call | solution.py:53
  72.1 12.9 %shard_map.114 = (f32[16,256]{1,0:T(8,128)}, bf16[256,512]{1,0:T(8,128)(2,1)}, bf16[256,512]{1,0:T(8,128)(2,1)}, bf16[256,2048]{1,0:T(8,128)(2,1)}) custom-call(s32[256,4]{1,0:T(8,128)} %copy.15.refs_0_, f32[256,1]{1,0:T(8,128)} %get-tuple-element.91.refs_1_, f32[256,1]{1,0:T(8,128)} %get-tuple-element.92.refs_2_, ...), custom_call_target="tpu_custom_call" | custom-call | tf_op jit(solution)/shard_map/pallas_call | solution.py:53
  86.7 1.7 %collective-permute-start.21 = (f32[16,256]{1,0:T(8,128)}, f32[16,256]{1,0:T(8,128)S(1)}, u32[]{:S(2)}, u32[]{:S(2)}) collective-permute-start(f32[16,256]{1,0:T(8,128)} %get-tuple-element.113.refs_5_), channel_id=1, source_target_pairs={{0,16},{8,24},{16,0},{24,8},{1,17},{9,25},{17,1},{25,9},{2,18},{10... | collective-permute-start | bytes 49160 | tf_op jit(solution)/shard_map/ppermute | solution.py:426
  89.1 1.4 collective-permute-done.22.refs_8_
  90.7 1.7 collective-permute-done.20.refs_6_
  93.0 6.8 %shard_map.115 = (bf16[512,1024]{1,0:T(8,128)(2,1)}, bf16[512,1024]{1,0:T(8,128)(2,1)}) custom-call(bf16[256,1024]{1,0:T(8,128)(2,1)} %get-tuple-element.108.refs_3_.refs_0_, bf16[256,1024]{1,0:T(8,128)(2,1)} %copy-done.8, bf16[256,1024]{1,0:T(8,128)(2,1)} %copy-done.7, bf16[256,512]{1,0:T(8,128)(2,1)} %copy-done.10, bf16[256,512]{1,0:T(8,128)(2,1)} %copy-done.9, ...), custom_call_target="tpu_custom_call" | custom-call | tf_op jit(solution)/shard_map/pallas_call | solution.py:53
  99.9 5.0 %shard_map.116 = (bf16[4,32,2560]{2,1,0:T(8,128)(2,1)}, bf16[2,4,32,1280]{3,2,1,0:T(8,128)(2,1)}, bf16[2,4,32,1280]{3,2,1,0:T(8,128)(2,1)}, bf16[4,32,1280]{2,1,0:T(8,128)(2,1)}, bf16[4,32,1280]{2,1,0:T(8,128)(2,1)}) custom-call(bf16[256,512]{1,0:T(8,128)(2,1)} %get-tuple-element.89.refs_0_, bf16[256,2048]{1,0:T(8,128)(2,1)} %get-tuple-element.101.refs_1_, ...), custom_call_target="tpu_custom_call" | custom-call | flops 1342177280 | bytes 5242880 | tf_op jit(solution)/shard_map/pallas_call | solution.py:53
  106.6 1.6 collective-permute-start.27
  108.2 12.1 %collective-permute-done.27.y = bf16[256,1024]{1,0:T(8,128)(2,1)S(1)} collective-permute-done((bf16[256,1024]{1,0:T(8,128)(2,1)S(1)}, bf16[256,1024]{1,0:T(8,128)(2,1)S(1)}, u32[]{:S(2)}, u32[]{:S(2)}) %collective-permute-start.27) | collective-permute-done | bytes 524320 | tf_op jit(solution)/shard_map/ppermute | solution.py:423
  122.6 1.9 %collective-permute-start.28 = (bf16[128,1024]{1,0:T(8,128)(2,1)}, bf16[128,1024]{1,0:T(8,128)(2,1)}, u32[]{:S(2)}, u32[]{:S(2)}) collective-permute-start(bf16[128,1024]{1,0:T(8,128)(2,1)} %get-tuple-element.132), channel_id=1, source_target_pairs={{0,4},{1,5},{2,6},{3,7},{4,0},{5,1},{6,2},{7,3},{8,12},{9,13},{10,... | collective-permute-start | bytes 786440 | tf_op jit(solution)/shard_map/ppermute | solution.py:423
  127.3 1.3 collective-permute-start.29
  129.9 7.1 %collective-permute-done.28 = bf16[128,1024]{1,0:T(8,128)(2,1)} collective-permute-done((bf16[128,1024]{1,0:T(8,128)(2,1)}, bf16[128,1024]{1,0:T(8,128)(2,1)}, u32[]{:S(2)}, u32[]{:S(2)}) %collective-permute-start.28) | collective-permute-done | bytes 262176 | tf_op jit(solution)/shard_map/ppermute | solution.py:423
  140.4 6.0 %collective-permute-done.32.refs_1_ = bf16[128,1024]{1,0:T(8,128)(2,1)S(1)} collective-permute-done((bf16[128,1024]{1,0:T(8,128)(2,1)S(1)}, bf16[128,1024]{1,0:T(8,128)(2,1)S(1)}, u32[]{:S(2)}, u32[]{:S(2)}) %collective-permute-start.32) | collective-permute-done | bytes 262176 | tf_op jit(solution)/shard_map/ppermute | solution.py:426
  147.0 2.8 %collective-permute-start.33 = (bf16[32,2560]{1,0:T(8,128)(2,1)S(1)}, bf16[32,2560]{1,0:T(8,128)(2,1)S(1)}, u32[]{:S(2)}, u32[]{:S(2)}) collective-permute-start(bf16[32,2560]{1,0:T(8,128)(2,1)S(1)} %get-tuple-element.145), channel_id=1, source_target_pairs={{0,4},{1,5},{2,6},{3,7},{4,0},{5,1},{6,2},{7,3},{8,12},{9,13},{10,... | collective-permute-start | bytes 491528 | tf_op jit(solution)/shard_map/ppermute | solution.py:423
  149.8 2.0 %collective-permute-start.38 = (bf16[128,1024]{1,0:T(8,128)(2,1)S(1)}, bf16[128,1024]{1,0:T(8,128)(2,1)S(1)}, u32[]{:S(2)}, u32[]{:S(2)}) collective-permute-start(bf16[128,1024]{1,0:T(8,128)(2,1)S(1)} %multiply_convert_fusion.refs_0_), channel_id=1, source_target_pairs={{0,24},{8,16},{16,8},{24,0},{1,25},{9,17},{17,9},{25,1},{2,26},{10... | collective-permute-start | bytes 786440 | tf_op jit(solution)/shard_map/ppermute | solution.py:426
  152.6 4.5 %collective-permute-done.33 = bf16[32,2560]{1,0:T(8,128)(2,1)S(1)} collective-permute-done((bf16[32,2560]{1,0:T(8,128)(2,1)S(1)}, bf16[32,2560]{1,0:T(8,128)(2,1)S(1)}, u32[]{:S(2)}, u32[]{:S(2)}) %collective-permute-start.33) | collective-permute-done | bytes 163872 | tf_op jit(solution)/shard_map/ppermute | solution.py:423
  157.2 2.0 %collective-permute-start.36 = (bf16[32,2560]{1,0:T(8,128)(2,1)S(1)}, bf16[32,2560]{1,0:T(8,128)(2,1)S(1)}, u32[]{:S(2)}, u32[]{:S(2)}) collective-permute-start(bf16[32,2560]{1,0:T(8,128)(2,1)S(1)} %add_convert_fusion.refs_0_), channel_id=1, source_target_pairs={{0,24},{8,16},{16,8},{24,0},{1,25},{9,17},{17,9},{25,1},{2,26},{10... | collective-permute-start | bytes 491528 | tf_op jit(solution)/shard_map/ppermute | solution.py:426
  160.8 6.6 %collective-permute-done.37.refs_2_ = bf16[128,1024]{1,0:T(8,128)(2,1)S(1)} collective-permute-done((bf16[128,1024]{1,0:T(8,128)(2,1)S(1)}, bf16[128,1024]{1,0:T(8,128)(2,1)S(1)}, u32[]{:S(2)}, u32[]{:S(2)}) %collective-permute-start.37) | collective-permute-done | bytes 262176 | tf_op jit(solution)/shard_map/ppermute | solution.py:426
  167.3 1.5 shard_map.123
  168.8 1.9 %collective-permute-done.35.refs_2_ = bf16[32,2560]{1,0:T(8,128)(2,1)S(1)} collective-permute-done((bf16[32,2560]{1,0:T(8,128)(2,1)S(1)}, bf16[32,2560]{1,0:T(8,128)(2,1)S(1)}, u32[]{:S(2)}, u32[]{:S(2)}) %collective-permute-start.35) | collective-permute-done | bytes 163872 | tf_op jit(solution)/shard_map/ppermute | solution.py:426
  (111 shorter events, 31.4 us)
Async XLA Ops:
  3.2 17.7 %collective-permute-start = (bf16[128,1024]{1,0:T(8,128)(2,1)S(1)}, bf16[128,1024]{1,0:T(8,128)(2,1)}, u32[]{:S(2)}, u32[]{:S(2)}) collective-permute-start(bf16[128,1024]{1,0:T(8,128)(2,1)S(1)} %get-tuple-element.77), channel_id=1, source_target_pairs={{0,4},{1,5},{2,6},{3,7},{4,0},{5,1},{6,2},{7,3},{8,12},{9,13},{10,... | collective-permute-start | bytes 786440 | tf_op jit(solution)/shard_map/ppermute | solution.py:423
  16.4 15.8 %collective-permute-start.4 = (bf16[256,1024]{1,0:T(8,128)(2,1)}, bf16[256,1024]{1,0:T(8,128)(2,1)S(1)}, u32[]{:S(2)}, u32[]{:S(2)}) collective-permute-start(bf16[256,1024]{1,0:T(8,128)(2,1)} %get-tuple-element.108.refs_3_.refs_0_), channel_id=1, source_target_pairs={{0,16},{8,24},{16,0},{24,8},{1,17},{9,25},{17,1},{25,9},{2,18},{10... | collective-permute-start | bytes 1572872 | tf_op jit(solution)/shard_map/ppermute | solution.py:426
  17.9 14.3 %collective-permute-start.3 = (bf16[256,1024]{1,0:T(8,128)(2,1)}, bf16[256,1024]{1,0:T(8,128)(2,1)S(1)}, u32[]{:S(2)}, u32[]{:S(2)}) collective-permute-start(bf16[256,1024]{1,0:T(8,128)(2,1)} %get-tuple-element.108.refs_3_.refs_0_), channel_id=1, source_target_pairs={{0,8},{8,0},{16,24},{24,16},{1,9},{9,1},{17,25},{25,17},{2,10},{10... | collective-permute-start | bytes 1572872 | tf_op jit(solution)/shard_map/ppermute | solution.py:426
  19.4 9.2 %collective-permute-start.1 = (bf16[128,1024]{1,0:T(8,128)(2,1)S(1)}, bf16[128,1024]{1,0:T(8,128)(2,1)S(1)}, u32[]{:S(2)}, u32[]{:S(2)}) collective-permute-start(bf16[128,1024]{1,0:T(8,128)(2,1)S(1)} %get-tuple-element.77), channel_id=1, source_target_pairs={{0,2},{1,3},{2,0},{3,1},{4,6},{5,7},{6,4},{7,5},{8,10},{9,11},{10,... | collective-permute-start | bytes 786440 | tf_op jit(solution)/shard_map/ppermute | solution.py:423
  20.9 11.2 %collective-permute-start.2 = (bf16[128,1024]{1,0:T(8,128)(2,1)}, bf16[128,1024]{1,0:T(8,128)(2,1)S(1)}, u32[]{:S(2)}, u32[]{:S(2)}) collective-permute-start(bf16[128,1024]{1,0:T(8,128)(2,1)} %collective-permute-done), channel_id=1, source_target_pairs={{0,2},{1,3},{2,0},{3,1},{4,6},{5,7},{6,4},{7,5},{8,10},{9,11},{10,... | collective-permute-start | bytes 786440 | tf_op jit(solution)/shard_map/ppermute | solution.py:423
  33.4 17.7 %collective-permute-start.10 = (bf16[384,1024]{1,0:T(8,128)(2,1)S(1)}, bf16[384,1024]{1,0:T(8,128)(2,1)}, u32[]{:S(2)}, u32[]{:S(2)}) collective-permute-start(bf16[384,1024]{1,0:T(8,128)(2,1)S(1)} %constant_dynamic-update-slice_fusion.refs_6_.refs_10_), channel_id=1, source_target_pairs={{0,16},{8,24},{16,0},{24,8},{1,17},{9,25},{17,1},{25,9},{2,18},{10... | collective-permute-start | bytes 2359304 | tf_op jit(solution)/shard_map/ppermute | solution.py:426
  34.0 17.8 %collective-permute-start.9 = (bf16[384,1024]{1,0:T(8,128)(2,1)S(1)}, bf16[384,1024]{1,0:T(8,128)(2,1)}, u32[]{:S(2)}, u32[]{:S(2)}) collective-permute-start(bf16[384,1024]{1,0:T(8,128)(2,1)S(1)} %constant_dynamic-update-slice_fusion.refs_6_.refs_10_), channel_id=1, source_target_pairs={{0,8},{8,0},{16,24},{24,16},{1,9},{9,1},{17,25},{25,17},{2,10},{10... | collective-permute-start | bytes 2359304 | tf_op jit(solution)/shard_map/ppermute | solution.py:426
  34.8 23.7 %collective-permute-start.14 = (bf16[384,1024]{1,0:T(8,128)(2,1)S(1)}, bf16[384,1024]{1,0:T(8,128)(2,1)S(1)}, u32[]{:S(2)}, u32[]{:S(2)}) collective-permute-start(bf16[384,1024]{1,0:T(8,128)(2,1)S(1)} %constant_dynamic-update-slice_fusion.refs_6_.refs_10_), channel_id=1, source_target_pairs={{0,1},{1,0},{2,3},{3,2},{4,5},{5,4},{6,7},{7,6},{8,9},{9,8},{10,11... | collective-permute-start | bytes 2359304 | tf_op jit(solution)/shard_map/ppermute | solution.py:429
  34.8 34.6 %all-to-all-start = ((bf16[8,48,1024]{2,1,0:T(8,128)(2,1)}), bf16[8,48,1024]{2,1,0:T(8,128)(2,1)}, u32[]{:S(2)}, u32[]{:S(2)}) async-start(bf16[8,48,1024]{2,1,0:T(8,128)(2,1)} %bitcast.3), calls=%async_computation | async-start | bytes 1572864 | tf_op jit(solution)/shard_map/all_to_all | solution.py:489
  39.7 14.5 %collective-permute-start.5 = (bf16[256,512]{1,0:T(8,128)(2,1)}, bf16[256,512]{1,0:T(8,128)(2,1)S(1)}, u32[]{:S(2)}, u32[]{:S(2)}) collective-permute-start(bf16[256,512]{1,0:T(8,128)(2,1)} %get-tuple-element.84), channel_id=1, source_target_pairs={{0,1},{1,0},{2,3},{3,2},{4,5},{5,4},{6,7},{7,6},{8,9},{9,8},{10,11... | collective-permute-start | bytes 786440 | tf_op jit(solution)/shard_map/ppermute | solution.py:429
  40.2 16.8 %collective-permute-start.6 = (bf16[256,512]{1,0:T(8,128)(2,1)}, bf16[256,512]{1,0:T(8,128)(2,1)S(1)}, u32[]{:S(2)}, u32[]{:S(2)}) collective-permute-start(bf16[256,512]{1,0:T(8,128)(2,1)} %get-tuple-element.85.refs_3_), channel_id=1, source_target_pairs={{0,1},{1,0},{2,3},{3,2},{4,5},{5,4},{6,7},{7,6},{8,9},{9,8},{10,11... | collective-permute-start | bytes 786440 | tf_op jit(solution)/shard_map/ppermute | solution.py:429
  51.9 6.7 %collective-permute-start.7 = (bf16[256,512]{1,0:T(8,128)(2,1)S(1)}, bf16[256,512]{1,0:T(8,128)(2,1)S(1)}, u32[]{:S(2)}, u32[]{:S(2)}) collective-permute-start(bf16[256,512]{1,0:T(8,128)(2,1)S(1)} %slice.12), channel_id=1, source_target_pairs={{0,16},{8,24},{16,0},{24,8},{1,17},{9,25},{17,1},{25,9},{2,18},{10... | collective-permute-start | bytes 786440 | tf_op jit(solution)/shard_map/ppermute | solution.py:426
  54.2 17.9 %collective-permute-start.13 = (bf16[512,1024]{1,0:T(8,128)(2,1)}, bf16[512,1024]{1,0:T(8,128)(2,1)}, u32[]{:S(2)}, u32[]{:S(2)}) collective-permute-start(bf16[512,1024]{1,0:T(8,128)(2,1)} %get-tuple-element.95.refs_5_.refs_9_), channel_id=1, source_target_pairs={{0,1},{1,0},{2,3},{3,2},{4,5},{5,4},{6,7},{7,6},{8,9},{9,8},{10,11... | collective-permute-start | bytes 3145736 | tf_op jit(solution)/shard_map/ppermute | solution.py:429
  57.0 11.0 %collective-permute-start.12 = (bf16[384,512]{1,0:T(8,128)(2,1)S(1)}, bf16[384,512]{1,0:T(8,128)(2,1)}, u32[]{:S(2)}, u32[]{:S(2)}) collective-permute-start(bf16[384,512]{1,0:T(8,128)(2,1)S(1)} %slice.17), channel_id=1, source_target_pairs={{0,8},{8,0},{16,24},{24,16},{1,9},{9,1},{17,25},{25,17},{2,10},{10... | collective-permute-start | bytes 1179656 | tf_op jit(solution)/shard_map/ppermute | solution.py:426
  57.5 10.6 %collective-permute-start.11 = (bf16[384,512]{1,0:T(8,128)(2,1)S(1)}, bf16[384,512]{1,0:T(8,128)(2,1)}, u32[]{:S(2)}, u32[]{:S(2)}) collective-permute-start(bf16[384,512]{1,0:T(8,128)(2,1)S(1)} %slice.16), channel_id=1, source_target_pairs={{0,16},{8,24},{16,0},{24,8},{1,17},{9,25},{17,1},{25,9},{2,18},{10... | collective-permute-start | bytes 1179656 | tf_op jit(solution)/shard_map/ppermute | solution.py:426
  58.5 13.5 %collective-permute-start.16 = (bf16[384,1024]{1,0:T(8,128)(2,1)}, bf16[384,1024]{1,0:T(8,128)(2,1)}, u32[]{:S(2)}, u32[]{:S(2)}) collective-permute-start(bf16[384,1024]{1,0:T(8,128)(2,1)} %collective-permute-done.10.refs_8_), channel_id=1, source_target_pairs={{0,1},{1,0},{2,3},{3,2},{4,5},{5,4},{6,7},{7,6},{8,9},{9,8},{10,11... | collective-permute-start | bytes 2359304 | tf_op jit(solution)/shard_map/ppermute | solution.py:429
  59.5 12.6 %collective-permute-start.15 = (bf16[384,1024]{1,0:T(8,128)(2,1)}, bf16[384,1024]{1,0:T(8,128)(2,1)}, u32[]{:S(2)}, u32[]{:S(2)}) collective-permute-start(bf16[384,1024]{1,0:T(8,128)(2,1)} %collective-permute-done.9.refs_7_), channel_id=1, source_target_pairs={{0,1},{1,0},{2,3},{3,2},{4,5},{5,4},{6,7},{7,6},{8,9},{9,8},{10,11... | collective-permute-start | bytes 2359304 | tf_op jit(solution)/shard_map/ppermute | solution.py:429
  85.1 7.3 %collective-permute-start.19 = (bf16[256,512]{1,0:T(8,128)(2,1)}, bf16[256,512]{1,0:T(8,128)(2,1)S(1)}, u32[]{:S(2)}, u32[]{:S(2)}) collective-permute-start(bf16[256,512]{1,0:T(8,128)(2,1)} %get-tuple-element.104), channel_id=1, source_target_pairs={{0,1},{1,0},{2,3},{3,2},{4,5},{5,4},{6,7},{7,6},{8,9},{9,8},{10,11... | collective-permute-start | bytes 786440 | tf_op jit(solution)/shard_map/ppermute | solution.py:429
  85.2 14.6 %collective-permute-start.23 = (bf16[256,2048]{1,0:T(8,128)(2,1)}, bf16[256,2048]{1,0:T(8,128)(2,1)}, u32[]{:S(2)}, u32[]{:S(2)}) collective-permute-start(bf16[256,2048]{1,0:T(8,128)(2,1)} %get-tuple-element.101.refs_1_), channel_id=1, source_target_pairs={{0,1},{1,0},{2,3},{3,2},{4,5},{5,4},{6,7},{7,6},{8,9},{9,8},{10,11... | collective-permute-start | bytes 3145736 | tf_op jit(solution)/shard_map/ppermute | solution.py:429
  104.8 17.4 %collective-permute-start.24 = (bf16[2,4,32,1280]{3,2,1,0:T(8,128)(2,1)}, bf16[2,4,32,1280]{3,2,1,0:T(8,128)(2,1)S(1)}, u32[]{:S(2)}, u32[]{:S(2)}) collective-permute-start(bf16[2,4,32,1280]{3,2,1,0:T(8,128)(2,1)} %get-tuple-element.123), channel_id=1, source_target_pairs={{0,8},{8,0},{16,24},{24,16},{1,9},{9,1},{17,25},{25,17},{2,10},{10... | collective-permute-start | bytes 1966088 | tf_op jit(solution)/shard_map/ppermute | solution.py:426
  105.6 17.0 %collective-permute-start.25 = (bf16[2,4,32,1280]{3,2,1,0:T(8,128)(2,1)}, bf16[2,4,32,1280]{3,2,1,0:T(8,128)(2,1)S(1)}, u32[]{:S(2)}, u32[]{:S(2)}) collective-permute-start(bf16[2,4,32,1280]{3,2,1,0:T(8,128)(2,1)} %get-tuple-element.124), channel_id=1, source_target_pairs={{0,16},{8,24},{16,0},{24,8},{1,17},{9,25},{17,1},{25,9},{2,18},{10... | collective-permute-start | bytes 1966088 | tf_op jit(solution)/shard_map/ppermute | solution.py:426
  106.6 13.8 %collective-permute-start.27 = (bf16[256,1024]{1,0:T(8,128)(2,1)S(1)}, bf16[256,1024]{1,0:T(8,128)(2,1)S(1)}, u32[]{:S(2)}, u32[]{:S(2)}) collective-permute-start(bf16[256,1024]{1,0:T(8,128)(2,1)S(1)} %get-tuple-element.128), channel_id=1, source_target_pairs={{0,2},{1,3},{2,0},{3,1},{4,6},{5,7},{6,4},{7,5},{8,10},{9,11},{10,... | collective-permute-start | bytes 1572872 | tf_op jit(solution)/shard_map/ppermute | solution.py:423
  122.6 14.4 %collective-permute-start.28 = (bf16[128,1024]{1,0:T(8,128)(2,1)}, bf16[128,1024]{1,0:T(8,128)(2,1)}, u32[]{:S(2)}, u32[]{:S(2)}) collective-permute-start(bf16[128,1024]{1,0:T(8,128)(2,1)} %get-tuple-element.132), channel_id=1, source_target_pairs={{0,4},{1,5},{2,6},{3,7},{4,0},{5,1},{6,2},{7,3},{8,12},{9,13},{10,... | collective-permute-start | bytes 786440 | tf_op jit(solution)/shard_map/ppermute | solution.py:423
  127.3 10.8 %collective-permute-start.29 = (bf16[4,32,1280]{2,1,0:T(8,128)(2,1)}, bf16[4,32,1280]{2,1,0:T(8,128)(2,1)S(1)}, u32[]{:S(2)}, u32[]{:S(2)}) collective-permute-start(bf16[4,32,1280]{2,1,0:T(8,128)(2,1)} %get-tuple-element.139), channel_id=1, source_target_pairs={{0,8},{8,0},{16,24},{24,16},{1,9},{9,1},{17,25},{25,17},{2,10},{10... | collective-permute-start | bytes 983048 | tf_op jit(solution)/shard_map/ppermute | solution.py:426
  128.6 9.5 %collective-permute-start.30 = (bf16[4,32,1280]{2,1,0:T(8,128)(2,1)S(1)}, bf16[4,32,1280]{2,1,0:T(8,128)(2,1)S(1)}, u32[]{:S(2)}, u32[]{:S(2)}) collective-permute-start(bf16[4,32,1280]{2,1,0:T(8,128)(2,1)S(1)} %get-tuple-element.140), channel_id=1, source_target_pairs={{0,16},{8,24},{16,0},{24,8},{1,17},{9,25},{17,1},{25,9},{2,18},{10... | collective-permute-start | bytes 983048 | tf_op jit(solution)/shard_map/ppermute | solution.py:426
  138.3 8.6 %collective-permute-start.31 = (bf16[64,2560]{1,0:T(8,128)(2,1)S(1)}, bf16[64,2560]{1,0:T(8,128)(2,1)S(1)}, u32[]{:S(2)}, u32[]{:S(2)}) collective-permute-start(bf16[64,2560]{1,0:T(8,128)(2,1)S(1)} %get-tuple-element.142), channel_id=1, source_target_pairs={{0,2},{1,3},{2,0},{3,1},{4,6},{5,7},{6,4},{7,5},{8,10},{9,11},{10,... | collective-permute-start | bytes 983048 | tf_op jit(solution)/shard_map/ppermute | solution.py:423
  147.0 10.1 %collective-permute-start.33 = (bf16[32,2560]{1,0:T(8,128)(2,1)S(1)}, bf16[32,2560]{1,0:T(8,128)(2,1)S(1)}, u32[]{:S(2)}, u32[]{:S(2)}) collective-permute-start(bf16[32,2560]{1,0:T(8,128)(2,1)S(1)} %get-tuple-element.145), channel_id=1, source_target_pairs={{0,4},{1,5},{2,6},{3,7},{4,0},{5,1},{6,2},{7,3},{8,12},{9,13},{10,... | collective-permute-start | bytes 491528 | tf_op jit(solution)/shard_map/ppermute | solution.py:423
  149.8 10.9 %collective-permute-start.38 = (bf16[128,1024]{1,0:T(8,128)(2,1)S(1)}, bf16[128,1024]{1,0:T(8,128)(2,1)S(1)}, u32[]{:S(2)}, u32[]{:S(2)}) collective-permute-start(bf16[128,1024]{1,0:T(8,128)(2,1)S(1)} %multiply_convert_fusion.refs_0_), channel_id=1, source_target_pairs={{0,24},{8,16},{16,8},{24,0},{1,25},{9,17},{17,9},{25,1},{2,26},{10... | collective-permute-start | bytes 786440 | tf_op jit(solution)/shard_map/ppermute | solution.py:426
  151.8 15.5 %collective-permute-start.37 = (bf16[128,1024]{1,0:T(8,128)(2,1)S(1)}, bf16[128,1024]{1,0:T(8,128)(2,1)S(1)}, u32[]{:S(2)}, u32[]{:S(2)}) collective-permute-start(bf16[128,1024]{1,0:T(8,128)(2,1)S(1)} %multiply_convert_fusion.refs_0_), channel_id=1, source_target_pairs={{0,16},{8,24},{16,0},{24,8},{1,17},{9,25},{17,1},{25,9},{2,18},{10... | collective-permute-start | bytes 786440 | tf_op jit(solution)/shard_map/ppermute | solution.py:426
  157.2 11.6 %collective-permute-start.36 = (bf16[32,2560]{1,0:T(8,128)(2,1)S(1)}, bf16[32,2560]{1,0:T(8,128)(2,1)S(1)}, u32[]{:S(2)}, u32[]{:S(2)}) collective-permute-start(bf16[32,2560]{1,0:T(8,128)(2,1)S(1)} %add_convert_fusion.refs_0_), channel_id=1, source_target_pairs={{0,24},{8,16},{16,8},{24,0},{1,25},{9,17},{17,9},{25,1},{2,26},{10... | collective-permute-start | bytes 491528 | tf_op jit(solution)/shard_map/ppermute | solution.py:426
  159.2 11.5 %collective-permute-start.35 = (bf16[32,2560]{1,0:T(8,128)(2,1)S(1)}, bf16[32,2560]{1,0:T(8,128)(2,1)S(1)}, u32[]{:S(2)}, u32[]{:S(2)}) collective-permute-start(bf16[32,2560]{1,0:T(8,128)(2,1)S(1)} %add_convert_fusion.refs_0_), channel_id=1, source_target_pairs={{0,16},{8,24},{16,0},{24,8},{1,17},{9,25},{17,1},{25,9},{2,18},{10... | collective-permute-start | bytes 491528 | tf_op jit(solution)/shard_map/ppermute | solution.py:426
  160.0 10.7 %collective-permute-start.34 = (bf16[32,2560]{1,0:T(8,128)(2,1)S(1)}, bf16[32,2560]{1,0:T(8,128)(2,1)S(1)}, u32[]{:S(2)}, u32[]{:S(2)}) collective-permute-start(bf16[32,2560]{1,0:T(8,128)(2,1)S(1)} %add_convert_fusion.refs_0_), channel_id=1, source_target_pairs={{0,8},{8,0},{16,24},{24,16},{1,9},{9,1},{17,25},{25,17},{2,10},{10... | collective-permute-start | bytes 491528 | tf_op jit(solution)/shard_map/ppermute | solution.py:426
  (27 other events, 266.9 us)

commit v15 on v14

--- a/solution.py
+++ b/solution.py
@@ -63,7 +63,7 @@
 
 def forward_kernel(
     owners, slot, lengths, dests, events, in_weight, out_weight,
-    keep, give, proj, slope, attn, attn_slope, normed_out, inv_out, gated_out, unit, unit_b, inv_len, outgoing,
+    keep, give, proj, slope, attn, attn_slope, normed_out, inv_out, gated_out, unit_b, inv_len, outgoing,
 ):
     tok = events.shape[0]
     hidden = out_weight.shape[1]
@@ -107,7 +107,7 @@
         attn_slope[h] = jnp.where(mask, sig * (1.0 + s * (1.0 - sig)) * scale, 0.0).astype(b16)
         outputs.append(dot(weight, v, NN))
     normed, inverse = center_scale(jnp.concatenate(outputs, 1))
-    normed_out[...] = normed
+    normed_out[...] = normed.astype(b16)
     inv_out[...] = inverse
     gated = (normed * proj[:, :hidden].astype(f32)).astype(b16)
     gated_out[...] = gated
@@ -115,7 +115,6 @@
     inverse = lax.rsqrt(jnp.sum(result * result, -1, keepdims=True) + epsilon)
     inv_len[...] = inverse
     yn = result * inverse
-    unit[...] = yn
     unit_b[...] = yn.astype(b16)
     row = iota((outgoing.shape[0], 1), 0)
     filled = jnp.zeros(row.shape, i32)
@@ -153,7 +152,7 @@
 
 def backward(up, inverse, out_weight, proj, slope, attn, attn_slope, normed_ref, grad):
     hidden = out_weight.shape[1]
-    normed = normed_ref[...]
+    normed = normed_ref[...].astype(f32)
     grad_gated = dot(up, out_weight[...], NN)
     grad[:, :hidden] = (grad_gated * normed * slope[:, :hidden].astype(f32)).astype(b16)
     grad_normed = grad_gated * proj[:, :hidden].astype(f32)
@@ -173,10 +172,10 @@
         grad[:, ck] = (dot(grad_score, proj[:, cq], TN) * slope[:, ck].astype(f32)).astype(b16)
 
 
-def score_kernel(groups, owners, share, chunks, places, cand, inv_len, inverse, unit_hbm, yn_hbm, *refs):
+def score_kernel(groups, owners, share, chunks, places, cand, inv_len, inverse, unit_hbm, *refs):
     count = len(places)
     pieces, saved_hbm, refs = refs[:count], refs[count : count + 6], refs[count + 6 :]
-    tags, up_keep, up_give, grad, table, spread, unit_b, unit, *saved, sems = refs
+    tags, up_keep, up_give, grad, table, spread, unit_b, *saved, sems = refs
     chips = owners // 2
     vocab_dev = share * groups
     grp, core = lax.axis_index("grp"), lax.axis_index("seq") % 2
@@ -199,8 +198,6 @@
         copy = pltpu.make_async_copy(pieces[n], table.at[pl.ds(at, rows), pl.ds(left, wide)], sems.at[n])
         copy.start()
         copies.setdefault(tuple(key), []).append(copy)
-    load_yn = pltpu.make_async_copy(yn_hbm, unit, sems.at[count + 1])
-    load_yn.start()
     load_saved = [
         pltpu.make_async_copy(x, y, sems.at[count + 2 + n]) for n, (x, y) in enumerate(zip(saved_hbm, saved))
     ]
@@ -266,8 +263,7 @@
         for j, off, step, hit in tiles(key):
             spread[:, at + off : at + off + step] = jnp.where(hit, amount[j][:, :step], 0.0).astype(b16)
     pulled = dot(spread[...], table[...], NN)
-    load_yn.wait()
-    yn = unit[...]
+    yn = yb.astype(f32)
     upstream = (pulled - yn * jnp.sum(yn * pulled, -1, keepdims=True)) * inv_len[...]
     mine, other = split_columns(upstream, owners, core)
     up_keep[...] = mine.astype(b16)
@@ -462,11 +458,11 @@
     got = [have[x] for x in distances(chips)[1:]]
     outs = [
         ((tok, width // 2), b16), ((tok, width // 2), b16), ((tok, 4 * hidden), b16), ((tok, 4 * hidden), b16),
-        ((HEADS, tok, tok), b16), ((HEADS, tok, tok), b16), ((tok, hidden), f32), ((tok, 1), f32),
-        ((tok, hidden), b16), ((tok, width), f32), ((tok, width), b16), ((tok, 1), f32),
+        ((HEADS, tok, tok), b16), ((HEADS, tok, tok), b16), ((tok, hidden), b16), ((tok, 1), f32),
+        ((tok, hidden), b16), ((tok, width), b16), ((tok, 1), f32),
         ((owners * slot, width), b16),
     ]
-    (keep, give, proj, slope, attn, attn_slope, normed, inverse, gated, unit, unit_b, inv_len, outgoing) = call(
+    (keep, give, proj, slope, attn, attn_slope, normed, inverse, gated, unit_b, inv_len, outgoing) = call(
         lambda *refs: forward_kernel(owners, slot, *refs), outs, [SMEM, SMEM, VMEM, VMEM, VMEM],
         [lengths, destinations, events, in_weight, out_weight],
         room=63,
@@ -493,17 +489,17 @@
     far_give, far_gated = to_core(give), to_core(gated)
     units = [p[3] for p in unit_sent]
     layer_out, = call(relay_kernel, [((tok, width), b16)], [VMEM], [arrived], room=63)
-    layer_out, score_unit, far_give, far_gated, units = lax.optimization_barrier(
-        (layer_out, unit, far_give, far_gated, units)
+    layer_out, inv_len, far_give, far_gated, units = lax.optimization_barrier(
+        (layer_out, inv_len, far_give, far_gated, units)
     )
     saved = [out_weight, proj, slope, attn, attn_slope, normed]
     tags, up_keep, up_give, grad = call(
         lambda *refs: score_kernel(groups, owners, share, chunks, [p[:5] for p in pieces], *refs),
         [((2 * owners, tok), f32), ((tok, width // 2), b16), ((tok, width // 2), b16), ((tok, 4 * hidden), b16)],
-        [VMEM] * 3 + [ANY] * (len(pieces) + 8),
-        [candidates, inv_len, inverse, unit_b, score_unit] + [p[5] for p in pieces] + saved,
+        [VMEM] * 3 + [ANY] * (len(pieces) + 7),
+        [candidates, inv_len, inverse, unit_b] + [p[5] for p in pieces] + saved,
         [pltpu.VMEM((vocab, width), b16), pltpu.VMEM((tok, vocab), b16), pltpu.VMEM((tok, width), b16),
-         pltpu.VMEM((tok, width), f32)] + [pltpu.VMEM(x.shape, x.dtype) for x in saved]
+        ] + [pltpu.VMEM(x.shape, x.dtype) for x in saved]
         + [pltpu.SemaphoreType.DMA((len(pieces) + 8,))],
         room=63,
     )

time: 172 us -> 172 us (level)
  starting transfers between devices: 43.8 us -> 45.9 us
    ppermute x21, starting transfers between devices: 23.1 us -> 25.5 us  [to_group(): return lax.ppermute(x, 'grp', [(a, a ^ k) for a in range(groups)])]
    ppermute x21, waiting for transfers between devices: 38.7 us -> 36.5 us  [to_group(): return lax.ppermute(x, 'grp', [(a, a ^ k) for a in range(groups)])]
  transfers between devices with their start and end apart: 40 -> 40, of which waited for: 19 -> 18; matrix products, arithmetic and copies ran while one was open for 2% -> 2% of each run, Pallas kernels for 16% -> 15%
where the time goes in v15:
time: 172 us; the launch traced here: 171 us
  waiting for transfers between devices  72.6 us (42%)
  starting transfers between devices  45.9 us (27%)
  Pallas kernels  42 us (24%)
  local copies, waits for them, and re-layouts  9.56 us (6%)
    pallas_call x13, Pallas kernels, call(): pl.pallas_call(kernel, out_shape=[jax.ShapeDtypeStruct(s, t) for s, t in...  42 us
    ppermute x21, waiting for transfers between devices, to_group(): return lax.ppermute(x, 'grp', [(a, a ^ k) for a in range(groups)])  36.5 us
    ppermute x7, waiting for transfers between devices, across(): return lax.ppermute(x, 'seq', pairs)  36.1 us
    ppermute x21, starting transfers between devices, to_group(): return lax.ppermute(x, 'grp', [(a, a ^ k) for a in range(groups)])  25.5 us
    ppermute x7, starting transfers between devices, across(): return lax.ppermute(x, 'seq', pairs)  13.8 us
    unnamed x40, local copies, waits for them, and re-layouts  6.66 us
    all_to_all x1, starting transfers between devices, body(): lax.all_to_all(outgoing.reshape(owners, slot, width), 'seq', 0, 0, tiled=...  4.88 us
  transfers between devices with their start and end apart: 40, of which 18 were waited for; matrix products, arithmetic and copies ran while one was open for 2% of the time, Pallas kernels for 15%

profile of v15, /device:TPU:0, one launch (start us, length us, event | category | flops | bytes accessed | tf_op | source)
XLA Modules:
  0.0 171.3 jit_solution(8518571051852579614)
XLA Ops:
  1.9 1.4 shard_map.112
  3.2 4.0 %collective-permute-start = (bf16[128,1024]{1,0:T(8,128)(2,1)S(1)}, bf16[128,1024]{1,0:T(8,128)(2,1)S(1)}, u32[]{:S(2)}, u32[]{:S(2)}) collective-permute-start(bf16[128,1024]{1,0:T(8,128)(2,1)S(1)} %get-tuple-element.76), channel_id=1, source_target_pairs={{0,4},{1,5},{2,6},{3,7},{4,0},{5,1},{6,2},{7,3},{8,12},{9,13},{10,... | collective-permute-start | bytes 786440 | tf_op jit(solution)/shard_map/ppermute | solution.py:419
  7.3 8.7 %shard_map.111 = (bf16[256,512]{1,0:T(8,128)(2,1)}, bf16[256,512]{1,0:T(8,128)(2,1)}, bf16[256,2048]{1,0:T(8,128)(2,1)}, bf16[256,2048]{1,0:T(8,128)(2,1)}, bf16...) custom-call(s32[1,8]{1,0:T(1,128)} %refs_0_.2, ...), custom_call_target="tpu_custom_call" | custom-call | tf_op jit(solution)/shard_map/pallas_call | solution.py:53
  16.0 1.5 collective-permute-start.4
  17.5 1.5 collective-permute-start.3
  19.0 1.6 collective-permute-start.1
  21.0 7.2 %collective-permute-done.1 = bf16[128,1024]{1,0:T(8,128)(2,1)S(1)} collective-permute-done((bf16[128,1024]{1,0:T(8,128)(2,1)S(1)}, bf16[128,1024]{1,0:T(8,128)(2,1)S(1)}, u32[]{:S(2)}, u32[]{:S(2)}) %collective-permute-start.1) | collective-permute-done | bytes 262176 | tf_op jit(solution)/shard_map/ppermute | solution.py:419
  28.2 3.6 %collective-permute-done.2 = bf16[128,1024]{1,0:T(8,128)(2,1)S(1)} collective-permute-done((bf16[128,1024]{1,0:T(8,128)(2,1)S(1)}, bf16[128,1024]{1,0:T(8,128)(2,1)S(1)}, u32[]{:S(2)}, u32[]{:S(2)}) %collective-permute-start.2) | collective-permute-done | bytes 262176 | tf_op jit(solution)/shard_map/ppermute | solution.py:419
  34.8 4.9 %all-to-all-start = ((bf16[8,48,1024]{2,1,0:T(8,128)(2,1)}), bf16[8,48,1024]{2,1,0:T(8,128)(2,1)}, u32[]{:S(2)}, u32[]{:S(2)}) async-start(bf16[8,48,1024]{2,1,0:T(8,128)(2,1)} %bitcast.3), calls=%async_computation | async-start | bytes 1572864 | tf_op jit(solution)/shard_map/all_to_all | solution.py:485
  40.3 10.5 %collective-permute-done.10.refs_7_ = bf16[384,1024]{1,0:T(8,128)(2,1)} collective-permute-done((bf16[384,1024]{1,0:T(8,128)(2,1)S(1)}, bf16[384,1024]{1,0:T(8,128)(2,1)}, u32[]{:S(2)}, u32[]{:S(2)}) %collective-permute-start.10) | collective-permute-done | bytes 786464 | tf_op jit(solution)/shard_map/ppermute | solution.py:422
  51.5 1.6 collective-permute-start.7
  57.1 1.9 %collective-permute-start.11 = (bf16[384,512]{1,0:T(8,128)(2,1)S(1)}, bf16[384,512]{1,0:T(8,128)(2,1)}, u32[]{:S(2)}, u32[]{:S(2)}) collective-permute-start(bf16[384,512]{1,0:T(8,128)(2,1)S(1)} %slice.16), channel_id=1, source_target_pairs={{0,16},{8,24},{16,0},{24,8},{1,17},{9,25},{17,1},{25,9},{2,18},{10... | collective-permute-start | bytes 1179656 | tf_op jit(solution)/shard_map/ppermute | solution.py:422
  60.5 7.2 %collective-permute-done.12.refs_9_ = bf16[384,512]{1,0:T(8,128)(2,1)} collective-permute-done((bf16[384,512]{1,0:T(8,128)(2,1)S(1)}, bf16[384,512]{1,0:T(8,128)(2,1)}, u32[]{:S(2)}, u32[]{:S(2)}) %collective-permute-start.12) | collective-permute-done | bytes 393248 | tf_op jit(solution)/shard_map/ppermute | solution.py:422
  69.5 2.7 %shard_map.113 = bf16[256,1024]{1,0:T(8,128)(2,1)} custom-call(bf16[384,1024]{1,0:T(8,128)(2,1)} %bitcast.2.arrived), custom_call_target="tpu_custom_call" | custom-call | tf_op jit(solution)/shard_map/pallas_call | solution.py:53
  72.3 12.9 %shard_map.114 = (f32[16,256]{1,0:T(8,128)}, bf16[256,512]{1,0:T(8,128)(2,1)}, bf16[256,512]{1,0:T(8,128)(2,1)}, bf16[256,2048]{1,0:T(8,128)(2,1)}) custom-call(s32[256,4]{1,0:T(8,128)} %copy.15.refs_0_, f32[256,1]{1,0:T(8,128)} %get-tuple-element.90.refs_1_, f32[256,1]{1,0:T(8,128)} %get-tuple-element.91.refs_2_, ...), custom_call_target="tpu_custom_call" | custom-call | tf_op jit(solution)/shard_map/pallas_call | solution.py:53
  85.8 1.9 %collective-permute-start.22 = (f32[16,256]{1,0:T(8,128)}, f32[16,256]{1,0:T(8,128)S(1)}, u32[]{:S(2)}, u32[]{:S(2)}) collective-permute-start(f32[16,256]{1,0:T(8,128)} %get-tuple-element.111.refs_5_), channel_id=1, source_target_pairs={{0,24},{8,16},{16,8},{24,0},{1,25},{9,17},{17,9},{25,1},{2,26},{10... | collective-permute-start | bytes 49160 | tf_op jit(solution)/shard_map/ppermute | solution.py:422
  92.5 6.7 %shard_map.115 = (bf16[512,1024]{1,0:T(8,128)(2,1)}, bf16[512,1024]{1,0:T(8,128)(2,1)}) custom-call(bf16[256,1024]{1,0:T(8,128)(2,1)} %get-tuple-element.106.refs_3_.refs_0_, bf16[256,1024]{1,0:T(8,128)(2,1)} %copy-done.8, bf16[256,1024]{1,0:T(8,128)(2,1)} %copy-done.7, bf16[256,512]{1,0:T(8,128)(2,1)} %copy-done.10, bf16[256,512]{1,0:T(8,128)(2,1)} %copy-done.9, ...), custom_call_target="tpu_custom_call" | custom-call | tf_op jit(solution)/shard_map/pallas_call | solution.py:53
  99.3 5.0 %shard_map.116 = (bf16[4,32,2560]{2,1,0:T(8,128)(2,1)}, bf16[2,4,32,1280]{3,2,1,0:T(8,128)(2,1)}, bf16[2,4,32,1280]{3,2,1,0:T(8,128)(2,1)}, bf16[4,32,1280]{2,1,0:T(8,128)(2,1)}, bf16[4,32,1280]{2,1,0:T(8,128)(2,1)}) custom-call(bf16[256,512]{1,0:T(8,128)(2,1)} %get-tuple-element.88.refs_0_, bf16[256,2048]{1,0:T(8,128)(2,1)} %get-tuple-element.99.refs_1_, ...), custom_call_target="tpu_custom_call" | custom-call | flops 1342177280 | bytes 5242880 | tf_op jit(solution)/shard_map/pallas_call | solution.py:53
  105.6 1.7 %collective-permute-start.25 = (bf16[2,4,32,1280]{3,2,1,0:T(8,128)(2,1)}, bf16[2,4,32,1280]{3,2,1,0:T(8,128)(2,1)S(1)}, u32[]{:S(2)}, u32[]{:S(2)}) collective-permute-start(bf16[2,4,32,1280]{3,2,1,0:T(8,128)(2,1)} %get-tuple-element.122), channel_id=1, source_target_pairs={{0,16},{8,24},{16,0},{24,8},{1,17},{9,25},{17,1},{25,9},{2,18},{10... | collective-permute-start | bytes 1966088 | tf_op jit(solution)/shard_map/ppermute | solution.py:422
  108.0 13.5 %collective-permute-done.27.y = bf16[256,1024]{1,0:T(8,128)(2,1)S(1)} collective-permute-done((bf16[256,1024]{1,0:T(8,128)(2,1)S(1)}, bf16[256,1024]{1,0:T(8,128)(2,1)S(1)}, u32[]{:S(2)}, u32[]{:S(2)}) %collective-permute-start.27) | collective-permute-done | bytes 524320 | tf_op jit(solution)/shard_map/ppermute | solution.py:419
  122.7 2.3 %collective-permute-start.28 = (bf16[128,1024]{1,0:T(8,128)(2,1)}, bf16[128,1024]{1,0:T(8,128)(2,1)S(1)}, u32[]{:S(2)}, u32[]{:S(2)}) collective-permute-start(bf16[128,1024]{1,0:T(8,128)(2,1)} %get-tuple-element.130), channel_id=1, source_target_pairs={{0,4},{1,5},{2,6},{3,7},{4,0},{5,1},{6,2},{7,3},{8,12},{9,13},{10,... | collective-permute-start | bytes 786440 | tf_op jit(solution)/shard_map/ppermute | solution.py:419
  129.7 7.3 %collective-permute-done.28 = bf16[128,1024]{1,0:T(8,128)(2,1)S(1)} collective-permute-done((bf16[128,1024]{1,0:T(8,128)(2,1)}, bf16[128,1024]{1,0:T(8,128)(2,1)S(1)}, u32[]{:S(2)}, u32[]{:S(2)}) %collective-permute-start.28) | collective-permute-done | bytes 262176 | tf_op jit(solution)/shard_map/ppermute | solution.py:419
  137.6 2.6 %collective-permute-start.31 = (bf16[64,2560]{1,0:T(8,128)(2,1)S(1)}, bf16[64,2560]{1,0:T(8,128)(2,1)S(1)}, u32[]{:S(2)}, u32[]{:S(2)}) collective-permute-start(bf16[64,2560]{1,0:T(8,128)(2,1)S(1)} %get-tuple-element.140), channel_id=1, source_target_pairs={{0,2},{1,3},{2,0},{3,1},{4,6},{5,7},{6,4},{7,5},{8,10},{9,11},{10,... | collective-permute-start | bytes 983048 | tf_op jit(solution)/shard_map/ppermute | solution.py:419
  140.9 5.6 %collective-permute-done.32.refs_1_ = bf16[128,1024]{1,0:T(8,128)(2,1)S(1)} collective-permute-done((bf16[128,1024]{1,0:T(8,128)(2,1)S(1)}, bf16[128,1024]{1,0:T(8,128)(2,1)S(1)}, u32[]{:S(2)}, u32[]{:S(2)}) %collective-permute-start.32) | collective-permute-done | bytes 262176 | tf_op jit(solution)/shard_map/ppermute | solution.py:422
  146.6 2.6 %collective-permute-start.33 = (bf16[32,2560]{1,0:T(8,128)(2,1)S(1)}, bf16[32,2560]{1,0:T(8,128)(2,1)S(1)}, u32[]{:S(2)}, u32[]{:S(2)}) collective-permute-start(bf16[32,2560]{1,0:T(8,128)(2,1)S(1)} %get-tuple-element.143), channel_id=1, source_target_pairs={{0,4},{1,5},{2,6},{3,7},{4,0},{5,1},{6,2},{7,3},{8,12},{9,13},{10,... | collective-permute-start | bytes 491528 | tf_op jit(solution)/shard_map/ppermute | solution.py:419
  150.5 1.4 collective-permute-start.37
  152.0 4.5 %collective-permute-done.33 = bf16[32,2560]{1,0:T(8,128)(2,1)S(1)} collective-permute-done((bf16[32,2560]{1,0:T(8,128)(2,1)S(1)}, bf16[32,2560]{1,0:T(8,128)(2,1)S(1)}, u32[]{:S(2)}, u32[]{:S(2)}) %collective-permute-start.33) | collective-permute-done | bytes 163872 | tf_op jit(solution)/shard_map/ppermute | solution.py:419
  156.6 1.4 collective-permute-start.36
  157.9 1.4 collective-permute-start.35
  160.1 6.6 %collective-permute-done.37.refs_2_ = bf16[128,1024]{1,0:T(8,128)(2,1)S(1)} collective-permute-done((bf16[128,1024]{1,0:T(8,128)(2,1)S(1)}, bf16[128,1024]{1,0:T(8,128)(2,1)S(1)}, u32[]{:S(2)}, u32[]{:S(2)}) %collective-permute-start.37) | collective-permute-done | bytes 262176 | tf_op jit(solution)/shard_map/ppermute | solution.py:422
  166.7 1.5 shard_map.123
  168.2 1.9 %collective-permute-done.35.refs_2_ = bf16[32,2560]{1,0:T(8,128)(2,1)S(1)} collective-permute-done((bf16[32,2560]{1,0:T(8,128)(2,1)S(1)}, bf16[32,2560]{1,0:T(8,128)(2,1)S(1)}, u32[]{:S(2)}, u32[]{:S(2)}) %collective-permute-start.35) | collective-permute-done | bytes 163872 | tf_op jit(solution)/shard_map/ppermute | solution.py:422
  (111 shorter events, 31.5 us)
Async XLA Ops:
  3.2 17.3 %collective-permute-start = (bf16[128,1024]{1,0:T(8,128)(2,1)S(1)}, bf16[128,1024]{1,0:T(8,128)(2,1)S(1)}, u32[]{:S(2)}, u32[]{:S(2)}) collective-permute-start(bf16[128,1024]{1,0:T(8,128)(2,1)S(1)} %get-tuple-element.76), channel_id=1, source_target_pairs={{0,4},{1,5},{2,6},{3,7},{4,0},{5,1},{6,2},{7,3},{8,12},{9,13},{10,... | collective-permute-start | bytes 786440 | tf_op jit(solution)/shard_map/ppermute | solution.py:419
  16.0 15.8 %collective-permute-start.4 = (bf16[256,1024]{1,0:T(8,128)(2,1)}, bf16[256,1024]{1,0:T(8,128)(2,1)S(1)}, u32[]{:S(2)}, u32[]{:S(2)}) collective-permute-start(bf16[256,1024]{1,0:T(8,128)(2,1)} %get-tuple-element.106.refs_3_.refs_0_), channel_id=1, source_target_pairs={{0,16},{8,24},{16,0},{24,8},{1,17},{9,25},{17,1},{25,9},{2,18},{10... | collective-permute-start | bytes 1572872 | tf_op jit(solution)/shard_map/ppermute | solution.py:422
  17.5 14.3 %collective-permute-start.3 = (bf16[256,1024]{1,0:T(8,128)(2,1)}, bf16[256,1024]{1,0:T(8,128)(2,1)S(1)}, u32[]{:S(2)}, u32[]{:S(2)}) collective-permute-start(bf16[256,1024]{1,0:T(8,128)(2,1)} %get-tuple-element.106.refs_3_.refs_0_), channel_id=1, source_target_pairs={{0,8},{8,0},{16,24},{24,16},{1,9},{9,1},{17,25},{25,17},{2,10},{10... | collective-permute-start | bytes 1572872 | tf_op jit(solution)/shard_map/ppermute | solution.py:422
  19.0 9.2 %collective-permute-start.1 = (bf16[128,1024]{1,0:T(8,128)(2,1)S(1)}, bf16[128,1024]{1,0:T(8,128)(2,1)S(1)}, u32[]{:S(2)}, u32[]{:S(2)}) collective-permute-start(bf16[128,1024]{1,0:T(8,128)(2,1)S(1)} %get-tuple-element.76), channel_id=1, source_target_pairs={{0,2},{1,3},{2,0},{3,1},{4,6},{5,7},{6,4},{7,5},{8,10},{9,11},{10,... | collective-permute-start | bytes 786440 | tf_op jit(solution)/shard_map/ppermute | solution.py:419
  20.6 11.2 %collective-permute-start.2 = (bf16[128,1024]{1,0:T(8,128)(2,1)S(1)}, bf16[128,1024]{1,0:T(8,128)(2,1)S(1)}, u32[]{:S(2)}, u32[]{:S(2)}) collective-permute-start(bf16[128,1024]{1,0:T(8,128)(2,1)S(1)} %collective-permute-done), channel_id=1, source_target_pairs={{0,2},{1,3},{2,0},{3,1},{4,6},{5,7},{6,4},{7,5},{8,10},{9,11},{10,... | collective-permute-start | bytes 786440 | tf_op jit(solution)/shard_map/ppermute | solution.py:419
  33.1 17.7 %collective-permute-start.10 = (bf16[384,1024]{1,0:T(8,128)(2,1)S(1)}, bf16[384,1024]{1,0:T(8,128)(2,1)}, u32[]{:S(2)}, u32[]{:S(2)}) collective-permute-start(bf16[384,1024]{1,0:T(8,128)(2,1)S(1)} %constant_dynamic-update-slice_fusion.refs_5_.refs_10_), channel_id=1, source_target_pairs={{0,16},{8,24},{16,0},{24,8},{1,17},{9,25},{17,1},{25,9},{2,18},{10... | collective-permute-start | bytes 2359304 | tf_op jit(solution)/shard_map/ppermute | solution.py:422
  33.6 17.9 %collective-permute-start.9 = (bf16[384,1024]{1,0:T(8,128)(2,1)S(1)}, bf16[384,1024]{1,0:T(8,128)(2,1)}, u32[]{:S(2)}, u32[]{:S(2)}) collective-permute-start(bf16[384,1024]{1,0:T(8,128)(2,1)S(1)} %constant_dynamic-update-slice_fusion.refs_5_.refs_10_), channel_id=1, source_target_pairs={{0,8},{8,0},{16,24},{24,16},{1,9},{9,1},{17,25},{25,17},{2,10},{10... | collective-permute-start | bytes 2359304 | tf_op jit(solution)/shard_map/ppermute | solution.py:422
  34.8 24.2 %collective-permute-start.14 = (bf16[384,1024]{1,0:T(8,128)(2,1)S(1)}, bf16[384,1024]{1,0:T(8,128)(2,1)S(1)}, u32[]{:S(2)}, u32[]{:S(2)}) collective-permute-start(bf16[384,1024]{1,0:T(8,128)(2,1)S(1)} %constant_dynamic-update-slice_fusion.refs_5_.refs_10_), channel_id=1, source_target_pairs={{0,1},{1,0},{2,3},{3,2},{4,5},{5,4},{6,7},{7,6},{8,9},{9,8},{10,11... | collective-permute-start | bytes 2359304 | tf_op jit(solution)/shard_map/ppermute | solution.py:425
  34.8 34.7 %all-to-all-start = ((bf16[8,48,1024]{2,1,0:T(8,128)(2,1)}), bf16[8,48,1024]{2,1,0:T(8,128)(2,1)}, u32[]{:S(2)}, u32[]{:S(2)}) async-start(bf16[8,48,1024]{2,1,0:T(8,128)(2,1)} %bitcast.3), calls=%async_computation | async-start | bytes 1572864 | tf_op jit(solution)/shard_map/all_to_all | solution.py:485
  39.7 13.4 %collective-permute-start.5 = (bf16[256,512]{1,0:T(8,128)(2,1)}, bf16[256,512]{1,0:T(8,128)(2,1)S(1)}, u32[]{:S(2)}, u32[]{:S(2)}) collective-permute-start(bf16[256,512]{1,0:T(8,128)(2,1)} %get-tuple-element.83), channel_id=1, source_target_pairs={{0,1},{1,0},{2,3},{3,2},{4,5},{5,4},{6,7},{7,6},{8,9},{9,8},{10,11... | collective-permute-start | bytes 786440 | tf_op jit(solution)/shard_map/ppermute | solution.py:425
  40.2 15.7 %collective-permute-start.6 = (bf16[256,512]{1,0:T(8,128)(2,1)}, bf16[256,512]{1,0:T(8,128)(2,1)S(1)}, u32[]{:S(2)}, u32[]{:S(2)}) collective-permute-start(bf16[256,512]{1,0:T(8,128)(2,1)} %get-tuple-element.84.refs_3_), channel_id=1, source_target_pairs={{0,1},{1,0},{2,3},{3,2},{4,5},{5,4},{6,7},{7,6},{8,9},{9,8},{10,11... | collective-permute-start | bytes 786440 | tf_op jit(solution)/shard_map/ppermute | solution.py:425
  51.5 7.5 %collective-permute-start.7 = (bf16[256,512]{1,0:T(8,128)(2,1)S(1)}, bf16[256,512]{1,0:T(8,128)(2,1)S(1)}, u32[]{:S(2)}, u32[]{:S(2)}) collective-permute-start(bf16[256,512]{1,0:T(8,128)(2,1)S(1)} %slice.12), channel_id=1, source_target_pairs={{0,16},{8,24},{16,0},{24,8},{1,17},{9,25},{17,1},{25,9},{2,18},{10... | collective-permute-start | bytes 786440 | tf_op jit(solution)/shard_map/ppermute | solution.py:422
  53.8 18.4 %collective-permute-start.13 = (bf16[512,1024]{1,0:T(8,128)(2,1)}, bf16[512,1024]{1,0:T(8,128)(2,1)}, u32[]{:S(2)}, u32[]{:S(2)}) collective-permute-start(bf16[512,1024]{1,0:T(8,128)(2,1)} %get-tuple-element.93.refs_4_.refs_9_), channel_id=1, source_target_pairs={{0,1},{1,0},{2,3},{3,2},{4,5},{5,4},{6,7},{7,6},{8,9},{9,8},{10,11... | collective-permute-start | bytes 3145736 | tf_op jit(solution)/shard_map/ppermute | solution.py:425
  55.9 11.7 %collective-permute-start.12 = (bf16[384,512]{1,0:T(8,128)(2,1)S(1)}, bf16[384,512]{1,0:T(8,128)(2,1)}, u32[]{:S(2)}, u32[]{:S(2)}) collective-permute-start(bf16[384,512]{1,0:T(8,128)(2,1)S(1)} %slice.17), channel_id=1, source_target_pairs={{0,8},{8,0},{16,24},{24,16},{1,9},{9,1},{17,25},{25,17},{2,10},{10... | collective-permute-start | bytes 1179656 | tf_op jit(solution)/shard_map/ppermute | solution.py:422
  57.1 11.5 %collective-permute-start.11 = (bf16[384,512]{1,0:T(8,128)(2,1)S(1)}, bf16[384,512]{1,0:T(8,128)(2,1)}, u32[]{:S(2)}, u32[]{:S(2)}) collective-permute-start(bf16[384,512]{1,0:T(8,128)(2,1)S(1)} %slice.16), channel_id=1, source_target_pairs={{0,16},{8,24},{16,0},{24,8},{1,17},{9,25},{17,1},{25,9},{2,18},{10... | collective-permute-start | bytes 1179656 | tf_op jit(solution)/shard_map/ppermute | solution.py:422
  59.0 13.2 %collective-permute-start.16 = (bf16[384,1024]{1,0:T(8,128)(2,1)}, bf16[384,1024]{1,0:T(8,128)(2,1)}, u32[]{:S(2)}, u32[]{:S(2)}) collective-permute-start(bf16[384,1024]{1,0:T(8,128)(2,1)} %collective-permute-done.10.refs_7_), channel_id=1, source_target_pairs={{0,1},{1,0},{2,3},{3,2},{4,5},{5,4},{6,7},{7,6},{8,9},{9,8},{10,11... | collective-permute-start | bytes 2359304 | tf_op jit(solution)/shard_map/ppermute | solution.py:425
  60.0 12.2 %collective-permute-start.15 = (bf16[384,1024]{1,0:T(8,128)(2,1)}, bf16[384,1024]{1,0:T(8,128)(2,1)}, u32[]{:S(2)}, u32[]{:S(2)}) collective-permute-start(bf16[384,1024]{1,0:T(8,128)(2,1)} %collective-permute-done.9.refs_6_), channel_id=1, source_target_pairs={{0,1},{1,0},{2,3},{3,2},{4,5},{5,4},{6,7},{7,6},{8,9},{9,8},{10,11... | collective-permute-start | bytes 2359304 | tf_op jit(solution)/shard_map/ppermute | solution.py:425
  85.7 13.6 %collective-permute-start.23 = (bf16[256,2048]{1,0:T(8,128)(2,1)}, bf16[256,2048]{1,0:T(8,128)(2,1)}, u32[]{:S(2)}, u32[]{:S(2)}) collective-permute-start(bf16[256,2048]{1,0:T(8,128)(2,1)} %get-tuple-element.99.refs_1_), channel_id=1, source_target_pairs={{0,1},{1,0},{2,3},{3,2},{4,5},{5,4},{6,7},{7,6},{8,9},{9,8},{10,11... | collective-permute-start | bytes 3145736 | tf_op jit(solution)/shard_map/ppermute | solution.py:425
  99.2 8.2 %collective-permute-start.26 = (bf16[512,1024]{1,0:T(8,128)(2,1)}, bf16[512,1024]{1,0:T(8,128)(2,1)S(1)}, u32[]{:S(2)}, u32[]{:S(2)}) collective-permute-start(bf16[512,1024]{1,0:T(8,128)(2,1)} %get-tuple-element.124), channel_id=1, source_target_pairs={{0,1},{1,0},{2,3},{3,2},{4,5},{5,4},{6,7},{7,6},{8,9},{9,8},{10,11... | collective-permute-start | bytes 3145736 | tf_op jit(solution)/shard_map/ppermute | solution.py:425
  104.3 17.9 %collective-permute-start.24 = (bf16[2,4,32,1280]{3,2,1,0:T(8,128)(2,1)}, bf16[2,4,32,1280]{3,2,1,0:T(8,128)(2,1)S(1)}, u32[]{:S(2)}, u32[]{:S(2)}) collective-permute-start(bf16[2,4,32,1280]{3,2,1,0:T(8,128)(2,1)} %get-tuple-element.121), channel_id=1, source_target_pairs={{0,8},{8,0},{16,24},{24,16},{1,9},{9,1},{17,25},{25,17},{2,10},{10... | collective-permute-start | bytes 1966088 | tf_op jit(solution)/shard_map/ppermute | solution.py:422
  105.6 17.0 %collective-permute-start.25 = (bf16[2,4,32,1280]{3,2,1,0:T(8,128)(2,1)}, bf16[2,4,32,1280]{3,2,1,0:T(8,128)(2,1)S(1)}, u32[]{:S(2)}, u32[]{:S(2)}) collective-permute-start(bf16[2,4,32,1280]{3,2,1,0:T(8,128)(2,1)} %get-tuple-element.122), channel_id=1, source_target_pairs={{0,16},{8,24},{16,0},{24,8},{1,17},{9,25},{17,1},{25,9},{2,18},{10... | collective-permute-start | bytes 1966088 | tf_op jit(solution)/shard_map/ppermute | solution.py:422
  107.7 13.8 %collective-permute-start.27 = (bf16[256,1024]{1,0:T(8,128)(2,1)S(1)}, bf16[256,1024]{1,0:T(8,128)(2,1)S(1)}, u32[]{:S(2)}, u32[]{:S(2)}) collective-permute-start(bf16[256,1024]{1,0:T(8,128)(2,1)S(1)} %get-tuple-element.126), channel_id=1, source_target_pairs={{0,2},{1,3},{2,0},{3,1},{4,6},{5,7},{6,4},{7,5},{8,10},{9,11},{10,... | collective-permute-start | bytes 1572872 | tf_op jit(solution)/shard_map/ppermute | solution.py:419
  122.7 14.3 %collective-permute-start.28 = (bf16[128,1024]{1,0:T(8,128)(2,1)}, bf16[128,1024]{1,0:T(8,128)(2,1)S(1)}, u32[]{:S(2)}, u32[]{:S(2)}) collective-permute-start(bf16[128,1024]{1,0:T(8,128)(2,1)} %get-tuple-element.130), channel_id=1, source_target_pairs={{0,4},{1,5},{2,6},{3,7},{4,0},{5,1},{6,2},{7,3},{8,12},{9,13},{10,... | collective-permute-start | bytes 786440 | tf_op jit(solution)/shard_map/ppermute | solution.py:419
  127.7 9.4 %collective-permute-start.29 = (bf16[4,32,1280]{2,1,0:T(8,128)(2,1)}, bf16[4,32,1280]{2,1,0:T(8,128)(2,1)S(1)}, u32[]{:S(2)}, u32[]{:S(2)}) collective-permute-start(bf16[4,32,1280]{2,1,0:T(8,128)(2,1)} %get-tuple-element.137), channel_id=1, source_target_pairs={{0,8},{8,0},{16,24},{24,16},{1,9},{9,1},{17,25},{25,17},{2,10},{10... | collective-permute-start | bytes 983048 | tf_op jit(solution)/shard_map/ppermute | solution.py:422
  129.0 8.4 %collective-permute-start.30 = (bf16[4,32,1280]{2,1,0:T(8,128)(2,1)S(1)}, bf16[4,32,1280]{2,1,0:T(8,128)(2,1)S(1)}, u32[]{:S(2)}, u32[]{:S(2)}) collective-permute-start(bf16[4,32,1280]{2,1,0:T(8,128)(2,1)S(1)} %get-tuple-element.138), channel_id=1, source_target_pairs={{0,16},{8,24},{16,0},{24,8},{1,17},{9,25},{17,1},{25,9},{2,18},{10... | collective-permute-start | bytes 983048 | tf_op jit(solution)/shard_map/ppermute | solution.py:422
  137.6 8.9 %collective-permute-start.31 = (bf16[64,2560]{1,0:T(8,128)(2,1)S(1)}, bf16[64,2560]{1,0:T(8,128)(2,1)S(1)}, u32[]{:S(2)}, u32[]{:S(2)}) collective-permute-start(bf16[64,2560]{1,0:T(8,128)(2,1)S(1)} %get-tuple-element.140), channel_id=1, source_target_pairs={{0,2},{1,3},{2,0},{3,1},{4,6},{5,7},{6,4},{7,5},{8,10},{9,11},{10,... | collective-permute-start | bytes 983048 | tf_op jit(solution)/shard_map/ppermute | solution.py:419
  146.6 9.9 %collective-permute-start.33 = (bf16[32,2560]{1,0:T(8,128)(2,1)S(1)}, bf16[32,2560]{1,0:T(8,128)(2,1)S(1)}, u32[]{:S(2)}, u32[]{:S(2)}) collective-permute-start(bf16[32,2560]{1,0:T(8,128)(2,1)S(1)} %get-tuple-element.143), channel_id=1, source_target_pairs={{0,4},{1,5},{2,6},{3,7},{4,0},{5,1},{6,2},{7,3},{8,12},{9,13},{10,... | collective-permute-start | bytes 491528 | tf_op jit(solution)/shard_map/ppermute | solution.py:419
  149.2 10.9 %collective-permute-start.38 = (bf16[128,1024]{1,0:T(8,128)(2,1)S(1)}, bf16[128,1024]{1,0:T(8,128)(2,1)S(1)}, u32[]{:S(2)}, u32[]{:S(2)}) collective-permute-start(bf16[128,1024]{1,0:T(8,128)(2,1)S(1)} %multiply_convert_fusion.refs_0_), channel_id=1, source_target_pairs={{0,24},{8,16},{16,8},{24,0},{1,25},{9,17},{17,9},{25,1},{2,26},{10... | collective-permute-start | bytes 786440 | tf_op jit(solution)/shard_map/ppermute | solution.py:422
  150.5 16.2 %collective-permute-start.37 = (bf16[128,1024]{1,0:T(8,128)(2,1)S(1)}, bf16[128,1024]{1,0:T(8,128)(2,1)S(1)}, u32[]{:S(2)}, u32[]{:S(2)}) collective-permute-start(bf16[128,1024]{1,0:T(8,128)(2,1)S(1)} %multiply_convert_fusion.refs_0_), channel_id=1, source_target_pairs={{0,16},{8,24},{16,0},{24,8},{1,17},{9,25},{17,1},{25,9},{2,18},{10... | collective-permute-start | bytes 786440 | tf_op jit(solution)/shard_map/ppermute | solution.py:422
  156.6 11.6 %collective-permute-start.36 = (bf16[32,2560]{1,0:T(8,128)(2,1)S(1)}, bf16[32,2560]{1,0:T(8,128)(2,1)S(1)}, u32[]{:S(2)}, u32[]{:S(2)}) collective-permute-start(bf16[32,2560]{1,0:T(8,128)(2,1)S(1)} %add_convert_fusion.refs_0_), channel_id=1, source_target_pairs={{0,24},{8,16},{16,8},{24,0},{1,25},{9,17},{17,9},{25,1},{2,26},{10... | collective-permute-start | bytes 491528 | tf_op jit(solution)/shard_map/ppermute | solution.py:422
  157.9 12.2 %collective-permute-start.35 = (bf16[32,2560]{1,0:T(8,128)(2,1)S(1)}, bf16[32,2560]{1,0:T(8,128)(2,1)S(1)}, u32[]{:S(2)}, u32[]{:S(2)}) collective-permute-start(bf16[32,2560]{1,0:T(8,128)(2,1)S(1)} %add_convert_fusion.refs_0_), channel_id=1, source_target_pairs={{0,16},{8,24},{16,0},{24,8},{1,17},{9,25},{17,1},{25,9},{2,18},{10... | collective-permute-start | bytes 491528 | tf_op jit(solution)/shard_map/ppermute | solution.py:422
  159.4 10.7 %collective-permute-start.34 = (bf16[32,2560]{1,0:T(8,128)(2,1)S(1)}, bf16[32,2560]{1,0:T(8,128)(2,1)S(1)}, u32[]{:S(2)}, u32[]{:S(2)}) collective-permute-start(bf16[32,2560]{1,0:T(8,128)(2,1)S(1)} %add_convert_fusion.refs_0_), channel_id=1, source_target_pairs={{0,8},{8,0},{16,24},{24,16},{1,9},{9,1},{17,25},{25,17},{2,10},{10... | collective-permute-start | bytes 491528 | tf_op jit(solution)/shard_map/ppermute | solution.py:422
  (27 other events, 272.8 us)
